TPU v7x, 32 devices: a whole 2x2x4 slice. The times are simulated.
32 devices in a mesh: groups: 2 (over y), store: 4 (over z), tensor: 4 (over x, core).
Axes of the slice: x: 2, y: 2, z: 4, core: 2. Of those that a mesh axis runs over, the one named last changes fastest.
Arguments:
- queries: bfloat16 [8, 256, 8192], P(('groups', 'store'), None, 'tensor'), parts along dimension 0, may hold values from -96 to 96
- question_kv: bfloat16 [8, 256, 2048], P(('groups', 'store'), None, 'tensor'), parts along dimension 0, may hold values from -4.2 to 4.2
- key_value_store: bfloat16 [64, 256, 2048], P(('groups', 'store'), None, 'tensor'), parts along dimension 0, may hold values from -6 to 6
- span_store_slot: int32 [64], P('groups'), parts along dimension 0, may hold values from 0 to 31, as said below
- retrieval: int32 [8, 16], P('groups'), parts along dimension 0, may hold values from 0 to 31, as said below
- recompute_rows: int32 [8, 16, 8], P(('groups', 'store')), parts along dimension 0, may hold values from 0 to 255, as said below
- recompute_hidden: bfloat16 [8, 16, 8, 8192], P(('groups', 'store')), parts along dimension 0, may hold values from -6 to 6
- kv_weight: bfloat16 [8192, 2048], P('store', 'tensor'), may hold values from -0.0625 to 0.0625
Outputs:
- attended: bfloat16 [8, 256, 8192], P(('groups', 'store'), None, 'tensor'), parts along dimension 0
- fresh_kv: bfloat16 [8, 16, 8, 2048], P(('groups', 'store'), None, None, 'tensor'), parts along dimension 0
There are 2 independent parts, one for each index of `groups`. A program takes and returns all parts, laid end to end along the dimension named above; an argument that names none is the same for every part. Nothing has to cross between parts.
Inputs may be any that keep to these rules, and one draw needn't show every extreme that they name: A permutation: span c is kept in store slot span_store_slot[c], and slot g lies with store index g // 8. `retrieval`: span ids; the spans of one request lie on at most 4 per store index, and every request reaches that number on some store index; spans of one request are distinct. `recompute_rows`: distinct within each request's span.
All inputs are finite; a program needn't handle non-finite values.
Results may differ from a plain program's by a relative error of at most 0.0051.
Values may be sent and summed in bfloat16 or wider, within the bound.
No kernel may reach another device: no remote copies, remote signals or barrier semaphores. Data moves between devices by JAX's collectives and lax.ppermute only.
A program may use at most 128 MiB of HBM per device.

v0:
```python
import jax
import jax.numpy as jnp
from jax import lax
from jax.sharding import PartitionSpec as P

HEAD_WIDTH = 128


def attend_rows(query_block, key_rows, value_rows, visible, score_scale):
    scores = jnp.dot(query_block, key_rows.T, preferred_element_type=jnp.float32) * score_scale
    scores = jnp.where(visible, scores, -jnp.inf)
    highest = jnp.max(scores, axis=1, keepdims=True)
    weights = jnp.exp(scores - highest)
    row_total = jnp.sum(weights, axis=1, keepdims=True)
    blended = jnp.dot(weights.astype(jnp.bfloat16), value_rows, preferred_element_type=jnp.float32)
    return (blended / row_total).astype(jnp.bfloat16)


def local(
    queries,
    question_kv,
    key_value_store,
    span_store_slot,
    retrieval,
    recompute_rows,
    recompute_hidden,
    kv_weight,
):
    n_store = lax.axis_size("store")
    myself = lax.axis_index("store")
    slot_count, span_len, kv_cols = key_value_store.shape
    span_count = retrieval.shape[1]
    recomp = recompute_rows.shape[2]
    model_width = recompute_hidden.shape[3]
    per_pair = max(1, span_count // n_store)
    hidden = recompute_hidden[0].reshape(span_count * recomp, model_width)
    fresh_kv = jnp.dot(
        hidden,
        lax.all_gather(kv_weight, "store", axis=0, tiled=True),
        preferred_element_type=jnp.float32,
    ).astype(jnp.bfloat16)
    home_slots = span_store_slot[retrieval]
    owners = home_slots // slot_count
    position_in_piece = home_slots - owners * slot_count
    shared = owners[:, :, None] == owners[:, None, :]
    column = jnp.arange(span_count, dtype=jnp.int32)
    before = column[None, :] < column[:, None]
    occurrence = jnp.sum((shared & before[None]).astype(jnp.int32), axis=2)
    partner_index = jnp.arange(n_store, dtype=jnp.int32)
    wanted = (owners[partner_index][:, None, :] == myself) & (
        occurrence[partner_index][:, None, :]
        == jnp.arange(per_pair, dtype=jnp.int32)[None, :, None]
    )
    local_slot = jnp.sum(jnp.where(wanted, position_in_piece[partner_index][:, None, :], 0), axis=2)
    outbox = key_value_store[local_slot.reshape(-1)].reshape(n_store, per_pair, span_len, kv_cols)
    received = lax.all_to_all(outbox, "store", split_axis=0, concat_axis=0, tiled=True)
    source_pos = owners[myself]
    fetched = received.reshape(n_store * per_pair, span_len, kv_cols)[
        source_pos * per_pair + occurrence[myself]
    ]
    fetched = fetched.at[column[:, None], recompute_rows[0]].set(
        fresh_kv.reshape(span_count, recomp, kv_cols)
    )
    question_len = queries.shape[1]
    heads_dev = queries.shape[2] // HEAD_WIDTH
    kv_heads_dev = kv_cols // (2 * HEAD_WIDTH)
    group_size = heads_dev // kv_heads_dev
    context_len = span_count * span_len
    total_len = context_len + question_len
    context_kv = jnp.concatenate([fetched.reshape(context_len, kv_cols), question_kv[0]], axis=0)
    context_kv = context_kv.reshape(total_len, kv_heads_dev, 2, HEAD_WIDTH)
    key_place = jnp.arange(total_len, dtype=jnp.int32)
    query_place = jnp.arange(question_len, dtype=jnp.int32)
    visible = (key_place[None, :] < context_len) | (
        key_place[None, :] - context_len <= query_place[:, None]
    )
    visible_pair = jnp.concatenate([visible, visible], axis=0)
    query_rows = queries[0].reshape(question_len, heads_dev, HEAD_WIDTH)

    def head_pair(pair_index):
        chosen = lax.dynamic_slice_in_dim(query_rows, 2 * pair_index, 2, 1)
        stacked = jnp.transpose(chosen, (1, 0, 2)).reshape(2 * question_len, HEAD_WIDTH)
        head_kv = lax.dynamic_index_in_dim(
            context_kv, 2 * pair_index // group_size, 1, keepdims=False
        )
        blended = attend_rows(
            stacked, head_kv[:, 0], head_kv[:, 1], visible_pair, HEAD_WIDTH ** (-0.5)
        )
        return blended.reshape(2, question_len, HEAD_WIDTH)

    outputs = lax.map(head_pair, jnp.arange(heads_dev // 2, dtype=jnp.int32))
    attended = jnp.transpose(outputs.reshape(heads_dev, question_len, HEAD_WIDTH), (1, 0, 2))
    attended = attended.reshape(1, question_len, heads_dev * HEAD_WIDTH)
    return (attended, fresh_kv.reshape(1, span_count, recomp, kv_cols))


def solution(mesh):
    in_specs = (
        P(("groups", "store"), None, "tensor"),
        P(("groups", "store"), None, "tensor"),
        P(("groups", "store"), None, "tensor"),
        P("groups"),
        P("groups", None),
        P(("groups", "store"), None, None),
        P(("groups", "store"), None, None, None),
        P("store", "tensor"),
    )
    out_specs = (
        P(("groups", "store"), None, "tensor"),
        P(("groups", "store"), None, None, "tensor"),
    )
    return jax.shard_map(local, mesh=mesh, in_specs=in_specs, out_specs=out_specs, check_vma=False)
```

profile of v0, /device:TPU:0, one launch (start us, length us, event | category | flops | bytes accessed | tf_op | source)
XLA Modules:
  0.0 436.4 jit_solution(17501843724904914522)
XLA Ops:
  15.2 6.4 %all-to-all-start = ((bf16[4,4,256,512]{3,2,1,0:T(8,128)(2,1)}), bf16[4,4,256,512]{3,2,1,0:T(8,128)(2,1)}, u32[]{:S(2)}, u32[]{:S(2)}) async-start(bf16[4,4,256,512]{3,2,1,0:T(8,128)(2,1)} %bitcast.60), calls=%async_computation | async-start | bytes 8388608 | tf_op jit(solution)/shard_map/all_to_all | solution.py:56
  26.8 200.8 %all-to-all-done = bf16[4,4,256,512]{3,2,1,0:T(8,128)(2,1)} async-done(((bf16[4,4,256,512]{3,2,1,0:T(8,128)(2,1)}), bf16[4,4,256,512]{3,2,1,0:T(8,128)(2,1)}, u32[]{:S(2)}, u32[]{:S(2)}) %all-to-all-start) | async-done | bytes 4194336 | tf_op jit(solution)/shard_map/all_to_all | solution.py:56
  227.6 5.0 %gather_fusion.5 = bf16[16,256,512]{2,1,0:T(8,128)(2,1)} fusion(bf16[16,256,512]{2,1,0:T(8,128)(2,1)} %bitcast.10, s32[1024]{0:T(1024)S(1)} %pad_clamp_fusion), kind=kCustom, calls=%fused_computation.5 | custom fusion | bytes 8388672 | tf_op jit(solution)/shard_map/gather | solution.py:58
  232.6 17.7 %all-gather.2.cloned.1.call-done = bf16[8192,512]{1,0:T(8,128)(2,1)} async-done(((bf16[2048,512]{1,0:T(8,128)(2,1)}), bf16[8192,512]{1,0:T(8,128)(2,1)}) %all-gather.2.cloned.1.call-update) | async-done | bytes 8388624 | tf_op jit(solution)/shard_map/all_gather | solution.py:39
  250.3 5.3 %fusion.14 = bf16[128,512]{1,0:T(8,128)(2,1)S(1)} fusion(bf16[8192,512]{1,0:T(8,128)(2,1)} %all-gather.2.cloned.1.call-done, bf16[1,16,8,8192]{3,2,1,0:T(8,128)(2,1)} %param.16), kind=kOutput, calls=%fused_computation.26 | convolution fusion | flops 1073807360 | bytes 10616832 | tf_op jit(solution)/shard_map/dot_general | solution.py:37
  255.6 16.7 %scatter_fusion = bf16[16,256,512]{2,1,0:T(8,128)(2,1)} fusion(bf16[16,256,512]{2,1,0:T(8,128)(2,1)} %gather_fusion.5, s32[128]{0:T(128)S(1)} %reshape.250, bf16[128,512]{1,0:T(8,128)(2,1)S(1)} %fusion.14), kind=kCustom, calls=%fused_computation.6 | custom fusion | bytes 394240 | tf_op jit(solution)/shard_map/scatter | solution.py:61
  272.3 6.9 %reshape.259 = bf16[4096,2,2,128]{3,2,1,0:T(2,128)(2,1)} reshape(bf16[16,256,512]{2,1,0:T(8,128)(2,1)} %scatter_fusion) | data formatting | bytes 8388608 | tf_op jit(solution)/shard_map/concatenate | solution.py:70
  279.2 11.3 %copy.34 = bf16[4096,2,2,128]{0,3,2,1:T(8,128)(2,1)} copy(bf16[4096,2,2,128]{3,2,1,0:T(2,128)(2,1)} %reshape.259) | data formatting | bytes 8388608 | tf_op jit(solution)/shard_map/concatenate | solution.py:70
  290.6 4.6 %pad_maximum_fusion = bf16[4352,2,2,128]{0,3,2,1:T(8,128)(2,1)} fusion(bf16[256,2,2,128]{0,3,2,1:T(8,128)(2,1)S(1)} %bitcast.63, bf16[4096,2,2,128]{0,3,2,1:T(8,128)(2,1)} %copy.34), kind=kLoop, calls=%fused_computation.21 | loop fusion | flops 8912896 | bytes 8912896 | tf_op jit(solution)/shard_map/concatenate | solution.py:70
  295.2 131.2 %while.12 = (s32[]{:T(128)}, bf16[8,2,256,128]{3,2,1,0:T(8,128)(2,1)}, s32[8]{0:T(128)S(1)}, bf16[256,16,128]{0,2,1:T(8,128)(2,1)S(1)}, bf16[4352,2,2,128]{0,3,2...) while((s32[]{:T(128)}, ...), condition=%wide.region_6.7_spmd, body=%wide.region_3.6_spmd.sunk | while | flops 1156578304 | bytes 50080656 | solution.py:91
  299.6 4.1 copy.42
  303.9 3.9 fusion.36
  316.0 4.1 copy.42
  320.3 3.9 fusion.36
  332.4 4.1 copy.42
  336.7 3.9 fusion.36
  348.8 4.1 copy.42
  353.1 3.9 fusion.36
  365.3 4.1 copy.42
  369.5 3.9 fusion.36
  381.7 4.1 copy.42
  385.9 3.9 fusion.36
  398.1 4.1 copy.42
  414.5 4.1 copy.42
  (120 shorter events, 85.3 us)
Async XLA Ops:
  7.2 5.3 %copy-start = (bf16[8,256,512]{2,1,0:T(8,128)(2,1)S(1)}, bf16[8,256,512]{2,1,0:T(8,128)(2,1)}, u32[]{:S(2)}) copy-start(bf16[8,256,512]{2,1,0:T(8,128)(2,1)} %param.12) | copy-start | bytes 6291460
  7.2 243.2 %all-gather.2.cloned.1.call-start = ((), (), s32[]{:S(2)}) async-start(), calls=%async_computation.1 | async-start | bytes 10485760 | tf_op jit(solution)/shard_map/all_gather | solution.py:39
  15.2 6.5 %copy-start.5 = (s32[1,16,8]{1,2,0:T(8,128)S(1)}, s32[1,16,8]{1,2,0:T(8,128)}, u32[]{:S(2)}) copy-start(s32[1,16,8]{1,2,0:T(8,128)} %param.15) | copy-start | bytes 1540
  15.2 6.6 %copy-start.4 = (bf16[1,256,512]{2,1,0:T(8,128)(2,1)S(1)}, bf16[1,256,512]{2,1,0:T(8,128)(2,1)}, u32[]{:S(2)}) copy-start(bf16[1,256,512]{2,1,0:T(8,128)(2,1)} %param.11) | copy-start | bytes 786436
  15.2 212.4 %all-to-all-start = ((bf16[4,4,256,512]{3,2,1,0:T(8,128)(2,1)}), bf16[4,4,256,512]{3,2,1,0:T(8,128)(2,1)}, u32[]{:S(2)}, u32[]{:S(2)}) async-start(bf16[4,4,256,512]{3,2,1,0:T(8,128)(2,1)} %bitcast.60), calls=%async_computation | async-start | bytes 8388608 | tf_op jit(solution)/shard_map/all_to_all | solution.py:56
  255.6 23.6 %copy-start.3 = (bf16[128,512]{1,0:T(8,128)(2,1)}, bf16[128,512]{1,0:T(8,128)(2,1)S(1)}, u32[]{:S(2)}) copy-start(bf16[128,512]{1,0:T(8,128)(2,1)S(1)} %fusion.14) | copy-start | bytes 393220
  279.2 11.3 %copy-start.2 = (bf16[1,256,512]{1,2,0:T(8,128)(2,1)S(1)}, bf16[1,256,512]{1,2,0:T(8,128)(2,1)}, u32[]{:S(2)}) copy-start(bf16[1,256,512]{1,2,0:T(8,128)(2,1)} %copy.30) | copy-start | bytes 786436
  307.8 1.6 copy-start.1
  324.2 1.6 copy-start.1
  340.7 1.6 copy-start.1
  357.1 1.6 copy-start.1
  373.5 1.6 copy-start.1
  389.9 1.6 copy-start.1
  406.3 1.6 copy-start.1
  422.7 1.6 copy-start.1
Sparse Core Ops, SparseCore 0:
  9.6 240.7 all-gather.1
where the time goes:
time: 439 us; the launch traced here: 436 us
  waiting for transfers between devices  219 us (50%)
  local copies, waits for them, and re-layouts  124 us (28%)
  matrix products  48 us (11%)
  other arithmetic  19.1 us (4%)
  between operations  14.2 us (3%)
  starting transfers between devices  6.49 us (1%)
  loops' own time  5.51 us (1%)
    all_to_all x1, waiting for transfers between devices, local(): lax.all_to_all(outbox, 'store', split_axis=0, concat_axis=0, tiled=True)  201 us
    dynamic_slice x16, local copies, waits for them, and re-layouts, head_pair(): lax.dynamic_index_in_dim(context_kv, 2 * pair_index // group_size, 1, kee...  58.8 us
    dot_general x8, matrix products, attend_rows(): jnp.dot(query_block, key_rows.T, preferred_element_type=jnp.float32)  31.4 us
    concatenate x2, local copies, waits for them, and re-layouts, local(): jnp.concatenate([fetched.reshape(context_len, kv_cols), question_kv[0]],...  18.2 us
    all_gather x1, waiting for transfers between devices, local(): lax.all_gather(kv_weight, 'store', axis=0, tiled=True)  17.7 us
    scatter x1, local copies, waits for them, and re-layouts, local(): fetched.at[column[:, None], recompute_rows[0]]  16.7 us
    dot_general x8, matrix products, attend_rows(): jnp.dot(weights.astype(jnp.bfloat16), value_rows, preferred_element_type=...  11.3 us
    reduce_sum x8, other arithmetic, attend_rows(): row_total = jnp.sum(weights, axis=1, keepdims=True)  10.8 us
  transfers between devices with their start and end apart: 2, of which 2 were waited for; matrix products, arithmetic and copies ran while one was open for 4% of the time, Pallas kernels for 0%

commit v1 on v0

v1 whole, which is shorter than its diff:
```python
import functools
import math

import jax
import jax.numpy as jnp
from jax import lax
from jax.experimental import pallas as pl
from jax.experimental.pallas import tpu as pltpu
from jax.sharding import PartitionSpec as P

HEAD_WIDTH = 128
EXP_SCALE = math.log2(math.e) * HEAD_WIDTH ** (-0.5)
VMEM_LIMIT = 48 * 1024 * 1024


def any_spec():
    return pl.BlockSpec(memory_space=pl.ANY)


def smem_spec():
    return pl.BlockSpec(memory_space=pltpu.SMEM)


def pack_kernel(spans, distances, with_hidden, n_deps, *refs):
    place_ref, slot_ref, retrieval_ref, store_ref = refs[:4]
    refs = refs[4:]
    if with_hidden:
        hidden_ref, refs = refs[0], refs[1:]
    refs = refs[n_deps:]
    n_out = len(spans) * len(distances) + (len(distances) if with_hidden else 0)
    outs, sems = refs[:n_out], refs[n_out]
    myself = place_ref[0]
    slot_count = store_ref.shape[0]
    copies = []

    def send(source, target):
        copy = pltpu.make_async_copy(source, target, sems.at[len(copies)])
        copy.start()
        copies.append(copy)

    place = 0
    if with_hidden:
        for distance in distances:
            target = outs[place]
            rows, width = target.shape
            first_row = pl.multiple_of(place_ref[1] * rows, rows)
            first_column = pl.multiple_of((myself ^ distance) * width, width)
            send(hidden_ref.at[pl.ds(first_row, rows), pl.ds(first_column, width)], target)
            place += 1
    for distance in distances:
        partner = myself ^ distance
        count = jnp.int32(0)
        chosen = [jnp.int32(0) for _ in spans]
        for j in range(retrieval_ref.shape[1]):
            home = slot_ref[retrieval_ref[partner, j]]
            mine = home // slot_count == myself
            for i, span in enumerate(spans):
                chosen[i] = jnp.where(mine & (count == span), home - myself * slot_count, chosen[i])
            count = count + jnp.where(mine, 1, 0)
        for slot in chosen:
            send(store_ref.at[slot], outs[place])
            place += 1
    for copy in copies:
        copy.wait()


def pack(place, slots, retrieval, store, hidden, spans, distances, deps, hidden_shape=None):
    with_hidden = hidden is not None
    _, span_len, kv_cols = store.shape
    shapes = []
    if with_hidden:
        shapes += [jax.ShapeDtypeStruct(hidden_shape, hidden.dtype)] * len(distances)
    shapes += [jax.ShapeDtypeStruct((span_len, kv_cols), store.dtype)] * (len(spans) * len(distances))
    operands = [place, slots, retrieval, store] + ([hidden] if with_hidden else []) + list(deps)
    outs = pl.pallas_call(
        functools.partial(pack_kernel, tuple(spans), tuple(distances), with_hidden, len(deps)),
        out_shape=shapes,
        in_specs=[smem_spec()] * 3 + [any_spec()] * (len(operands) - 3),
        out_specs=[any_spec()] * len(shapes),
        scratch_shapes=[pltpu.SemaphoreType.DMA((len(shapes),))],
        name="pack_spans",
    )(*operands)
    hidden_pieces = outs[: len(distances)] if with_hidden else []
    rest = outs[len(hidden_pieces) :]
    per = len(spans)
    return list(hidden_pieces), [list(rest[i * per : (i + 1) * per]) for i in range(len(distances))]


def attend_kernel(n_pieces, with_question, with_fresh, first, last, n_deps, *refs):
    table_ref, query_ref, question_ref = refs[:3]
    refs = refs[3:]
    piece_refs, refs = refs[:n_pieces], refs[n_pieces:]
    if with_fresh:
        fresh_ref, refs = refs[0], refs[1:]
    if not first:
        blend_in, stats_in = refs[:2]
        refs = refs[2:]
    refs = refs[n_deps:]
    if last:
        out_ref, refs = refs[0], refs[1:]
    else:
        blend_out, stats_out = refs[:2]
        refs = refs[2:]
    keys, values = refs
    width = HEAD_WIDTH
    question_len = query_ref.shape[0]
    group_size = query_ref.shape[1] // width
    span_len = piece_refs[0].shape[0]
    spare_key = question_ref[0:1, :width].astype(jnp.float32)
    row = lax.broadcasted_iota(jnp.int32, (span_len, width), 0)
    for i in range(n_pieces):
        stale = row < jnp.where(table_ref[i, 0] == 0, span_len, 0)
        for column in range(1, table_ref.shape[1]):
            stale = stale | (row == table_ref[i, column])
        here = pl.ds(i * span_len, span_len)
        block = piece_refs[i][...].astype(jnp.float32)
        keys[here, :] = jnp.where(stale, spare_key, block[:, :width]).astype(keys.dtype)
        values[here, :width] = jnp.where(stale, 0.0, block[:, width:]).astype(values.dtype)
        values[here, width:] = jnp.where(stale, 0.0, 1.0).astype(values.dtype)
    base = n_pieces * span_len
    for ref in ([fresh_ref] if with_fresh else []) + ([question_ref] if with_question else []):
        here = pl.ds(base, ref.shape[0])
        keys[here, :] = ref[:, :width]
        values[here, :width] = ref[:, width:]
        values[here, width:] = jnp.ones((ref.shape[0], width), values.dtype)
        base += ref.shape[0]
    plain = base - (question_len if with_question else 0)
    pair = 2
    rows = pair * question_len
    for start in range(0, group_size, pair):
        query = jnp.concatenate(
            [query_ref[:, h * width : (h + 1) * width] for h in range(start, start + pair)], axis=0
        )
        contract = (((1,), (1,)), ((), ()))
        scores = [
            lax.dot_general(query, keys[:plain, :], contract, preferred_element_type=jnp.float32)
        ]
        if with_question:
            asked = lax.dot_general(
                query, keys[plain:, :], contract, preferred_element_type=jnp.float32
            )
            asked = asked.reshape(pair, question_len, question_len)
            q_place = lax.broadcasted_iota(jnp.int32, asked.shape, 1)
            k_place = lax.broadcasted_iota(jnp.int32, asked.shape, 2)
            asked = jnp.where(k_place <= q_place, asked, -jnp.inf)
            scores.append(asked.reshape(rows, question_len))
        highest = functools.reduce(
            jnp.maximum, [jnp.max(part, axis=1, keepdims=True) for part in scores]
        )
        here = pl.ds(start * question_len, rows)
        if not first:
            stats = stats_in[here, :]
            before = stats[:, :1]
            row_total = stats[:, width // 2 : width // 2 + 1]
            highest = jnp.maximum(highest, before)
            fade = jnp.exp2((before - highest) * EXP_SCALE)
        blend = 0.0
        offset = 0
        for part in scores:
            probs = jnp.exp2((part - highest) * EXP_SCALE).astype(jnp.bfloat16)
            blend = blend + jnp.dot(
                probs,
                values[offset : offset + part.shape[1], :],
                preferred_element_type=jnp.float32,
            )
            offset += part.shape[1]
        total = blend[:, width:]
        blend = blend[:, :width]
        if not first:
            blend = blend + blend_in[here, :] * fade
            total = total + row_total * fade
        if last:
            done = (blend / total).astype(out_ref.dtype)
            for h in range(pair):
                out_ref[:, (start + h) * width : (start + h + 1) * width] = done[
                    h * question_len : (h + 1) * question_len
                ]
        else:
            lane = lax.broadcasted_iota(jnp.int32, (rows, width), 1)
            blend_out[here, :] = blend
            stats_out[here, :] = jnp.where(lane < width // 2, highest, total)


def attend(table, queries, question, pieces, fresh, state, with_question, last, deps):
    question_len, query_cols = queries.shape
    span_len, kv_cols = pieces[0].shape
    kv_heads = kv_cols // (2 * HEAD_WIDTH)
    group_cols = query_cols // kv_heads
    group_rows = group_cols // HEAD_WIDTH * question_len
    first = state is None
    pair_cols = 2 * HEAD_WIDTH

    def by_head(rows, columns):
        return pl.BlockSpec((rows, columns), lambda k: (0, k))

    state_spec = pl.BlockSpec((group_rows, HEAD_WIDTH), lambda k: (k, 0))
    operands = [table, queries, question] + list(pieces)
    specs = [smem_spec(), by_head(question_len, group_cols), by_head(question_len, pair_cols)]
    specs += [by_head(span_len, pair_cols)] * len(pieces)
    length = len(pieces) * span_len + (question_len if with_question else 0)
    if fresh is not None:
        operands.append(fresh)
        specs.append(by_head(fresh.shape[0], pair_cols))
        length += fresh.shape[0]
    if not first:
        operands += list(state)
        specs += [state_spec] * 2
    operands += list(deps)
    specs += [any_spec()] * len(deps)
    if last:
        out_shape = jax.ShapeDtypeStruct(queries.shape, queries.dtype)
        out_specs = by_head(question_len, group_cols)
    else:
        out_shape = [jax.ShapeDtypeStruct((kv_heads * group_rows, HEAD_WIDTH), jnp.float32)] * 2
        out_specs = [state_spec] * 2
    work = query_cols // HEAD_WIDTH * question_len * length
    return pl.pallas_call(
        functools.partial(
            attend_kernel, len(pieces), with_question, fresh is not None, first, last, len(deps)
        ),
        grid=(kv_heads,),
        out_shape=out_shape,
        in_specs=specs,
        out_specs=out_specs,
        scratch_shapes=[
            pltpu.VMEM((length, HEAD_WIDTH), jnp.bfloat16),
            pltpu.VMEM((length, 2 * HEAD_WIDTH), jnp.bfloat16),
        ],
        compiler_params=pltpu.CompilerParams(vmem_limit_bytes=VMEM_LIMIT),
        cost_estimate=pl.CostEstimate(
            flops=work * 8 * HEAD_WIDTH, bytes_accessed=8 * 1024 * 1024, transcendentals=work
        ),
        name="attend_spans",
    )(*operands)


def local(
    queries,
    question_kv,
    key_value_store,
    span_store_slot,
    retrieval,
    recompute_rows,
    recompute_hidden,
    kv_weight,
):
    n_store = lax.axis_size("store")
    n_tensor = lax.axis_size("tensor")
    myself = lax.axis_index("store")
    slot_count, span_len, kv_cols = key_value_store.shape
    span_count = retrieval.shape[1]
    recomp = recompute_rows.shape[2]
    model_width = recompute_hidden.shape[3]
    per_pair = max(1, span_count // n_store)
    fresh_rows = span_count * recomp
    shard_rows = fresh_rows // n_tensor
    shard_width = model_width // n_store
    place = jnp.stack([myself, lax.axis_index("tensor")]).astype(jnp.int32)
    hidden = recompute_hidden.reshape(fresh_rows, model_width)
    question = question_kv[0]
    query_rows = queries[0]

    def exchange(piece, distance):
        if distance == 0:
            return piece
        return lax.ppermute(piece, "store", [(i, i ^ distance) for i in range(n_store)])

    away = list(range(n_store - 1, 0, -1))
    everyone = away + [0]

    owners = span_store_slot[retrieval[myself]] // slot_count
    column = jnp.arange(span_count, dtype=jnp.int32)
    earlier = (owners[:, None] == owners[None, :]) & (column[None, :] < column[:, None])
    rank = jnp.sum(earlier.astype(jnp.int32), axis=1)
    source = myself ^ jnp.arange(n_store, dtype=jnp.int32)
    match = (owners[None, None, :] == source[:, None, None]) & (
        rank[None, None, :] == jnp.arange(per_pair, dtype=jnp.int32)[None, :, None]
    )
    match = match.astype(jnp.int32)
    listed = jnp.concatenate(
        [jnp.ones((span_count, 1), jnp.int32), recompute_rows[0]], axis=1
    )
    table = jnp.sum(match[:, :, :, None] * listed[None, None], axis=2)

    def rows_of(keys):
        return jnp.stack([table[distance, span] for distance, span in keys])

    hidden_out, out = pack(
        place, span_store_slot, retrieval, key_value_store, hidden, [0], everyone, [],
        (shard_rows, shard_width),
    )
    hidden_in = [exchange(piece, d) for piece, d in zip(hidden_out, everyone)]
    rounds = [[exchange(piece[0], d) for piece, d in zip(out[: len(away)], away)]]
    own = [(0, 0, out[-1][0])]
    if per_pair > 1:
        _, out = pack(
            place, span_store_slot, retrieval, key_value_store, None, list(range(1, per_pair)), [0], []
        )
        own += [(0, span, piece) for span, piece in zip(range(1, per_pair), out[0])]
        _, out = pack(place, span_store_slot, retrieval, key_value_store, None, [1], away, [])
        rounds.append([exchange(piece[0], d) for piece, d in zip(out, away)])

    state = attend(
        rows_of([(d, s) for d, s, _ in own]), query_rows, question, [p for _, _, p in own],
        None, None, True, False, [],
    )

    gathered = lax.all_gather(jnp.stack(hidden_in[::-1]), "tensor", axis=0)
    partial = jnp.dot(
        gathered.reshape(n_tensor * n_store * shard_rows, shard_width),
        kv_weight,
        preferred_element_type=jnp.float32,
    )
    partial = partial.reshape(n_tensor, n_store, shard_rows, kv_cols)
    bits = n_store.bit_length() - 1
    partial = partial.reshape((n_tensor,) + (2,) * bits + (shard_rows, kv_cols))
    for bit in range(bits):
        axis = bits - bit
        kept, sent = lax.index_in_dim(partial, 0, axis, False), lax.index_in_dim(partial, 1, axis, False)
        partial = kept + exchange(sent.astype(jnp.bfloat16), 1 << bit).astype(jnp.float32)
    fresh = partial.reshape(fresh_rows, kv_cols).astype(jnp.bfloat16)

    for span in range(per_pair):
        arrived = rounds[span]
        deps = []
        if span + 2 < per_pair:
            _, out = pack(
                place, span_store_slot, retrieval, key_value_store, None, [span + 2], away, arrived
            )
            rounds.append([exchange(piece[0], d) for piece, d in zip(out, away)])
            deps = [out[0][0]]
        batches = [list(range(i, min(i + 4, len(away)))) for i in range(0, len(away), 4)]
        for number, batch in enumerate(batches):
            last = span == per_pair - 1 and number == len(batches) - 1
            with_fresh = span == max(0, per_pair - 2) and number == len(batches) - 1
            result = attend(
                rows_of([(away[i], span) for i in batch]), query_rows, question,
                [arrived[i] for i in batch], fresh if with_fresh else None, state, False, last, deps,
            )
            state = result
    attended = state
    return (attended[None], fresh.reshape(1, span_count, recomp, kv_cols))


def solution(mesh):
    in_specs = (
        P(("groups", "store"), None, "tensor"),
        P(("groups", "store"), None, "tensor"),
        P(("groups", "store"), None, "tensor"),
        P("groups"),
        P("groups", None),
        P(("groups", "store"), None, None),
        P(("groups", "store"), None, None, None),
        P("store", "tensor"),
    )
    out_specs = (
        P(("groups", "store"), None, "tensor"),
        P(("groups", "store"), None, None, "tensor"),
    )
    return jax.shard_map(local, mesh=mesh, in_specs=in_specs, out_specs=out_specs, check_vma=False)
```

time: 439 us -> 276 us (0.63)
  waiting for transfers between devices: 219 us -> 9.19 us
  Pallas kernels: 0 us -> 204 us
  local copies, waits for them, and re-layouts: 124 us -> 13.2 us
  matrix products: 48 us -> 2.99 us
  starting transfers between devices: 6.49 us -> 27.8 us
  other arithmetic: 19.1 us -> 4.16 us
  loops' own time: 5.51 us -> 0 us
    pallas_call x0 -> x10, Pallas kernels: none -> 204 us  [the longest x5 153 us: pack(): pl.pallas_call(functools.partial(pack_kernel, tuple(spans), tuple(distanc...]
    all_to_all x1 -> x0, waiting for transfers between devices: 201 us -> none  [local(): lax.all_to_all(outbox, 'store', split_axis=0, concat_axis=0, tiled=True)]
    dynamic_slice x40 -> x0, local copies, waits for them, and re-layouts: 64.7 us -> none  [the longest x16 58.8 us: head_pair(): lax.dynamic_index_in_dim(context_kv, 2 * pair_index // group_size, 1, kee...]
    dot_general x17 -> x1, matrix products: 48 us -> 2.99 us  [local(): jnp.dot(gathered.reshape(n_tensor * n_store * shard_rows, shard_width), k...]
    ppermute x0 -> x17, starting transfers between devices: none -> 27.8 us  [exchange(): lax.ppermute(piece, 'store', [(i, i ^ distance) for i in range(n_store)])]
    concatenate x4 -> x1, local copies, waits for them, and re-layouts: 18.4 us -> 0.01 us  [local(): jnp.concatenate([jnp.ones((span_count, 1), jnp.int32), recompute_rows[0]]...]
    all_gather x1, waiting for transfers between devices: 17.7 us -> 0.01 us  [local(): gathered = lax.all_gather(jnp.stack(hidden_in[::-1]), 'tensor', axis=0)]
    scatter x1 -> x0, local copies, waits for them, and re-layouts: 16.7 us -> none  [local(): fetched.at[column[:, None], recompute_rows[0]]]
  transfers between devices with their start and end apart: 2 -> 18, of which waited for: 2 -> 2; matrix products, arithmetic and copies ran while one was open for 4% -> 2% of each run, Pallas kernels for 0% -> 52%
where the time goes in v1:
time: 276 us
  Pallas kernels  204 us (74%)
  starting transfers between devices  27.8 us (10%)
  between operations  14.4 us (5%)
  local copies, waits for them, and re-layouts  13.2 us (5%)
  waiting for transfers between devices  9.19 us (3%)
  other arithmetic  4.16 us (2%)
  matrix products  2.99 us (1%)
    pallas_call x5, Pallas kernels, pack(): pl.pallas_call(functools.partial(pack_kernel, tuple(spans), tuple(distanc...  153 us
    pallas_call x5, Pallas kernels, attend(): pl.pallas_call(functools.partial(attend_kernel, len(pieces), with_questio...  51.5 us
    ppermute x17, starting transfers between devices, exchange(): lax.ppermute(piece, 'store', [(i, i ^ distance) for i in range(n_store)])  27.8 us
    unnamed x58, local copies, waits for them, and re-layouts  12 us
    ppermute x17, waiting for transfers between devices, exchange(): lax.ppermute(piece, 'store', [(i, i ^ distance) for i in range(n_store)])  9.17 us
  transfers between devices with their start and end apart: 18, of which 2 were waited for; matrix products, arithmetic and copies ran while one was open for 2% of the time, Pallas kernels for 52%

profile of v1, /device:TPU:0, one launch (start us, length us, event | category | flops | bytes accessed | tf_op | source)
XLA Modules:
  0.0 276.0 jit_solution(13813715005118514079)
XLA Ops:
  7.8 49.5 %pack_spans.7 = (bf16[32,2048]{1,0:T(8,128)(2,1)}, bf16[32,2048]{1,0:T(8,128)(2,1)}, bf16[32,2048]{1,0:T(8,128)(2,1)}, bf16[32,2048]{1,0:T(8,128)(2,1)}, bf16[25...) custom-call(s32[2]{0:T(128)} %pad_add_fusion.5.refs_0_, ...), custom_call_target="tpu_custom_call" | custom-call | tf_op jit(solution)/shard_map/pack_spans/pallas_call | solution.py:75
  57.3 4.1 %collective-permute-start.13 = (bf16[32,2048]{1,0:T(8,128)(2,1)}, bf16[32,2048]{1,0:T(8,128)(2,1)S(1)}, u32[]{:S(2)}, u32[]{:S(2)}) collective-permute-start(bf16[32,2048]{1,0:T(8,128)(2,1)} %get-tuple-element.44), channel_id=1, source_target_pairs={{0,8},{4,12},{8,0},{12,4},{1,9},{5,13},{9,1},{13,5},{2,10},{6,14},... | collective-permute-start | bytes 393224 | tf_op jit(solution)/shard_map/ppermute | solution.py:266
  61.4 1.3 collective-permute-start.14
  63.0 8.6 %collective-permute-done.13 = bf16[32,2048]{1,0:T(8,128)(2,1)S(1)} collective-permute-done((bf16[32,2048]{1,0:T(8,128)(2,1)}, bf16[32,2048]{1,0:T(8,128)(2,1)S(1)}, u32[]{:S(2)}, u32[]{:S(2)}) %collective-permute-start.13) | collective-permute-done | bytes 131104 | tf_op jit(solution)/shard_map/ppermute | solution.py:266
  72.2 1.8 pad_maximum_fusion
  73.9 3.6 %collective-permute-start.6 = (bf16[256,512]{1,0:T(8,128)(2,1)}, bf16[256,512]{1,0:T(8,128)(2,1)S(1)}, u32[]{:S(2)}, u32[]{:S(2)}) collective-permute-start(bf16[256,512]{1,0:T(8,128)(2,1)} %get-tuple-element.36), channel_id=1, source_target_pairs={{0,12},{4,8},{8,4},{12,0},{1,13},{5,9},{9,5},{13,1},{2,14},{6,10},... | collective-permute-start | bytes 786440 | tf_op jit(solution)/shard_map/ppermute | solution.py:266
  78.7 25.8 %pack_spans.5 = (bf16[256,512]{1,0:T(8,128)(2,1)}, bf16[256,512]{1,0:T(8,128)(2,1)}, bf16[256,512]{1,0:T(8,128)(2,1)}) custom-call(s32[2]{0:T(128)} %pad_add_fusion.5.refs_0_, s32[32]{0:T(128)} %refs_1_.9, s32[4,16]{1,0:T(4,128)} %refs_2_.9, bf16[8,256,512]{2,1,0:T(8,128)(2,1)} %refs_3_.9), custom_call_target="tpu_custom_call" | custom-call | tf_op jit(solution)/shard_map/pack_spans/pallas_call | solution.py:75
  104.5 3.3 %collective-permute-start = (bf16[256,512]{1,0:T(8,128)(2,1)}, bf16[256,512]{1,0:T(8,128)(2,1)S(1)}, u32[]{:S(2)}, u32[]{:S(2)}) collective-permute-start(bf16[256,512]{1,0:T(8,128)(2,1)} %get-tuple-element.30), channel_id=1, source_target_pairs={{0,12},{4,8},{8,4},{12,0},{1,13},{5,9},{9,5},{13,1},{2,14},{6,10},... | collective-permute-start | bytes 786440 | tf_op jit(solution)/shard_map/ppermute | solution.py:266
  107.8 25.8 %pack_spans.9 = (bf16[256,512]{1,0:T(8,128)(2,1)}, bf16[256,512]{1,0:T(8,128)(2,1)}, bf16[256,512]{1,0:T(8,128)(2,1)}) custom-call(s32[2]{0:T(128)} %pad_add_fusion.5.refs_0_, s32[32]{0:T(128)} %refs_1_.9, s32[4,16]{1,0:T(4,128)} %refs_2_.9, bf16[8,256,512]{2,1,0:T(8,128)(2,1)} %refs_3_.9), custom_call_target="tpu_custom_call" | custom-call | tf_op jit(solution)/shard_map/pack_spans/pallas_call | solution.py:75
  142.4 9.8 %attend_spans.5 = (f32[4096,128]{1,0:T(8,128)S(1)}, f32[4096,128]{1,0:T(8,128)}) custom-call(s32[4,9]{1,0:T(4,128)S(1)} %pad_add_fusion.4.refs_0_, bf16[256,2048]{1,0:T(8,128)(2,1)S(1)} %bitcast.60, bf16[256,512]{1,0:T(8,128)(2,1)S(1)} %bitcast.65, bf16[256,512]{1,0:T(8,128)(2,1)S(1)} %copy-done.16, bf16[256,512]{1,0:T(8,128)(2,1)S(1)} %copy-done.19, ...), custom_call_target="tpu_custom_call" | custom-call | flops 5368709120 | bytes 8388608 | tf_op jit(solution)/shard_map/attend_spans/pallas_call | solution.py:217
  152.2 1.3 copy-done.22
  156.2 25.8 %pack_spans.8 = (bf16[256,512]{1,0:T(8,128)(2,1)}, bf16[256,512]{1,0:T(8,128)(2,1)}, bf16[256,512]{1,0:T(8,128)(2,1)}) custom-call(s32[2]{0:T(128)} %pad_add_fusion.5.refs_0_, s32[32]{0:T(128)} %refs_1_.9, s32[4,16]{1,0:T(4,128)} %refs_2_.9, bf16[8,256,512]{2,1,0:T(8,128)(2,1)} %refs_3_.9, bf16[256,512]{1,0:T(8,128)(2,1)} %copy-done.5, ...), custom_call_target="tpu_custom_call" | custom-call | tf_op jit(solution)/shard_map/pack_spans/pallas_call | solution.py:75
  182.0 3.3 %collective-permute-start.9 = (bf16[256,512]{1,0:T(8,128)(2,1)}, bf16[256,512]{1,0:T(8,128)(2,1)}, u32[]{:S(2)}, u32[]{:S(2)}) collective-permute-start(bf16[256,512]{1,0:T(8,128)(2,1)} %get-tuple-element.39.refs_8_), channel_id=1, source_target_pairs={{0,12},{4,8},{8,4},{12,0},{1,13},{5,9},{9,5},{13,1},{2,14},{6,10},... | collective-permute-start | bytes 786440 | tf_op jit(solution)/shard_map/ppermute | solution.py:266
  187.2 25.8 %pack_spans.6 = (bf16[256,512]{1,0:T(8,128)(2,1)}, bf16[256,512]{1,0:T(8,128)(2,1)}, bf16[256,512]{1,0:T(8,128)(2,1)}) custom-call(s32[2]{0:T(128)} %pad_add_fusion.5.refs_0_, s32[32]{0:T(128)} %refs_1_.9, s32[4,16]{1,0:T(4,128)} %refs_2_.9, bf16[8,256,512]{2,1,0:T(8,128)(2,1)} %refs_3_.9, bf16[256,512]{1,0:T(8,128)(2,1)} %copy-done.1, ...), custom_call_target="tpu_custom_call" | custom-call | tf_op jit(solution)/shard_map/pack_spans/pallas_call | solution.py:75
  212.9 3.3 %collective-permute-start.3 = (bf16[256,512]{1,0:T(8,128)(2,1)}, bf16[256,512]{1,0:T(8,128)(2,1)}, u32[]{:S(2)}, u32[]{:S(2)}) collective-permute-start(bf16[256,512]{1,0:T(8,128)(2,1)} %get-tuple-element.33.refs_8_), channel_id=1, source_target_pairs={{0,12},{4,8},{8,4},{12,0},{1,13},{5,9},{9,5},{13,1},{2,14},{6,10},... | collective-permute-start | bytes 786440 | tf_op jit(solution)/shard_map/ppermute | solution.py:266
  216.3 3.0 %fusion = f32[4,2,2,32,512]{4,3,2,1,0:T(8,128)S(1)} fusion(bf16[4,2,2,32,2048]{4,3,2,1,0:T(8,128)(2,1)} %bitcast.92, bf16[2048,512]{1,0:T(8,128)(2,1)S(1)} %copy-done), kind=kOutput, calls=%fused_computation.1 | convolution fusion | flops 1073741824 | bytes 5242880 | tf_op jit(solution)/shard_map/dot_general | solution.py:309
  219.5 10.7 %attend_spans.6 = (f32[4096,128]{1,0:T(8,128)S(1)}, f32[4096,128]{1,0:T(8,128)}) custom-call(s32[3,9]{1,0:T(4,128)S(1)} %pad_add_fusion.3.refs_0_, bf16[256,2048]{1,0:T(8,128)(2,1)S(1)} %bitcast.61, bf16[256,512]{1,0:T(8,128)(2,1)S(1)} %bitcast.66, bf16[256,512]{1,0:T(8,128)(2,1)S(1)} %copy-done.6, bf16[256,512]{1,0:T(8,128)(2,1)S(1)} %copy-done.8, ...), custom_call_target="tpu_custom_call" | custom-call | flops 3221225472 | bytes 8388608 | tf_op jit(solution)/shard_map/attend_spans/pallas_call | solution.py:217
  230.2 1.3 copy-done.24
  232.8 10.9 %attend_spans.7 = (f32[4096,128]{1,0:T(8,128)S(1)}, f32[4096,128]{1,0:T(8,128)}) custom-call(s32[3,9]{1,0:T(4,128)S(1)} %pad_add_fusion.2.refs_0_, bf16[256,2048]{1,0:T(8,128)(2,1)S(1)} %bitcast.62, bf16[256,512]{1,0:T(8,128)(2,1)S(1)} %bitcast.67, bf16[256,512]{1,0:T(8,128)(2,1)S(1)} %copy-done.2, bf16[256,512]{1,0:T(8,128)(2,1)S(1)} %copy-done.4, ...), custom_call_target="tpu_custom_call" | custom-call | flops 3221225472 | bytes 8388608 | tf_op jit(solution)/shard_map/attend_spans/pallas_call | solution.py:217
  243.7 1.3 copy-done.23
  245.0 1.8 collective-permute-start.4
  246.9 2.0 collective-permute-start.5
  248.9 10.1 %attend_spans.8 = (f32[4096,128]{1,0:T(8,128)S(1)}, f32[4096,128]{1,0:T(8,128)}) custom-call(s32[3,9]{1,0:T(4,128)S(1)} %pad_add_fusion.1.refs_0_, bf16[256,2048]{1,0:T(8,128)(2,1)S(1)} %bitcast.63, bf16[256,512]{1,0:T(8,128)(2,1)S(1)} %bitcast.68, bf16[256,512]{1,0:T(8,128)(2,1)} %collective-permute-done.9.refs_3_, ...), custom_call_target="tpu_custom_call" | custom-call | flops 3758096384 | bytes 8388608 | tf_op jit(solution)/shard_map/attend_spans/pallas_call | solution.py:217
  259.1 10.0 %attend_spans.9 = bf16[256,2048]{1,0:T(8,128)(2,1)} custom-call(s32[3,9]{1,0:T(4,128)S(1)} %pad_add_fusion.refs_0_, bf16[256,2048]{1,0:T(8,128)(2,1)S(1)} %bitcast.64, bf16[256,512]{1,0:T(8,128)(2,1)S(1)} %bitcast.69, bf16[256,512]{1,0:T(8,128)(2,1)} %collective-permute-done.3.refs_3_, bf16[256,512]{1,0:T(8,128)(2,1)S(1)} %collective-permute-done.4.refs_4_, ...), custom_call_target="tpu_custom_call" | custom-call | flops 3221225472 | bytes 8388608 | tf_op jit(solution)/shard_map/attend_spans/pallas_call | solution.py:217
  (104 shorter events, 17.3 us)
Async XLA Ops:
  7.2 209.1 %copy-start = (bf16[2048,512]{1,0:T(8,128)(2,1)S(1)}, bf16[2048,512]{1,0:T(8,128)(2,1)}, u32[]{:S(2)}) copy-start(bf16[2048,512]{1,0:T(8,128)(2,1)} %param.15) | copy-start | bytes 6291460
  7.2 209.1 %all-gather.3.cloned.1.call-start = ((), (), s32[]{:S(2)}) async-start(), calls=%async_computation | async-start | bytes 2621440 | tf_op jit(solution)/shard_map/all_gather | solution.py:308
  57.3 14.3 %collective-permute-start.13 = (bf16[32,2048]{1,0:T(8,128)(2,1)}, bf16[32,2048]{1,0:T(8,128)(2,1)S(1)}, u32[]{:S(2)}, u32[]{:S(2)}) collective-permute-start(bf16[32,2048]{1,0:T(8,128)(2,1)} %get-tuple-element.44), channel_id=1, source_target_pairs={{0,8},{4,12},{8,0},{12,4},{1,9},{5,13},{9,1},{13,5},{2,10},{6,14},... | collective-permute-start | bytes 393224 | tf_op jit(solution)/shard_map/ppermute | solution.py:266
  61.4 10.2 %collective-permute-start.14 = (bf16[32,2048]{1,0:T(8,128)(2,1)}, bf16[32,2048]{1,0:T(8,128)(2,1)S(1)}, u32[]{:S(2)}, u32[]{:S(2)}) collective-permute-start(bf16[32,2048]{1,0:T(8,128)(2,1)} %get-tuple-element.45), channel_id=1, source_target_pairs={{0,12},{4,8},{8,4},{12,0},{1,13},{5,9},{9,5},{13,1},{2,14},{6,10},... | collective-permute-start | bytes 393224 | tf_op jit(solution)/shard_map/ppermute | solution.py:266
  62.8 9.4 %collective-permute-start.12 = (bf16[32,2048]{1,0:T(8,128)(2,1)}, bf16[32,2048]{1,0:T(8,128)(2,1)S(1)}, u32[]{:S(2)}, u32[]{:S(2)}) collective-permute-start(bf16[32,2048]{1,0:T(8,128)(2,1)} %get-tuple-element.43), channel_id=1, source_target_pairs={{0,4},{4,0},{8,12},{12,8},{1,5},{5,1},{9,13},{13,9},{2,6},{6,2},{1... | collective-permute-start | bytes 393224 | tf_op jit(solution)/shard_map/ppermute | solution.py:266
  73.9 79.6 %collective-permute-start.6 = (bf16[256,512]{1,0:T(8,128)(2,1)}, bf16[256,512]{1,0:T(8,128)(2,1)S(1)}, u32[]{:S(2)}, u32[]{:S(2)}) collective-permute-start(bf16[256,512]{1,0:T(8,128)(2,1)} %get-tuple-element.36), channel_id=1, source_target_pairs={{0,12},{4,8},{8,4},{12,0},{1,13},{5,9},{9,5},{13,1},{2,14},{6,10},... | collective-permute-start | bytes 786440 | tf_op jit(solution)/shard_map/ppermute | solution.py:266
  77.5 77.3 %collective-permute-start.7 = (bf16[256,512]{1,0:T(8,128)(2,1)}, bf16[256,512]{1,0:T(8,128)(2,1)S(1)}, u32[]{:S(2)}, u32[]{:S(2)}) collective-permute-start(bf16[256,512]{1,0:T(8,128)(2,1)} %get-tuple-element.37), channel_id=1, source_target_pairs={{0,8},{4,12},{8,0},{12,4},{1,9},{5,13},{9,1},{13,5},{2,10},{6,14},... | collective-permute-start | bytes 786440 | tf_op jit(solution)/shard_map/ppermute | solution.py:266
  78.2 56.1 %copy-start.25 = (s32[32]{0:T(128)S(1)}, s32[32]{0:T(128)}, u32[]{:S(2)}) copy-start(s32[32]{0:T(128)} %refs_1_.9) | copy-start | bytes 388
  78.2 56.8 %copy-start.26 = (s32[1,16,8]{1,2,0:T(8,128)S(1)}, s32[1,16,8]{1,2,0:T(8,128)}, u32[]{:S(2)}) copy-start(s32[1,16,8]{1,2,0:T(8,128)} %param.13) | copy-start | bytes 1540
  78.2 76.6 %collective-permute-start.8 = (bf16[256,512]{1,0:T(8,128)(2,1)}, bf16[256,512]{1,0:T(8,128)(2,1)S(1)}, u32[]{:S(2)}, u32[]{:S(2)}) collective-permute-start(bf16[256,512]{1,0:T(8,128)(2,1)} %get-tuple-element.38), channel_id=1, source_target_pairs={{0,4},{4,0},{8,12},{12,8},{1,5},{5,1},{9,13},{13,9},{2,6},{6,2},{1... | collective-permute-start | bytes 786440 | tf_op jit(solution)/shard_map/ppermute | solution.py:266
  104.5 80.8 %collective-permute-start = (bf16[256,512]{1,0:T(8,128)(2,1)}, bf16[256,512]{1,0:T(8,128)(2,1)S(1)}, u32[]{:S(2)}, u32[]{:S(2)}) collective-permute-start(bf16[256,512]{1,0:T(8,128)(2,1)} %get-tuple-element.30), channel_id=1, source_target_pairs={{0,12},{4,8},{8,4},{12,0},{1,13},{5,9},{9,5},{13,1},{2,14},{6,10},... | collective-permute-start | bytes 786440 | tf_op jit(solution)/shard_map/ppermute | solution.py:266
  107.8 78.7 %collective-permute-start.1 = (bf16[256,512]{1,0:T(8,128)(2,1)}, bf16[256,512]{1,0:T(8,128)(2,1)S(1)}, u32[]{:S(2)}, u32[]{:S(2)}) collective-permute-start(bf16[256,512]{1,0:T(8,128)(2,1)} %get-tuple-element.31), channel_id=1, source_target_pairs={{0,8},{4,12},{8,0},{12,4},{1,9},{5,13},{9,1},{13,5},{2,10},{6,14},... | collective-permute-start | bytes 786440 | tf_op jit(solution)/shard_map/ppermute | solution.py:266
  153.5 32.9 %collective-permute-start.2 = (bf16[256,512]{1,0:T(8,128)(2,1)}, bf16[256,512]{1,0:T(8,128)(2,1)}, u32[]{:S(2)}, u32[]{:S(2)}) collective-permute-start(bf16[256,512]{1,0:T(8,128)(2,1)} %get-tuple-element.32), channel_id=1, source_target_pairs={{0,4},{4,0},{8,12},{12,8},{1,5},{5,1},{9,13},{13,9},{2,6},{6,2},{1... | collective-permute-start | bytes 786440 | tf_op jit(solution)/shard_map/ppermute | solution.py:266
  182.0 64.9 %collective-permute-start.9 = (bf16[256,512]{1,0:T(8,128)(2,1)}, bf16[256,512]{1,0:T(8,128)(2,1)}, u32[]{:S(2)}, u32[]{:S(2)}) collective-permute-start(bf16[256,512]{1,0:T(8,128)(2,1)} %get-tuple-element.39.refs_8_), channel_id=1, source_target_pairs={{0,12},{4,8},{8,4},{12,0},{1,13},{5,9},{9,5},{13,1},{2,14},{6,10},... | collective-permute-start | bytes 786440 | tf_op jit(solution)/shard_map/ppermute | solution.py:266
  185.3 63.7 %collective-permute-start.10 = (bf16[256,512]{1,0:T(8,128)(2,1)}, bf16[256,512]{1,0:T(8,128)(2,1)}, u32[]{:S(2)}, u32[]{:S(2)}) collective-permute-start(bf16[256,512]{1,0:T(8,128)(2,1)} %get-tuple-element.40), channel_id=1, source_target_pairs={{0,8},{4,12},{8,0},{12,4},{1,9},{5,13},{9,1},{13,5},{2,10},{6,14},... | collective-permute-start | bytes 786440 | tf_op jit(solution)/shard_map/ppermute | solution.py:266
  185.3 63.6 %collective-permute-start.11 = (bf16[256,512]{1,0:T(8,128)(2,1)}, bf16[256,512]{1,0:T(8,128)(2,1)}, u32[]{:S(2)}, u32[]{:S(2)}) collective-permute-start(bf16[256,512]{1,0:T(8,128)(2,1)} %get-tuple-element.41), channel_id=1, source_target_pairs={{0,4},{4,0},{8,12},{12,8},{1,5},{5,1},{9,13},{13,9},{2,6},{6,2},{1... | collective-permute-start | bytes 786440 | tf_op jit(solution)/shard_map/ppermute | solution.py:266
  212.9 46.1 %collective-permute-start.3 = (bf16[256,512]{1,0:T(8,128)(2,1)}, bf16[256,512]{1,0:T(8,128)(2,1)}, u32[]{:S(2)}, u32[]{:S(2)}) collective-permute-start(bf16[256,512]{1,0:T(8,128)(2,1)} %get-tuple-element.33.refs_8_), channel_id=1, source_target_pairs={{0,12},{4,8},{8,4},{12,0},{1,13},{5,9},{9,5},{13,1},{2,14},{6,10},... | collective-permute-start | bytes 786440 | tf_op jit(solution)/shard_map/ppermute | solution.py:266
  219.3 12.2 %collective-permute-start.15 = (bf16[4,2,32,512]{3,2,1,0:T(8,128)(2,1)S(1)}, bf16[4,2,32,512]{3,2,1,0:T(8,128)(2,1)S(1)}, u32[]{:S(2)}, u32[]{:S(2)}) collective-permute-start(bf16[4,2,32,512]{3,2,1,0:T(8,128)(2,1)S(1)} %fusion.3), channel_id=1, source_target_pairs={{0,4},{4,0},{8,12},{12,8},{1,5},{5,1},{9,13},{13,9},{2,6},{6,2},{1... | collective-permute-start | bytes 786440 | tf_op jit(solution)/shard_map/ppermute | solution.py:266
  219.5 13.3 %copy-start.2 = (bf16[256,512]{1,0:T(8,128)(2,1)S(1)}, bf16[256,512]{1,0:T(8,128)(2,1)}, u32[]{:S(2)}) copy-start(bf16[256,512]{1,0:T(8,128)(2,1)} %copy-done.1) | copy-start | bytes 786436
  219.5 13.3 %copy-start.4 = (bf16[256,512]{1,0:T(8,128)(2,1)S(1)}, bf16[256,512]{1,0:T(8,128)(2,1)}, u32[]{:S(2)}) copy-start(bf16[256,512]{1,0:T(8,128)(2,1)} %copy-done.3) | copy-start | bytes 786436
  231.6 13.4 %collective-permute-start.16 = (bf16[4,32,512]{2,1,0:T(8,128)(2,1)S(1)}, bf16[4,32,512]{2,1,0:T(8,128)(2,1)S(1)}, u32[]{:S(2)}, u32[]{:S(2)}) collective-permute-start(bf16[4,32,512]{2,1,0:T(8,128)(2,1)S(1)} %fusion.6), channel_id=1, source_target_pairs={{0,8},{4,12},{8,0},{12,4},{1,9},{5,13},{9,1},{13,5},{2,10},{6,14},... | collective-permute-start | bytes 393224 | tf_op jit(solution)/shard_map/ppermute | solution.py:266
  232.8 14.1 %copy-start.27 = (bf16[256,512]{1,0:T(8,128)(2,1)S(1)}, bf16[256,512]{1,0:T(8,128)(2,1)}, u32[]{:S(2)}) copy-start(bf16[256,512]{1,0:T(8,128)(2,1)} %get-tuple-element.35) | copy-start | bytes 786436
  245.0 14.1 %collective-permute-start.4 = (bf16[256,512]{1,0:T(8,128)(2,1)S(1)}, bf16[256,512]{1,0:T(8,128)(2,1)S(1)}, u32[]{:S(2)}, u32[]{:S(2)}) collective-permute-start(bf16[256,512]{1,0:T(8,128)(2,1)S(1)} %copy-done.28), channel_id=1, source_target_pairs={{0,8},{4,12},{8,0},{12,4},{1,9},{5,13},{9,1},{13,5},{2,10},{6,14},... | collective-permute-start | bytes 786440 | tf_op jit(solution)/shard_map/ppermute | solution.py:266
  246.9 12.2 %collective-permute-start.5 = (bf16[256,512]{1,0:T(8,128)(2,1)S(1)}, bf16[256,512]{1,0:T(8,128)(2,1)S(1)}, u32[]{:S(2)}, u32[]{:S(2)}) collective-permute-start(bf16[256,512]{1,0:T(8,128)(2,1)S(1)} %copy-done.27), channel_id=1, source_target_pairs={{0,4},{4,0},{8,12},{12,8},{1,5},{5,1},{9,13},{13,9},{2,6},{6,2},{1... | collective-permute-start | bytes 786440 | tf_op jit(solution)/shard_map/ppermute | solution.py:266
  (23 other events, 71.3 us)
Sparse Core Ops, SparseCore 0:
  74.1 24.3 all-gather.2

commit v2 on v1

--- a/solution.py
+++ b/solution.py
@@ -10,7 +10,7 @@
 
 HEAD_WIDTH = 128
 EXP_SCALE = math.log2(math.e) * HEAD_WIDTH ** (-0.5)
-VMEM_LIMIT = 48 * 1024 * 1024
+VMEM_LIMIT = 60 * 1024 * 1024
 
 
 def any_spec():
@@ -27,16 +27,17 @@
     if with_hidden:
         hidden_ref, refs = refs[0], refs[1:]
     refs = refs[n_deps:]
-    n_out = len(spans) * len(distances) + (len(distances) if with_hidden else 0)
-    outs, sems = refs[:n_out], refs[n_out]
+    n_away = len([distance for distance in distances if distance])
+    n_out = len(spans) * n_away + (len(distances) if with_hidden else 0)
+    outs, bounces, sems = refs[:n_out], refs[n_out : 2 * n_out], refs[2 * n_out]
     myself = place_ref[0]
     slot_count = store_ref.shape[0]
     copies = []
 
     def send(source, target):
-        copy = pltpu.make_async_copy(source, target, sems.at[len(copies)])
+        copy = pltpu.make_async_copy(source, bounces[place], sems.at[place])
         copy.start()
-        copies.append(copy)
+        copies.append((copy, target))
 
     place = 0
     if with_hidden:
@@ -48,6 +49,8 @@
             send(hidden_ref.at[pl.ds(first_row, rows), pl.ds(first_column, width)], target)
             place += 1
     for distance in distances:
+        if distance == 0:
+            continue
         partner = myself ^ distance
         count = jnp.int32(0)
         chosen = [jnp.int32(0) for _ in spans]
@@ -60,7 +63,13 @@
         for slot in chosen:
             send(store_ref.at[slot], outs[place])
             place += 1
-    for copy in copies:
+    leaving = []
+    for i, (copy, target) in enumerate(copies):
+        copy.wait()
+        copy = pltpu.make_async_copy(bounces[i], target, sems.at[i])
+        copy.start()
+        leaving.append(copy)
+    for copy in leaving:
         copy.wait()
 
 
@@ -70,25 +79,28 @@
     shapes = []
     if with_hidden:
         shapes += [jax.ShapeDtypeStruct(hidden_shape, hidden.dtype)] * len(distances)
-    shapes += [jax.ShapeDtypeStruct((span_len, kv_cols), store.dtype)] * (len(spans) * len(distances))
+    n_away = len([distance for distance in distances if distance])
+    shapes += [jax.ShapeDtypeStruct((span_len, kv_cols), store.dtype)] * (len(spans) * n_away)
     operands = [place, slots, retrieval, store] + ([hidden] if with_hidden else []) + list(deps)
     outs = pl.pallas_call(
         functools.partial(pack_kernel, tuple(spans), tuple(distances), with_hidden, len(deps)),
         out_shape=shapes,
         in_specs=[smem_spec()] * 3 + [any_spec()] * (len(operands) - 3),
         out_specs=[any_spec()] * len(shapes),
-        scratch_shapes=[pltpu.SemaphoreType.DMA((len(shapes),))],
+        scratch_shapes=[pltpu.VMEM(shape.shape, shape.dtype) for shape in shapes]
+        + [pltpu.SemaphoreType.DMA((len(shapes),))],
+        compiler_params=pltpu.CompilerParams(vmem_limit_bytes=VMEM_LIMIT),
         name="pack_spans",
     )(*operands)
     hidden_pieces = outs[: len(distances)] if with_hidden else []
     rest = outs[len(hidden_pieces) :]
     per = len(spans)
-    return list(hidden_pieces), [list(rest[i * per : (i + 1) * per]) for i in range(len(distances))]
+    return list(hidden_pieces), [list(rest[i * per : (i + 1) * per]) for i in range(n_away)]
 
 
 def attend_kernel(n_pieces, with_question, with_fresh, first, last, n_deps, *refs):
-    table_ref, query_ref, question_ref = refs[:3]
-    refs = refs[3:]
+    _, table_ref, query_ref, question_ref = refs[:4]
+    refs = refs[4:]
     piece_refs, refs = refs[:n_pieces], refs[n_pieces:]
     if with_fresh:
         fresh_ref, refs = refs[0], refs[1:]
@@ -181,9 +193,9 @@
             stats_out[here, :] = jnp.where(lane < width // 2, highest, total)
 
 
-def attend(table, queries, question, pieces, fresh, state, with_question, last, deps):
+def attend(table, queries, question, pieces, slots, fresh, state, with_question, last, deps):
     question_len, query_cols = queries.shape
-    span_len, kv_cols = pieces[0].shape
+    span_len, kv_cols = pieces[0].shape[-2:]
     kv_heads = kv_cols // (2 * HEAD_WIDTH)
     group_cols = query_cols // kv_heads
     group_rows = group_cols // HEAD_WIDTH * question_len
@@ -191,12 +203,19 @@
     pair_cols = 2 * HEAD_WIDTH
 
     def by_head(rows, columns):
-        return pl.BlockSpec((rows, columns), lambda k: (0, k))
-
-    state_spec = pl.BlockSpec((group_rows, HEAD_WIDTH), lambda k: (k, 0))
+        return pl.BlockSpec((rows, columns), lambda k, slots: (0, k))
+
+    def by_slot(place):
+        return pl.BlockSpec((None, span_len, pair_cols), lambda k, slots: (slots[place], 0, k))
+
+    state_spec = pl.BlockSpec((group_rows, HEAD_WIDTH), lambda k, slots: (k, 0))
     operands = [table, queries, question] + list(pieces)
     specs = [smem_spec(), by_head(question_len, group_cols), by_head(question_len, pair_cols)]
-    specs += [by_head(span_len, pair_cols)] * len(pieces)
+    if slots is None:
+        specs += [by_head(span_len, pair_cols)] * len(pieces)
+        slots = jnp.zeros((1,), jnp.int32)
+    else:
+        specs += [by_slot(place) for place in range(len(pieces))]
     length = len(pieces) * span_len + (question_len if with_question else 0)
     if fresh is not None:
         operands.append(fresh)
@@ -218,20 +237,23 @@
         functools.partial(
             attend_kernel, len(pieces), with_question, fresh is not None, first, last, len(deps)
         ),
-        grid=(kv_heads,),
         out_shape=out_shape,
-        in_specs=specs,
-        out_specs=out_specs,
-        scratch_shapes=[
-            pltpu.VMEM((length, HEAD_WIDTH), jnp.bfloat16),
-            pltpu.VMEM((length, 2 * HEAD_WIDTH), jnp.bfloat16),
-        ],
+        grid_spec=pltpu.PrefetchScalarGridSpec(
+            num_scalar_prefetch=1,
+            grid=(kv_heads,),
+            in_specs=specs,
+            out_specs=out_specs,
+            scratch_shapes=[
+                pltpu.VMEM((length, HEAD_WIDTH), jnp.bfloat16),
+                pltpu.VMEM((length, 2 * HEAD_WIDTH), jnp.bfloat16),
+            ],
+        ),
         compiler_params=pltpu.CompilerParams(vmem_limit_bytes=VMEM_LIMIT),
         cost_estimate=pl.CostEstimate(
             flops=work * 8 * HEAD_WIDTH, bytes_accessed=8 * 1024 * 1024, transcendentals=work
         ),
         name="attend_spans",
-    )(*operands)
+    )(slots, *operands)
 
 
 def local(
@@ -268,7 +290,8 @@
     away = list(range(n_store - 1, 0, -1))
     everyone = away + [0]
 
-    owners = span_store_slot[retrieval[myself]] // slot_count
+    home_slots = span_store_slot[retrieval[myself]]
+    owners = home_slots // slot_count
     column = jnp.arange(span_count, dtype=jnp.int32)
     earlier = (owners[:, None] == owners[None, :]) & (column[None, :] < column[:, None])
     rank = jnp.sum(earlier.astype(jnp.int32), axis=1)
@@ -281,6 +304,7 @@
         [jnp.ones((span_count, 1), jnp.int32), recompute_rows[0]], axis=1
     )
     table = jnp.sum(match[:, :, :, None] * listed[None, None], axis=2)
+    own_slots = jnp.sum(match[0] * (home_slots % slot_count)[None], axis=1)
 
     def rows_of(keys):
         return jnp.stack([table[distance, span] for distance, span in keys])
@@ -290,19 +314,14 @@
         (shard_rows, shard_width),
     )
     hidden_in = [exchange(piece, d) for piece, d in zip(hidden_out, everyone)]
-    rounds = [[exchange(piece[0], d) for piece, d in zip(out[: len(away)], away)]]
-    own = [(0, 0, out[-1][0])]
+    rounds = [[exchange(piece[0], d) for piece, d in zip(out, away)]]
     if per_pair > 1:
-        _, out = pack(
-            place, span_store_slot, retrieval, key_value_store, None, list(range(1, per_pair)), [0], []
-        )
-        own += [(0, span, piece) for span, piece in zip(range(1, per_pair), out[0])]
         _, out = pack(place, span_store_slot, retrieval, key_value_store, None, [1], away, [])
         rounds.append([exchange(piece[0], d) for piece, d in zip(out, away)])
 
     state = attend(
-        rows_of([(d, s) for d, s, _ in own]), query_rows, question, [p for _, _, p in own],
-        None, None, True, False, [],
+        rows_of([(0, span) for span in range(per_pair)]), query_rows, question,
+        [key_value_store] * per_pair, own_slots, None, None, True, False, [],
     )
 
     gathered = lax.all_gather(jnp.stack(hidden_in[::-1]), "tensor", axis=0)
@@ -335,7 +354,8 @@
             with_fresh = span == max(0, per_pair - 2) and number == len(batches) - 1
             result = attend(
                 rows_of([(away[i], span) for i in batch]), query_rows, question,
-                [arrived[i] for i in batch], fresh if with_fresh else None, state, False, last, deps,
+                [arrived[i] for i in batch], None, fresh if with_fresh else None, state, False, last,
+                deps,
             )
             state = result
     attended = state

time: 276 us -> 156 us (0.57)
  Pallas kernels: 204 us -> 66.7 us
  waiting for transfers between devices: 9.19 us -> 31.8 us
  local copies, waits for them, and re-layouts: 13.2 us -> 4.15 us
  other arithmetic: 4.16 us -> 8.43 us
    pallas_call x5 -> x4, Pallas kernels: 153 us -> 11.2 us  [pack(): pl.pallas_call(functools.partial(pack_kernel, tuple(spans), tuple(distanc...]
    ppermute x17, waiting for transfers between devices: 9.17 us -> 31.8 us  [exchange(): lax.ppermute(piece, 'store', [(i, i ^ distance) for i in range(n_store)])]
    unnamed x58 -> x26, local copies, waits for them, and re-layouts: 12 us -> 2.98 us
    pallas_call x5, Pallas kernels: 51.5 us -> 55.5 us  [attend(): pl.pallas_call(functools.partial(attend_kernel, len(pieces), with_questio...]
    another operation x5, other arithmetic: 0.05 us -> 2.92 us  [rows_of(): return jnp.stack([table[distance, span] for distance, span in keys])]
  transfers between devices with their start and end apart: 18 -> 18, of which waited for: 2 -> 6; matrix products, arithmetic and copies ran while one was open for 2% -> 6% of each run, Pallas kernels for 52% -> 34%
where the time goes in v2:
time: 156 us
  Pallas kernels  66.7 us (43%)
  waiting for transfers between devices  31.8 us (20%)
  starting transfers between devices  27.7 us (18%)
  between operations  14.2 us (9%)
  other arithmetic  8.43 us (5%)
  local copies, waits for them, and re-layouts  4.15 us (3%)
  matrix products  2.84 us (2%)
    pallas_call x5, Pallas kernels, attend(): pl.pallas_call(functools.partial(attend_kernel, len(pieces), with_questio...  55.5 us
    ppermute x17, waiting for transfers between devices, exchange(): lax.ppermute(piece, 'store', [(i, i ^ distance) for i in range(n_store)])  31.8 us
    ppermute x17, starting transfers between devices, exchange(): lax.ppermute(piece, 'store', [(i, i ^ distance) for i in range(n_store)])  27.6 us
    pallas_call x4, Pallas kernels, pack(): pl.pallas_call(functools.partial(pack_kernel, tuple(spans), tuple(distanc...  11.2 us
  transfers between devices with their start and end apart: 18, of which 6 were waited for; matrix products, arithmetic and copies ran while one was open for 6% of the time, Pallas kernels for 34%

profile of v2, /device:TPU:0, one launch (start us, length us, event | category | flops | bytes accessed | tf_op | source)
XLA Modules:
  0.0 155.9 jit_solution(2775760727322822281)
XLA Ops:
  7.9 2.9 %pack_spans.6 = (bf16[32,2048]{1,0:T(8,128)(2,1)}, bf16[32,2048]{1,0:T(8,128)(2,1)}, bf16[32,2048]{1,0:T(8,128)(2,1)}, bf16[32,2048]{1,0:T(8,128)(2,1)}, bf16[25...) custom-call(s32[2]{0:T(128)} %pad_add_fusion.5.refs_0_, s32[32]{0:T(128)} %refs_1_.7, ...), custom_call_target="tpu_custom_call" | custom-call | tf_op jit(solution)/shard_map/pack_spans/pallas_call | solution.py:85
  10.8 4.1 %collective-permute-start.13 = (bf16[32,2048]{1,0:T(8,128)(2,1)}, bf16[32,2048]{1,0:T(8,128)(2,1)S(1)}, u32[]{:S(2)}, u32[]{:S(2)}) collective-permute-start(bf16[32,2048]{1,0:T(8,128)(2,1)} %get-tuple-element.40), channel_id=1, source_target_pairs={{0,8},{4,12},{8,0},{12,4},{1,9},{5,13},{9,1},{13,5},{2,10},{6,14},... | collective-permute-start | bytes 393224 | tf_op jit(solution)/shard_map/ppermute | solution.py:288
  14.9 1.3 collective-permute-start.14
  16.5 8.6 %collective-permute-done.13 = bf16[32,2048]{1,0:T(8,128)(2,1)S(1)} collective-permute-done((bf16[32,2048]{1,0:T(8,128)(2,1)}, bf16[32,2048]{1,0:T(8,128)(2,1)S(1)}, u32[]{:S(2)}, u32[]{:S(2)}) %collective-permute-start.13) | collective-permute-done | bytes 131104 | tf_op jit(solution)/shard_map/ppermute | solution.py:288
  25.7 1.8 %pad_maximum_fusion = bf16[4,32,2048]{2,1,0:T(8,128)(2,1)} fusion(bf16[1,32,2048]{2,1,0:T(8,128)(2,1)S(1)} %bitcast.69, bf16[1,32,2048]{2,1,0:T(8,128)(2,1)S(1)} %bitcast.68, bf16[1,32,2048]{2,1,0:T(8,128)(2,1)S(1)} %bitcast.70, bf16[1,32,2048]{2,1,0:T(8,128)(2,1)} %bitcast.67), kind=kLoop, calls=%fused_computation.6 | loop fusion | flops 786432 | bytes 1048576 | tf_op jit(solution)/shard_map/stack | solution.py:327
  27.5 3.6 %collective-permute-start.6 = (bf16[256,512]{1,0:T(8,128)(2,1)}, bf16[256,512]{1,0:T(8,128)(2,1)S(1)}, u32[]{:S(2)}, u32[]{:S(2)}) collective-permute-start(bf16[256,512]{1,0:T(8,128)(2,1)} %get-tuple-element.32), channel_id=1, source_target_pairs={{0,12},{4,8},{8,4},{12,0},{1,13},{5,9},{9,5},{13,1},{2,14},{6,10},... | collective-permute-start | bytes 786440 | tf_op jit(solution)/shard_map/ppermute | solution.py:288
  32.2 2.8 %pack_spans.4 = (bf16[256,512]{1,0:T(8,128)(2,1)}, bf16[256,512]{1,0:T(8,128)(2,1)}, bf16[256,512]{1,0:T(8,128)(2,1)}) custom-call(s32[2]{0:T(128)} %pad_add_fusion.5.refs_0_, s32[32]{0:T(128)} %refs_1_.7, s32[4,16]{1,0:T(4,128)} %refs_2_.7, bf16[8,256,512]{2,1,0:T(8,128)(2,1)} %refs_7_.1), custom_call_target="tpu_custom_call" | custom-call | tf_op jit(solution)/shard_map/pack_spans/pallas_call | solution.py:85
  35.0 3.3 %collective-permute-start = (bf16[256,512]{1,0:T(8,128)(2,1)}, bf16[256,512]{1,0:T(8,128)(2,1)S(1)}, u32[]{:S(2)}, u32[]{:S(2)}) collective-permute-start(bf16[256,512]{1,0:T(8,128)(2,1)} %get-tuple-element.26), channel_id=1, source_target_pairs={{0,12},{4,8},{8,4},{12,0},{1,13},{5,9},{9,5},{13,1},{2,14},{6,10},... | collective-permute-start | bytes 786440 | tf_op jit(solution)/shard_map/ppermute | solution.py:288
  42.3 11.8 %attend_spans.5 = (f32[4096,128]{1,0:T(8,128)}, f32[4096,128]{1,0:T(8,128)}) custom-call(s32[4]{0:T(128)} %fusion.9.refs_0_, s32[4,9]{1,0:T(4,128)} %pad_add_fusion.4.refs_1_, bf16[256,2048]{1,0:T(8,128)(2,1)} %bitcast.89, bf16[256,512]{1,0:T(8,128)(2,1)} %bitcast.94, bf16[8,256,512]{2,1,0:T(8,128)(2,1)} %refs_7_.1, bf16[8,256,512]{2,1,0:T(8,128)(2,1)} %refs_7_.1, ...), custom_call_target="tpu_custom_call" | custom-call | flops 5368709120 | bytes 8388608 | tf_op jit(solution)/shard_map/attend_spans/pallas_call | solution.py:236
  54.7 1.2 collective-permute-start.2
  57.7 7.3 %collective-permute-done.7.refs_5_ = bf16[256,512]{1,0:T(8,128)(2,1)S(1)} collective-permute-done((bf16[256,512]{1,0:T(8,128)(2,1)}, bf16[256,512]{1,0:T(8,128)(2,1)S(1)}, u32[]{:S(2)}, u32[]{:S(2)}) %collective-permute-start.7) | collective-permute-done | bytes 262176 | tf_op jit(solution)/shard_map/ppermute | solution.py:288
  65.7 2.8 %pack_spans.7 = (bf16[256,512]{1,0:T(8,128)(2,1)}, bf16[256,512]{1,0:T(8,128)(2,1)}, bf16[256,512]{1,0:T(8,128)(2,1)}) custom-call(s32[2]{0:T(128)} %pad_add_fusion.5.refs_0_, s32[32]{0:T(128)} %refs_1_.7, s32[4,16]{1,0:T(4,128)} %refs_2_.7, bf16[8,256,512]{2,1,0:T(8,128)(2,1)} %refs_7_.1, bf16[256,512]{1,0:T(8,128)(2,1)} %copy-done.4, ...), custom_call_target="tpu_custom_call" | custom-call | tf_op jit(solution)/shard_map/pack_spans/pallas_call | solution.py:85
  68.5 3.6 %collective-permute-start.9 = (bf16[256,512]{1,0:T(8,128)(2,1)}, bf16[256,512]{1,0:T(8,128)(2,1)}, u32[]{:S(2)}, u32[]{:S(2)}) collective-permute-start(bf16[256,512]{1,0:T(8,128)(2,1)} %get-tuple-element.35.refs_9_), channel_id=1, source_target_pairs={{0,12},{4,8},{8,4},{12,0},{1,13},{5,9},{9,5},{13,1},{2,14},{6,10},... | collective-permute-start | bytes 786440 | tf_op jit(solution)/shard_map/ppermute | solution.py:288
  72.9 14.6 %collective-permute-done.1.refs_5_ = bf16[256,512]{1,0:T(8,128)(2,1)S(1)} collective-permute-done((bf16[256,512]{1,0:T(8,128)(2,1)}, bf16[256,512]{1,0:T(8,128)(2,1)S(1)}, u32[]{:S(2)}, u32[]{:S(2)}) %collective-permute-start.1) | collective-permute-done | bytes 262176 | tf_op jit(solution)/shard_map/ppermute | solution.py:288
  88.9 2.8 %pack_spans.5 = (bf16[256,512]{1,0:T(8,128)(2,1)}, bf16[256,512]{1,0:T(8,128)(2,1)}, bf16[256,512]{1,0:T(8,128)(2,1)}) custom-call(s32[2]{0:T(128)} %pad_add_fusion.5.refs_0_, s32[32]{0:T(128)} %refs_1_.7, s32[4,16]{1,0:T(4,128)} %refs_2_.7, bf16[8,256,512]{2,1,0:T(8,128)(2,1)} %refs_7_.1, bf16[256,512]{1,0:T(8,128)(2,1)} %copy-done.2, ...), custom_call_target="tpu_custom_call" | custom-call | tf_op jit(solution)/shard_map/pack_spans/pallas_call | solution.py:85
  91.7 3.6 %collective-permute-start.3 = (bf16[256,512]{1,0:T(8,128)(2,1)}, bf16[256,512]{1,0:T(8,128)(2,1)}, u32[]{:S(2)}, u32[]{:S(2)}) collective-permute-start(bf16[256,512]{1,0:T(8,128)(2,1)} %get-tuple-element.29.refs_9_), channel_id=1, source_target_pairs={{0,12},{4,8},{8,4},{12,0},{1,13},{5,9},{9,5},{13,1},{2,14},{6,10},... | collective-permute-start | bytes 786440 | tf_op jit(solution)/shard_map/ppermute | solution.py:288
  95.3 2.8 %fusion = f32[4,2,2,32,512]{4,3,2,1,0:T(8,128)S(1)} fusion(bf16[4,2,2,32,2048]{4,3,2,1,0:T(8,128)(2,1)} %bitcast.88, bf16[2048,512]{1,0:T(8,128)(2,1)S(1)} %copy-done), kind=kOutput, calls=%fused_computation.1 | convolution fusion | flops 1073741824 | bytes 5242880 | tf_op jit(solution)/shard_map/dot_general | solution.py:328
  98.3 11.2 %attend_spans.6 = (f32[4096,128]{1,0:T(8,128)}, f32[4096,128]{1,0:T(8,128)}) custom-call(s32[1]{0:T(128)} %constant.33.clone.1.refs_0_, s32[3,9]{1,0:T(4,128)} %pad_add_fusion.3.refs_1_, bf16[256,2048]{1,0:T(8,128)(2,1)} %bitcast.90, bf16[256,512]{1,0:T(8,128)(2,1)} %bitcast.95, bf16[256,512]{1,0:T(8,128)(2,1)} %copy-done.4, bf16[256,512]{1,0:T(8,128)(2,1)} %copy-done.5, ...), custom_call_target="tpu_custom_call" | custom-call | flops 3221225472 | bytes 8388608 | tf_op jit(solution)/shard_map/attend_spans/pallas_call | solution.py:236
  110.0 1.7 %collective-permute-start.16 = (bf16[4,32,512]{2,1,0:T(8,128)(2,1)S(1)}, bf16[4,32,512]{2,1,0:T(8,128)(2,1)S(1)}, u32[]{:S(2)}, u32[]{:S(2)}) collective-permute-start(bf16[4,32,512]{2,1,0:T(8,128)(2,1)S(1)} %fusion.6), channel_id=1, source_target_pairs={{0,8},{4,12},{8,0},{12,4},{1,9},{5,13},{9,1},{13,5},{2,10},{6,14},... | collective-permute-start | bytes 393224 | tf_op jit(solution)/shard_map/ppermute | solution.py:288
  111.7 11.4 %attend_spans.7 = (f32[4096,128]{1,0:T(8,128)}, f32[4096,128]{1,0:T(8,128)}) custom-call(s32[1]{0:T(128)} %constant.33.clone.1.refs_0_, s32[3,9]{1,0:T(4,128)} %pad_add_fusion.2.refs_1_, bf16[256,2048]{1,0:T(8,128)(2,1)} %bitcast.91, bf16[256,512]{1,0:T(8,128)(2,1)} %bitcast.96, bf16[256,512]{1,0:T(8,128)(2,1)} %copy-done.2, bf16[256,512]{1,0:T(8,128)(2,1)} %copy-done.3, ...), custom_call_target="tpu_custom_call" | custom-call | flops 3221225472 | bytes 8388608 | tf_op jit(solution)/shard_map/attend_spans/pallas_call | solution.py:236
  123.1 1.4 collective-permute-start.4
  125.1 1.5 collective-permute-start.5
  126.7 10.6 %attend_spans.8 = (f32[4096,128]{1,0:T(8,128)}, f32[4096,128]{1,0:T(8,128)}) custom-call(s32[1]{0:T(128)} %constant.33.clone.1.refs_0_, s32[3,9]{1,0:T(4,128)} %pad_add_fusion.1.refs_1_, bf16[256,2048]{1,0:T(8,128)(2,1)} %bitcast.92, bf16[256,512]{1,0:T(8,128)(2,1)} %bitcast.97, bf16[256,512]{1,0:T(8,128)(2,1)} %collective-permute-done.9.refs_4_, ...), custom_call_target="tpu_custom_call" | custom-call | flops 3758096384 | bytes 8388608 | tf_op jit(solution)/shard_map/attend_spans/pallas_call | solution.py:236
  138.5 10.6 %attend_spans.9 = bf16[256,2048]{1,0:T(8,128)(2,1)} custom-call(s32[1]{0:T(128)} %constant.33.clone.1.refs_0_, s32[3,9]{1,0:T(4,128)} %pad_add_fusion.refs_1_, bf16[256,2048]{1,0:T(8,128)(2,1)} %bitcast.93, bf16[256,512]{1,0:T(8,128)(2,1)} %bitcast.98, bf16[256,512]{1,0:T(8,128)(2,1)} %collective-permute-done.3.refs_4_, bf16[256,512]{1,0:T(8,128)(2,1)} %copy-done.11, ...), custom_call_target="tpu_custom_call" | custom-call | flops 3221225472 | bytes 8388608 | tf_op jit(solution)/shard_map/attend_spans/pallas_call | solution.py:236
  (72 shorter events, 14.5 us)
Async XLA Ops:
  7.2 88.1 %copy-start = (bf16[2048,512]{1,0:T(8,128)(2,1)S(1)}, bf16[2048,512]{1,0:T(8,128)(2,1)}, u32[]{:S(2)}) copy-start(bf16[2048,512]{1,0:T(8,128)(2,1)} %param.15) | copy-start | bytes 6291460
  7.2 88.1 %all-gather.3.cloned.1.call-start = ((), (), s32[]{:S(2)}) async-start(), calls=%async_computation | async-start | bytes 2621440 | tf_op jit(solution)/shard_map/all_gather | solution.py:327
  10.8 28.1 %copy-start.1 = (s32[32]{0:T(128)S(1)}, s32[32]{0:T(128)}, u32[]{:S(2)}) copy-start(s32[32]{0:T(128)} %refs_1_.7) | copy-start | bytes 388
  10.8 14.3 %collective-permute-start.13 = (bf16[32,2048]{1,0:T(8,128)(2,1)}, bf16[32,2048]{1,0:T(8,128)(2,1)S(1)}, u32[]{:S(2)}, u32[]{:S(2)}) collective-permute-start(bf16[32,2048]{1,0:T(8,128)(2,1)} %get-tuple-element.40), channel_id=1, source_target_pairs={{0,8},{4,12},{8,0},{12,4},{1,9},{5,13},{9,1},{13,5},{2,10},{6,14},... | collective-permute-start | bytes 393224 | tf_op jit(solution)/shard_map/ppermute | solution.py:288
  14.9 10.2 %collective-permute-start.14 = (bf16[32,2048]{1,0:T(8,128)(2,1)}, bf16[32,2048]{1,0:T(8,128)(2,1)S(1)}, u32[]{:S(2)}, u32[]{:S(2)}) collective-permute-start(bf16[32,2048]{1,0:T(8,128)(2,1)} %get-tuple-element.41), channel_id=1, source_target_pairs={{0,12},{4,8},{8,4},{12,0},{1,13},{5,9},{9,5},{13,1},{2,14},{6,10},... | collective-permute-start | bytes 393224 | tf_op jit(solution)/shard_map/ppermute | solution.py:288
  16.3 9.4 %collective-permute-start.12 = (bf16[32,2048]{1,0:T(8,128)(2,1)}, bf16[32,2048]{1,0:T(8,128)(2,1)S(1)}, u32[]{:S(2)}, u32[]{:S(2)}) collective-permute-start(bf16[32,2048]{1,0:T(8,128)(2,1)} %get-tuple-element.39), channel_id=1, source_target_pairs={{0,4},{4,0},{8,12},{12,8},{1,5},{5,1},{9,13},{13,9},{2,6},{6,2},{1... | collective-permute-start | bytes 393224 | tf_op jit(solution)/shard_map/ppermute | solution.py:288
  25.7 14.0 %copy-start.7 = (s32[1,16,8]{1,2,0:T(8,128)S(1)}, s32[1,16,8]{1,2,0:T(8,128)}, u32[]{:S(2)}) copy-start(s32[1,16,8]{1,2,0:T(8,128)} %param.13) | copy-start | bytes 1540
  27.5 27.2 %collective-permute-start.6 = (bf16[256,512]{1,0:T(8,128)(2,1)}, bf16[256,512]{1,0:T(8,128)(2,1)S(1)}, u32[]{:S(2)}, u32[]{:S(2)}) collective-permute-start(bf16[256,512]{1,0:T(8,128)(2,1)} %get-tuple-element.32), channel_id=1, source_target_pairs={{0,12},{4,8},{8,4},{12,0},{1,13},{5,9},{9,5},{13,1},{2,14},{6,10},... | collective-permute-start | bytes 786440 | tf_op jit(solution)/shard_map/ppermute | solution.py:288
  31.0 33.9 %collective-permute-start.7 = (bf16[256,512]{1,0:T(8,128)(2,1)}, bf16[256,512]{1,0:T(8,128)(2,1)S(1)}, u32[]{:S(2)}, u32[]{:S(2)}) collective-permute-start(bf16[256,512]{1,0:T(8,128)(2,1)} %get-tuple-element.33), channel_id=1, source_target_pairs={{0,8},{4,12},{8,0},{12,4},{1,9},{5,13},{9,1},{13,5},{2,10},{6,14},... | collective-permute-start | bytes 786440 | tf_op jit(solution)/shard_map/ppermute | solution.py:288
  31.7 33.3 %collective-permute-start.8 = (bf16[256,512]{1,0:T(8,128)(2,1)}, bf16[256,512]{1,0:T(8,128)(2,1)}, u32[]{:S(2)}, u32[]{:S(2)}) collective-permute-start(bf16[256,512]{1,0:T(8,128)(2,1)} %get-tuple-element.34), channel_id=1, source_target_pairs={{0,4},{4,0},{8,12},{12,8},{1,5},{5,1},{9,13},{13,9},{2,6},{6,2},{1... | collective-permute-start | bytes 786440 | tf_op jit(solution)/shard_map/ppermute | solution.py:288
  35.0 37.1 %collective-permute-start = (bf16[256,512]{1,0:T(8,128)(2,1)}, bf16[256,512]{1,0:T(8,128)(2,1)S(1)}, u32[]{:S(2)}, u32[]{:S(2)}) collective-permute-start(bf16[256,512]{1,0:T(8,128)(2,1)} %get-tuple-element.26), channel_id=1, source_target_pairs={{0,12},{4,8},{8,4},{12,0},{1,13},{5,9},{9,5},{13,1},{2,14},{6,10},... | collective-permute-start | bytes 786440 | tf_op jit(solution)/shard_map/ppermute | solution.py:288
  38.3 49.2 %collective-permute-start.1 = (bf16[256,512]{1,0:T(8,128)(2,1)}, bf16[256,512]{1,0:T(8,128)(2,1)S(1)}, u32[]{:S(2)}, u32[]{:S(2)}) collective-permute-start(bf16[256,512]{1,0:T(8,128)(2,1)} %get-tuple-element.27), channel_id=1, source_target_pairs={{0,8},{4,12},{8,0},{12,4},{1,9},{5,13},{9,1},{13,5},{2,10},{6,14},... | collective-permute-start | bytes 786440 | tf_op jit(solution)/shard_map/ppermute | solution.py:288
  42.3 12.3 %copy-start.8 = (bf16[256,512]{1,0:T(8,128)(2,1)S(1)}, bf16[256,512]{1,0:T(8,128)(2,1)}, u32[]{:S(2)}) copy-start(bf16[256,512]{1,0:T(8,128)(2,1)} %get-tuple-element.28) | copy-start | bytes 786436
  54.7 32.8 %collective-permute-start.2 = (bf16[256,512]{1,0:T(8,128)(2,1)S(1)}, bf16[256,512]{1,0:T(8,128)(2,1)S(1)}, u32[]{:S(2)}, u32[]{:S(2)}) collective-permute-start(bf16[256,512]{1,0:T(8,128)(2,1)S(1)} %copy-done.8), channel_id=1, source_target_pairs={{0,4},{4,0},{8,12},{12,8},{1,5},{5,1},{9,13},{13,9},{2,6},{6,2},{1... | collective-permute-start | bytes 786440 | tf_op jit(solution)/shard_map/ppermute | solution.py:288
  68.5 56.7 %collective-permute-start.9 = (bf16[256,512]{1,0:T(8,128)(2,1)}, bf16[256,512]{1,0:T(8,128)(2,1)}, u32[]{:S(2)}, u32[]{:S(2)}) collective-permute-start(bf16[256,512]{1,0:T(8,128)(2,1)} %get-tuple-element.35.refs_9_), channel_id=1, source_target_pairs={{0,12},{4,8},{8,4},{12,0},{1,13},{5,9},{9,5},{13,1},{2,14},{6,10},... | collective-permute-start | bytes 786440 | tf_op jit(solution)/shard_map/ppermute | solution.py:288
  72.1 54.6 %collective-permute-start.10 = (bf16[256,512]{1,0:T(8,128)(2,1)}, bf16[256,512]{1,0:T(8,128)(2,1)}, u32[]{:S(2)}, u32[]{:S(2)}) collective-permute-start(bf16[256,512]{1,0:T(8,128)(2,1)} %get-tuple-element.36), channel_id=1, source_target_pairs={{0,8},{4,12},{8,0},{12,4},{1,9},{5,13},{9,1},{13,5},{2,10},{6,14},... | collective-permute-start | bytes 786440 | tf_op jit(solution)/shard_map/ppermute | solution.py:288
  72.1 15.4 %copy-start.2 = (bf16[256,512]{1,0:T(8,128)(2,1)}, bf16[256,512]{1,0:T(8,128)(2,1)S(1)}, u32[]{:S(2)}) copy-start(bf16[256,512]{1,0:T(8,128)(2,1)S(1)} %collective-permute-done.refs_4_) | copy-start | bytes 786436
  72.1 54.5 %collective-permute-start.11 = (bf16[256,512]{1,0:T(8,128)(2,1)}, bf16[256,512]{1,0:T(8,128)(2,1)}, u32[]{:S(2)}, u32[]{:S(2)}) collective-permute-start(bf16[256,512]{1,0:T(8,128)(2,1)} %get-tuple-element.37), channel_id=1, source_target_pairs={{0,4},{4,0},{8,12},{12,8},{1,5},{5,1},{9,13},{13,9},{2,6},{6,2},{1... | collective-permute-start | bytes 786440 | tf_op jit(solution)/shard_map/ppermute | solution.py:288
  91.7 45.6 %collective-permute-start.3 = (bf16[256,512]{1,0:T(8,128)(2,1)}, bf16[256,512]{1,0:T(8,128)(2,1)}, u32[]{:S(2)}, u32[]{:S(2)}) collective-permute-start(bf16[256,512]{1,0:T(8,128)(2,1)} %get-tuple-element.29.refs_9_), channel_id=1, source_target_pairs={{0,12},{4,8},{8,4},{12,0},{1,13},{5,9},{9,5},{13,1},{2,14},{6,10},... | collective-permute-start | bytes 786440 | tf_op jit(solution)/shard_map/ppermute | solution.py:288
  98.2 11.7 %collective-permute-start.15 = (bf16[4,2,32,512]{3,2,1,0:T(8,128)(2,1)S(1)}, bf16[4,2,32,512]{3,2,1,0:T(8,128)(2,1)S(1)}, u32[]{:S(2)}, u32[]{:S(2)}) collective-permute-start(bf16[4,2,32,512]{3,2,1,0:T(8,128)(2,1)S(1)} %fusion.3), channel_id=1, source_target_pairs={{0,4},{4,0},{8,12},{12,8},{1,5},{5,1},{9,13},{13,9},{2,6},{6,2},{1... | collective-permute-start | bytes 786440 | tf_op jit(solution)/shard_map/ppermute | solution.py:288
  110.0 13.1 %collective-permute-start.16 = (bf16[4,32,512]{2,1,0:T(8,128)(2,1)S(1)}, bf16[4,32,512]{2,1,0:T(8,128)(2,1)S(1)}, u32[]{:S(2)}, u32[]{:S(2)}) collective-permute-start(bf16[4,32,512]{2,1,0:T(8,128)(2,1)S(1)} %fusion.6), channel_id=1, source_target_pairs={{0,8},{4,12},{8,0},{12,4},{1,9},{5,13},{9,1},{13,5},{2,10},{6,14},... | collective-permute-start | bytes 393224 | tf_op jit(solution)/shard_map/ppermute | solution.py:288
  111.7 13.4 %copy-start.9 = (bf16[256,512]{1,0:T(8,128)(2,1)S(1)}, bf16[256,512]{1,0:T(8,128)(2,1)}, u32[]{:S(2)}) copy-start(bf16[256,512]{1,0:T(8,128)(2,1)} %get-tuple-element.31) | copy-start | bytes 786436
  123.1 14.5 %collective-permute-start.4 = (bf16[256,512]{1,0:T(8,128)(2,1)S(1)}, bf16[256,512]{1,0:T(8,128)(2,1)S(1)}, u32[]{:S(2)}, u32[]{:S(2)}) collective-permute-start(bf16[256,512]{1,0:T(8,128)(2,1)S(1)} %copy-done.10), channel_id=1, source_target_pairs={{0,8},{4,12},{8,0},{12,4},{1,9},{5,13},{9,1},{13,5},{2,10},{6,14},... | collective-permute-start | bytes 786440 | tf_op jit(solution)/shard_map/ppermute | solution.py:288
  125.1 12.5 %collective-permute-start.5 = (bf16[256,512]{1,0:T(8,128)(2,1)S(1)}, bf16[256,512]{1,0:T(8,128)(2,1)S(1)}, u32[]{:S(2)}, u32[]{:S(2)}) collective-permute-start(bf16[256,512]{1,0:T(8,128)(2,1)S(1)} %copy-done.9), channel_id=1, source_target_pairs={{0,4},{4,0},{8,12},{12,8},{1,5},{5,1},{9,13},{13,9},{2,6},{6,2},{1... | collective-permute-start | bytes 786440 | tf_op jit(solution)/shard_map/ppermute | solution.py:288
  (7 other events, 25.4 us)
Sparse Core Ops, SparseCore 0:
  27.6 24.3 all-gather.2

commit v3 on v0

v3 whole, which is shorter than its diff:
```python
import functools
import math

import jax
import jax.numpy as jnp
from jax import lax
from jax.experimental import pallas as pl
from jax.experimental.pallas import tpu as pltpu
from jax.sharding import PartitionSpec as P

HEAD_WIDTH = 128
EXP_SCALE = math.log2(math.e) * HEAD_WIDTH ** (-0.5)
PAIR = 2
VMEM_LIMIT = 28 * 1024 * 1024
PACK_VMEM_LIMIT = 28 * 1024 * 1024


def hbm_spec():
    return pl.BlockSpec(memory_space=pltpu.HBM)


def smem_spec():
    return pl.BlockSpec(memory_space=pltpu.SMEM)


def vmem_spec():
    return pl.BlockSpec(memory_space=pltpu.VMEM)


def after(array, *others):
    return lax.optimization_barrier((array,) + others)[0]


def pack_kernel(messages, shard, with_table, *refs):
    slot_ref, retrieval_ref, store_ref, hidden_ref = refs[:4]
    refs = refs[4:]
    if with_table:
        rows_ref, refs = refs[0], refs[1:]
    outs, refs = refs[: len(messages)], refs[len(messages) :]
    if with_table:
        table_ref, refs = refs[0], refs[1:]
    sems = refs[0]
    myself = lax.axis_index("store")
    tensor = lax.axis_index("tensor")
    slot_count, _, kv_cols = store_ref.shape
    span_count = retrieval_ref.shape[1]
    shard_rows, shard_width = shard
    copies = []

    def send(source, target):
        copy = pltpu.make_async_copy(source, target, sems.at[len(copies)])
        copy.start()
        copies.append(copy)

    for target, (distance, with_hidden, pieces) in zip(outs, messages):
        if with_hidden:
            base = sum(rows for _, _, rows in pieces)
            first_row = pl.multiple_of(tensor * shard_rows, shard_rows)
            for i in range(shard_width // kv_cols):
                column = pl.multiple_of((myself ^ distance) * shard_width + i * kv_cols, kv_cols)
                send(
                    hidden_ref.at[pl.ds(first_row, shard_rows), pl.ds(column, kv_cols)],
                    target.at[pl.ds(base + i * shard_rows, shard_rows)],
                )
    for distance in sorted({message[0] for message in messages}, reverse=True):
        wanted = []
        for target, message in zip(outs, messages):
            base = 0
            for span, start, rows in message[2] if message[0] == distance else ():
                wanted.append((span, pl.ds(start, rows), target.at[pl.ds(base, rows)]))
                base += rows
        if not wanted:
            continue
        count = jnp.int32(0)
        chosen = [jnp.int32(0) for _ in wanted]
        for j in range(span_count):
            home = slot_ref[retrieval_ref[myself ^ distance, j]]
            mine = home // slot_count == myself
            for i, (span, _, _) in enumerate(wanted):
                chosen[i] = jnp.where(mine & (count == span), home - myself * slot_count, chosen[i])
            count = count + jnp.where(mine, 1, 0)
        for slot, (_, rows, target) in zip(chosen, wanted):
            send(store_ref.at[slot, rows], target)
    if with_table:
        lines, columns = table_ref.shape
        per_pair = lines >> (lax.axis_size("store").bit_length() - 1)

        def clear(line, carry):
            for column in range(columns):
                table_ref[line, column] = 0
            return carry

        def fill(j, carry):
            home = slot_ref[retrieval_ref[myself, j]]
            owner = home // slot_count
            first = (owner ^ myself) * per_pair
            taken = jnp.int32(0)
            for span in range(per_pair):
                taken = taken + table_ref[first + span, 0]
            line = first + jnp.minimum(taken, per_pair - 1)
            table_ref[line, 0] = 1
            for column in range(rows_ref.shape[1]):
                table_ref[line, 1 + column] = rows_ref[j, column]
            table_ref[line, columns - 1] = home - owner * slot_count
            return carry

        lax.fori_loop(0, lines, clear, 0)
        lax.fori_loop(0, span_count, fill, 0)
    for copy in copies:
        copy.wait()


def pack(slots, retrieval, store, hidden, rows, messages, shard, lines):
    kv_cols = store.shape[2]
    with_table = rows is not None
    blocks = shard[1] // kv_cols
    shapes, n_copies = [], 0
    for _, with_hidden, pieces in messages:
        length = sum(rows for _, _, rows in pieces) + (blocks * shard[0] if with_hidden else 0)
        shapes.append(jax.ShapeDtypeStruct((length, kv_cols), store.dtype))
        n_copies += len(pieces) + (blocks if with_hidden else 0)
    specs = [vmem_spec()] * len(shapes)
    operands = [slots, retrieval, store, hidden]
    in_specs = [smem_spec()] * 2 + [hbm_spec()] * 2
    if with_table:
        operands.append(rows)
        in_specs.append(smem_spec())
        shapes.append(jax.ShapeDtypeStruct((lines, rows.shape[1] + 2), jnp.int32))
        specs.append(smem_spec())
    outs = pl.pallas_call(
        functools.partial(pack_kernel, messages, shard, with_table),
        out_shape=shapes,
        in_specs=in_specs,
        out_specs=specs,
        scratch_shapes=[pltpu.SemaphoreType.DMA((n_copies,))],
        compiler_params=pltpu.CompilerParams(vmem_limit_bytes=PACK_VMEM_LIMIT),
        cost_estimate=pl.CostEstimate(flops=0, bytes_accessed=0, transcendentals=0),
        name="pack_spans",
    )(*operands)
    return list(outs[: len(messages)]), outs[-1] if with_table else None


def project_kernel(shard_rows, distances, *refs):
    block_refs, (weight_ref, partial_ref, sent_ref) = refs[:-3], refs[-3:]
    n_store, group_rows, kv_cols = partial_ref.shape
    pieces = weight_ref.shape[0] // kv_cols
    total = 0.0
    for piece in range(pieces):
        rows = []
        for d in range(n_store):
            for ref in block_refs:
                length = n_store * pieces * shard_rows
                for base in range(0, ref.shape[0], length):
                    start = base + (d * pieces + piece) * shard_rows
                    rows.append(ref[start : start + shard_rows, :])
        total = total + jnp.dot(
            jnp.concatenate(rows, axis=0),
            weight_ref[piece * kv_cols : (piece + 1) * kv_cols, :],
            preferred_element_type=jnp.float32,
        )
    tensor = lax.axis_index("tensor")
    for d in range(n_store):
        for i, distance in enumerate(distances):
            base = d * group_rows + i * shard_rows
            block = total[base : base + shard_rows, :]
            row = pl.multiple_of((tensor ^ distance) * shard_rows, shard_rows)
            partial_ref[d, pl.ds(row, shard_rows), :] = block
            if d % 2:
                sent_ref[d // 2, pl.ds(row, shard_rows), :] = block.astype(sent_ref.dtype)


def project(blocks, weight, n_store, shard_rows, distances):
    group_rows = sum(block.shape[0] for block in blocks) * weight.shape[1]
    group_rows = group_rows // (n_store * weight.shape[0])
    kv_cols = weight.shape[1]
    return pl.pallas_call(
        functools.partial(project_kernel, shard_rows, tuple(distances)),
        out_shape=[
            jax.ShapeDtypeStruct((n_store, group_rows, kv_cols), jnp.float32),
            jax.ShapeDtypeStruct((n_store // 2, group_rows, kv_cols), jnp.bfloat16),
        ],
        in_specs=[vmem_spec()] * (len(blocks) + 1),
        out_specs=[vmem_spec()] * 2,
        compiler_params=pltpu.CompilerParams(vmem_limit_bytes=VMEM_LIMIT),
        cost_estimate=pl.CostEstimate(flops=0, bytes_accessed=0, transcendentals=0),
        name="project_rows",
    )(*blocks, weight)


def attend_kernel(parts, with_store, with_question, with_fresh, first, last, *refs):
    table_ref, query_ref, question_ref = refs[:3]
    refs = refs[3:]
    if with_store:
        store_ref, refs = refs[0], refs[1:]
    else:
        piece_refs, refs = refs[: len(parts)], refs[len(parts) :]
    if with_fresh:
        fresh_ref, refs = refs[0], refs[1:]
    if not first:
        blend_in, stats_in = refs[:2]
        refs = refs[2:]
    if last:
        out_ref, keys, values, out_stage, sems = refs
    else:
        blend_out, stats_out, keys, values = refs
    width = HEAD_WIDTH
    question_len, query_cols = query_ref.shape
    kv_heads = question_ref.shape[1] // (2 * width)
    group_cols = query_cols // kv_heads
    group_size = group_cols // width
    rows = PAIR * question_len
    pairs = group_size // PAIR
    contract = (((1,), (1,)), ((), ()))

    def out_copy(step, column):
        columns = pl.ds(column, PAIR * width)
        return pltpu.make_async_copy(out_stage.at[:, columns], out_ref.at[:, columns], sems.at[step])

    def one_kv_head(k, carry):
        key_at = pl.ds(pl.multiple_of(k * 2 * width, 2 * width), width)
        value_at = pl.ds(pl.multiple_of(k * 2 * width + width, width), width)
        spare_key = question_ref[0:8, key_at][0:1].astype(jnp.float32)
        base = 0
        for i, (line, start, length) in enumerate(parts):
            if with_store:
                slot = table_ref[line, table_ref.shape[1] - 1]
                key, value = store_ref[slot, :, key_at], store_ref[slot, :, value_at]
            else:
                key, value = piece_refs[i][:length, key_at], piece_refs[i][:length, value_at]
            row = start + lax.broadcasted_iota(jnp.int32, (length, width), 0)
            stale = row < jnp.where(table_ref[line, 0] == 0, start + length, 0)
            for column in range(1, table_ref.shape[1] - 1):
                stale = stale | (row == table_ref[line, column])
            here = slice(base, base + length)
            keys[here, :] = jnp.where(stale, spare_key, key.astype(jnp.float32)).astype(keys.dtype)
            values[here, :width] = jnp.where(stale, 0.0, value.astype(jnp.float32)).astype(values.dtype)
            values[here, width:] = jnp.where(stale, 0.0, 1.0).astype(values.dtype)
            base += length
        for ref in ([fresh_ref] if with_fresh else []) + ([question_ref] if with_question else []):
            here = slice(base, base + ref.shape[0])
            keys[here, :] = ref[:, key_at]
            values[here, :width] = ref[:, value_at]
            values[here, width:] = jnp.ones((ref.shape[0], width), values.dtype)
            base += ref.shape[0]
        plain = base - (question_len if with_question else 0)

        def query_columns(start):
            return pl.ds(pl.multiple_of(k * group_cols + start * width, width), width)

        def score(pair):
            query = jnp.concatenate(
                [query_ref[:, query_columns(pair * PAIR + h)] for h in range(PAIR)], axis=0
            )
            parts = [
                lax.dot_general(query, keys[:plain, :], contract, preferred_element_type=jnp.float32)
            ]
            if with_question:
                asked = lax.dot_general(
                    query, keys[plain:base, :], contract, preferred_element_type=jnp.float32
                )
                asked = asked.reshape(PAIR, question_len, question_len)
                q_place = lax.broadcasted_iota(jnp.int32, asked.shape, 1)
                k_place = lax.broadcasted_iota(jnp.int32, asked.shape, 2)
                asked = jnp.where(k_place <= q_place, asked, -jnp.inf)
                parts.append(asked.reshape(rows, question_len))
            return parts

        upcoming = score(0)
        for pair in range(pairs):
            scores = upcoming
            if pair + 1 < pairs:
                upcoming = score(pair + 1)
            highest = functools.reduce(
                jnp.maximum, [jnp.max(part, axis=1, keepdims=True) for part in scores]
            )
            here = pl.ds(pl.multiple_of((k * pairs + pair) * rows, rows), rows)
            if not first:
                stats = stats_in[here, :]
                before = stats[:, :1]
                row_total = stats[:, width // 2 : width // 2 + 1]
                highest = jnp.maximum(highest, before)
                fade = jnp.exp2((before - highest) * EXP_SCALE)
            blend = 0.0
            offset = 0
            for part in scores:
                probs = jnp.exp2((part - highest) * EXP_SCALE).astype(jnp.bfloat16)
                blend = blend + jnp.dot(
                    probs,
                    values[offset : offset + part.shape[1], :],
                    preferred_element_type=jnp.float32,
                )
                offset += part.shape[1]
            total = blend[:, width:]
            blend = blend[:, :width]
            if not first:
                blend = blend + blend_in[here, :] * fade
                total = total + row_total * fade
            if last:
                done = (blend / total).astype(out_ref.dtype)
                for h in range(PAIR):
                    out_stage[:, query_columns(pair * PAIR + h)] = done[
                        h * question_len : (h + 1) * question_len
                    ]
                out_copy(
                    k * pairs + pair,
                    pl.multiple_of(k * group_cols + pair * PAIR * width, PAIR * width),
                ).start()
            else:
                lane = lax.broadcasted_iota(jnp.int32, (rows, width), 1)
                blend_out[here, :] = blend
                stats_out[here, :] = jnp.where(lane < width // 2, highest, total)
        return carry

    lax.fori_loop(0, kv_heads, one_kv_head, 0)
    if last:
        for step in range(kv_heads * pairs):
            out_copy(step, step * PAIR * width).wait()


def attend(table, queries, question, parts, pieces, store, fresh, state, with_question, last):
    question_len, query_cols = queries.shape
    heads = query_cols // HEAD_WIDTH
    pairs = heads // PAIR
    first = state is None
    operands = [table, queries, question] + ([store] if store is not None else list(pieces))
    length = sum(rows for _, _, rows in parts) + (question_len if with_question else 0)
    if fresh is not None:
        operands.append(fresh)
        length += fresh.shape[0]
    if not first:
        operands += list(state)
    scratch = [
        pltpu.VMEM((length, HEAD_WIDTH), jnp.bfloat16),
        pltpu.VMEM((length, 2 * HEAD_WIDTH), jnp.bfloat16),
    ]
    if last:
        out_shape = jax.ShapeDtypeStruct(queries.shape, queries.dtype)
        out_specs = hbm_spec()
        scratch += [pltpu.VMEM(queries.shape, queries.dtype), pltpu.SemaphoreType.DMA((pairs,))]
    else:
        out_shape = [jax.ShapeDtypeStruct((heads * question_len, HEAD_WIDTH), jnp.float32)] * 2
        out_specs = [vmem_spec()] * 2
    return pl.pallas_call(
        functools.partial(
            attend_kernel, tuple(parts), store is not None, with_question, fresh is not None, first,
            last,
        ),
        out_shape=out_shape,
        in_specs=[smem_spec()] + [vmem_spec()] * (len(operands) - 1),
        out_specs=out_specs,
        scratch_shapes=scratch,
        compiler_params=pltpu.CompilerParams(vmem_limit_bytes=VMEM_LIMIT),
        cost_estimate=pl.CostEstimate(
            flops=heads * question_len * length * 8 * HEAD_WIDTH, bytes_accessed=0, transcendentals=0
        ),
        name="attend_spans",
    )(*operands)


def local(
    queries,
    question_kv,
    key_value_store,
    span_store_slot,
    retrieval,
    recompute_rows,
    recompute_hidden,
    kv_weight,
):
    n_store = lax.axis_size("store")
    n_tensor = lax.axis_size("tensor")
    slot_count, span_len, kv_cols = key_value_store.shape
    span_count = retrieval.shape[1]
    recomp = recompute_rows.shape[2]
    model_width = recompute_hidden.shape[3]
    shard_rows = span_count * recomp // n_tensor
    per_pair = max(1, span_count // n_store)
    fresh_rows = span_count * recomp
    hidden = recompute_hidden.reshape(fresh_rows, model_width)
    question = question_kv[0]
    query_rows = queries[0]

    def exchange(piece, distance, axis, content):
        size = lax.axis_size(axis)
        with jax.named_scope(content + str(distance)):
            return lax.ppermute(piece, axis, [(i, i ^ distance) for i in range(size)])

    shard = (shard_rows, model_width // n_store)

    def packed(messages, rows=None):
        return pack(
            span_store_slot, retrieval, key_value_store, hidden, rows, messages, shard,
            n_store * per_pair,
        )

    away = list(range(n_store - 1, 0, -1))
    stages = [[(span, 0, span_len)] for span in range(per_pair)]
    if per_pair > 1:
        half = span_len // 2
        stages[-1:] = [[(per_pair - 1, start, half)] for start in (0, half)]
    messages = [[(d, i == 0, pieces) for d in away] for i, pieces in enumerate(stages)]
    outbox, _ = packed(messages[0])
    arrived = [[exchange(piece, d, "store", "stage0_") for piece, d in zip(outbox, away)]]
    later = [message for stage in messages[1:] for message in stage]
    (hidden_own, *outbox), table = packed([(0, True, [])] + later, recompute_rows[0])

    def block(parts, pieces, state, fresh=None, last=False):
        return attend(
            table, query_rows, question, parts, pieces, None if pieces else key_value_store, fresh,
            state, not pieces, last,
        )

    def parts_of(number):
        return [(d * per_pair + span, start, rows) for d, _, p in messages[number] for span, start, rows in p]

    def behind(pieces, state):
        return list(lax.optimization_barrier((*pieces, state[1]))[:-1])

    state = block([(span, 0, span_len) for span in range(per_pair)], [], None)
    states = [state]
    arrived[0] = behind(arrived[0], state)
    for number in range(1, len(stages)):
        here, outbox = outbox[: len(away)], outbox[len(away) :]
        before = arrived[-1]
        coming = [
            exchange(after(piece, earlier), d, "store", "stage%d_" % number)
            for piece, earlier, d in zip(here, before, away)
        ]
        states.append(block(parts_of(number - 1), before, states[-1]))
        arrived.append(behind(coming, states[-1]))

    def paced(array, step):
        return after(array, *arrived[min(step, len(arrived) - 1)])

    first_row = arrived[0][0].shape[0] - hidden_own.shape[0]
    blocks = [hidden_own] + [piece[first_row:] for piece in arrived[0][::-1]]
    distances = [0]
    for step, bit in enumerate(reversed(range(n_tensor.bit_length() - 1))):
        distances += [distance ^ (1 << bit) for distance in distances]
        blocks[-1] = paced(blocks[-1], step)
        gathered = jnp.concatenate(blocks, axis=0)
        blocks = [gathered, exchange(gathered, 1 << bit, "tensor", "hidden")]
    step = n_tensor.bit_length() - 1
    blocks[-1] = paced(blocks[-1], step)
    partial, sent = project(blocks, kv_weight, n_store, shard_rows, distances)
    for bit in range(n_store.bit_length() - 1):
        if bit:
            sent = paced(partial[1::2].astype(jnp.bfloat16), step + bit)
        partial = partial[0::2] + exchange(sent, 1 << bit, "store", "partial").astype(jnp.float32)
    fresh = partial[0].astype(jnp.bfloat16)
    fresh_out = fresh.reshape(1, span_count, recomp, kv_cols)

    state, parts, size = states[-1], parts_of(len(stages) - 1), 6
    for i in range(0, len(away), size):
        last = i + size >= len(away)
        state = block(
            parts[i : i + size], arrived[-1][i : i + size], state, fresh if last else None, last
        )
    return (state[None], fresh_out)


def solution(mesh):
    in_specs = (
        P(("groups", "store"), None, "tensor"),
        P(("groups", "store"), None, "tensor"),
        P(("groups", "store"), None, "tensor"),
        P("groups"),
        P("groups", None),
        P(("groups", "store"), None, None),
        P(("groups", "store"), None, None, None),
        P("store", "tensor"),
    )
    out_specs = (
        P(("groups", "store"), None, "tensor"),
        P(("groups", "store"), None, None, "tensor"),
    )
    return jax.shard_map(local, mesh=mesh, in_specs=in_specs, out_specs=out_specs, check_vma=False)
```

time: 439 us -> 139 us (0.32)
  waiting for transfers between devices: 219 us -> 44.6 us
  local copies, waits for them, and re-layouts: 124 us -> 6.32 us
  Pallas kernels: 0 us -> 59.2 us
  matrix products: 48 us -> 0 us
  starting transfers between devices: 6.49 us -> 27.1 us
  other arithmetic: 19.1 us -> 0.79 us
  between operations: 14.2 us -> 1.08 us
  loops' own time: 5.51 us -> 0 us
    all_to_all x1 -> x0, waiting for transfers between devices: 201 us -> none  [local(): lax.all_to_all(outbox, 'store', split_axis=0, concat_axis=0, tiled=True)]
    dynamic_slice x40 -> x0, local copies, waits for them, and re-layouts: 64.7 us -> none  [the longest x16 58.8 us: head_pair(): lax.dynamic_index_in_dim(context_kv, 2 * pair_index // group_size, 1, kee...]
    pallas_call x0 -> x9, Pallas kernels: none -> 59.2 us  [the longest x6 51.5 us: attend(): pl.pallas_call(functools.partial(attend_kernel, tuple(parts), store is no...]
    dot_general x17 -> x0, matrix products: 48 us -> none  [the longest x8 31.4 us: attend_rows(): jnp.dot(query_block, key_rows.T, preferred_element_type=jnp.float32)]
    ppermute x0 -> x19, waiting for transfers between devices: none -> 44.6 us  [exchange(): return lax.ppermute(piece, axis, [(i, i ^ distance) for i in range(size)])]
    ppermute x0 -> x19, starting transfers between devices: none -> 27.1 us  [exchange(): return lax.ppermute(piece, axis, [(i, i ^ distance) for i in range(size)])]
    concatenate x4 -> x1, local copies, waits for them, and re-layouts: 18.4 us -> 0.03 us  [local(): gathered = jnp.concatenate(blocks, axis=0)]
    all_gather x1 -> x0, waiting for transfers between devices: 17.7 us -> none  [local(): lax.all_gather(kv_weight, 'store', axis=0, tiled=True)]
  transfers between devices with their start and end apart: 2 -> 19, of which waited for: 2 -> 5; matrix products, arithmetic and copies ran while one was open for 4% -> 0% of each run, Pallas kernels for 0% -> 35%
where the time goes in v3:
time: 139 us
  Pallas kernels  59.2 us (43%)
  waiting for transfers between devices  44.6 us (32%)
  starting transfers between devices  27.1 us (19%)
  local copies, waits for them, and re-layouts  6.32 us (5%)
    pallas_call x6, Pallas kernels, attend(): pl.pallas_call(functools.partial(attend_kernel, tuple(parts), store is no...  51.5 us
    ppermute x19, waiting for transfers between devices, exchange(): return lax.ppermute(piece, axis, [(i, i ^ distance) for i in range(size)])  44.6 us
    ppermute x19, starting transfers between devices, exchange(): return lax.ppermute(piece, axis, [(i, i ^ distance) for i in range(size)])  27.1 us
    pallas_call x2, Pallas kernels, pack(): pl.pallas_call(functools.partial(pack_kernel, messages, shard, with_table...  6.41 us
    unnamed x28, local copies, waits for them, and re-layouts  6.15 us
  transfers between devices with their start and end apart: 19, of which 5 were waited for; matrix products, arithmetic and copies ran while one was open for 0% of the time, Pallas kernels for 35%

profile of v3, /device:TPU:0, one launch (start us, length us, event | category | flops | bytes accessed | tf_op | source)
XLA Modules:
  0.0 139.1 jit_solution(2545394373995071334)
XLA Ops:
  0.6 1.6 %copy-done = bf16[1,16,8,8192]{3,2,1,0:T(8,128)(2,1)S(1)} copy-done((bf16[1,16,8,8192]{3,2,1,0:T(8,128)(2,1)S(1)}, bf16[1,16,8,8192]{3,2,1,0:T(8,128)(2,1)}, u32[]{:S(2)}) %copy-start) | copy-done | bytes 2097176
  2.2 1.6 %copy-done.2 = bf16[8,256,512]{2,1,0:T(8,128)(2,1)S(1)} copy-done((bf16[8,256,512]{2,1,0:T(8,128)(2,1)S(1)}, bf16[8,256,512]{2,1,0:T(8,128)(2,1)}, u32[]{:S(2)}) %copy-start.2) | copy-done | bytes 2097176
  5.2 2.3 %pack_spans.3 = (bf16[384,512]{1,0:T(8,128)(2,1)}, bf16[384,512]{1,0:T(8,128)(2,1)}, bf16[384,512]{1,0:T(8,128)(2,1)}) custom-call(s32[32]{0:T(128)S(1)} %copy-done.8, s32[4,16]{1,0:T(4,128)S(1)} %copy-done.6, bf16[8,256,512]{2,1,0:T(8,128)(2,1)S(1)} %copy-done.2, bf16[128,8192]{1,0:T(8,128)(2,1)S(1)} %bitcast.9), custom_call_target="tpu_custom_call" | custom-call | tf_op jit(solution)/shard_map/pack_spans/pallas_call | solution.py:130
  7.5 5.1 %collective-permute-start = (bf16[384,512]{1,0:T(8,128)(2,1)}, bf16[384,512]{1,0:T(8,128)(2,1)S(1)}, u32[]{:S(2)}, u32[]{:S(2)}) collective-permute-start(bf16[384,512]{1,0:T(8,128)(2,1)} %get-tuple-element.67), channel_id=1, source_target_pairs={{0,12},{4,8},{8,4},{12,0},{1,13},{5,9},{9,5},{13,1},{2,14},{6,10},... | collective-permute-start | bytes 1179656 | tf_op jit(solution)/shard_map/stage0_3/ppermute | solution.py:386
  14.9 4.1 %pack_spans.2 = (bf16[128,512]{1,0:T(8,128)(2,1)S(1)}, bf16[256,512]{1,0:T(8,128)(2,1)S(1)}, bf16[256,512]{1,0:T(8,128)(2,1)S(1)}, bf16[256,512]{1,0:T(8,128)(2,...) custom-call(s32[32]{0:T(128)S(1)} %copy-done.9, ...), custom_call_target="tpu_custom_call" | custom-call | tf_op jit(solution)/shard_map/pack_spans/pallas_call | solution.py:130
  19.1 8.3 %attend_spans.6 = (f32[4096,128]{1,0:T(8,128)S(1)}, f32[4096,128]{1,0:T(8,128)S(1)}) custom-call(s32[16,10]{1,0:T(8,128)S(1)} %get-tuple-element.62.refs_0_, bf16[256,2048]{1,0:T(8,128)(2,1)S(1)} %bitcast.11, bf16[256,512]{1,0:T(8,128)(2,1)S(1)} %bitcast.17, bf16[8,256,512]{2,1,0:T(8,128)(2,1)S(1)} %copy-done.4), custom_call_target="tpu_custom_call" | custom-call | flops 5368709120 | tf_op jit(solution)/shard_map/attend_spans/pallas_call | solution.py:343
  27.4 19.0 %collective-permute-done.1.refs_4_ = bf16[384,512]{1,0:T(8,128)(2,1)S(1)} collective-permute-done((bf16[384,512]{1,0:T(8,128)(2,1)}, bf16[384,512]{1,0:T(8,128)(2,1)S(1)}, u32[]{:S(2)}, u32[]{:S(2)}) %collective-permute-start.1) | collective-permute-done | bytes 393248 | tf_op jit(solution)/shard_map/stage0_2/ppermute | solution.py:386
  48.0 2.5 %collective-permute-start.3 = (bf16[256,512]{1,0:T(8,128)(2,1)S(1)}, bf16[256,512]{1,0:T(8,128)(2,1)S(1)}, u32[]{:S(2)}, u32[]{:S(2)}) collective-permute-start(bf16[256,512]{1,0:T(8,128)(2,1)S(1)} %get-tuple-element.72), channel_id=1, source_target_pairs={{0,12},{4,8},{8,4},{12,0},{1,13},{5,9},{9,5},{13,1},{2,14},{6,10},... | collective-permute-start | bytes 786440 | tf_op jit(solution)/shard_map/stage1_3/ppermute | solution.py:386
  50.5 1.9 %collective-permute-start.5 = (bf16[256,512]{1,0:T(8,128)(2,1)S(1)}, bf16[256,512]{1,0:T(8,128)(2,1)S(1)}, u32[]{:S(2)}, u32[]{:S(2)}) collective-permute-start(bf16[256,512]{1,0:T(8,128)(2,1)S(1)} %get-tuple-element.78), channel_id=1, source_target_pairs={{0,4},{4,0},{8,12},{12,8},{1,5},{5,1},{9,13},{13,9},{2,6},{6,2},{1... | collective-permute-start | bytes 786440 | tf_op jit(solution)/shard_map/stage1_1/ppermute | solution.py:386
  52.4 9.3 %attend_spans.7 = (f32[4096,128]{1,0:T(8,128)S(1)}, f32[4096,128]{1,0:T(8,128)S(1)}) custom-call(s32[16,10]{1,0:T(8,128)S(1)} %get-tuple-element.62.refs_0_, bf16[256,2048]{1,0:T(8,128)(2,1)S(1)} %bitcast.12, bf16[256,512]{1,0:T(8,128)(2,1)S(1)} %bitcast.18, bf16[384,512]{1,0:T(8,128)(2,1)S(1)} %collective-permute-done.refs_3_, ...), custom_call_target="tpu_custom_call" | custom-call | flops 3221225472 | tf_op jit(solution)/shard_map/attend_spans/pallas_call | solution.py:343
  61.7 9.3 %collective-permute-done.4.refs_4_ = bf16[256,512]{1,0:T(8,128)(2,1)S(1)} collective-permute-done((bf16[256,512]{1,0:T(8,128)(2,1)S(1)}, bf16[256,512]{1,0:T(8,128)(2,1)S(1)}, u32[]{:S(2)}, u32[]{:S(2)}) %collective-permute-start.4) | collective-permute-done | bytes 262176 | tf_op jit(solution)/shard_map/stage1_2/ppermute | solution.py:386
  71.1 1.6 %collective-permute-start.6 = (bf16[256,512]{1,0:T(8,128)(2,1)S(1)}, bf16[256,512]{1,0:T(8,128)(2,1)S(1)}, u32[]{:S(2)}, u32[]{:S(2)}) collective-permute-start(bf16[256,512]{1,0:T(8,128)(2,1)S(1)} %get-tuple-element.82), channel_id=1, source_target_pairs={{0,12},{4,8},{8,4},{12,0},{1,13},{5,9},{9,5},{13,1},{2,14},{6,10},... | collective-permute-start | bytes 786440 | tf_op jit(solution)/shard_map/stage2_3/ppermute | solution.py:386
  72.7 2.8 %collective-permute-start.8 = (bf16[256,512]{1,0:T(8,128)(2,1)S(1)}, bf16[256,512]{1,0:T(8,128)(2,1)S(1)}, u32[]{:S(2)}, u32[]{:S(2)}) collective-permute-start(bf16[256,512]{1,0:T(8,128)(2,1)S(1)} %get-tuple-element.88), channel_id=1, source_target_pairs={{0,4},{4,0},{8,12},{12,8},{1,5},{5,1},{9,13},{13,9},{2,6},{6,2},{1... | collective-permute-start | bytes 786440 | tf_op jit(solution)/shard_map/stage2_1/ppermute | solution.py:386
  75.6 9.2 %attend_spans.8 = (f32[4096,128]{1,0:T(8,128)S(1)}, f32[4096,128]{1,0:T(8,128)S(1)}) custom-call(s32[16,10]{1,0:T(8,128)S(1)} %get-tuple-element.62.refs_0_, bf16[256,2048]{1,0:T(8,128)(2,1)S(1)} %bitcast.13, bf16[256,512]{1,0:T(8,128)(2,1)S(1)} %bitcast.19, bf16[256,512]{1,0:T(8,128)(2,1)S(1)} %collective-permute-done.3.refs_3_, ...), custom_call_target="tpu_custom_call" | custom-call | flops 3221225472 | tf_op jit(solution)/shard_map/attend_spans/pallas_call | solution.py:343
  84.8 10.1 %collective-permute-done.7.refs_4_ = bf16[256,512]{1,0:T(8,128)(2,1)S(1)} collective-permute-done((bf16[256,512]{1,0:T(8,128)(2,1)S(1)}, bf16[256,512]{1,0:T(8,128)(2,1)S(1)}, u32[]{:S(2)}, u32[]{:S(2)}) %collective-permute-start.7) | collective-permute-done | bytes 262176 | tf_op jit(solution)/shard_map/stage2_2/ppermute | solution.py:386
  94.8 2.3 %collective-permute-start.9 = (bf16[128,512]{1,0:T(8,128)(2,1)S(1)}, bf16[128,512]{1,0:T(8,128)(2,1)S(1)}, u32[]{:S(2)}, u32[]{:S(2)}) collective-permute-start(bf16[128,512]{1,0:T(8,128)(2,1)S(1)} %get-tuple-element.92), channel_id=1, source_target_pairs={{0,12},{4,8},{8,4},{12,0},{1,13},{5,9},{9,5},{13,1},{2,14},{6,10},... | collective-permute-start | bytes 393224 | tf_op jit(solution)/shard_map/stage3_3/ppermute | solution.py:386
  97.1 2.1 %collective-permute-start.11 = (bf16[128,512]{1,0:T(8,128)(2,1)S(1)}, bf16[128,512]{1,0:T(8,128)(2,1)S(1)}, u32[]{:S(2)}, u32[]{:S(2)}) collective-permute-start(bf16[128,512]{1,0:T(8,128)(2,1)S(1)} %get-tuple-element.98), channel_id=1, source_target_pairs={{0,4},{4,0},{8,12},{12,8},{1,5},{5,1},{9,13},{13,9},{2,6},{6,2},{1... | collective-permute-start | bytes 393224 | tf_op jit(solution)/shard_map/stage3_1/ppermute | solution.py:386
  100.6 9.2 %attend_spans.9 = (f32[4096,128]{1,0:T(8,128)S(1)}, f32[4096,128]{1,0:T(8,128)S(1)}) custom-call(s32[16,10]{1,0:T(8,128)S(1)} %get-tuple-element.62.refs_0_, bf16[256,2048]{1,0:T(8,128)(2,1)S(1)} %bitcast.14, bf16[256,512]{1,0:T(8,128)(2,1)S(1)} %bitcast.20, bf16[256,512]{1,0:T(8,128)(2,1)S(1)} %collective-permute-done.6.refs_3_, ...), custom_call_target="tpu_custom_call" | custom-call | flops 3221225472 | tf_op jit(solution)/shard_map/attend_spans/pallas_call | solution.py:343
  109.9 2.4 %collective-permute-start.12 = (bf16[128,512]{1,0:T(8,128)(2,1)S(1)}, bf16[128,512]{1,0:T(8,128)(2,1)S(1)}, u32[]{:S(2)}, u32[]{:S(2)}) collective-permute-start(bf16[128,512]{1,0:T(8,128)(2,1)S(1)} %get-tuple-element.102), channel_id=1, source_target_pairs={{0,12},{4,8},{8,4},{12,0},{1,13},{5,9},{9,5},{13,1},{2,14},{6,10},... | collective-permute-start | bytes 393224 | tf_op jit(solution)/shard_map/stage4_3/ppermute | solution.py:386
  114.4 2.0 %collective-permute-start.18 = (bf16[1,128,512]{2,1,0:T(8,128)(2,1)S(1)}, bf16[1,128,512]{2,1,0:T(8,128)(2,1)S(1)}, u32[]{:S(2)}, u32[]{:S(2)}) collective-permute-start(bf16[1,128,512]{2,1,0:T(8,128)(2,1)S(1)} %slice.40), channel_id=1, source_target_pairs={{0,8},{4,12},{8,0},{12,4},{1,9},{5,13},{9,1},{13,5},{2,10},{6,14},... | collective-permute-start | bytes 393224 | tf_op jit(solution)/shard_map/partial2/ppermute | solution.py:386
  116.4 6.7 %attend_spans.10 = (f32[4096,128]{1,0:T(8,128)S(1)}, f32[4096,128]{1,0:T(8,128)S(1)}) custom-call(s32[16,10]{1,0:T(8,128)S(1)} %get-tuple-element.62.refs_0_, bf16[256,2048]{1,0:T(8,128)(2,1)S(1)} %bitcast.15, bf16[256,512]{1,0:T(8,128)(2,1)S(1)} %bitcast.21, bf16[128,512]{1,0:T(8,128)(2,1)S(1)} %collective-permute-done.9.refs_3_, ...), custom_call_target="tpu_custom_call" | custom-call | flops 1610612736 | tf_op jit(solution)/shard_map/attend_spans/pallas_call | solution.py:343
  123.1 4.2 %collective-permute-done.13.refs_4_ = bf16[128,512]{1,0:T(8,128)(2,1)S(1)} collective-permute-done((bf16[128,512]{1,0:T(8,128)(2,1)S(1)}, bf16[128,512]{1,0:T(8,128)(2,1)S(1)}, u32[]{:S(2)}, u32[]{:S(2)}) %collective-permute-start.13) | collective-permute-done | bytes 131104 | tf_op jit(solution)/shard_map/stage4_2/ppermute | solution.py:386
  127.3 2.0 %collective-permute-done.18 = bf16[1,128,512]{2,1,0:T(8,128)(2,1)S(1)} collective-permute-done((bf16[1,128,512]{2,1,0:T(8,128)(2,1)S(1)}, bf16[1,128,512]{2,1,0:T(8,128)(2,1)S(1)}, u32[]{:S(2)}, u32[]{:S(2)}) %collective-permute-start.18) | collective-permute-done | bytes 131104 | tf_op jit(solution)/shard_map/partial2/ppermute | solution.py:386
  130.0 8.8 %attend_spans.11 = bf16[256,2048]{1,0:T(8,128)(2,1)} custom-call(s32[16,10]{1,0:T(8,128)S(1)} %get-tuple-element.62.refs_0_, bf16[256,2048]{1,0:T(8,128)(2,1)S(1)} %bitcast.16, bf16[256,512]{1,0:T(8,128)(2,1)S(1)} %bitcast.22, bf16[128,512]{1,0:T(8,128)(2,1)S(1)} %collective-permute-done.12.refs_3_, bf16[128,512]{1,0:T(8,128)(2,1)S(1)} %collective-permute-done.13.refs_4_, ...), custom_call_target="tpu_custom_call" | custom-call | flops 2147483648 | tf_op jit(solution)/shard_map/attend_spans/pallas_call | solution.py:343
  (60 shorter events, 9.7 us)
Async XLA Ops:
  5.2 8.1 %copy-start.12 = (s32[1,16,8]{1,2,0:T(8,128)S(1)}, s32[1,16,8]{1,2,0:T(8,128)}, u32[]{:S(2)}) copy-start(s32[1,16,8]{1,2,0:T(8,128)} %param.13) | copy-start | bytes 1540
  5.2 8.2 %copy-start.1 = (bf16[1,16,8,8192]{3,2,1,0:T(8,128)(2,1)S(1)}, bf16[1,16,8,8192]{3,2,1,0:T(8,128)(2,1)}, u32[]{:S(2)}) copy-start(bf16[1,16,8,8192]{3,2,1,0:T(8,128)(2,1)} %param.14) | copy-start | bytes 6291460
  5.2 8.2 %copy-start.7 = (s32[4,16]{1,0:T(4,128)S(1)}, s32[4,16]{1,0:T(4,128)}, u32[]{:S(2)}) copy-start(s32[4,16]{1,0:T(4,128)} %refs_1_.3) | copy-start | bytes 772
  5.2 8.2 %copy-start.9 = (s32[32]{0:T(128)S(1)}, s32[32]{0:T(128)}, u32[]{:S(2)}) copy-start(s32[32]{0:T(128)} %refs_0_.3) | copy-start | bytes 388
  7.5 19.9 %collective-permute-start = (bf16[384,512]{1,0:T(8,128)(2,1)}, bf16[384,512]{1,0:T(8,128)(2,1)S(1)}, u32[]{:S(2)}, u32[]{:S(2)}) collective-permute-start(bf16[384,512]{1,0:T(8,128)(2,1)} %get-tuple-element.67), channel_id=1, source_target_pairs={{0,12},{4,8},{8,4},{12,0},{1,13},{5,9},{9,5},{13,1},{2,14},{6,10},... | collective-permute-start | bytes 1179656 | tf_op jit(solution)/shard_map/stage0_3/ppermute | solution.py:386
  12.6 33.8 %collective-permute-start.1 = (bf16[384,512]{1,0:T(8,128)(2,1)}, bf16[384,512]{1,0:T(8,128)(2,1)S(1)}, u32[]{:S(2)}, u32[]{:S(2)}) collective-permute-start(bf16[384,512]{1,0:T(8,128)(2,1)} %get-tuple-element.68), channel_id=1, source_target_pairs={{0,8},{4,12},{8,0},{12,4},{1,9},{5,13},{9,1},{13,5},{2,10},{6,14},... | collective-permute-start | bytes 1179656 | tf_op jit(solution)/shard_map/stage0_2/ppermute | solution.py:386
  12.6 33.8 %collective-permute-start.2 = (bf16[384,512]{1,0:T(8,128)(2,1)}, bf16[384,512]{1,0:T(8,128)(2,1)S(1)}, u32[]{:S(2)}, u32[]{:S(2)}) collective-permute-start(bf16[384,512]{1,0:T(8,128)(2,1)} %get-tuple-element.69), channel_id=1, source_target_pairs={{0,4},{4,0},{8,12},{12,8},{1,5},{5,1},{9,13},{13,9},{2,6},{6,2},{1... | collective-permute-start | bytes 1179656 | tf_op jit(solution)/shard_map/stage0_1/ppermute | solution.py:386
  46.5 24.5 %collective-permute-start.15 = (bf16[512,512]{1,0:T(8,128)(2,1)S(1)}, bf16[512,512]{1,0:T(8,128)(2,1)S(1)}, u32[]{:S(2)}, u32[]{:S(2)}) collective-permute-start(bf16[512,512]{1,0:T(8,128)(2,1)S(1)} %pad_maximum_fusion), channel_id=1, source_target_pairs={{0,2},{1,3},{2,0},{3,1},{4,6},{5,7},{6,4},{7,5},{8,10},{9,11},{10,... | collective-permute-start | bytes 1572872 | tf_op jit(solution)/shard_map/hidden2/ppermute | solution.py:386
  48.0 13.7 %collective-permute-start.3 = (bf16[256,512]{1,0:T(8,128)(2,1)S(1)}, bf16[256,512]{1,0:T(8,128)(2,1)S(1)}, u32[]{:S(2)}, u32[]{:S(2)}) collective-permute-start(bf16[256,512]{1,0:T(8,128)(2,1)S(1)} %get-tuple-element.72), channel_id=1, source_target_pairs={{0,12},{4,8},{8,4},{12,0},{1,13},{5,9},{9,5},{13,1},{2,14},{6,10},... | collective-permute-start | bytes 786440 | tf_op jit(solution)/shard_map/stage1_3/ppermute | solution.py:386
  50.5 20.5 %collective-permute-start.4 = (bf16[256,512]{1,0:T(8,128)(2,1)S(1)}, bf16[256,512]{1,0:T(8,128)(2,1)S(1)}, u32[]{:S(2)}, u32[]{:S(2)}) collective-permute-start(bf16[256,512]{1,0:T(8,128)(2,1)S(1)} %get-tuple-element.75), channel_id=1, source_target_pairs={{0,8},{4,12},{8,0},{12,4},{1,9},{5,13},{9,1},{13,5},{2,10},{6,14},... | collective-permute-start | bytes 786440 | tf_op jit(solution)/shard_map/stage1_2/ppermute | solution.py:386
  50.5 20.5 %collective-permute-start.5 = (bf16[256,512]{1,0:T(8,128)(2,1)S(1)}, bf16[256,512]{1,0:T(8,128)(2,1)S(1)}, u32[]{:S(2)}, u32[]{:S(2)}) collective-permute-start(bf16[256,512]{1,0:T(8,128)(2,1)S(1)} %get-tuple-element.78), channel_id=1, source_target_pairs={{0,4},{4,0},{8,12},{12,8},{1,5},{5,1},{9,13},{13,9},{2,6},{6,2},{1... | collective-permute-start | bytes 786440 | tf_op jit(solution)/shard_map/stage1_1/ppermute | solution.py:386
  71.0 28.2 %collective-permute-start.16 = (bf16[1024,512]{1,0:T(8,128)(2,1)S(1)}, bf16[1024,512]{1,0:T(8,128)(2,1)S(1)}, u32[]{:S(2)}, u32[]{:S(2)}) collective-permute-start(bf16[1024,512]{1,0:T(8,128)(2,1)S(1)} %constant_dynamic-update-slice_fusion.refs_0_), channel_id=1, source_target_pairs={{0,1},{1,0},{2,3},{3,2},{4,5},{5,4},{6,7},{7,6},{8,9},{9,8},{10,11... | collective-permute-start | bytes 3145736 | tf_op jit(solution)/shard_map/hidden1/ppermute | solution.py:386
  71.1 13.6 %collective-permute-start.6 = (bf16[256,512]{1,0:T(8,128)(2,1)S(1)}, bf16[256,512]{1,0:T(8,128)(2,1)S(1)}, u32[]{:S(2)}, u32[]{:S(2)}) collective-permute-start(bf16[256,512]{1,0:T(8,128)(2,1)S(1)} %get-tuple-element.82), channel_id=1, source_target_pairs={{0,12},{4,8},{8,4},{12,0},{1,13},{5,9},{9,5},{13,1},{2,14},{6,10},... | collective-permute-start | bytes 786440 | tf_op jit(solution)/shard_map/stage2_3/ppermute | solution.py:386
  72.7 22.1 %collective-permute-start.7 = (bf16[256,512]{1,0:T(8,128)(2,1)S(1)}, bf16[256,512]{1,0:T(8,128)(2,1)S(1)}, u32[]{:S(2)}, u32[]{:S(2)}) collective-permute-start(bf16[256,512]{1,0:T(8,128)(2,1)S(1)} %get-tuple-element.85), channel_id=1, source_target_pairs={{0,8},{4,12},{8,0},{12,4},{1,9},{5,13},{9,1},{13,5},{2,10},{6,14},... | collective-permute-start | bytes 786440 | tf_op jit(solution)/shard_map/stage2_2/ppermute | solution.py:386
  72.7 22.1 %collective-permute-start.8 = (bf16[256,512]{1,0:T(8,128)(2,1)S(1)}, bf16[256,512]{1,0:T(8,128)(2,1)S(1)}, u32[]{:S(2)}, u32[]{:S(2)}) collective-permute-start(bf16[256,512]{1,0:T(8,128)(2,1)S(1)} %get-tuple-element.88), channel_id=1, source_target_pairs={{0,4},{4,0},{8,12},{12,8},{1,5},{5,1},{9,13},{13,9},{2,6},{6,2},{1... | collective-permute-start | bytes 786440 | tf_op jit(solution)/shard_map/stage2_1/ppermute | solution.py:386
  75.6 23.7 %copy-start.5 = (bf16[2048,512]{1,0:T(8,128)(2,1)S(1)}, bf16[2048,512]{1,0:T(8,128)(2,1)}, u32[]{:S(2)}) copy-start(bf16[2048,512]{1,0:T(8,128)(2,1)} %refs_2_.5) | copy-start | bytes 6291460
  94.8 15.0 %collective-permute-start.9 = (bf16[128,512]{1,0:T(8,128)(2,1)S(1)}, bf16[128,512]{1,0:T(8,128)(2,1)S(1)}, u32[]{:S(2)}, u32[]{:S(2)}) collective-permute-start(bf16[128,512]{1,0:T(8,128)(2,1)S(1)} %get-tuple-element.92), channel_id=1, source_target_pairs={{0,12},{4,8},{8,4},{12,0},{1,13},{5,9},{9,5},{13,1},{2,14},{6,10},... | collective-permute-start | bytes 393224 | tf_op jit(solution)/shard_map/stage3_3/ppermute | solution.py:386
  97.1 12.7 %collective-permute-start.10 = (bf16[128,512]{1,0:T(8,128)(2,1)S(1)}, bf16[128,512]{1,0:T(8,128)(2,1)S(1)}, u32[]{:S(2)}, u32[]{:S(2)}) collective-permute-start(bf16[128,512]{1,0:T(8,128)(2,1)S(1)} %get-tuple-element.95), channel_id=1, source_target_pairs={{0,8},{4,12},{8,0},{12,4},{1,9},{5,13},{9,1},{13,5},{2,10},{6,14},... | collective-permute-start | bytes 393224 | tf_op jit(solution)/shard_map/stage3_2/ppermute | solution.py:386
  97.1 12.7 %collective-permute-start.11 = (bf16[128,512]{1,0:T(8,128)(2,1)S(1)}, bf16[128,512]{1,0:T(8,128)(2,1)S(1)}, u32[]{:S(2)}, u32[]{:S(2)}) collective-permute-start(bf16[128,512]{1,0:T(8,128)(2,1)S(1)} %get-tuple-element.98), channel_id=1, source_target_pairs={{0,4},{4,0},{8,12},{12,8},{1,5},{5,1},{9,13},{13,9},{2,6},{6,2},{1... | collective-permute-start | bytes 393224 | tf_op jit(solution)/shard_map/stage3_1/ppermute | solution.py:386
  100.5 13.8 %collective-permute-start.17 = (bf16[2,128,512]{2,1,0:T(8,128)(2,1)S(1)}, bf16[2,128,512]{2,1,0:T(8,128)(2,1)S(1)}, u32[]{:S(2)}, u32[]{:S(2)}) collective-permute-start(bf16[2,128,512]{2,1,0:T(8,128)(2,1)S(1)} %get-tuple-element.119), channel_id=1, source_target_pairs={{0,4},{4,0},{8,12},{12,8},{1,5},{5,1},{9,13},{13,9},{2,6},{6,2},{1... | collective-permute-start | bytes 786440 | tf_op jit(solution)/shard_map/partial1/ppermute | solution.py:386
  109.9 13.3 %collective-permute-start.12 = (bf16[128,512]{1,0:T(8,128)(2,1)S(1)}, bf16[128,512]{1,0:T(8,128)(2,1)S(1)}, u32[]{:S(2)}, u32[]{:S(2)}) collective-permute-start(bf16[128,512]{1,0:T(8,128)(2,1)S(1)} %get-tuple-element.102), channel_id=1, source_target_pairs={{0,12},{4,8},{8,4},{12,0},{1,13},{5,9},{9,5},{13,1},{2,14},{6,10},... | collective-permute-start | bytes 393224 | tf_op jit(solution)/shard_map/stage4_3/ppermute | solution.py:386
  112.2 15.1 %collective-permute-start.13 = (bf16[128,512]{1,0:T(8,128)(2,1)S(1)}, bf16[128,512]{1,0:T(8,128)(2,1)S(1)}, u32[]{:S(2)}, u32[]{:S(2)}) collective-permute-start(bf16[128,512]{1,0:T(8,128)(2,1)S(1)} %get-tuple-element.105), channel_id=1, source_target_pairs={{0,8},{4,12},{8,0},{12,4},{1,9},{5,13},{9,1},{13,5},{2,10},{6,14},... | collective-permute-start | bytes 393224 | tf_op jit(solution)/shard_map/stage4_2/ppermute | solution.py:386
  113.4 13.9 %collective-permute-start.14 = (bf16[128,512]{1,0:T(8,128)(2,1)S(1)}, bf16[128,512]{1,0:T(8,128)(2,1)S(1)}, u32[]{:S(2)}, u32[]{:S(2)}) collective-permute-start(bf16[128,512]{1,0:T(8,128)(2,1)S(1)} %get-tuple-element.108), channel_id=1, source_target_pairs={{0,4},{4,0},{8,12},{12,8},{1,5},{5,1},{9,13},{13,9},{2,6},{6,2},{1... | collective-permute-start | bytes 393224 | tf_op jit(solution)/shard_map/stage4_1/ppermute | solution.py:386
  114.4 14.9 %collective-permute-start.18 = (bf16[1,128,512]{2,1,0:T(8,128)(2,1)S(1)}, bf16[1,128,512]{2,1,0:T(8,128)(2,1)S(1)}, u32[]{:S(2)}, u32[]{:S(2)}) collective-permute-start(bf16[1,128,512]{2,1,0:T(8,128)(2,1)S(1)} %slice.40), channel_id=1, source_target_pairs={{0,8},{4,12},{8,0},{12,4},{1,9},{5,13},{9,1},{13,5},{2,10},{6,14},... | collective-permute-start | bytes 393224 | tf_op jit(solution)/shard_map/partial2/ppermute | solution.py:386
  (8 other events, 18.5 us)

commit v4 on v3

--- a/solution.py
+++ b/solution.py
@@ -12,7 +12,7 @@
 EXP_SCALE = math.log2(math.e) * HEAD_WIDTH ** (-0.5)
 PAIR = 2
 VMEM_LIMIT = 28 * 1024 * 1024
-PACK_VMEM_LIMIT = 28 * 1024 * 1024
+FIRST_VMEM_LIMIT = 60 * 1024 * 1024
 
 
 def hbm_spec():
@@ -133,7 +133,7 @@
         in_specs=in_specs,
         out_specs=specs,
         scratch_shapes=[pltpu.SemaphoreType.DMA((n_copies,))],
-        compiler_params=pltpu.CompilerParams(vmem_limit_bytes=PACK_VMEM_LIMIT),
+        compiler_params=pltpu.CompilerParams(vmem_limit_bytes=VMEM_LIMIT if with_table else FIRST_VMEM_LIMIT),
         cost_estimate=pl.CostEstimate(flops=0, bytes_accessed=0, transcendentals=0),
         name="pack_spans",
     )(*operands)
@@ -187,22 +187,21 @@
     )(*blocks, weight)
 
 
-def attend_kernel(parts, with_store, with_question, with_fresh, first, last, *refs):
+def attend_kernel(parts, n_pieces, with_store, with_question, with_fresh, first, last, *refs):
     table_ref, query_ref, question_ref = refs[:3]
     refs = refs[3:]
     if with_store:
         store_ref, refs = refs[0], refs[1:]
-    else:
-        piece_refs, refs = refs[: len(parts)], refs[len(parts) :]
+    piece_refs, refs = refs[:n_pieces], refs[n_pieces:]
     if with_fresh:
         fresh_ref, refs = refs[0], refs[1:]
     if not first:
-        blend_in, stats_in = refs[:2]
-        refs = refs[2:]
+        blend_in, total_in, highest_in = refs[:3]
+        refs = refs[3:]
     if last:
-        out_ref, keys, values, out_stage, sems = refs
+        out_ref, keys, values, live, out_stage, sems = refs
     else:
-        blend_out, stats_out, keys, values = refs
+        blend_out, total_out, highest_out, keys, values, live = refs
     width = HEAD_WIDTH
     question_len, query_cols = query_ref.shape
     kv_heads = question_ref.shape[1] // (2 * width)
@@ -216,31 +215,39 @@
         columns = pl.ds(column, PAIR * width)
         return pltpu.make_async_copy(out_stage.at[:, columns], out_ref.at[:, columns], sems.at[step])
 
+    base = 0
+    for line, start, length, _, _ in parts:
+        row = start + lax.broadcasted_iota(jnp.int32, (length, width), 0)
+        stale = row < jnp.where(table_ref[line, 0] == 0, start + length, 0)
+        for column in range(1, table_ref.shape[1] - 1):
+            stale = stale | (row == table_ref[line, column])
+        live[base : base + length, :] = jnp.where(stale, 0.0, 1.0).astype(live.dtype)
+        base += length
+    values[:base, width:] = live[:base, :]
+    if values.shape[0] > base:
+        values[base:, width:] = jnp.ones((values.shape[0] - base, width), values.dtype)
+
     def one_kv_head(k, carry):
         key_at = pl.ds(pl.multiple_of(k * 2 * width, 2 * width), width)
         value_at = pl.ds(pl.multiple_of(k * 2 * width + width, width), width)
         spare_key = question_ref[0:8, key_at][0:1].astype(jnp.float32)
         base = 0
-        for i, (line, start, length) in enumerate(parts):
+        for line, start, length, source, offset in parts:
+            here = slice(base, base + length)
             if with_store:
                 slot = table_ref[line, table_ref.shape[1] - 1]
                 key, value = store_ref[slot, :, key_at], store_ref[slot, :, value_at]
             else:
-                key, value = piece_refs[i][:length, key_at], piece_refs[i][:length, value_at]
-            row = start + lax.broadcasted_iota(jnp.int32, (length, width), 0)
-            stale = row < jnp.where(table_ref[line, 0] == 0, start + length, 0)
-            for column in range(1, table_ref.shape[1] - 1):
-                stale = stale | (row == table_ref[line, column])
-            here = slice(base, base + length)
-            keys[here, :] = jnp.where(stale, spare_key, key.astype(jnp.float32)).astype(keys.dtype)
-            values[here, :width] = jnp.where(stale, 0.0, value.astype(jnp.float32)).astype(values.dtype)
-            values[here, width:] = jnp.where(stale, 0.0, 1.0).astype(values.dtype)
+                at = slice(offset, offset + length)
+                key, value = piece_refs[source][at, key_at], piece_refs[source][at, value_at]
+            read = live[here, :].astype(jnp.float32) > 0.5
+            keys[here, :] = jnp.where(read, key.astype(jnp.float32), spare_key).astype(keys.dtype)
+            values[here, :width] = jnp.where(read, value.astype(jnp.float32), 0.0).astype(values.dtype)
             base += length
         for ref in ([fresh_ref] if with_fresh else []) + ([question_ref] if with_question else []):
             here = slice(base, base + ref.shape[0])
             keys[here, :] = ref[:, key_at]
             values[here, :width] = ref[:, value_at]
-            values[here, width:] = jnp.ones((ref.shape[0], width), values.dtype)
             base += ref.shape[0]
         plain = base - (question_len if with_question else 0)
 
@@ -273,28 +280,27 @@
             highest = functools.reduce(
                 jnp.maximum, [jnp.max(part, axis=1, keepdims=True) for part in scores]
             )
+            highest = jnp.broadcast_to(highest, (rows, width))
             here = pl.ds(pl.multiple_of((k * pairs + pair) * rows, rows), rows)
             if not first:
-                stats = stats_in[here, :]
-                before = stats[:, :1]
-                row_total = stats[:, width // 2 : width // 2 + 1]
+                before = highest_in[here, :]
                 highest = jnp.maximum(highest, before)
                 fade = jnp.exp2((before - highest) * EXP_SCALE)
             blend = 0.0
             offset = 0
             for part in scores:
-                probs = jnp.exp2((part - highest) * EXP_SCALE).astype(jnp.bfloat16)
+                length = part.shape[1]
+                shift = jnp.concatenate([highest] * (length // width), axis=1)
+                probs = jnp.exp2((part - shift) * EXP_SCALE).astype(jnp.bfloat16)
                 blend = blend + jnp.dot(
-                    probs,
-                    values[offset : offset + part.shape[1], :],
-                    preferred_element_type=jnp.float32,
+                    probs, values[offset : offset + length, :], preferred_element_type=jnp.float32
                 )
-                offset += part.shape[1]
+                offset += length
             total = blend[:, width:]
             blend = blend[:, :width]
             if not first:
                 blend = blend + blend_in[here, :] * fade
-                total = total + row_total * fade
+                total = total + total_in[here, :] * fade
             if last:
                 done = (blend / total).astype(out_ref.dtype)
                 for h in range(PAIR):
@@ -306,9 +312,9 @@
                     pl.multiple_of(k * group_cols + pair * PAIR * width, PAIR * width),
                 ).start()
             else:
-                lane = lax.broadcasted_iota(jnp.int32, (rows, width), 1)
                 blend_out[here, :] = blend
-                stats_out[here, :] = jnp.where(lane < width // 2, highest, total)
+                total_out[here, :] = total
+                highest_out[here, :] = highest
         return carry
 
     lax.fori_loop(0, kv_heads, one_kv_head, 0)
@@ -322,8 +328,9 @@
     heads = query_cols // HEAD_WIDTH
     pairs = heads // PAIR
     first = state is None
-    operands = [table, queries, question] + ([store] if store is not None else list(pieces))
-    length = sum(rows for _, _, rows in parts) + (question_len if with_question else 0)
+    operands = [table, queries, question] + ([store] if store is not None else []) + list(pieces)
+    held = sum(part[2] for part in parts)
+    length = held + (question_len if with_question else 0)
     if fresh is not None:
         operands.append(fresh)
         length += fresh.shape[0]
@@ -332,18 +339,19 @@
     scratch = [
         pltpu.VMEM((length, HEAD_WIDTH), jnp.bfloat16),
         pltpu.VMEM((length, 2 * HEAD_WIDTH), jnp.bfloat16),
+        pltpu.VMEM((held, HEAD_WIDTH), jnp.bfloat16),
     ]
     if last:
         out_shape = jax.ShapeDtypeStruct(queries.shape, queries.dtype)
         out_specs = hbm_spec()
         scratch += [pltpu.VMEM(queries.shape, queries.dtype), pltpu.SemaphoreType.DMA((pairs,))]
     else:
-        out_shape = [jax.ShapeDtypeStruct((heads * question_len, HEAD_WIDTH), jnp.float32)] * 2
-        out_specs = [vmem_spec()] * 2
+        out_shape = [jax.ShapeDtypeStruct((heads * question_len, HEAD_WIDTH), jnp.float32)] * 3
+        out_specs = [vmem_spec()] * 3
     return pl.pallas_call(
         functools.partial(
-            attend_kernel, tuple(parts), store is not None, with_question, fresh is not None, first,
-            last,
+            attend_kernel, tuple(parts), len(pieces), store is not None, with_question,
+            fresh is not None, first, last,
         ),
         out_shape=out_shape,
         in_specs=[smem_spec()] + [vmem_spec()] * (len(operands) - 1),
@@ -394,68 +402,101 @@
         )
 
     away = list(range(n_store - 1, 0, -1))
-    stages = [[(span, 0, span_len)] for span in range(per_pair)]
-    if per_pair > 1:
-        half = span_len // 2
-        stages[-1:] = [[(per_pair - 1, start, half)] for start in (0, half)]
-    messages = [[(d, i == 0, pieces) for d in away] for i, pieces in enumerate(stages)]
-    outbox, _ = packed(messages[0])
-    arrived = [[exchange(piece, d, "store", "stage0_") for piece, d in zip(outbox, away)]]
-    later = [message for stage in messages[1:] for message in stage]
-    (hidden_own, *outbox), table = packed([(0, True, [])] + later, recompute_rows[0])
-
-    def block(parts, pieces, state, fresh=None, last=False):
+    half = span_len // 2
+
+    def cuts(distance):
+        if per_pair == 1:
+            return [span_len]
+        if distance == 1:
+            return [(per_pair - 1) * span_len, 0, span_len]
+        if distance % 2:
+            return [span_len] * (per_pair - 1) + [half] * 2
+        return [span_len + half] + [span_len] * (per_pair - 3) + [half] * 3
+
+    def pieces_of(first, length):
+        pieces = []
+        while length:
+            span, start = divmod(first, span_len)
+            rows = min(span_len - start, length)
+            pieces.append((span, start, rows))
+            first, length = first + rows, length - rows
+        return pieces
+
+    messages = {}
+    for d in away:
+        first = 0
+        for number, length in enumerate(cuts(d)):
+            if length:
+                messages[d, number] = (d, not number, pieces_of(first, length))
+            first += length
+    outbox, _ = packed([messages[d, 0] for d in away])
+    coming = [exchange(piece, d, "store", "spans0_") for piece, d in zip(outbox, away)]
+    count = 1 + max(number for _, number in messages)
+    later = [(d, number) for number in range(1, count) for d in away if (d, number) in messages]
+    (hidden_own, *outbox), table = packed(
+        [(0, True, [])] + [messages[key] for key in later], recompute_rows[0]
+    )
+    outbox = dict(zip(later, outbox))
+
+    def behind(pieces, state):
+        return [after(piece, state[2]) for piece in pieces]
+
+    def block(keys, state, fresh=None, last=False):
+        parts = []
+        for source, (d, number) in enumerate(keys):
+            offset = 0
+            for span, start, rows in messages[d, number][2]:
+                parts.append((d * per_pair + span, start, rows, source, offset))
+                offset += rows
+        if not keys:
+            parts = [(span, 0, span_len, 0, 0) for span in range(per_pair)]
         return attend(
-            table, query_rows, question, parts, pieces, None if pieces else key_value_store, fresh,
-            state, not pieces, last,
+            table, query_rows, question, parts, [arrived[key] for key in keys],
+            None if keys else key_value_store, fresh, state, not keys, last,
         )
 
-    def parts_of(number):
-        return [(d * per_pair + span, start, rows) for d, _, p in messages[number] for span, start, rows in p]
-
-    def behind(pieces, state):
-        return list(lax.optimization_barrier((*pieces, state[1]))[:-1])
-
-    state = block([(span, 0, span_len) for span in range(per_pair)], [], None)
-    states = [state]
-    arrived[0] = behind(arrived[0], state)
-    for number in range(1, len(stages)):
-        here, outbox = outbox[: len(away)], outbox[len(away) :]
-        before = arrived[-1]
+    arrived = {}
+    state = block([], None)
+    arrived.update(zip([(d, 0) for d in away], behind(coming, state)))
+    for number in range(1, count):
+        keys = [key for key in later if key[1] == number]
         coming = [
-            exchange(after(piece, earlier), d, "store", "stage%d_" % number)
-            for piece, earlier, d in zip(here, before, away)
+            exchange(
+                after(outbox[key], arrived[key[0] if key[0] > 1 else away[0], number - 1]),
+                key[0], "store", "spans%d_" % number,
+            )
+            for key in keys
         ]
-        states.append(block(parts_of(number - 1), before, states[-1]))
-        arrived.append(behind(coming, states[-1]))
-
-    def paced(array, step):
-        return after(array, *arrived[min(step, len(arrived) - 1)])
-
-    first_row = arrived[0][0].shape[0] - hidden_own.shape[0]
-    blocks = [hidden_own] + [piece[first_row:] for piece in arrived[0][::-1]]
+        state = block([(d, number - 1) for d in away if (d, number - 1) in arrived], state)
+        arrived.update(zip(keys, behind(coming, state)))
+
+    blocks = [hidden_own]
+    for d in away[::-1]:
+        piece = arrived[d, 0]
+        blocks.append(piece[piece.shape[0] - hidden_own.shape[0] :])
     distances = [0]
     for step, bit in enumerate(reversed(range(n_tensor.bit_length() - 1))):
         distances += [distance ^ (1 << bit) for distance in distances]
-        blocks[-1] = paced(blocks[-1], step)
+        if step and per_pair > 1:
+            blocks[-1] = after(blocks[-1], *[arrived[d, 1] for d in away if d > 1])
         gathered = jnp.concatenate(blocks, axis=0)
         blocks = [gathered, exchange(gathered, 1 << bit, "tensor", "hidden")]
-    step = n_tensor.bit_length() - 1
-    blocks[-1] = paced(blocks[-1], step)
     partial, sent = project(blocks, kv_weight, n_store, shard_rows, distances)
     for bit in range(n_store.bit_length() - 1):
         if bit:
-            sent = paced(partial[1::2].astype(jnp.bfloat16), step + bit)
+            sent = partial[1::2].astype(jnp.bfloat16)
         partial = partial[0::2] + exchange(sent, 1 << bit, "store", "partial").astype(jnp.float32)
     fresh = partial[0].astype(jnp.bfloat16)
     fresh_out = fresh.reshape(1, span_count, recomp, kv_cols)
 
-    state, parts, size = states[-1], parts_of(len(stages) - 1), 6
-    for i in range(0, len(away), size):
-        last = i + size >= len(away)
-        state = block(
-            parts[i : i + size], arrived[-1][i : i + size], state, fresh if last else None, last
-        )
+    keys = [(d, count - 1) for d in away if (d, count - 1) in arrived]
+    size = 1 if per_pair > 1 else 6
+    batches = [keys[i : i + size] for i in range(0, len(keys), size)]
+    for i, keys in enumerate(batches):
+        joins, last = i == max(0, len(batches) - 2), i == len(batches) - 1
+        if i:
+            arrived.update(zip(keys, behind([arrived[key] for key in keys], state)))
+        state = block(keys, state, fresh if joins else None, last)
     return (state[None], fresh_out)
 
 

time: 139 us -> 130 us (0.935)
  Pallas kernels: 59.2 us -> 49.6 us
  starting transfers between devices: 27.1 us -> 31.7 us
  local copies, waits for them, and re-layouts: 6.32 us -> 2.71 us
    pallas_call x6 -> x7, Pallas kernels: 51.5 us -> 40.3 us  [attend(): pl.pallas_call(functools.partial(attend_kernel, tuple(parts), len(pieces)...]
    ppermute x19 -> x16, starting transfers between devices: 27.1 us -> 31.7 us  [exchange(): return lax.ppermute(piece, axis, [(i, i ^ distance) for i in range(size)])]
    unnamed x28 -> x19, local copies, waits for them, and re-layouts: 6.15 us -> 1.63 us
    pallas_call x2, Pallas kernels: 6.41 us -> 8.08 us  [pack(): pl.pallas_call(functools.partial(pack_kernel, messages, shard, with_table...]
    ppermute x19 -> x16, waiting for transfers between devices: 44.6 us -> 43.7 us  [exchange(): return lax.ppermute(piece, axis, [(i, i ^ distance) for i in range(size)])]
  transfers between devices with their start and end apart: 19 -> 16, of which waited for: 5 -> 5; matrix products, arithmetic and copies ran while one was open for 0% -> 1% of each run, Pallas kernels for 35% -> 30%
where the time goes in v4:
time: 130 us
  Pallas kernels  49.6 us (38%)
  waiting for transfers between devices  43.7 us (34%)
  starting transfers between devices  31.7 us (24%)
  local copies, waits for them, and re-layouts  2.71 us (2%)
    ppermute x16, waiting for transfers between devices, exchange(): return lax.ppermute(piece, axis, [(i, i ^ distance) for i in range(size)])  43.7 us
    pallas_call x7, Pallas kernels, attend(): pl.pallas_call(functools.partial(attend_kernel, tuple(parts), len(pieces)...  40.3 us
    ppermute x16, starting transfers between devices, exchange(): return lax.ppermute(piece, axis, [(i, i ^ distance) for i in range(size)])  31.7 us
    pallas_call x2, Pallas kernels, pack(): pl.pallas_call(functools.partial(pack_kernel, messages, shard, with_table...  8.08 us
  transfers between devices with their start and end apart: 16, of which 5 were waited for; matrix products, arithmetic and copies ran while one was open for 1% of the time, Pallas kernels for 30%

profile of v4, /device:TPU:0, one launch (start us, length us, event | category | flops | bytes accessed | tf_op | source)
XLA Modules:
  0.0 129.5 jit_solution(654128369166491450)
XLA Ops:
  0.7 3.9 %pack_spans.3 = (bf16[384,512]{1,0:T(8,128)(2,1)}, bf16[512,512]{1,0:T(8,128)(2,1)}, bf16[896,512]{1,0:T(8,128)(2,1)}) custom-call(s32[32]{0:T(128)} %refs_0_.3, s32[4,16]{1,0:T(4,128)} %refs_1_.3, bf16[8,256,512]{2,1,0:T(8,128)(2,1)} %refs_3_.1, bf16[128,8192]{1,0:T(8,128)(2,1)} %bitcast.16), custom_call_target="tpu_custom_call" | custom-call | tf_op jit(solution)/shard_map/pack_spans/pallas_call | solution.py:130
  4.5 3.1 %collective-permute-start.3 = (bf16[896,512]{1,0:T(8,128)(2,1)}, bf16[896,512]{1,0:T(8,128)(2,1)}, u32[]{:S(2)}, u32[]{:S(2)}) collective-permute-start(bf16[896,512]{1,0:T(8,128)(2,1)} %get-tuple-element.70), channel_id=1, source_target_pairs={{0,4},{4,0},{8,12},{12,8},{1,5},{5,1},{9,13},{13,9},{2,6},{6,2},{1... | collective-permute-start | bytes 2752520 | tf_op jit(solution)/shard_map/spans0_1/ppermute | solution.py:394
  7.6 2.6 %collective-permute-start = (bf16[512,512]{1,0:T(8,128)(2,1)}, bf16[512,512]{1,0:T(8,128)(2,1)S(1)}, u32[]{:S(2)}, u32[]{:S(2)}) collective-permute-start(bf16[512,512]{1,0:T(8,128)(2,1)} %get-tuple-element.64), channel_id=1, source_target_pairs={{0,8},{4,12},{8,0},{12,4},{1,9},{5,13},{9,1},{13,5},{2,10},{6,14},... | collective-permute-start | bytes 1572872 | tf_op jit(solution)/shard_map/spans0_2/ppermute | solution.py:394
  10.3 1.6 %copy-done.2 = bf16[8,256,512]{2,1,0:T(8,128)(2,1)S(1)} copy-done((bf16[8,256,512]{2,1,0:T(8,128)(2,1)S(1)}, bf16[8,256,512]{2,1,0:T(8,128)(2,1)}, u32[]{:S(2)}) %copy-start.2) | copy-done | bytes 2097176
  11.9 4.2 %pack_spans.2 = (bf16[128,512]{1,0:T(8,128)(2,1)S(1)}, bf16[256,512]{1,0:T(8,128)(2,1)S(1)}, bf16[256,512]{1,0:T(8,128)(2,1)S(1)}, bf16[256,512]{1,0:T(8,128)(2,...) custom-call(s32[32]{0:T(128)S(1)} %copy-done.7, ...), custom_call_target="tpu_custom_call" | custom-call | tf_op jit(solution)/shard_map/pack_spans/pallas_call | solution.py:130
  16.2 8.7 %attend_spans.7 = (f32[4096,128]{1,0:T(8,128)S(1)}, f32[4096,128]{1,0:T(8,128)S(1)}, f32[4096,128]{1,0:T(8,128)S(1)}) custom-call(s32[16,10]{1,0:T(8,128)S(1)} %get-tuple-element.59.refs_0_, bf16[256,2048]{1,0:T(8,128)(2,1)S(1)} %bitcast.9, bf16[256,512]{1,0:T(8,128)(2,1)S(1)} %bitcast.18, bf16[8,256,512]{2,1,0:T(8,128)(2,1)S(1)} %copy-done.3), custom_call_target="tpu_custom_call" | custom-call | flops 5368709120 | tf_op jit(solution)/shard_map/attend_spans/pallas_call | solution.py:351
  24.8 25.3 %collective-permute-done.2.refs_3_ = bf16[384,512]{1,0:T(8,128)(2,1)S(1)} collective-permute-done((bf16[384,512]{1,0:T(8,128)(2,1)}, bf16[384,512]{1,0:T(8,128)(2,1)S(1)}, u32[]{:S(2)}, u32[]{:S(2)}) %collective-permute-start.2) | collective-permute-done | bytes 393248 | tf_op jit(solution)/shard_map/spans0_3/ppermute | solution.py:394
  54.0 1.6 %collective-permute-start.12 = (bf16[512,512]{1,0:T(8,128)(2,1)S(1)}, bf16[512,512]{1,0:T(8,128)(2,1)S(1)}, u32[]{:S(2)}, u32[]{:S(2)}) collective-permute-start(bf16[512,512]{1,0:T(8,128)(2,1)S(1)} %pad_maximum_fusion), channel_id=1, source_target_pairs={{0,2},{1,3},{2,0},{3,1},{4,6},{5,7},{6,4},{7,5},{8,10},{9,11},{10,... | collective-permute-start | bytes 1572872 | tf_op jit(solution)/shard_map/hidden2/ppermute | solution.py:394
  55.6 11.3 %attend_spans.8 = (f32[4096,128]{1,0:T(8,128)S(1)}, f32[4096,128]{1,0:T(8,128)S(1)}, f32[4096,128]{1,0:T(8,128)S(1)}) custom-call(s32[16,10]{1,0:T(8,128)S(1)} %get-tuple-element.59.refs_0_, bf16[256,2048]{1,0:T(8,128)(2,1)S(1)} %bitcast.10, bf16[256,512]{1,0:T(8,128)(2,1)S(1)} %bitcast.19, bf16[384,512]{1,0:T(8,128)(2,1)S(1)} %collective-permute-done.2.refs_3_, ...), custom_call_target="tpu_custom_call" | custom-call | flops 5905580032 | tf_op jit(solution)/shard_map/attend_spans/pallas_call | solution.py:351
  66.9 6.2 %collective-permute-done.1.refs_4_ = bf16[256,512]{1,0:T(8,128)(2,1)S(1)} collective-permute-done((bf16[256,512]{1,0:T(8,128)(2,1)S(1)}, bf16[256,512]{1,0:T(8,128)(2,1)S(1)}, u32[]{:S(2)}, u32[]{:S(2)}) %collective-permute-start.1) | collective-permute-done | bytes 262176 | tf_op jit(solution)/shard_map/spans1_2/ppermute | solution.py:394
  73.2 2.2 %collective-permute-start.7 = (bf16[256,512]{1,0:T(8,128)(2,1)S(1)}, bf16[256,512]{1,0:T(8,128)(2,1)S(1)}, u32[]{:S(2)}, u32[]{:S(2)}) collective-permute-start(bf16[256,512]{1,0:T(8,128)(2,1)S(1)} %get-tuple-element.86), channel_id=1, source_target_pairs={{0,12},{4,8},{8,4},{12,0},{1,13},{5,9},{9,5},{13,1},{2,14},{6,10},... | collective-permute-start | bytes 786440 | tf_op jit(solution)/shard_map/spans2_3/ppermute | solution.py:394
  75.4 2.3 %collective-permute-start.4 = (bf16[128,512]{1,0:T(8,128)(2,1)S(1)}, bf16[128,512]{1,0:T(8,128)(2,1)S(1)}, u32[]{:S(2)}, u32[]{:S(2)}) collective-permute-start(bf16[128,512]{1,0:T(8,128)(2,1)S(1)} %get-tuple-element.76), channel_id=1, source_target_pairs={{0,8},{4,12},{8,0},{12,4},{1,9},{5,13},{9,1},{13,5},{2,10},{6,14},... | collective-permute-start | bytes 393224 | tf_op jit(solution)/shard_map/spans2_2/ppermute | solution.py:394
  79.0 4.7 %attend_spans.9 = (f32[4096,128]{1,0:T(8,128)S(1)}, f32[4096,128]{1,0:T(8,128)S(1)}, f32[4096,128]{1,0:T(8,128)S(1)}) custom-call(s32[16,10]{1,0:T(8,128)S(1)} %get-tuple-element.59.refs_0_, bf16[256,2048]{1,0:T(8,128)(2,1)S(1)} %bitcast.11, bf16[256,512]{1,0:T(8,128)(2,1)S(1)} %bitcast.20, bf16[256,512]{1,0:T(8,128)(2,1)S(1)} %collective-permute-done.5.refs_3_, ...), custom_call_target="tpu_custom_call" | custom-call | flops 2147483648 | tf_op jit(solution)/shard_map/attend_spans/pallas_call | solution.py:351
  83.7 6.8 %collective-permute-done.4.refs_4_ = bf16[128,512]{1,0:T(8,128)(2,1)S(1)} collective-permute-done((bf16[128,512]{1,0:T(8,128)(2,1)S(1)}, bf16[128,512]{1,0:T(8,128)(2,1)S(1)}, u32[]{:S(2)}, u32[]{:S(2)}) %collective-permute-start.4) | collective-permute-done | bytes 131104 | tf_op jit(solution)/shard_map/spans2_2/ppermute | solution.py:394
  90.5 3.4 %collective-permute-start.6 = (bf16[128,512]{1,0:T(8,128)(2,1)S(1)}, bf16[128,512]{1,0:T(8,128)(2,1)S(1)}, u32[]{:S(2)}, u32[]{:S(2)}) collective-permute-start(bf16[128,512]{1,0:T(8,128)(2,1)S(1)} %get-tuple-element.84), channel_id=1, source_target_pairs={{0,8},{4,12},{8,0},{12,4},{1,9},{5,13},{9,1},{13,5},{2,10},{6,14},... | collective-permute-start | bytes 393224 | tf_op jit(solution)/shard_map/spans3_2/ppermute | solution.py:394
  93.9 1.8 %collective-permute-start.10 = (bf16[128,512]{1,0:T(8,128)(2,1)S(1)}, bf16[128,512]{1,0:T(8,128)(2,1)S(1)}, u32[]{:S(2)}, u32[]{:S(2)}) collective-permute-start(bf16[128,512]{1,0:T(8,128)(2,1)S(1)} %get-tuple-element.97), channel_id=1, source_target_pairs={{0,12},{4,8},{8,4},{12,0},{1,13},{5,9},{9,5},{13,1},{2,14},{6,10},... | collective-permute-start | bytes 393224 | tf_op jit(solution)/shard_map/spans3_3/ppermute | solution.py:394
  95.7 6.0 %attend_spans.10 = (f32[4096,128]{1,0:T(8,128)S(1)}, f32[4096,128]{1,0:T(8,128)S(1)}, f32[4096,128]{1,0:T(8,128)S(1)}) custom-call(s32[16,10]{1,0:T(8,128)S(1)} %get-tuple-element.59.refs_0_, bf16[256,2048]{1,0:T(8,128)(2,1)S(1)} %bitcast.12, bf16[256,512]{1,0:T(8,128)(2,1)S(1)} %bitcast.21, bf16[256,512]{1,0:T(8,128)(2,1)S(1)} %collective-permute-done.7.refs_3_, ...), custom_call_target="tpu_custom_call" | custom-call | flops 2684354560 | tf_op jit(solution)/shard_map/attend_spans/pallas_call | solution.py:351
  101.6 2.2 %collective-permute-done.6.refs_4_ = bf16[128,512]{1,0:T(8,128)(2,1)S(1)} collective-permute-done((bf16[128,512]{1,0:T(8,128)(2,1)S(1)}, bf16[128,512]{1,0:T(8,128)(2,1)S(1)}, u32[]{:S(2)}, u32[]{:S(2)}) %collective-permute-start.6) | collective-permute-done | bytes 131104 | tf_op jit(solution)/shard_map/spans3_2/ppermute | solution.py:394
  103.8 1.8 %collective-permute-start.11 = (bf16[128,512]{1,0:T(8,128)(2,1)S(1)}, bf16[128,512]{1,0:T(8,128)(2,1)S(1)}, u32[]{:S(2)}, u32[]{:S(2)}) collective-permute-start(bf16[128,512]{1,0:T(8,128)(2,1)S(1)} %get-tuple-element.104), channel_id=1, source_target_pairs={{0,12},{4,8},{8,4},{12,0},{1,13},{5,9},{9,5},{13,1},{2,14},{6,10},... | collective-permute-start | bytes 393224 | tf_op jit(solution)/shard_map/spans4_3/ppermute | solution.py:394
  105.8 10.0 %collective-permute-start.15 = (bf16[1,128,512]{2,1,0:T(8,128)(2,1)S(1)}, bf16[1,128,512]{2,1,0:T(8,128)(2,1)S(1)}, u32[]{:S(2)}, u32[]{:S(2)}) collective-permute-start(bf16[1,128,512]{2,1,0:T(8,128)(2,1)S(1)} %slice.41), channel_id=1, source_target_pairs={{0,8},{4,12},{8,0},{12,4},{1,9},{5,13},{9,1},{13,5},{2,10},{6,14},... | collective-permute-start | bytes 393224 | tf_op jit(solution)/shard_map/partial2/ppermute | solution.py:394
  115.8 3.2 %attend_spans.11 = (f32[4096,128]{1,0:T(8,128)S(1)}, f32[4096,128]{1,0:T(8,128)S(1)}, f32[4096,128]{1,0:T(8,128)S(1)}) custom-call(s32[16,10]{1,0:T(8,128)S(1)} %get-tuple-element.59.refs_0_, bf16[256,2048]{1,0:T(8,128)(2,1)S(1)} %bitcast.13, bf16[256,512]{1,0:T(8,128)(2,1)S(1)} %bitcast.22, bf16[128,512]{1,0:T(8,128)(2,1)S(1)} %collective-permute-done.10.refs_3_, ...), custom_call_target="tpu_custom_call" | custom-call | flops 1073741824 | tf_op jit(solution)/shard_map/attend_spans/pallas_call | solution.py:351
  119.0 3.1 %collective-permute-done.15 = bf16[1,128,512]{2,1,0:T(8,128)(2,1)S(1)} collective-permute-done((bf16[1,128,512]{2,1,0:T(8,128)(2,1)S(1)}, bf16[1,128,512]{2,1,0:T(8,128)(2,1)S(1)}, u32[]{:S(2)}, u32[]{:S(2)}) %collective-permute-start.15) | collective-permute-done | bytes 131104 | tf_op jit(solution)/shard_map/partial2/ppermute | solution.py:394
  122.8 3.1 %attend_spans.12 = (f32[4096,128]{1,0:T(8,128)S(1)}, f32[4096,128]{1,0:T(8,128)S(1)}, f32[4096,128]{1,0:T(8,128)S(1)}) custom-call(s32[16,10]{1,0:T(8,128)S(1)} %get-tuple-element.59.refs_0_, bf16[256,2048]{1,0:T(8,128)(2,1)S(1)} %bitcast.14, bf16[256,512]{1,0:T(8,128)(2,1)S(1)} %bitcast.23, bf16[128,512]{1,0:T(8,128)(2,1)S(1)} %collective-permute-done.11.refs_3_, ...), custom_call_target="tpu_custom_call" | custom-call | flops 1073741824 | tf_op jit(solution)/shard_map/attend_spans/pallas_call | solution.py:351
  125.8 3.5 %attend_spans.13 = bf16[256,2048]{1,0:T(8,128)(2,1)} custom-call(s32[16,10]{1,0:T(8,128)S(1)} %get-tuple-element.59.refs_0_, bf16[256,2048]{1,0:T(8,128)(2,1)S(1)} %bitcast.15, bf16[256,512]{1,0:T(8,128)(2,1)S(1)} %bitcast.24, bf16[128,512]{1,0:T(8,128)(2,1)S(1)} %collective-permute-done.9.refs_3_, f32[4096,128]{1,0:T(8,128)S(1)} %get-tuple-element.114.refs_4_, ...), custom_call_target="tpu_custom_call" | custom-call | flops 536870912 | tf_op jit(solution)/shard_map/attend_spans/pallas_call | solution.py:351
  (46 shorter events, 6.2 us)
Async XLA Ops:
  0.6 9.6 %copy-start.8 = (s32[1,16,8]{1,2,0:T(8,128)S(1)}, s32[1,16,8]{1,2,0:T(8,128)}, u32[]{:S(2)}) copy-start(s32[1,16,8]{1,2,0:T(8,128)} %param.13) | copy-start | bytes 1540
  0.6 9.7 %copy-start.1 = (bf16[1,16,8,8192]{3,2,1,0:T(8,128)(2,1)S(1)}, bf16[1,16,8,8192]{3,2,1,0:T(8,128)(2,1)}, u32[]{:S(2)}) copy-start(bf16[1,16,8,8192]{3,2,1,0:T(8,128)(2,1)} %param.14) | copy-start | bytes 6291460
  0.7 9.7 %copy-start.6 = (s32[4,16]{1,0:T(4,128)S(1)}, s32[4,16]{1,0:T(4,128)}, u32[]{:S(2)}) copy-start(s32[4,16]{1,0:T(4,128)} %refs_1_.3) | copy-start | bytes 772
  0.7 9.6 %copy-start.7 = (s32[32]{0:T(128)S(1)}, s32[32]{0:T(128)}, u32[]{:S(2)}) copy-start(s32[32]{0:T(128)} %refs_0_.3) | copy-start | bytes 388
  4.5 48.5 %collective-permute-start.3 = (bf16[896,512]{1,0:T(8,128)(2,1)}, bf16[896,512]{1,0:T(8,128)(2,1)}, u32[]{:S(2)}, u32[]{:S(2)}) collective-permute-start(bf16[896,512]{1,0:T(8,128)(2,1)} %get-tuple-element.70), channel_id=1, source_target_pairs={{0,4},{4,0},{8,12},{12,8},{1,5},{5,1},{9,13},{13,9},{2,6},{6,2},{1... | collective-permute-start | bytes 2752520 | tf_op jit(solution)/shard_map/spans0_1/ppermute | solution.py:394
  7.6 44.0 %collective-permute-start = (bf16[512,512]{1,0:T(8,128)(2,1)}, bf16[512,512]{1,0:T(8,128)(2,1)S(1)}, u32[]{:S(2)}, u32[]{:S(2)}) collective-permute-start(bf16[512,512]{1,0:T(8,128)(2,1)} %get-tuple-element.64), channel_id=1, source_target_pairs={{0,8},{4,12},{8,0},{12,4},{1,9},{5,13},{9,1},{13,5},{2,10},{6,14},... | collective-permute-start | bytes 1572872 | tf_op jit(solution)/shard_map/spans0_2/ppermute | solution.py:394
  10.2 39.9 %collective-permute-start.2 = (bf16[384,512]{1,0:T(8,128)(2,1)}, bf16[384,512]{1,0:T(8,128)(2,1)S(1)}, u32[]{:S(2)}, u32[]{:S(2)}) collective-permute-start(bf16[384,512]{1,0:T(8,128)(2,1)} %get-tuple-element.68), channel_id=1, source_target_pairs={{0,12},{4,8},{8,4},{12,0},{1,13},{5,9},{9,5},{13,1},{2,14},{6,10},... | collective-permute-start | bytes 1179656 | tf_op jit(solution)/shard_map/spans0_3/ppermute | solution.py:394
  11.9 4.2 %copy-start = (bf16[1,256,2048]{2,1,0:T(8,128)(2,1)S(1)}, bf16[1,256,2048]{2,1,0:T(8,128)(2,1)}, u32[]{:S(2)}) copy-start(bf16[1,256,2048]{2,1,0:T(8,128)(2,1)} %param.8) | copy-start | bytes 3145732
  11.9 4.3 %copy-start.3 = (bf16[8,256,512]{2,1,0:T(8,128)(2,1)S(1)}, bf16[8,256,512]{2,1,0:T(8,128)(2,1)}, u32[]{:S(2)}) copy-start(bf16[8,256,512]{2,1,0:T(8,128)(2,1)} %refs_3_.1) | copy-start | bytes 6291460
  11.9 4.3 %copy-start.4 = (bf16[1,256,512]{2,1,0:T(8,128)(2,1)S(1)}, bf16[1,256,512]{2,1,0:T(8,128)(2,1)}, u32[]{:S(2)}) copy-start(bf16[1,256,512]{2,1,0:T(8,128)(2,1)} %param.9) | copy-start | bytes 786436
  50.1 23.0 %collective-permute-start.5 = (bf16[256,512]{1,0:T(8,128)(2,1)S(1)}, bf16[256,512]{1,0:T(8,128)(2,1)S(1)}, u32[]{:S(2)}, u32[]{:S(2)}) collective-permute-start(bf16[256,512]{1,0:T(8,128)(2,1)S(1)} %get-tuple-element.78), channel_id=1, source_target_pairs={{0,12},{4,8},{8,4},{12,0},{1,13},{5,9},{9,5},{13,1},{2,14},{6,10},... | collective-permute-start | bytes 786440 | tf_op jit(solution)/shard_map/spans1_3/ppermute | solution.py:394
  51.6 21.5 %collective-permute-start.1 = (bf16[256,512]{1,0:T(8,128)(2,1)S(1)}, bf16[256,512]{1,0:T(8,128)(2,1)S(1)}, u32[]{:S(2)}, u32[]{:S(2)}) collective-permute-start(bf16[256,512]{1,0:T(8,128)(2,1)S(1)} %get-tuple-element.67), channel_id=1, source_target_pairs={{0,8},{4,12},{8,0},{12,4},{1,9},{5,13},{9,1},{13,5},{2,10},{6,14},... | collective-permute-start | bytes 786440 | tf_op jit(solution)/shard_map/spans1_2/ppermute | solution.py:394
  54.0 19.1 %collective-permute-start.12 = (bf16[512,512]{1,0:T(8,128)(2,1)S(1)}, bf16[512,512]{1,0:T(8,128)(2,1)S(1)}, u32[]{:S(2)}, u32[]{:S(2)}) collective-permute-start(bf16[512,512]{1,0:T(8,128)(2,1)S(1)} %pad_maximum_fusion), channel_id=1, source_target_pairs={{0,2},{1,3},{2,0},{3,1},{4,6},{5,7},{6,4},{7,5},{8,10},{9,11},{10,... | collective-permute-start | bytes 1572872 | tf_op jit(solution)/shard_map/hidden2/ppermute | solution.py:394
  55.6 22.1 %copy-start.5 = (bf16[2048,512]{1,0:T(8,128)(2,1)S(1)}, bf16[2048,512]{1,0:T(8,128)(2,1)}, u32[]{:S(2)}) copy-start(bf16[2048,512]{1,0:T(8,128)(2,1)} %refs_2_.5) | copy-start | bytes 6291460
  73.1 4.5 %collective-permute-start.13 = (bf16[1024,512]{1,0:T(8,128)(2,1)S(1)}, bf16[1024,512]{1,0:T(8,128)(2,1)S(1)}, u32[]{:S(2)}, u32[]{:S(2)}) collective-permute-start(bf16[1024,512]{1,0:T(8,128)(2,1)S(1)} %constant_dynamic-update-slice_fusion.refs_0_), channel_id=1, source_target_pairs={{0,1},{1,0},{2,3},{3,2},{4,5},{5,4},{6,7},{7,6},{8,9},{9,8},{10,11... | collective-permute-start | bytes 3145736 | tf_op jit(solution)/shard_map/hidden1/ppermute | solution.py:394
  73.2 20.6 %collective-permute-start.7 = (bf16[256,512]{1,0:T(8,128)(2,1)S(1)}, bf16[256,512]{1,0:T(8,128)(2,1)S(1)}, u32[]{:S(2)}, u32[]{:S(2)}) collective-permute-start(bf16[256,512]{1,0:T(8,128)(2,1)S(1)} %get-tuple-element.86), channel_id=1, source_target_pairs={{0,12},{4,8},{8,4},{12,0},{1,13},{5,9},{9,5},{13,1},{2,14},{6,10},... | collective-permute-start | bytes 786440 | tf_op jit(solution)/shard_map/spans2_3/ppermute | solution.py:394
  75.4 18.5 %collective-permute-start.8 = (bf16[256,512]{1,0:T(8,128)(2,1)S(1)}, bf16[256,512]{1,0:T(8,128)(2,1)S(1)}, u32[]{:S(2)}, u32[]{:S(2)}) collective-permute-start(bf16[256,512]{1,0:T(8,128)(2,1)S(1)} %get-tuple-element.89), channel_id=1, source_target_pairs={{0,4},{4,0},{8,12},{12,8},{1,5},{5,1},{9,13},{13,9},{2,6},{6,2},{1... | collective-permute-start | bytes 786440 | tf_op jit(solution)/shard_map/spans2_1/ppermute | solution.py:394
  75.4 15.1 %collective-permute-start.4 = (bf16[128,512]{1,0:T(8,128)(2,1)S(1)}, bf16[128,512]{1,0:T(8,128)(2,1)S(1)}, u32[]{:S(2)}, u32[]{:S(2)}) collective-permute-start(bf16[128,512]{1,0:T(8,128)(2,1)S(1)} %get-tuple-element.76), channel_id=1, source_target_pairs={{0,8},{4,12},{8,0},{12,4},{1,9},{5,13},{9,1},{13,5},{2,10},{6,14},... | collective-permute-start | bytes 393224 | tf_op jit(solution)/shard_map/spans2_2/ppermute | solution.py:394
  78.9 26.7 %collective-permute-start.14 = (bf16[2,128,512]{2,1,0:T(8,128)(2,1)S(1)}, bf16[2,128,512]{2,1,0:T(8,128)(2,1)S(1)}, u32[]{:S(2)}, u32[]{:S(2)}) collective-permute-start(bf16[2,128,512]{2,1,0:T(8,128)(2,1)S(1)} %get-tuple-element.109), channel_id=1, source_target_pairs={{0,4},{4,0},{8,12},{12,8},{1,5},{5,1},{9,13},{13,9},{2,6},{6,2},{1... | collective-permute-start | bytes 786440 | tf_op jit(solution)/shard_map/partial1/ppermute | solution.py:394
  90.5 13.3 %collective-permute-start.6 = (bf16[128,512]{1,0:T(8,128)(2,1)S(1)}, bf16[128,512]{1,0:T(8,128)(2,1)S(1)}, u32[]{:S(2)}, u32[]{:S(2)}) collective-permute-start(bf16[128,512]{1,0:T(8,128)(2,1)S(1)} %get-tuple-element.84), channel_id=1, source_target_pairs={{0,8},{4,12},{8,0},{12,4},{1,9},{5,13},{9,1},{13,5},{2,10},{6,14},... | collective-permute-start | bytes 393224 | tf_op jit(solution)/shard_map/spans3_2/ppermute | solution.py:394
  93.9 9.9 %collective-permute-start.10 = (bf16[128,512]{1,0:T(8,128)(2,1)S(1)}, bf16[128,512]{1,0:T(8,128)(2,1)S(1)}, u32[]{:S(2)}, u32[]{:S(2)}) collective-permute-start(bf16[128,512]{1,0:T(8,128)(2,1)S(1)} %get-tuple-element.97), channel_id=1, source_target_pairs={{0,12},{4,8},{8,4},{12,0},{1,13},{5,9},{9,5},{13,1},{2,14},{6,10},... | collective-permute-start | bytes 393224 | tf_op jit(solution)/shard_map/spans3_3/ppermute | solution.py:394
  103.8 15.1 %collective-permute-start.9 = (bf16[128,512]{1,0:T(8,128)(2,1)S(1)}, bf16[128,512]{1,0:T(8,128)(2,1)S(1)}, u32[]{:S(2)}, u32[]{:S(2)}) collective-permute-start(bf16[128,512]{1,0:T(8,128)(2,1)S(1)} %get-tuple-element.95), channel_id=1, source_target_pairs={{0,8},{4,12},{8,0},{12,4},{1,9},{5,13},{9,1},{13,5},{2,10},{6,14},... | collective-permute-start | bytes 393224 | tf_op jit(solution)/shard_map/spans4_2/ppermute | solution.py:394
  103.8 15.1 %collective-permute-start.11 = (bf16[128,512]{1,0:T(8,128)(2,1)S(1)}, bf16[128,512]{1,0:T(8,128)(2,1)S(1)}, u32[]{:S(2)}, u32[]{:S(2)}) collective-permute-start(bf16[128,512]{1,0:T(8,128)(2,1)S(1)} %get-tuple-element.104), channel_id=1, source_target_pairs={{0,12},{4,8},{8,4},{12,0},{1,13},{5,9},{9,5},{13,1},{2,14},{6,10},... | collective-permute-start | bytes 393224 | tf_op jit(solution)/shard_map/spans4_3/ppermute | solution.py:394
  105.8 16.3 %collective-permute-start.15 = (bf16[1,128,512]{2,1,0:T(8,128)(2,1)S(1)}, bf16[1,128,512]{2,1,0:T(8,128)(2,1)S(1)}, u32[]{:S(2)}, u32[]{:S(2)}) collective-permute-start(bf16[1,128,512]{2,1,0:T(8,128)(2,1)S(1)} %slice.41), channel_id=1, source_target_pairs={{0,8},{4,12},{8,0},{12,4},{1,9},{5,13},{9,1},{13,5},{2,10},{6,14},... | collective-permute-start | bytes 393224 | tf_op jit(solution)/shard_map/partial2/ppermute | solution.py:394
  (1 other events, 1.6 us)

commit v5 on v4

--- a/solution.py
+++ b/solution.py
@@ -408,10 +408,10 @@
         if per_pair == 1:
             return [span_len]
         if distance == 1:
-            return [(per_pair - 1) * span_len, 0, span_len]
+            return [span_len + half, 0, span_len + half] + [span_len] * (per_pair - 3)
         if distance % 2:
-            return [span_len] * (per_pair - 1) + [half] * 2
-        return [span_len + half] + [span_len] * (per_pair - 3) + [half] * 3
+            return [half] + [span_len] * (per_pair - 2) + [half] * 3
+        return [span_len] * (per_pair - 2) + [half] * 4
 
     def pieces_of(first, length):
         pieces = []
@@ -455,6 +455,26 @@
             None if keys else key_value_store, fresh, state, not keys, last,
         )
 
+    def recomputed():
+        blocks = [hidden_own]
+        for d in away[::-1]:
+            piece = arrived[d, 0]
+            blocks.append(piece[piece.shape[0] - hidden_own.shape[0] :])
+        distances = [0]
+        for step, bit in enumerate(reversed(range(n_tensor.bit_length() - 1))):
+            distances += [distance ^ (1 << bit) for distance in distances]
+            if step and per_pair > 1:
+                blocks[-1] = after(blocks[-1], *[arrived[d, 1] for d in away if d > 1])
+            gathered = jnp.concatenate(blocks, axis=0)
+            blocks = [gathered, exchange(gathered, 1 << bit, "tensor", "hidden")]
+        partial, sent = project(blocks, kv_weight, n_store, shard_rows, distances)
+        for bit in range(n_store.bit_length() - 1):
+            if bit:
+                sent = partial[1::2].astype(jnp.bfloat16)
+            partial = partial[0::2] + exchange(sent, 1 << bit, "store", "partial").astype(jnp.float32)
+        fresh = partial[0].astype(jnp.bfloat16)
+        return fresh
+
     arrived = {}
     state = block([], None)
     arrived.update(zip([(d, 0) for d in away], behind(coming, state)))
@@ -467,37 +487,24 @@
             )
             for key in keys
         ]
-        state = block([(d, number - 1) for d in away if (d, number - 1) in arrived], state)
+        keys_here = [(d, number - 1) for d in away if (d, number - 1) in arrived]
+        joins = number == max(1, count - 2)
+        if joins:
+            fresh = recomputed()
+        state = block(keys_here, state, fresh if joins else None)
         arrived.update(zip(keys, behind(coming, state)))
-
-    blocks = [hidden_own]
-    for d in away[::-1]:
-        piece = arrived[d, 0]
-        blocks.append(piece[piece.shape[0] - hidden_own.shape[0] :])
-    distances = [0]
-    for step, bit in enumerate(reversed(range(n_tensor.bit_length() - 1))):
-        distances += [distance ^ (1 << bit) for distance in distances]
-        if step and per_pair > 1:
-            blocks[-1] = after(blocks[-1], *[arrived[d, 1] for d in away if d > 1])
-        gathered = jnp.concatenate(blocks, axis=0)
-        blocks = [gathered, exchange(gathered, 1 << bit, "tensor", "hidden")]
-    partial, sent = project(blocks, kv_weight, n_store, shard_rows, distances)
-    for bit in range(n_store.bit_length() - 1):
-        if bit:
-            sent = partial[1::2].astype(jnp.bfloat16)
-        partial = partial[0::2] + exchange(sent, 1 << bit, "store", "partial").astype(jnp.float32)
-    fresh = partial[0].astype(jnp.bfloat16)
-    fresh_out = fresh.reshape(1, span_count, recomp, kv_cols)
 
     keys = [(d, count - 1) for d in away if (d, count - 1) in arrived]
     size = 1 if per_pair > 1 else 6
     batches = [keys[i : i + size] for i in range(0, len(keys), size)]
+    if count == 1:
+        fresh = recomputed()
     for i, keys in enumerate(batches):
-        joins, last = i == max(0, len(batches) - 2), i == len(batches) - 1
+        joins, last = count == 1 and i == 0, i == len(batches) - 1
         if i:
             arrived.update(zip(keys, behind([arrived[key] for key in keys], state)))
         state = block(keys, state, fresh if joins else None, last)
-    return (state[None], fresh_out)
+    return (state[None], fresh.reshape(1, span_count, recomp, kv_cols))
 
 
 def solution(mesh):

time: 130 us -> 133 us (1.023)
  starting transfers between devices: 31.7 us -> 35.8 us
  waiting for transfers between devices: 43.7 us -> 42 us
  Pallas kernels: 49.6 us -> 51.1 us
    ppermute x16 -> x19, starting transfers between devices: 31.7 us -> 35.8 us  [exchange(): return lax.ppermute(piece, axis, [(i, i ^ distance) for i in range(size)])]
    ppermute x16 -> x19, waiting for transfers between devices: 43.7 us -> 42 us  [exchange(): return lax.ppermute(piece, axis, [(i, i ^ distance) for i in range(size)])]
    pallas_call x7 -> x8, Pallas kernels: 40.3 us -> 41.3 us  [attend(): pl.pallas_call(functools.partial(attend_kernel, tuple(parts), len(pieces)...]
  transfers between devices with their start and end apart: 16 -> 19, of which waited for: 5 -> 8; matrix products, arithmetic and copies ran while one was open for 1% -> 1% of each run, Pallas kernels for 30% -> 31%
where the time goes in v5:
time: 133 us
  Pallas kernels  51.1 us (38%)
  waiting for transfers between devices  42 us (32%)
  starting transfers between devices  35.8 us (27%)
  local copies, waits for them, and re-layouts  1.81 us (1%)
    ppermute x19, waiting for transfers between devices, exchange(): return lax.ppermute(piece, axis, [(i, i ^ distance) for i in range(size)])  42 us
    pallas_call x8, Pallas kernels, attend(): pl.pallas_call(functools.partial(attend_kernel, tuple(parts), len(pieces)...  41.3 us
    ppermute x19, starting transfers between devices, exchange(): return lax.ppermute(piece, axis, [(i, i ^ distance) for i in range(size)])  35.8 us
    pallas_call x2, Pallas kernels, pack(): pl.pallas_call(functools.partial(pack_kernel, messages, shard, with_table...  8.59 us
  transfers between devices with their start and end apart: 19, of which 8 were waited for; matrix products, arithmetic and copies ran while one was open for 1% of the time, Pallas kernels for 31%

profile of v5, /device:TPU:0, one launch (start us, length us, event | category | flops | bytes accessed | tf_op | source)
XLA Modules:
  0.0 132.6 jit_solution(16258381911276751439)
XLA Ops:
  0.7 3.5 %pack_spans.3 = (bf16[256,512]{1,0:T(8,128)(2,1)}, bf16[384,512]{1,0:T(8,128)(2,1)}, bf16[512,512]{1,0:T(8,128)(2,1)}) custom-call(s32[32]{0:T(128)} %refs_0_.3, s32[4,16]{1,0:T(4,128)} %refs_1_.3, bf16[8,256,512]{2,1,0:T(8,128)(2,1)} %refs_3_.1, bf16[128,8192]{1,0:T(8,128)(2,1)} %bitcast.17), custom_call_target="tpu_custom_call" | custom-call | tf_op jit(solution)/shard_map/pack_spans/pallas_call | solution.py:130
  4.1 4.1 %collective-permute-start = (bf16[384,512]{1,0:T(8,128)(2,1)}, bf16[384,512]{1,0:T(8,128)(2,1)S(1)}, u32[]{:S(2)}, u32[]{:S(2)}) collective-permute-start(bf16[384,512]{1,0:T(8,128)(2,1)} %get-tuple-element.77), channel_id=1, source_target_pairs={{0,8},{4,12},{8,0},{12,4},{1,9},{5,13},{9,1},{13,5},{2,10},{6,14},... | collective-permute-start | bytes 1179656 | tf_op jit(solution)/shard_map/spans0_2/ppermute | solution.py:394
  11.5 5.1 %pack_spans.2 = (bf16[128,512]{1,0:T(8,128)(2,1)S(1)}, bf16[256,512]{1,0:T(8,128)(2,1)S(1)}, bf16[256,512]{1,0:T(8,128)(2,1)S(1)}, bf16[256,512]{1,0:T(8,128)(2,...) custom-call(s32[32]{0:T(128)S(1)} %copy-done.7, ...), custom_call_target="tpu_custom_call" | custom-call | tf_op jit(solution)/shard_map/pack_spans/pallas_call | solution.py:130
  16.7 8.7 %attend_spans.8 = (f32[4096,128]{1,0:T(8,128)S(1)}, f32[4096,128]{1,0:T(8,128)S(1)}, f32[4096,128]{1,0:T(8,128)S(1)}) custom-call(s32[16,10]{1,0:T(8,128)S(1)} %get-tuple-element.71.refs_0_, bf16[256,2048]{1,0:T(8,128)(2,1)S(1)} %bitcast.9, bf16[256,512]{1,0:T(8,128)(2,1)S(1)} %bitcast.19, bf16[8,256,512]{2,1,0:T(8,128)(2,1)S(1)} %copy-done.3), custom_call_target="tpu_custom_call" | custom-call | flops 5368709120 | tf_op jit(solution)/shard_map/attend_spans/pallas_call | solution.py:351
  25.5 7.0 %collective-permute-done.refs_4_ = bf16[384,512]{1,0:T(8,128)(2,1)S(1)} collective-permute-done((bf16[384,512]{1,0:T(8,128)(2,1)}, bf16[384,512]{1,0:T(8,128)(2,1)S(1)}, u32[]{:S(2)}, u32[]{:S(2)}) %collective-permute-start) | collective-permute-done | bytes 393248 | tf_op jit(solution)/shard_map/spans0_2/ppermute | solution.py:394
  32.5 3.3 %collective-permute-done.3.refs_5_ = bf16[512,512]{1,0:T(8,128)(2,1)S(1)} collective-permute-done((bf16[512,512]{1,0:T(8,128)(2,1)}, bf16[512,512]{1,0:T(8,128)(2,1)S(1)}, u32[]{:S(2)}, u32[]{:S(2)}) %collective-permute-start.3) | collective-permute-done | bytes 524320 | tf_op jit(solution)/shard_map/spans0_1/ppermute | solution.py:394
  37.5 3.5 %collective-permute-start.5 = (bf16[256,512]{1,0:T(8,128)(2,1)S(1)}, bf16[256,512]{1,0:T(8,128)(2,1)S(1)}, u32[]{:S(2)}, u32[]{:S(2)}) collective-permute-start(bf16[256,512]{1,0:T(8,128)(2,1)S(1)} %get-tuple-element.91), channel_id=1, source_target_pairs={{0,12},{4,8},{8,4},{12,0},{1,13},{5,9},{9,5},{13,1},{2,14},{6,10},... | collective-permute-start | bytes 786440 | tf_op jit(solution)/shard_map/spans1_3/ppermute | solution.py:394
  41.6 6.3 %attend_spans.9 = (f32[4096,128]{1,0:T(8,128)S(1)}, f32[4096,128]{1,0:T(8,128)S(1)}, f32[4096,128]{1,0:T(8,128)S(1)}) custom-call(s32[16,10]{1,0:T(8,128)S(1)} %get-tuple-element.71.refs_0_, bf16[256,2048]{1,0:T(8,128)(2,1)S(1)} %bitcast.10, bf16[256,512]{1,0:T(8,128)(2,1)S(1)} %bitcast.20, bf16[256,512]{1,0:T(8,128)(2,1)S(1)} %collective-permute-done.2.refs_3_, ...), custom_call_target="tpu_custom_call" | custom-call | flops 3221225472 | tf_op jit(solution)/shard_map/attend_spans/pallas_call | solution.py:351
  47.9 14.5 %collective-permute-done.1.refs_4_ = bf16[256,512]{1,0:T(8,128)(2,1)S(1)} collective-permute-done((bf16[256,512]{1,0:T(8,128)(2,1)S(1)}, bf16[256,512]{1,0:T(8,128)(2,1)S(1)}, u32[]{:S(2)}, u32[]{:S(2)}) %collective-permute-start.1) | collective-permute-done | bytes 262176 | tf_op jit(solution)/shard_map/spans1_2/ppermute | solution.py:394
  63.3 2.9 %collective-permute-start.7 = (bf16[256,512]{1,0:T(8,128)(2,1)S(1)}, bf16[256,512]{1,0:T(8,128)(2,1)S(1)}, u32[]{:S(2)}, u32[]{:S(2)}) collective-permute-start(bf16[256,512]{1,0:T(8,128)(2,1)S(1)} %get-tuple-element.99), channel_id=1, source_target_pairs={{0,12},{4,8},{8,4},{12,0},{1,13},{5,9},{9,5},{13,1},{2,14},{6,10},... | collective-permute-start | bytes 786440 | tf_op jit(solution)/shard_map/spans2_3/ppermute | solution.py:394
  68.6 2.0 %collective-permute-start.4 = (bf16[128,512]{1,0:T(8,128)(2,1)S(1)}, bf16[128,512]{1,0:T(8,128)(2,1)S(1)}, u32[]{:S(2)}, u32[]{:S(2)}) collective-permute-start(bf16[128,512]{1,0:T(8,128)(2,1)S(1)} %get-tuple-element.89), channel_id=1, source_target_pairs={{0,8},{4,12},{8,0},{12,4},{1,9},{5,13},{9,1},{13,5},{2,10},{6,14},... | collective-permute-start | bytes 393224 | tf_op jit(solution)/shard_map/spans2_2/ppermute | solution.py:394
  70.6 4.6 %attend_spans.10 = (f32[4096,128]{1,0:T(8,128)S(1)}, f32[4096,128]{1,0:T(8,128)S(1)}, f32[4096,128]{1,0:T(8,128)S(1)}) custom-call(s32[16,10]{1,0:T(8,128)S(1)} %get-tuple-element.71.refs_0_, bf16[256,2048]{1,0:T(8,128)(2,1)S(1)} %bitcast.11, bf16[256,512]{1,0:T(8,128)(2,1)S(1)} %bitcast.21, bf16[256,512]{1,0:T(8,128)(2,1)S(1)} %collective-permute-done.5.refs_3_, ...), custom_call_target="tpu_custom_call" | custom-call | flops 2147483648 | tf_op jit(solution)/shard_map/attend_spans/pallas_call | solution.py:351
  75.2 6.6 %collective-permute-done.7.refs_3_ = bf16[256,512]{1,0:T(8,128)(2,1)S(1)} collective-permute-done((bf16[256,512]{1,0:T(8,128)(2,1)S(1)}, bf16[256,512]{1,0:T(8,128)(2,1)S(1)}, u32[]{:S(2)}, u32[]{:S(2)}) %collective-permute-start.7) | collective-permute-done | bytes 262176 | tf_op jit(solution)/shard_map/spans2_3/ppermute | solution.py:394
  82.7 4.1 %collective-permute-done.4.refs_4_ = bf16[128,512]{1,0:T(8,128)(2,1)S(1)} collective-permute-done((bf16[128,512]{1,0:T(8,128)(2,1)S(1)}, bf16[128,512]{1,0:T(8,128)(2,1)S(1)}, u32[]{:S(2)}, u32[]{:S(2)}) %collective-permute-start.4) | collective-permute-done | bytes 131104 | tf_op jit(solution)/shard_map/spans2_2/ppermute | solution.py:394
  86.8 3.4 %collective-permute-start.6 = (bf16[128,512]{1,0:T(8,128)(2,1)S(1)}, bf16[128,512]{1,0:T(8,128)(2,1)S(1)}, u32[]{:S(2)}, u32[]{:S(2)}) collective-permute-start(bf16[128,512]{1,0:T(8,128)(2,1)S(1)} %get-tuple-element.97), channel_id=1, source_target_pairs={{0,8},{4,12},{8,0},{12,4},{1,9},{5,13},{9,1},{13,5},{2,10},{6,14},... | collective-permute-start | bytes 393224 | tf_op jit(solution)/shard_map/spans3_2/ppermute | solution.py:394
  90.3 5.6 %collective-permute-start.15 = (bf16[1,128,512]{2,1,0:T(8,128)(2,1)S(1)}, bf16[1,128,512]{2,1,0:T(8,128)(2,1)S(1)}, u32[]{:S(2)}, u32[]{:S(2)}) collective-permute-start(bf16[1,128,512]{2,1,0:T(8,128)(2,1)S(1)} %slice.41), channel_id=1, source_target_pairs={{0,8},{4,12},{8,0},{12,4},{1,9},{5,13},{9,1},{13,5},{2,10},{6,14},... | collective-permute-start | bytes 393224 | tf_op jit(solution)/shard_map/partial2/ppermute | solution.py:394
  96.0 6.4 %attend_spans.11 = (f32[4096,128]{1,0:T(8,128)S(1)}, f32[4096,128]{1,0:T(8,128)S(1)}, f32[4096,128]{1,0:T(8,128)S(1)}) custom-call(s32[16,10]{1,0:T(8,128)S(1)} %get-tuple-element.71.refs_0_, bf16[256,2048]{1,0:T(8,128)(2,1)S(1)} %bitcast.12, bf16[256,512]{1,0:T(8,128)(2,1)S(1)} %bitcast.22, bf16[256,512]{1,0:T(8,128)(2,1)S(1)} %collective-permute-done.7.refs_3_, ...), custom_call_target="tpu_custom_call" | custom-call | flops 3221225472 | tf_op jit(solution)/shard_map/attend_spans/pallas_call | solution.py:351
  102.5 4.8 %collective-permute-start.17 = (bf16[128,512]{1,0:T(8,128)(2,1)S(1)}, bf16[128,512]{1,0:T(8,128)(2,1)S(1)}, u32[]{:S(2)}, u32[]{:S(2)}) collective-permute-start(bf16[128,512]{1,0:T(8,128)(2,1)S(1)} %get-tuple-element.125), channel_id=1, source_target_pairs={{0,12},{4,8},{8,4},{12,0},{1,13},{5,9},{9,5},{13,1},{2,14},{6,10},... | collective-permute-start | bytes 393224 | tf_op jit(solution)/shard_map/spans4_3/ppermute | solution.py:394
  108.0 5.9 %attend_spans.12 = (f32[4096,128]{1,0:T(8,128)S(1)}, f32[4096,128]{1,0:T(8,128)S(1)}, f32[4096,128]{1,0:T(8,128)S(1)}) custom-call(s32[16,10]{1,0:T(8,128)S(1)} %get-tuple-element.71.refs_0_, bf16[256,2048]{1,0:T(8,128)(2,1)S(1)} %bitcast.13, bf16[256,512]{1,0:T(8,128)(2,1)S(1)} %bitcast.23, bf16[128,512]{1,0:T(8,128)(2,1)S(1)} %collective-permute-done.10.refs_3_, ...), custom_call_target="tpu_custom_call" | custom-call | flops 2684354560 | tf_op jit(solution)/shard_map/attend_spans/pallas_call | solution.py:351
  114.4 2.8 %collective-permute-start.18 = (bf16[128,512]{1,0:T(8,128)(2,1)S(1)}, bf16[128,512]{1,0:T(8,128)(2,1)S(1)}, u32[]{:S(2)}, u32[]{:S(2)}) collective-permute-start(bf16[128,512]{1,0:T(8,128)(2,1)S(1)} %get-tuple-element.132), channel_id=1, source_target_pairs={{0,12},{4,8},{8,4},{12,0},{1,13},{5,9},{9,5},{13,1},{2,14},{6,10},... | collective-permute-start | bytes 393224 | tf_op jit(solution)/shard_map/spans5_3/ppermute | solution.py:394
  117.2 3.2 %attend_spans.13 = (f32[4096,128]{1,0:T(8,128)S(1)}, f32[4096,128]{1,0:T(8,128)S(1)}, f32[4096,128]{1,0:T(8,128)S(1)}) custom-call(s32[16,10]{1,0:T(8,128)S(1)} %get-tuple-element.71.refs_0_, bf16[256,2048]{1,0:T(8,128)(2,1)S(1)} %bitcast.14, bf16[256,512]{1,0:T(8,128)(2,1)S(1)} %bitcast.24, bf16[128,512]{1,0:T(8,128)(2,1)S(1)} %collective-permute-done.17.refs_3_, ...), custom_call_target="tpu_custom_call" | custom-call | flops 1073741824 | tf_op jit(solution)/shard_map/attend_spans/pallas_call | solution.py:351
  120.3 5.8 %collective-permute-done.16.refs_3_ = bf16[128,512]{1,0:T(8,128)(2,1)S(1)} collective-permute-done((bf16[128,512]{1,0:T(8,128)(2,1)S(1)}, bf16[128,512]{1,0:T(8,128)(2,1)S(1)}, u32[]{:S(2)}, u32[]{:S(2)}) %collective-permute-start.16) | collective-permute-done | bytes 131104 | tf_op jit(solution)/shard_map/spans5_2/ppermute | solution.py:394
  126.2 2.7 %attend_spans.14 = (f32[4096,128]{1,0:T(8,128)S(1)}, f32[4096,128]{1,0:T(8,128)S(1)}, f32[4096,128]{1,0:T(8,128)S(1)}) custom-call(s32[16,10]{1,0:T(8,128)S(1)} %get-tuple-element.71.refs_0_, bf16[256,2048]{1,0:T(8,128)(2,1)S(1)} %bitcast.15, bf16[256,512]{1,0:T(8,128)(2,1)S(1)} %bitcast.25, bf16[128,512]{1,0:T(8,128)(2,1)S(1)} %collective-permute-done.18.refs_3_, ...), custom_call_target="tpu_custom_call" | custom-call | flops 536870912 | tf_op jit(solution)/shard_map/attend_spans/pallas_call | solution.py:351
  128.9 3.5 %attend_spans.15 = bf16[256,2048]{1,0:T(8,128)(2,1)} custom-call(s32[16,10]{1,0:T(8,128)S(1)} %get-tuple-element.71.refs_0_, bf16[256,2048]{1,0:T(8,128)(2,1)S(1)} %bitcast.16, bf16[256,512]{1,0:T(8,128)(2,1)S(1)} %bitcast.26, bf16[128,512]{1,0:T(8,128)(2,1)S(1)} %collective-permute-done.16.refs_3_, f32[4096,128]{1,0:T(8,128)S(1)} %get-tuple-element.138.refs_4_, ...), custom_call_target="tpu_custom_call" | custom-call | flops 536870912 | tf_op jit(solution)/shard_map/attend_spans/pallas_call | solution.py:351
  (53 shorter events, 11.3 us)
Async XLA Ops:
  0.6 9.2 %copy-start.8 = (s32[1,16,8]{1,2,0:T(8,128)S(1)}, s32[1,16,8]{1,2,0:T(8,128)}, u32[]{:S(2)}) copy-start(s32[1,16,8]{1,2,0:T(8,128)} %param.13) | copy-start | bytes 1540
  0.6 9.2 %copy-start.1 = (bf16[1,16,8,8192]{3,2,1,0:T(8,128)(2,1)S(1)}, bf16[1,16,8,8192]{3,2,1,0:T(8,128)(2,1)}, u32[]{:S(2)}) copy-start(bf16[1,16,8,8192]{3,2,1,0:T(8,128)(2,1)} %param.14) | copy-start | bytes 6291460
  0.7 9.2 %copy-start.6 = (s32[4,16]{1,0:T(4,128)S(1)}, s32[4,16]{1,0:T(4,128)}, u32[]{:S(2)}) copy-start(s32[4,16]{1,0:T(4,128)} %refs_1_.3) | copy-start | bytes 772
  0.7 9.2 %copy-start.7 = (s32[32]{0:T(128)S(1)}, s32[32]{0:T(128)}, u32[]{:S(2)}) copy-start(s32[32]{0:T(128)} %refs_0_.3) | copy-start | bytes 388
  4.1 28.3 %collective-permute-start = (bf16[384,512]{1,0:T(8,128)(2,1)}, bf16[384,512]{1,0:T(8,128)(2,1)S(1)}, u32[]{:S(2)}, u32[]{:S(2)}) collective-permute-start(bf16[384,512]{1,0:T(8,128)(2,1)} %get-tuple-element.77), channel_id=1, source_target_pairs={{0,8},{4,12},{8,0},{12,4},{1,9},{5,13},{9,1},{13,5},{2,10},{6,14},... | collective-permute-start | bytes 1179656 | tf_op jit(solution)/shard_map/spans0_2/ppermute | solution.py:394
  8.2 17.3 %collective-permute-start.2 = (bf16[256,512]{1,0:T(8,128)(2,1)}, bf16[256,512]{1,0:T(8,128)(2,1)S(1)}, u32[]{:S(2)}, u32[]{:S(2)}) collective-permute-start(bf16[256,512]{1,0:T(8,128)(2,1)} %get-tuple-element.81), channel_id=1, source_target_pairs={{0,12},{4,8},{8,4},{12,0},{1,13},{5,9},{9,5},{13,1},{2,14},{6,10},... | collective-permute-start | bytes 786440 | tf_op jit(solution)/shard_map/spans0_3/ppermute | solution.py:394
  9.6 26.2 %collective-permute-start.3 = (bf16[512,512]{1,0:T(8,128)(2,1)}, bf16[512,512]{1,0:T(8,128)(2,1)S(1)}, u32[]{:S(2)}, u32[]{:S(2)}) collective-permute-start(bf16[512,512]{1,0:T(8,128)(2,1)} %get-tuple-element.83), channel_id=1, source_target_pairs={{0,4},{4,0},{8,12},{12,8},{1,5},{5,1},{9,13},{13,9},{2,6},{6,2},{1... | collective-permute-start | bytes 1572872 | tf_op jit(solution)/shard_map/spans0_1/ppermute | solution.py:394
  35.9 26.6 %collective-permute-start.12 = (bf16[512,512]{1,0:T(8,128)(2,1)S(1)}, bf16[512,512]{1,0:T(8,128)(2,1)S(1)}, u32[]{:S(2)}, u32[]{:S(2)}) collective-permute-start(bf16[512,512]{1,0:T(8,128)(2,1)S(1)} %pad_maximum_fusion), channel_id=1, source_target_pairs={{0,2},{1,3},{2,0},{3,1},{4,6},{5,7},{6,4},{7,5},{8,10},{9,11},{10,... | collective-permute-start | bytes 1572872 | tf_op jit(solution)/shard_map/hidden2/ppermute | solution.py:394
  37.5 10.4 %collective-permute-start.5 = (bf16[256,512]{1,0:T(8,128)(2,1)S(1)}, bf16[256,512]{1,0:T(8,128)(2,1)S(1)}, u32[]{:S(2)}, u32[]{:S(2)}) collective-permute-start(bf16[256,512]{1,0:T(8,128)(2,1)S(1)} %get-tuple-element.91), channel_id=1, source_target_pairs={{0,12},{4,8},{8,4},{12,0},{1,13},{5,9},{9,5},{13,1},{2,14},{6,10},... | collective-permute-start | bytes 786440 | tf_op jit(solution)/shard_map/spans1_3/ppermute | solution.py:394
  41.0 21.5 %collective-permute-start.1 = (bf16[256,512]{1,0:T(8,128)(2,1)S(1)}, bf16[256,512]{1,0:T(8,128)(2,1)S(1)}, u32[]{:S(2)}, u32[]{:S(2)}) collective-permute-start(bf16[256,512]{1,0:T(8,128)(2,1)S(1)} %get-tuple-element.80), channel_id=1, source_target_pairs={{0,8},{4,12},{8,0},{12,4},{1,9},{5,13},{9,1},{13,5},{2,10},{6,14},... | collective-permute-start | bytes 786440 | tf_op jit(solution)/shard_map/spans1_2/ppermute | solution.py:394
  41.6 24.6 %copy-start.5 = (bf16[2048,512]{1,0:T(8,128)(2,1)S(1)}, bf16[2048,512]{1,0:T(8,128)(2,1)}, u32[]{:S(2)}) copy-start(bf16[2048,512]{1,0:T(8,128)(2,1)} %refs_2_.5) | copy-start | bytes 6291460
  62.5 3.7 %collective-permute-start.13 = (bf16[1024,512]{1,0:T(8,128)(2,1)S(1)}, bf16[1024,512]{1,0:T(8,128)(2,1)S(1)}, u32[]{:S(2)}, u32[]{:S(2)}) collective-permute-start(bf16[1024,512]{1,0:T(8,128)(2,1)S(1)} %constant_dynamic-update-slice_fusion.refs_0_), channel_id=1, source_target_pairs={{0,1},{1,0},{2,3},{3,2},{4,5},{5,4},{6,7},{7,6},{8,9},{9,8},{10,11... | collective-permute-start | bytes 3145736 | tf_op jit(solution)/shard_map/hidden1/ppermute | solution.py:394
  62.6 27.6 %collective-permute-start.8 = (bf16[384,512]{1,0:T(8,128)(2,1)S(1)}, bf16[384,512]{1,0:T(8,128)(2,1)S(1)}, u32[]{:S(2)}, u32[]{:S(2)}) collective-permute-start(bf16[384,512]{1,0:T(8,128)(2,1)S(1)} %get-tuple-element.102), channel_id=1, source_target_pairs={{0,4},{4,0},{8,12},{12,8},{1,5},{5,1},{9,13},{13,9},{2,6},{6,2},{1... | collective-permute-start | bytes 1179656 | tf_op jit(solution)/shard_map/spans2_1/ppermute | solution.py:394
  63.3 18.5 %collective-permute-start.7 = (bf16[256,512]{1,0:T(8,128)(2,1)S(1)}, bf16[256,512]{1,0:T(8,128)(2,1)S(1)}, u32[]{:S(2)}, u32[]{:S(2)}) collective-permute-start(bf16[256,512]{1,0:T(8,128)(2,1)S(1)} %get-tuple-element.99), channel_id=1, source_target_pairs={{0,12},{4,8},{8,4},{12,0},{1,13},{5,9},{9,5},{13,1},{2,14},{6,10},... | collective-permute-start | bytes 786440 | tf_op jit(solution)/shard_map/spans2_3/ppermute | solution.py:394
  67.4 22.8 %collective-permute-start.14 = (bf16[2,128,512]{2,1,0:T(8,128)(2,1)S(1)}, bf16[2,128,512]{2,1,0:T(8,128)(2,1)S(1)}, u32[]{:S(2)}, u32[]{:S(2)}) collective-permute-start(bf16[2,128,512]{2,1,0:T(8,128)(2,1)S(1)} %get-tuple-element.118), channel_id=1, source_target_pairs={{0,4},{4,0},{8,12},{12,8},{1,5},{5,1},{9,13},{13,9},{2,6},{6,2},{1... | collective-permute-start | bytes 786440 | tf_op jit(solution)/shard_map/partial1/ppermute | solution.py:394
  68.6 18.3 %collective-permute-start.4 = (bf16[128,512]{1,0:T(8,128)(2,1)S(1)}, bf16[128,512]{1,0:T(8,128)(2,1)S(1)}, u32[]{:S(2)}, u32[]{:S(2)}) collective-permute-start(bf16[128,512]{1,0:T(8,128)(2,1)S(1)} %get-tuple-element.89), channel_id=1, source_target_pairs={{0,8},{4,12},{8,0},{12,4},{1,9},{5,13},{9,1},{13,5},{2,10},{6,14},... | collective-permute-start | bytes 393224 | tf_op jit(solution)/shard_map/spans2_2/ppermute | solution.py:394
  81.7 20.7 %collective-permute-start.10 = (bf16[128,512]{1,0:T(8,128)(2,1)S(1)}, bf16[128,512]{1,0:T(8,128)(2,1)S(1)}, u32[]{:S(2)}, u32[]{:S(2)}) collective-permute-start(bf16[128,512]{1,0:T(8,128)(2,1)S(1)} %get-tuple-element.110), channel_id=1, source_target_pairs={{0,12},{4,8},{8,4},{12,0},{1,13},{5,9},{9,5},{13,1},{2,14},{6,10},... | collective-permute-start | bytes 393224 | tf_op jit(solution)/shard_map/spans3_3/ppermute | solution.py:394
  82.7 24.6 %collective-permute-start.11 = (bf16[256,512]{1,0:T(8,128)(2,1)S(1)}, bf16[256,512]{1,0:T(8,128)(2,1)S(1)}, u32[]{:S(2)}, u32[]{:S(2)}) collective-permute-start(bf16[256,512]{1,0:T(8,128)(2,1)S(1)} %get-tuple-element.113), channel_id=1, source_target_pairs={{0,4},{4,0},{8,12},{12,8},{1,5},{5,1},{9,13},{13,9},{2,6},{6,2},{1... | collective-permute-start | bytes 786440 | tf_op jit(solution)/shard_map/spans3_1/ppermute | solution.py:394
  86.8 15.6 %collective-permute-start.6 = (bf16[128,512]{1,0:T(8,128)(2,1)S(1)}, bf16[128,512]{1,0:T(8,128)(2,1)S(1)}, u32[]{:S(2)}, u32[]{:S(2)}) collective-permute-start(bf16[128,512]{1,0:T(8,128)(2,1)S(1)} %get-tuple-element.97), channel_id=1, source_target_pairs={{0,8},{4,12},{8,0},{12,4},{1,9},{5,13},{9,1},{13,5},{2,10},{6,14},... | collective-permute-start | bytes 393224 | tf_op jit(solution)/shard_map/spans3_2/ppermute | solution.py:394
  90.3 17.0 %collective-permute-start.15 = (bf16[1,128,512]{2,1,0:T(8,128)(2,1)S(1)}, bf16[1,128,512]{2,1,0:T(8,128)(2,1)S(1)}, u32[]{:S(2)}, u32[]{:S(2)}) collective-permute-start(bf16[1,128,512]{2,1,0:T(8,128)(2,1)S(1)} %slice.41), channel_id=1, source_target_pairs={{0,8},{4,12},{8,0},{12,4},{1,9},{5,13},{9,1},{13,5},{2,10},{6,14},... | collective-permute-start | bytes 393224 | tf_op jit(solution)/shard_map/partial2/ppermute | solution.py:394
  102.4 12.0 %collective-permute-start.9 = (bf16[128,512]{1,0:T(8,128)(2,1)S(1)}, bf16[128,512]{1,0:T(8,128)(2,1)S(1)}, u32[]{:S(2)}, u32[]{:S(2)}) collective-permute-start(bf16[128,512]{1,0:T(8,128)(2,1)S(1)} %get-tuple-element.108), channel_id=1, source_target_pairs={{0,8},{4,12},{8,0},{12,4},{1,9},{5,13},{9,1},{13,5},{2,10},{6,14},... | collective-permute-start | bytes 393224 | tf_op jit(solution)/shard_map/spans4_2/ppermute | solution.py:394
  102.5 11.9 %collective-permute-start.17 = (bf16[128,512]{1,0:T(8,128)(2,1)S(1)}, bf16[128,512]{1,0:T(8,128)(2,1)S(1)}, u32[]{:S(2)}, u32[]{:S(2)}) collective-permute-start(bf16[128,512]{1,0:T(8,128)(2,1)S(1)} %get-tuple-element.125), channel_id=1, source_target_pairs={{0,12},{4,8},{8,4},{12,0},{1,13},{5,9},{9,5},{13,1},{2,14},{6,10},... | collective-permute-start | bytes 393224 | tf_op jit(solution)/shard_map/spans4_3/ppermute | solution.py:394
  114.4 11.8 %collective-permute-start.16 = (bf16[128,512]{1,0:T(8,128)(2,1)S(1)}, bf16[128,512]{1,0:T(8,128)(2,1)S(1)}, u32[]{:S(2)}, u32[]{:S(2)}) collective-permute-start(bf16[128,512]{1,0:T(8,128)(2,1)S(1)} %get-tuple-element.123), channel_id=1, source_target_pairs={{0,8},{4,12},{8,0},{12,4},{1,9},{5,13},{9,1},{13,5},{2,10},{6,14},... | collective-permute-start | bytes 393224 | tf_op jit(solution)/shard_map/spans5_2/ppermute | solution.py:394
  114.4 11.8 %collective-permute-start.18 = (bf16[128,512]{1,0:T(8,128)(2,1)S(1)}, bf16[128,512]{1,0:T(8,128)(2,1)S(1)}, u32[]{:S(2)}, u32[]{:S(2)}) collective-permute-start(bf16[128,512]{1,0:T(8,128)(2,1)S(1)} %get-tuple-element.132), channel_id=1, source_target_pairs={{0,12},{4,8},{8,4},{12,0},{1,13},{5,9},{9,5},{13,1},{2,14},{6,10},... | collective-permute-start | bytes 393224 | tf_op jit(solution)/shard_map/spans5_3/ppermute | solution.py:394
  (4 other events, 17.1 us)

commit v6 on v5

--- a/solution.py
+++ b/solution.py
@@ -10,6 +10,7 @@
 
 HEAD_WIDTH = 128
 EXP_SCALE = math.log2(math.e) * HEAD_WIDTH ** (-0.5)
+EXP_LIMIT = 64.0
 PAIR = 2
 VMEM_LIMIT = 28 * 1024 * 1024
 FIRST_VMEM_LIMIT = 60 * 1024 * 1024
@@ -194,14 +195,23 @@
         store_ref, refs = refs[0], refs[1:]
     piece_refs, refs = refs[:n_pieces], refs[n_pieces:]
     if with_fresh:
-        fresh_ref, refs = refs[0], refs[1:]
+        own_ref, other_ref = refs[:2]
+        refs = refs[2:]
     if not first:
-        blend_in, total_in, highest_in = refs[:3]
+        blend_in, total_in, shift_in = refs[:3]
         refs = refs[3:]
     if last:
-        out_ref, keys, values, live, out_stage, sems = refs
+        out_ref, refs = refs[0], refs[1:]
     else:
-        blend_out, total_out, highest_out, keys, values, live = refs
+        blend_out, total_out, shift_out = refs[:3]
+        refs = refs[3:]
+    if with_fresh:
+        fresh_out, refs = refs[0], refs[1:]
+    keys, values, live, refs = refs[0], refs[1], refs[2], refs[3:]
+    if with_fresh:
+        fresh_ref, fresh_sem, refs = refs[0], refs[1], refs[2:]
+    if last:
+        out_stage, sems = refs
     width = HEAD_WIDTH
     question_len, query_cols = query_ref.shape
     kv_heads = question_ref.shape[1] // (2 * width)
@@ -215,6 +225,12 @@
         columns = pl.ds(column, PAIR * width)
         return pltpu.make_async_copy(out_stage.at[:, columns], out_ref.at[:, columns], sems.at[step])
 
+    def fresh_copy():
+        return pltpu.make_async_copy(fresh_ref, fresh_out, fresh_sem)
+
+    if with_fresh:
+        fresh_ref[...] = (own_ref[...] + other_ref[...].astype(jnp.float32)).astype(fresh_ref.dtype)
+        fresh_copy().start()
     base = 0
     for line, start, length, _, _ in parts:
         row = start + lax.broadcasted_iota(jnp.int32, (length, width), 0)
@@ -226,8 +242,9 @@
     values[:base, width:] = live[:base, :]
     if values.shape[0] > base:
         values[base:, width:] = jnp.ones((values.shape[0] - base, width), values.dtype)
-
-    def one_kv_head(k, carry):
+    plain = values.shape[0] - (question_len if with_question else 0)
+
+    def load(k):
         key_at = pl.ds(pl.multiple_of(k * 2 * width, 2 * width), width)
         value_at = pl.ds(pl.multiple_of(k * 2 * width + width, width), width)
         spare_key = question_ref[0:8, key_at][0:1].astype(jnp.float32)
@@ -249,78 +266,117 @@
             keys[here, :] = ref[:, key_at]
             values[here, :width] = ref[:, value_at]
             base += ref.shape[0]
-        plain = base - (question_len if with_question else 0)
-
-        def query_columns(start):
-            return pl.ds(pl.multiple_of(k * group_cols + start * width, width), width)
-
-        def score(pair):
-            query = jnp.concatenate(
-                [query_ref[:, query_columns(pair * PAIR + h)] for h in range(PAIR)], axis=0
+
+    def query_columns(k, start):
+        return pl.ds(pl.multiple_of(k * group_cols + start * width, width), width)
+
+    def score(k, pair):
+        query = jnp.concatenate(
+            [query_ref[:, query_columns(k, pair * PAIR + h)] for h in range(PAIR)], axis=0
+        )
+        scores = [
+            lax.dot_general(query, keys[:plain, :], contract, preferred_element_type=jnp.float32)
+        ]
+        if with_question:
+            asked = lax.dot_general(
+                query, keys[plain:, :], contract, preferred_element_type=jnp.float32
             )
-            parts = [
-                lax.dot_general(query, keys[:plain, :], contract, preferred_element_type=jnp.float32)
-            ]
-            if with_question:
-                asked = lax.dot_general(
-                    query, keys[plain:base, :], contract, preferred_element_type=jnp.float32
-                )
-                asked = asked.reshape(PAIR, question_len, question_len)
-                q_place = lax.broadcasted_iota(jnp.int32, asked.shape, 1)
-                k_place = lax.broadcasted_iota(jnp.int32, asked.shape, 2)
-                asked = jnp.where(k_place <= q_place, asked, -jnp.inf)
-                parts.append(asked.reshape(rows, question_len))
-            return parts
-
-        upcoming = score(0)
+            asked = asked.reshape(PAIR, question_len, question_len)
+            q_place = lax.broadcasted_iota(jnp.int32, asked.shape, 1)
+            k_place = lax.broadcasted_iota(jnp.int32, asked.shape, 2)
+            asked = jnp.where(k_place <= q_place, asked, -jnp.inf)
+            scores.append(asked.reshape(rows, question_len))
+        return scores
+
+    def over(scores, shift):
+        return [
+            part - jnp.concatenate([shift] * (part.shape[1] // width), axis=1) for part in scores
+        ]
+
+    def blended(apart):
+        blend, offset = 0.0, 0
+        for part in apart:
+            probs = jnp.exp2(part * EXP_SCALE).astype(jnp.bfloat16)
+            blend = blend + jnp.dot(
+                probs, values[offset : offset + part.shape[1], :], preferred_element_type=jnp.float32
+            )
+            offset += part.shape[1]
+        return blend[:, :width], blend[:, width:]
+
+    def new_shift(scores):
+        highest = functools.reduce(
+            jnp.maximum, [jnp.max(part, axis=1, keepdims=True) for part in scores]
+        )
+        return jnp.broadcast_to(highest, (rows, width))
+
+    def finish(k, pair, here, blend, total, shift):
+        if last:
+            done = (blend / total).astype(out_ref.dtype)
+            for h in range(PAIR):
+                out_stage[:, query_columns(k, pair * PAIR + h)] = done[
+                    h * question_len : (h + 1) * question_len
+                ]
+            column = pl.multiple_of(k * group_cols + pair * PAIR * width, PAIR * width)
+            out_copy(k * pairs + pair, column).start()
+        else:
+            blend_out[here, :] = blend
+            total_out[here, :] = total
+            shift_out[here, :] = shift
+
+    def wait_out():
+        for step in range(kv_heads * pairs if last else 0):
+            out_copy(step, step * PAIR * width).wait()
+
+    def one_kv_head(k, worst):
+        load(k)
+        upcoming = score(k, 0)
         for pair in range(pairs):
             scores = upcoming
             if pair + 1 < pairs:
-                upcoming = score(pair + 1)
-            highest = functools.reduce(
-                jnp.maximum, [jnp.max(part, axis=1, keepdims=True) for part in scores]
-            )
-            highest = jnp.broadcast_to(highest, (rows, width))
+                upcoming = score(k, pair + 1)
             here = pl.ds(pl.multiple_of((k * pairs + pair) * rows, rows), rows)
+            shift = new_shift(scores) if first else shift_in[here, :]
+            apart = over(scores, shift)
+            blend, total = blended(apart)
             if not first:
-                before = highest_in[here, :]
-                highest = jnp.maximum(highest, before)
-                fade = jnp.exp2((before - highest) * EXP_SCALE)
-            blend = 0.0
-            offset = 0
-            for part in scores:
-                length = part.shape[1]
-                shift = jnp.concatenate([highest] * (length // width), axis=1)
-                probs = jnp.exp2((part - shift) * EXP_SCALE).astype(jnp.bfloat16)
-                blend = blend + jnp.dot(
-                    probs, values[offset : offset + length, :], preferred_element_type=jnp.float32
-                )
-                offset += length
-            total = blend[:, width:]
-            blend = blend[:, :width]
-            if not first:
-                blend = blend + blend_in[here, :] * fade
-                total = total + total_in[here, :] * fade
-            if last:
-                done = (blend / total).astype(out_ref.dtype)
-                for h in range(PAIR):
-                    out_stage[:, query_columns(pair * PAIR + h)] = done[
-                        h * question_len : (h + 1) * question_len
-                    ]
-                out_copy(
-                    k * pairs + pair,
-                    pl.multiple_of(k * group_cols + pair * PAIR * width, PAIR * width),
-                ).start()
-            else:
-                blend_out[here, :] = blend
-                total_out[here, :] = total
-                highest_out[here, :] = highest
-        return carry
-
-    lax.fori_loop(0, kv_heads, one_kv_head, 0)
-    if last:
-        for step in range(kv_heads * pairs):
-            out_copy(step, step * PAIR * width).wait()
+                for part in apart:
+                    most = jnp.max(part.reshape(rows // 8, 8, part.shape[1]), axis=0)
+                    for column in range(0, part.shape[1], width):
+                        worst = jnp.maximum(worst, most[:, column : column + width])
+                blend = blend + blend_in[here, :]
+                total = total + total_in[here, :]
+            finish(k, pair, here, blend, total, shift)
+        return worst
+
+    worst = lax.fori_loop(0, kv_heads, one_kv_head, jnp.full((8, width), -jnp.inf, jnp.float32))
+    wait_out()
+
+    def again(k, carry):
+        load(k)
+
+        def one_pair(pair, carry):
+            here = pl.ds(pl.multiple_of((k * pairs + pair) * rows, rows), rows)
+            scores = score(k, pair)
+            before = shift_in[here, :]
+            shift = jnp.maximum(new_shift(scores), before)
+            fade = jnp.exp2((before - shift) * EXP_SCALE)
+            blend, total = blended(over(scores, shift))
+            blend = blend + blend_in[here, :] * fade
+            total = total + total_in[here, :] * fade
+            finish(k, pair, here, blend, total, shift)
+            return carry
+
+        return lax.fori_loop(0, pairs, one_pair, carry)
+
+    if not first:
+
+        @pl.when(jnp.max(worst) * EXP_SCALE > EXP_LIMIT)
+        def _():
+            lax.fori_loop(0, kv_heads, again, 0)
+            wait_out()
+
+    if with_fresh:
+        fresh_copy().wait()
 
 
 def attend(table, queries, question, parts, pieces, store, fresh, state, with_question, last):
@@ -332,8 +388,8 @@
     held = sum(part[2] for part in parts)
     length = held + (question_len if with_question else 0)
     if fresh is not None:
-        operands.append(fresh)
-        length += fresh.shape[0]
+        operands += list(fresh)
+        length += fresh[0].shape[0]
     if not first:
         operands += list(state)
     scratch = [
@@ -342,13 +398,18 @@
         pltpu.VMEM((held, HEAD_WIDTH), jnp.bfloat16),
     ]
     if last:
-        out_shape = jax.ShapeDtypeStruct(queries.shape, queries.dtype)
-        out_specs = hbm_spec()
-        scratch += [pltpu.VMEM(queries.shape, queries.dtype), pltpu.SemaphoreType.DMA((pairs,))]
+        out_shape = [jax.ShapeDtypeStruct(queries.shape, queries.dtype)]
+        out_specs = [hbm_spec()]
     else:
         out_shape = [jax.ShapeDtypeStruct((heads * question_len, HEAD_WIDTH), jnp.float32)] * 3
         out_specs = [vmem_spec()] * 3
-    return pl.pallas_call(
+    if fresh is not None:
+        out_shape.append(jax.ShapeDtypeStruct(fresh[0].shape, jnp.bfloat16))
+        out_specs.append(hbm_spec())
+        scratch += [pltpu.VMEM(fresh[0].shape, jnp.bfloat16), pltpu.SemaphoreType.DMA]
+    if last:
+        scratch += [pltpu.VMEM(queries.shape, queries.dtype), pltpu.SemaphoreType.DMA((pairs,))]
+    outs = pl.pallas_call(
         functools.partial(
             attend_kernel, tuple(parts), len(pieces), store is not None, with_question,
             fresh is not None, first, last,
@@ -359,10 +420,14 @@
         scratch_shapes=scratch,
         compiler_params=pltpu.CompilerParams(vmem_limit_bytes=VMEM_LIMIT),
         cost_estimate=pl.CostEstimate(
-            flops=heads * question_len * length * 8 * HEAD_WIDTH, bytes_accessed=0, transcendentals=0
+            flops=64 * heads * question_len * length * HEAD_WIDTH, bytes_accessed=0, transcendentals=0
         ),
         name="attend_spans",
     )(*operands)
+    rows = None
+    if fresh is not None:
+        *outs, rows = outs
+    return outs, rows
 
 
 def local(
@@ -408,10 +473,10 @@
         if per_pair == 1:
             return [span_len]
         if distance == 1:
-            return [span_len + half, 0, span_len + half] + [span_len] * (per_pair - 3)
+            return [2 * span_len, (per_pair - 2) * span_len]
         if distance % 2:
-            return [half] + [span_len] * (per_pair - 2) + [half] * 3
-        return [span_len] * (per_pair - 2) + [half] * 4
+            return [span_len] * (per_pair - 2) + [span_len + half, half]
+        return [span_len + half] + [span_len] * (per_pair - 2) + [half]
 
     def pieces_of(first, length):
         pieces = []
@@ -427,84 +492,89 @@
         first = 0
         for number, length in enumerate(cuts(d)):
             if length:
-                messages[d, number] = (d, not number, pieces_of(first, length))
+                messages[d, number] = (d, False, pieces_of(first, length))
             first += length
-    outbox, _ = packed([messages[d, 0] for d in away])
-    coming = [exchange(piece, d, "store", "spans0_") for piece, d in zip(outbox, away)]
     count = 1 + max(number for _, number in messages)
-    later = [(d, number) for number in range(1, count) for d in away if (d, number) in messages]
+    soon = [(d, 0) for d in away if d > 1]
+    later = [key for number in range(count) for d in away for key in [(d, number)] if key in messages]
+    later = [key for key in later if key not in soon]
+    outbox, _ = packed([(d, True, []) for d in away] + [messages[key] for key in soon])
+    hidden_in = {d: exchange(piece, d, "store", "columns") for d, piece in zip(away, outbox)}
+    coming = [exchange(piece, key[0], "store", "spans0_") for key, piece in zip(soon, outbox[len(away) :])]
     (hidden_own, *outbox), table = packed(
         [(0, True, [])] + [messages[key] for key in later], recompute_rows[0]
     )
     outbox = dict(zip(later, outbox))
+    coming.append(exchange(after(outbox[1, 0], hidden_in[1]), 1, "store", "spans0_"))
 
     def behind(pieces, state):
-        return [after(piece, state[2]) for piece in pieces]
-
-    def block(keys, state, fresh=None, last=False):
-        parts = []
+        return [after(piece, state[0]) for piece in pieces]
+
+    def block(keys, state, own=(), with_question=False, fresh=None, last=False):
+        parts = [(span, 0, span_len, 0, 0) for span in own]
         for source, (d, number) in enumerate(keys):
             offset = 0
             for span, start, rows in messages[d, number][2]:
                 parts.append((d * per_pair + span, start, rows, source, offset))
                 offset += rows
-        if not keys:
-            parts = [(span, 0, span_len, 0, 0) for span in range(per_pair)]
         return attend(
             table, query_rows, question, parts, [arrived[key] for key in keys],
-            None if keys else key_value_store, fresh, state, not keys, last,
+            key_value_store if own else None, fresh, state, with_question, last,
         )
 
     def recomputed():
-        blocks = [hidden_own]
-        for d in away[::-1]:
-            piece = arrived[d, 0]
-            blocks.append(piece[piece.shape[0] - hidden_own.shape[0] :])
+        blocks = [hidden_own] + behind([hidden_in[d] for d in away[::-1]], state)
         distances = [0]
         for step, bit in enumerate(reversed(range(n_tensor.bit_length() - 1))):
             distances += [distance ^ (1 << bit) for distance in distances]
-            if step and per_pair > 1:
-                blocks[-1] = after(blocks[-1], *[arrived[d, 1] for d in away if d > 1])
             gathered = jnp.concatenate(blocks, axis=0)
+            if not step:
+                yield gathered
             blocks = [gathered, exchange(gathered, 1 << bit, "tensor", "hidden")]
         partial, sent = project(blocks, kv_weight, n_store, shard_rows, distances)
-        for bit in range(n_store.bit_length() - 1):
+        bits = n_store.bit_length() - 1
+        for bit in range(bits):
             if bit:
                 sent = partial[1::2].astype(jnp.bfloat16)
-            partial = partial[0::2] + exchange(sent, 1 << bit, "store", "partial").astype(jnp.float32)
-        fresh = partial[0].astype(jnp.bfloat16)
-        return fresh
+            if bit == 1:
+                yield sent
+            other = exchange(sent, 1 << bit, "store", "partial")
+            if bit + 1 < bits:
+                partial = partial[0::2] + other.astype(jnp.float32)
+        yield partial[0], other[0]
 
     arrived = {}
-    state = block([], None)
-    arrived.update(zip([(d, 0) for d in away], behind(coming, state)))
+    steps = recomputed()
+    middle = (per_pair + 1) // 2
+    state, _ = block([], None, range(middle), True)
+    state = [after(state[0], next(steps)), *state[1:]]
+    if per_pair > 1:
+        state, _ = block([], state, range(middle, per_pair))
+    arrived.update(zip(soon + [(1, 0)], behind(coming, state)))
+    fresh = rows = None
     for number in range(1, count):
         keys = [key for key in later if key[1] == number]
         coming = [
-            exchange(
-                after(outbox[key], arrived[key[0] if key[0] > 1 else away[0], number - 1]),
-                key[0], "store", "spans%d_" % number,
-            )
+            exchange(after(outbox[key], arrived[key[0], number - 1]), key[0], "store", "spans%d_" % number)
             for key in keys
         ]
-        keys_here = [(d, number - 1) for d in away if (d, number - 1) in arrived]
-        joins = number == max(1, count - 2)
+        if number == 2:
+            state = [after(state[0], next(steps)), *state[1:]]
+        if number == count - 1:
+            *_, fresh = steps
+        here = [(d, number - 1) for d in away if (d, number - 1) in arrived]
+        state, rows = block(here, state, fresh=fresh)
+        arrived.update(zip(keys, behind(coming, state)))
+    keys = [(d, count - 1) for d in away[::-1] if (d, count - 1) in arrived]
+    size = 6
+    batches = [keys[i : i + size] for i in range(0, len(keys), size)]
+    for i, keys in enumerate(batches):
+        joins, last = rows is None, i == len(batches) - 1
         if joins:
-            fresh = recomputed()
-        state = block(keys_here, state, fresh if joins else None)
-        arrived.update(zip(keys, behind(coming, state)))
-
-    keys = [(d, count - 1) for d in away if (d, count - 1) in arrived]
-    size = 1 if per_pair > 1 else 6
-    batches = [keys[i : i + size] for i in range(0, len(keys), size)]
-    if count == 1:
-        fresh = recomputed()
-    for i, keys in enumerate(batches):
-        joins, last = count == 1 and i == 0, i == len(batches) - 1
-        if i:
-            arrived.update(zip(keys, behind([arrived[key] for key in keys], state)))
-        state = block(keys, state, fresh if joins else None, last)
-    return (state[None], fresh.reshape(1, span_count, recomp, kv_cols))
+            *_, fresh = steps
+        state, now = block(keys, state, fresh=fresh if joins else None, last=last)
+        rows = now if joins else rows
+    return (state[0][None], rows.reshape(1, span_count, recomp, kv_cols))
 
 
 def solution(mesh):

time: 133 us -> 126 us (0.947)
  waiting for transfers between devices: 42 us -> 54.9 us
  starting transfers between devices: 35.8 us -> 24.4 us
  Pallas kernels: 51.1 us -> 43.9 us
    ppermute x19 -> x17, waiting for transfers between devices: 42 us -> 54.9 us  [exchange(): return lax.ppermute(piece, axis, [(i, i ^ distance) for i in range(size)])]
    ppermute x19 -> x17, starting transfers between devices: 35.8 us -> 24.4 us  [exchange(): return lax.ppermute(piece, axis, [(i, i ^ distance) for i in range(size)])]
    pallas_call x8 -> x6, Pallas kernels: 41.3 us -> 35.1 us  [attend(): pl.pallas_call(functools.partial(attend_kernel, tuple(parts), len(pieces)...]
  transfers between devices with their start and end apart: 19 -> 17, of which waited for: 8 -> 5; matrix products, arithmetic and copies ran while one was open for 1% -> 0% of each run, Pallas kernels for 31% -> 29%
where the time goes in v6:
time: 126 us
  waiting for transfers between devices  54.9 us (44%)
  Pallas kernels  43.9 us (35%)
  starting transfers between devices  24.4 us (19%)
  local copies, waits for them, and re-layouts  1.85 us (1%)
    ppermute x17, waiting for transfers between devices, exchange(): return lax.ppermute(piece, axis, [(i, i ^ distance) for i in range(size)])  54.9 us
    pallas_call x6, Pallas kernels, attend(): pl.pallas_call(functools.partial(attend_kernel, tuple(parts), len(pieces)...  35.1 us
    ppermute x17, starting transfers between devices, exchange(): return lax.ppermute(piece, axis, [(i, i ^ distance) for i in range(size)])  24.4 us
    pallas_call x2, Pallas kernels, pack(): pl.pallas_call(functools.partial(pack_kernel, messages, shard, with_table...  7.58 us
  transfers between devices with their start and end apart: 17, of which 5 were waited for; matrix products, arithmetic and copies ran while one was open for 0% of the time, Pallas kernels for 29%

profile of v6, /device:TPU:0, one launch (start us, length us, event | category | flops | bytes accessed | tf_op | source)
XLA Modules:
  0.0 126.3 jit_solution(433524015244146017)
XLA Ops:
  0.7 3.3 %pack_spans.3 = (bf16[128,512]{1,0:T(8,128)(2,1)}, bf16[128,512]{1,0:T(8,128)(2,1)}, bf16[128,512]{1,0:T(8,128)(2,1)}, bf16[256,512]{1,0:T(8,128)(2,1)}, bf16[384,512]{1,0:T(8,128)(2,1)}) custom-call(s32[32]{0:T(128)} %refs_0_.3, s32[4,16]{1,0:T(4,128)} %refs_1_.3, bf16[8,256,512]{2,1,0:T(8,128)(2,1)} %refs_3_.3, bf16[128,8192]{1,0:T(8,128)(2,1)} %bitcast.9), custom_call_target="tpu_custom_call" | custom-call | tf_op jit(solution)/shard_map/pack_spans/pallas_call | solution.py:131
  3.9 3.1 %collective-permute-start.1 = (bf16[128,512]{1,0:T(8,128)(2,1)}, bf16[128,512]{1,0:T(8,128)(2,1)S(1)}, u32[]{:S(2)}, u32[]{:S(2)}) collective-permute-start(bf16[128,512]{1,0:T(8,128)(2,1)} %get-tuple-element.65), channel_id=1, source_target_pairs={{0,4},{4,0},{8,12},{12,8},{1,5},{5,1},{9,13},{13,9},{2,6},{6,2},{1... | collective-permute-start | bytes 393224 | tf_op jit(solution)/shard_map/columns1/ppermute | solution.py:459
  7.0 2.6 %collective-permute-start.2 = (bf16[128,512]{1,0:T(8,128)(2,1)}, bf16[128,512]{1,0:T(8,128)(2,1)S(1)}, u32[]{:S(2)}, u32[]{:S(2)}) collective-permute-start(bf16[128,512]{1,0:T(8,128)(2,1)} %get-tuple-element.67), channel_id=1, source_target_pairs={{0,8},{4,12},{8,0},{12,4},{1,9},{5,13},{9,1},{13,5},{2,10},{6,14},... | collective-permute-start | bytes 393224 | tf_op jit(solution)/shard_map/columns2/ppermute | solution.py:459
  9.7 1.6 %copy-done.1 = bf16[8,256,512]{2,1,0:T(8,128)(2,1)S(1)} copy-done((bf16[8,256,512]{2,1,0:T(8,128)(2,1)S(1)}, bf16[8,256,512]{2,1,0:T(8,128)(2,1)}, u32[]{:S(2)}) %copy-start.1) | copy-done | bytes 2097176
  11.3 4.3 %pack_spans.2 = (bf16[128,512]{1,0:T(8,128)(2,1)S(1)}, bf16[512,512]{1,0:T(8,128)(2,1)S(1)}, bf16[256,512]{1,0:T(8,128)(2,1)S(1)}, bf16[256,512]{1,0:T(8,128)(2,...) custom-call(s32[32]{0:T(128)S(1)} %copy-done.5, ...), custom_call_target="tpu_custom_call" | custom-call | tf_op jit(solution)/shard_map/pack_spans/pallas_call | solution.py:131
  15.7 5.5 %attend_spans.6 = (f32[4096,128]{1,0:T(8,128)S(1)}, f32[4096,128]{1,0:T(8,128)S(1)}, f32[4096,128]{1,0:T(8,128)S(1)}) custom-call(s32[16,10]{1,0:T(8,128)S(1)} %get-tuple-element.58.refs_0_, bf16[256,2048]{1,0:T(8,128)(2,1)S(1)} %bitcast.11, bf16[256,512]{1,0:T(8,128)(2,1)S(1)} %bitcast.17, bf16[8,256,512]{2,1,0:T(8,128)(2,1)S(1)} %copy-done.2), custom_call_target="tpu_custom_call" | custom-call | flops 25769803776 | tf_op jit(solution)/shard_map/attend_spans/pallas_call | solution.py:412
  21.3 1.8 %collective-permute-start.10 = (bf16[512,512]{1,0:T(8,128)(2,1)S(1)}, bf16[512,512]{1,0:T(8,128)(2,1)S(1)}, u32[]{:S(2)}, u32[]{:S(2)}) collective-permute-start(bf16[512,512]{1,0:T(8,128)(2,1)S(1)} %get-tuple-element.115), channel_id=1, source_target_pairs={{0,2},{1,3},{2,0},{3,1},{4,6},{5,7},{6,4},{7,5},{8,10},{9,11},{10,... | collective-permute-start | bytes 1572872 | tf_op jit(solution)/shard_map/hidden2/ppermute | solution.py:459
  23.1 3.6 %collective-permute-start.5 = (bf16[256,512]{1,0:T(8,128)(2,1)S(1)}, bf16[256,512]{1,0:T(8,128)(2,1)S(1)}, u32[]{:S(2)}, u32[]{:S(2)}) collective-permute-start(bf16[256,512]{1,0:T(8,128)(2,1)S(1)} %copy-done.10), channel_id=1, source_target_pairs={{0,12},{4,8},{8,4},{12,0},{1,13},{5,9},{9,5},{13,1},{2,14},{6,10},... | collective-permute-start | bytes 786440 | tf_op jit(solution)/shard_map/spans0_3/ppermute | solution.py:459
  26.7 0.8 collective-permute-start.6
  27.5 7.0 %collective-permute-done.10 = bf16[512,512]{1,0:T(8,128)(2,1)S(1)} collective-permute-done((bf16[512,512]{1,0:T(8,128)(2,1)S(1)}, bf16[512,512]{1,0:T(8,128)(2,1)S(1)}, u32[]{:S(2)}, u32[]{:S(2)}) %collective-permute-start.10) | collective-permute-done | bytes 524320 | tf_op jit(solution)/shard_map/hidden2/ppermute | solution.py:459
  34.6 4.6 %attend_spans.7 = (f32[4096,128]{1,0:T(8,128)S(1)}, f32[4096,128]{1,0:T(8,128)S(1)}, f32[4096,128]{1,0:T(8,128)S(1)}) custom-call(s32[16,10]{1,0:T(8,128)S(1)} %get-tuple-element.58.refs_0_, bf16[256,2048]{1,0:T(8,128)(2,1)S(1)} %bitcast.12, bf16[256,512]{1,0:T(8,128)(2,1)S(1)} %bitcast.18, bf16[8,256,512]{2,1,0:T(8,128)(2,1)S(1)} %copy-done.2, ...), custom_call_target="tpu_custom_call" | custom-call | flops 17179869184 | tf_op jit(solution)/shard_map/attend_spans/pallas_call | solution.py:412
  39.2 3.6 %collective-permute-start.8 = (bf16[256,512]{1,0:T(8,128)(2,1)S(1)}, bf16[256,512]{1,0:T(8,128)(2,1)S(1)}, u32[]{:S(2)}, u32[]{:S(2)}) collective-permute-start(bf16[256,512]{1,0:T(8,128)(2,1)S(1)} %get-tuple-element.88), channel_id=1, source_target_pairs={{0,12},{4,8},{8,4},{12,0},{1,13},{5,9},{9,5},{13,1},{2,14},{6,10},... | collective-permute-start | bytes 786440 | tf_op jit(solution)/shard_map/spans1_3/ppermute | solution.py:459
  42.8 20.1 %collective-permute-done.refs_4_ = bf16[384,512]{1,0:T(8,128)(2,1)S(1)} collective-permute-done((bf16[384,512]{1,0:T(8,128)(2,1)S(1)}, bf16[384,512]{1,0:T(8,128)(2,1)S(1)}, u32[]{:S(2)}, u32[]{:S(2)}) %collective-permute-start) | collective-permute-done | bytes 393248 | tf_op jit(solution)/shard_map/spans0_2/ppermute | solution.py:459
  63.0 3.5 %collective-permute-start.9 = (bf16[512,512]{1,0:T(8,128)(2,1)S(1)}, bf16[512,512]{1,0:T(8,128)(2,1)S(1)}, u32[]{:S(2)}, u32[]{:S(2)}) collective-permute-start(bf16[512,512]{1,0:T(8,128)(2,1)S(1)} %get-tuple-element.91), channel_id=1, source_target_pairs={{0,4},{4,0},{8,12},{12,8},{1,5},{5,1},{9,13},{13,9},{2,6},{6,2},{1... | collective-permute-start | bytes 1572872 | tf_op jit(solution)/shard_map/spans1_1/ppermute | solution.py:459
  66.5 1.2 project_rows.1
  67.8 8.2 %attend_spans.8 = (f32[4096,128]{1,0:T(8,128)S(1)}, f32[4096,128]{1,0:T(8,128)S(1)}, f32[4096,128]{1,0:T(8,128)S(1)}) custom-call(s32[16,10]{1,0:T(8,128)S(1)} %get-tuple-element.58.refs_0_, bf16[256,2048]{1,0:T(8,128)(2,1)S(1)} %bitcast.13, bf16[256,512]{1,0:T(8,128)(2,1)S(1)} %bitcast.19, bf16[256,512]{1,0:T(8,128)(2,1)S(1)} %collective-permute-done.5.refs_3_, ...), custom_call_target="tpu_custom_call" | custom-call | flops 38654705664 | tf_op jit(solution)/shard_map/attend_spans/pallas_call | solution.py:412
  76.1 2.8 %collective-permute-start.14 = (bf16[384,512]{1,0:T(8,128)(2,1)S(1)}, bf16[384,512]{1,0:T(8,128)(2,1)S(1)}, u32[]{:S(2)}, u32[]{:S(2)}) collective-permute-start(bf16[384,512]{1,0:T(8,128)(2,1)S(1)} %get-tuple-element.102), channel_id=1, source_target_pairs={{0,12},{4,8},{8,4},{12,0},{1,13},{5,9},{9,5},{13,1},{2,14},{6,10},... | collective-permute-start | bytes 1179656 | tf_op jit(solution)/shard_map/spans2_3/ppermute | solution.py:459
  79.6 10.1 %collective-permute-done.12 = bf16[2,128,512]{2,1,0:T(8,128)(2,1)S(1)} collective-permute-done((bf16[2,128,512]{2,1,0:T(8,128)(2,1)S(1)}, bf16[2,128,512]{2,1,0:T(8,128)(2,1)S(1)}, u32[]{:S(2)}, u32[]{:S(2)}) %collective-permute-start.12) | collective-permute-done | bytes 262176 | tf_op jit(solution)/shard_map/partial1/ppermute | solution.py:459
  89.9 7.4 %attend_spans.9 = (f32[4096,128]{1,0:T(8,128)S(1)}, f32[4096,128]{1,0:T(8,128)S(1)}, f32[4096,128]{1,0:T(8,128)S(1)}) custom-call(s32[16,10]{1,0:T(8,128)S(1)} %get-tuple-element.58.refs_0_, bf16[256,2048]{1,0:T(8,128)(2,1)S(1)} %bitcast.14, bf16[256,512]{1,0:T(8,128)(2,1)S(1)} %bitcast.20, bf16[256,512]{1,0:T(8,128)(2,1)S(1)} %collective-permute-done.8.refs_3_, ...), custom_call_target="tpu_custom_call" | custom-call | flops 34359738368 | tf_op jit(solution)/shard_map/attend_spans/pallas_call | solution.py:412
  97.3 15.7 %collective-permute-done.7.refs_4_ = bf16[256,512]{1,0:T(8,128)(2,1)S(1)} collective-permute-done((bf16[256,512]{1,0:T(8,128)(2,1)S(1)}, bf16[256,512]{1,0:T(8,128)(2,1)S(1)}, u32[]{:S(2)}, u32[]{:S(2)}) %collective-permute-start.7) | collective-permute-done | bytes 262176 | tf_op jit(solution)/shard_map/spans2_2/ppermute | solution.py:459
  113.1 1.7 %collective-permute-start.16 = (bf16[128,512]{1,0:T(8,128)(2,1)S(1)}, bf16[128,512]{1,0:T(8,128)(2,1)S(1)}, u32[]{:S(2)}, u32[]{:S(2)}) collective-permute-start(bf16[128,512]{1,0:T(8,128)(2,1)S(1)} %get-tuple-element.109), channel_id=1, source_target_pairs={{0,12},{4,8},{8,4},{12,0},{1,13},{5,9},{9,5},{13,1},{2,14},{6,10},... | collective-permute-start | bytes 393224 | tf_op jit(solution)/shard_map/spans3_3/ppermute | solution.py:459
  114.8 5.9 %attend_spans.10 = (f32[4096,128]{1,0:T(8,128)S(1)}, f32[4096,128]{1,0:T(8,128)S(1)}, f32[4096,128]{1,0:T(8,128)S(1)}, bf16[128,512]{1,0:T(8,128)(2,1)}) custom-call(s32[16,10]{1,0:T(8,128)S(1)} %get-tuple-element.58.refs_0_, bf16[256,2048]{1,0:T(8,128)(2,1)S(1)} %bitcast.15, bf16[256,512]{1,0:T(8,128)(2,1)S(1)} %bitcast.21, ...), custom_call_target="tpu_custom_call" | custom-call | flops 25769803776 | tf_op jit(solution)/shard_map/attend_spans/pallas_call | solution.py:412
  120.7 1.9 %collective-permute-done.13.refs_3_ = bf16[128,512]{1,0:T(8,128)(2,1)S(1)} collective-permute-done((bf16[128,512]{1,0:T(8,128)(2,1)S(1)}, bf16[128,512]{1,0:T(8,128)(2,1)S(1)}, u32[]{:S(2)}, u32[]{:S(2)}) %collective-permute-start.13) | collective-permute-done | bytes 131104 | tf_op jit(solution)/shard_map/spans3_2/ppermute | solution.py:459
  122.6 3.5 %attend_spans.11 = bf16[256,2048]{1,0:T(8,128)(2,1)} custom-call(s32[16,10]{1,0:T(8,128)S(1)} %get-tuple-element.58.refs_0_, bf16[256,2048]{1,0:T(8,128)(2,1)S(1)} %bitcast.16, bf16[256,512]{1,0:T(8,128)(2,1)S(1)} %bitcast.22, bf16[128,512]{1,0:T(8,128)(2,1)S(1)} %collective-permute-done.13.refs_3_, bf16[128,512]{1,0:T(8,128)(2,1)S(1)} %collective-permute-done.16.refs_4_, ...), custom_call_target="tpu_custom_call" | custom-call | flops 8589934592 | tf_op jit(solution)/shard_map/attend_spans/pallas_call | solution.py:412
  (50 shorter events, 1.4 us)
Async XLA Ops:
  0.6 9.0 %copy-start.8 = (s32[1,16,8]{1,2,0:T(8,128)S(1)}, s32[1,16,8]{1,2,0:T(8,128)}, u32[]{:S(2)}) copy-start(s32[1,16,8]{1,2,0:T(8,128)} %param.13) | copy-start | bytes 1540
  0.6 9.1 %copy-start = (bf16[1,16,8,8192]{3,2,1,0:T(8,128)(2,1)S(1)}, bf16[1,16,8,8192]{3,2,1,0:T(8,128)(2,1)}, u32[]{:S(2)}) copy-start(bf16[1,16,8,8192]{3,2,1,0:T(8,128)(2,1)} %param.14) | copy-start | bytes 6291460
  0.7 9.1 %copy-start.4 = (s32[4,16]{1,0:T(4,128)S(1)}, s32[4,16]{1,0:T(4,128)}, u32[]{:S(2)}) copy-start(s32[4,16]{1,0:T(4,128)} %refs_1_.3) | copy-start | bytes 772
  0.7 9.0 %copy-start.5 = (s32[32]{0:T(128)S(1)}, s32[32]{0:T(128)}, u32[]{:S(2)}) copy-start(s32[32]{0:T(128)} %refs_0_.3) | copy-start | bytes 388
  3.9 17.3 %collective-permute-start.1 = (bf16[128,512]{1,0:T(8,128)(2,1)}, bf16[128,512]{1,0:T(8,128)(2,1)S(1)}, u32[]{:S(2)}, u32[]{:S(2)}) collective-permute-start(bf16[128,512]{1,0:T(8,128)(2,1)} %get-tuple-element.65), channel_id=1, source_target_pairs={{0,4},{4,0},{8,12},{12,8},{1,5},{5,1},{9,13},{13,9},{2,6},{6,2},{1... | collective-permute-start | bytes 393224 | tf_op jit(solution)/shard_map/columns1/ppermute | solution.py:459
  7.0 14.2 %collective-permute-start.2 = (bf16[128,512]{1,0:T(8,128)(2,1)}, bf16[128,512]{1,0:T(8,128)(2,1)S(1)}, u32[]{:S(2)}, u32[]{:S(2)}) collective-permute-start(bf16[128,512]{1,0:T(8,128)(2,1)} %get-tuple-element.67), channel_id=1, source_target_pairs={{0,8},{4,12},{8,0},{12,4},{1,9},{5,13},{9,1},{13,5},{2,10},{6,14},... | collective-permute-start | bytes 393224 | tf_op jit(solution)/shard_map/columns2/ppermute | solution.py:459
  9.6 11.6 %collective-permute-start.3 = (bf16[128,512]{1,0:T(8,128)(2,1)}, bf16[128,512]{1,0:T(8,128)(2,1)S(1)}, u32[]{:S(2)}, u32[]{:S(2)}) collective-permute-start(bf16[128,512]{1,0:T(8,128)(2,1)} %get-tuple-element.69), channel_id=1, source_target_pairs={{0,12},{4,8},{8,4},{12,0},{1,13},{5,9},{9,5},{13,1},{2,14},{6,10},... | collective-permute-start | bytes 393224 | tf_op jit(solution)/shard_map/columns3/ppermute | solution.py:459
  15.7 7.5 %copy-start.10 = (bf16[256,512]{1,0:T(8,128)(2,1)S(1)}, bf16[256,512]{1,0:T(8,128)(2,1)}, u32[]{:S(2)}) copy-start(bf16[256,512]{1,0:T(8,128)(2,1)} %get-tuple-element.77) | copy-start | bytes 786436
  15.7 11.0 %copy-start.9 = (bf16[384,512]{1,0:T(8,128)(2,1)S(1)}, bf16[384,512]{1,0:T(8,128)(2,1)}, u32[]{:S(2)}) copy-start(bf16[384,512]{1,0:T(8,128)(2,1)} %get-tuple-element.62) | copy-start | bytes 1179652
  21.3 13.2 %collective-permute-start.10 = (bf16[512,512]{1,0:T(8,128)(2,1)S(1)}, bf16[512,512]{1,0:T(8,128)(2,1)S(1)}, u32[]{:S(2)}, u32[]{:S(2)}) collective-permute-start(bf16[512,512]{1,0:T(8,128)(2,1)S(1)} %get-tuple-element.115), channel_id=1, source_target_pairs={{0,2},{1,3},{2,0},{3,1},{4,6},{5,7},{6,4},{7,5},{8,10},{9,11},{10,... | collective-permute-start | bytes 1572872 | tf_op jit(solution)/shard_map/hidden2/ppermute | solution.py:459
  23.1 16.1 %collective-permute-start.5 = (bf16[256,512]{1,0:T(8,128)(2,1)S(1)}, bf16[256,512]{1,0:T(8,128)(2,1)S(1)}, u32[]{:S(2)}, u32[]{:S(2)}) collective-permute-start(bf16[256,512]{1,0:T(8,128)(2,1)S(1)} %copy-done.10), channel_id=1, source_target_pairs={{0,12},{4,8},{8,4},{12,0},{1,13},{5,9},{9,5},{13,1},{2,14},{6,10},... | collective-permute-start | bytes 786440 | tf_op jit(solution)/shard_map/spans0_3/ppermute | solution.py:459
  26.7 36.2 %collective-permute-start = (bf16[384,512]{1,0:T(8,128)(2,1)S(1)}, bf16[384,512]{1,0:T(8,128)(2,1)S(1)}, u32[]{:S(2)}, u32[]{:S(2)}) collective-permute-start(bf16[384,512]{1,0:T(8,128)(2,1)S(1)} %copy-done.9), channel_id=1, source_target_pairs={{0,8},{4,12},{8,0},{12,4},{1,9},{5,13},{9,1},{13,5},{2,10},{6,14},... | collective-permute-start | bytes 1179656 | tf_op jit(solution)/shard_map/spans0_2/ppermute | solution.py:459
  26.7 36.2 %collective-permute-start.6 = (bf16[512,512]{1,0:T(8,128)(2,1)S(1)}, bf16[512,512]{1,0:T(8,128)(2,1)S(1)}, u32[]{:S(2)}, u32[]{:S(2)}) collective-permute-start(bf16[512,512]{1,0:T(8,128)(2,1)S(1)} %get-tuple-element.80), channel_id=1, source_target_pairs={{0,4},{4,0},{8,12},{12,8},{1,5},{5,1},{9,13},{13,9},{2,6},{6,2},{1... | collective-permute-start | bytes 1572872 | tf_op jit(solution)/shard_map/spans0_1/ppermute | solution.py:459
  34.5 31.9 %collective-permute-start.11 = (bf16[1024,512]{1,0:T(8,128)(2,1)S(1)}, bf16[1024,512]{1,0:T(8,128)(2,1)S(1)}, u32[]{:S(2)}, u32[]{:S(2)}) collective-permute-start(bf16[1024,512]{1,0:T(8,128)(2,1)S(1)} %constant_dynamic-update-slice_fusion.4.refs_0_), channel_id=1, source_target_pairs={{0,1},{1,0},{2,3},{3,2},{4,5},{5,4},{6,7},{7,6},{8,9},{9,8},{10,11... | collective-permute-start | bytes 3145736 | tf_op jit(solution)/shard_map/hidden1/ppermute | solution.py:459
  34.6 31.8 %copy-start.3 = (bf16[2048,512]{1,0:T(8,128)(2,1)S(1)}, bf16[2048,512]{1,0:T(8,128)(2,1)}, u32[]{:S(2)}) copy-start(bf16[2048,512]{1,0:T(8,128)(2,1)} %refs_2_.5) | copy-start | bytes 6291460
  39.2 36.8 %collective-permute-start.8 = (bf16[256,512]{1,0:T(8,128)(2,1)S(1)}, bf16[256,512]{1,0:T(8,128)(2,1)S(1)}, u32[]{:S(2)}, u32[]{:S(2)}) collective-permute-start(bf16[256,512]{1,0:T(8,128)(2,1)S(1)} %get-tuple-element.88), channel_id=1, source_target_pairs={{0,12},{4,8},{8,4},{12,0},{1,13},{5,9},{9,5},{13,1},{2,14},{6,10},... | collective-permute-start | bytes 786440 | tf_op jit(solution)/shard_map/spans1_3/ppermute | solution.py:459
  63.0 13.1 %collective-permute-start.4 = (bf16[256,512]{1,0:T(8,128)(2,1)S(1)}, bf16[256,512]{1,0:T(8,128)(2,1)S(1)}, u32[]{:S(2)}, u32[]{:S(2)}) collective-permute-start(bf16[256,512]{1,0:T(8,128)(2,1)S(1)} %get-tuple-element.76), channel_id=1, source_target_pairs={{0,8},{4,12},{8,0},{12,4},{1,9},{5,13},{9,1},{13,5},{2,10},{6,14},... | collective-permute-start | bytes 786440 | tf_op jit(solution)/shard_map/spans1_2/ppermute | solution.py:459
  63.0 16.6 %collective-permute-start.9 = (bf16[512,512]{1,0:T(8,128)(2,1)S(1)}, bf16[512,512]{1,0:T(8,128)(2,1)S(1)}, u32[]{:S(2)}, u32[]{:S(2)}) collective-permute-start(bf16[512,512]{1,0:T(8,128)(2,1)S(1)} %get-tuple-element.91), channel_id=1, source_target_pairs={{0,4},{4,0},{8,12},{12,8},{1,5},{5,1},{9,13},{13,9},{2,6},{6,2},{1... | collective-permute-start | bytes 1572872 | tf_op jit(solution)/shard_map/spans1_1/ppermute | solution.py:459
  67.7 22.0 %collective-permute-start.12 = (bf16[2,128,512]{2,1,0:T(8,128)(2,1)S(1)}, bf16[2,128,512]{2,1,0:T(8,128)(2,1)S(1)}, u32[]{:S(2)}, u32[]{:S(2)}) collective-permute-start(bf16[2,128,512]{2,1,0:T(8,128)(2,1)S(1)} %get-tuple-element.94), channel_id=1, source_target_pairs={{0,4},{4,0},{8,12},{12,8},{1,5},{5,1},{9,13},{13,9},{2,6},{6,2},{1... | collective-permute-start | bytes 786440 | tf_op jit(solution)/shard_map/partial1/ppermute | solution.py:459
  76.1 21.2 %collective-permute-start.14 = (bf16[384,512]{1,0:T(8,128)(2,1)S(1)}, bf16[384,512]{1,0:T(8,128)(2,1)S(1)}, u32[]{:S(2)}, u32[]{:S(2)}) collective-permute-start(bf16[384,512]{1,0:T(8,128)(2,1)S(1)} %get-tuple-element.102), channel_id=1, source_target_pairs={{0,12},{4,8},{8,4},{12,0},{1,13},{5,9},{9,5},{13,1},{2,14},{6,10},... | collective-permute-start | bytes 1179656 | tf_op jit(solution)/shard_map/spans2_3/ppermute | solution.py:459
  78.9 34.2 %collective-permute-start.7 = (bf16[256,512]{1,0:T(8,128)(2,1)S(1)}, bf16[256,512]{1,0:T(8,128)(2,1)S(1)}, u32[]{:S(2)}, u32[]{:S(2)}) collective-permute-start(bf16[256,512]{1,0:T(8,128)(2,1)S(1)} %get-tuple-element.86), channel_id=1, source_target_pairs={{0,8},{4,12},{8,0},{12,4},{1,9},{5,13},{9,1},{13,5},{2,10},{6,14},... | collective-permute-start | bytes 786440 | tf_op jit(solution)/shard_map/spans2_2/ppermute | solution.py:459
  89.8 25.0 %collective-permute-start.15 = (bf16[1,128,512]{2,1,0:T(8,128)(2,1)S(1)}, bf16[1,128,512]{2,1,0:T(8,128)(2,1)S(1)}, u32[]{:S(2)}, u32[]{:S(2)}) collective-permute-start(bf16[1,128,512]{2,1,0:T(8,128)(2,1)S(1)} %slice.19), channel_id=1, source_target_pairs={{0,8},{4,12},{8,0},{12,4},{1,9},{5,13},{9,1},{13,5},{2,10},{6,14},... | collective-permute-start | bytes 393224 | tf_op jit(solution)/shard_map/partial2/ppermute | solution.py:459
  113.1 7.7 %collective-permute-start.16 = (bf16[128,512]{1,0:T(8,128)(2,1)S(1)}, bf16[128,512]{1,0:T(8,128)(2,1)S(1)}, u32[]{:S(2)}, u32[]{:S(2)}) collective-permute-start(bf16[128,512]{1,0:T(8,128)(2,1)S(1)} %get-tuple-element.109), channel_id=1, source_target_pairs={{0,12},{4,8},{8,4},{12,0},{1,13},{5,9},{9,5},{13,1},{2,14},{6,10},... | collective-permute-start | bytes 393224 | tf_op jit(solution)/shard_map/spans3_3/ppermute | solution.py:459
  114.7 7.9 %collective-permute-start.13 = (bf16[128,512]{1,0:T(8,128)(2,1)S(1)}, bf16[128,512]{1,0:T(8,128)(2,1)S(1)}, u32[]{:S(2)}, u32[]{:S(2)}) collective-permute-start(bf16[128,512]{1,0:T(8,128)(2,1)S(1)} %get-tuple-element.100), channel_id=1, source_target_pairs={{0,8},{4,12},{8,0},{12,4},{1,9},{5,13},{9,1},{13,5},{2,10},{6,14},... | collective-permute-start | bytes 393224 | tf_op jit(solution)/shard_map/spans3_2/ppermute | solution.py:459
  (4 other events, 14.6 us)

commit v7 on v6

--- a/solution.py
+++ b/solution.py
@@ -523,7 +523,7 @@
         )
 
     def recomputed():
-        blocks = [hidden_own] + behind([hidden_in[d] for d in away[::-1]], state)
+        blocks = [hidden_own] + [hidden_in[d] for d in away[::-1]]
         distances = [0]
         for step, bit in enumerate(reversed(range(n_tensor.bit_length() - 1))):
             distances += [distance ^ (1 << bit) for distance in distances]

time: 126 us -> 130 us (1.032)
  starting transfers between devices: 24.4 us -> 31.3 us
  waiting for transfers between devices: 54.9 us -> 51.8 us
    ppermute x17, starting transfers between devices: 24.4 us -> 31.3 us  [exchange(): return lax.ppermute(piece, axis, [(i, i ^ distance) for i in range(size)])]
    ppermute x17, waiting for transfers between devices: 54.9 us -> 51.8 us  [exchange(): return lax.ppermute(piece, axis, [(i, i ^ distance) for i in range(size)])]
  transfers between devices with their start and end apart: 17 -> 17, of which waited for: 5 -> 5; matrix products, arithmetic and copies ran while one was open for 0% -> 0% of each run, Pallas kernels for 29% -> 28%
where the time goes in v7:
time: 130 us
  waiting for transfers between devices  51.8 us (40%)
  Pallas kernels  43.7 us (34%)
  starting transfers between devices  31.3 us (24%)
  local copies, waits for them, and re-layouts  1.84 us (1%)
    ppermute x17, waiting for transfers between devices, exchange(): return lax.ppermute(piece, axis, [(i, i ^ distance) for i in range(size)])  51.8 us
    pallas_call x6, Pallas kernels, attend(): pl.pallas_call(functools.partial(attend_kernel, tuple(parts), len(pieces)...  34.9 us
    ppermute x17, starting transfers between devices, exchange(): return lax.ppermute(piece, axis, [(i, i ^ distance) for i in range(size)])  31.3 us
    pallas_call x2, Pallas kernels, pack(): pl.pallas_call(functools.partial(pack_kernel, messages, shard, with_table...  7.58 us
  transfers between devices with their start and end apart: 17, of which 5 were waited for; matrix products, arithmetic and copies ran while one was open for 0% of the time, Pallas kernels for 28%

profile of v7, /device:TPU:0, one launch (start us, length us, event | category | flops | bytes accessed | tf_op | source)
XLA Modules:
  0.0 129.7 jit_solution(12600483746858579475)
XLA Ops:
  0.7 3.3 %pack_spans.3 = (bf16[128,512]{1,0:T(8,128)(2,1)}, bf16[128,512]{1,0:T(8,128)(2,1)}, bf16[128,512]{1,0:T(8,128)(2,1)}, bf16[256,512]{1,0:T(8,128)(2,1)}, bf16[384,512]{1,0:T(8,128)(2,1)}) custom-call(s32[32]{0:T(128)} %refs_0_.3, s32[4,16]{1,0:T(4,128)} %refs_1_.3, bf16[8,256,512]{2,1,0:T(8,128)(2,1)} %refs_3_.3, bf16[128,8192]{1,0:T(8,128)(2,1)} %bitcast.9), custom_call_target="tpu_custom_call" | custom-call | tf_op jit(solution)/shard_map/pack_spans/pallas_call | solution.py:131
  3.9 3.1 %collective-permute-start.1 = (bf16[128,512]{1,0:T(8,128)(2,1)}, bf16[128,512]{1,0:T(8,128)(2,1)S(1)}, u32[]{:S(2)}, u32[]{:S(2)}) collective-permute-start(bf16[128,512]{1,0:T(8,128)(2,1)} %get-tuple-element.62), channel_id=1, source_target_pairs={{0,4},{4,0},{8,12},{12,8},{1,5},{5,1},{9,13},{13,9},{2,6},{6,2},{1... | collective-permute-start | bytes 393224 | tf_op jit(solution)/shard_map/columns1/ppermute | solution.py:459
  7.0 2.6 %collective-permute-start.2 = (bf16[128,512]{1,0:T(8,128)(2,1)}, bf16[128,512]{1,0:T(8,128)(2,1)S(1)}, u32[]{:S(2)}, u32[]{:S(2)}) collective-permute-start(bf16[128,512]{1,0:T(8,128)(2,1)} %get-tuple-element.63), channel_id=1, source_target_pairs={{0,8},{4,12},{8,0},{12,4},{1,9},{5,13},{9,1},{13,5},{2,10},{6,14},... | collective-permute-start | bytes 393224 | tf_op jit(solution)/shard_map/columns2/ppermute | solution.py:459
  9.6 3.8 %collective-permute-start.5 = (bf16[256,512]{1,0:T(8,128)(2,1)}, bf16[256,512]{1,0:T(8,128)(2,1)S(1)}, u32[]{:S(2)}, u32[]{:S(2)}) collective-permute-start(bf16[256,512]{1,0:T(8,128)(2,1)} %get-tuple-element.71), channel_id=1, source_target_pairs={{0,12},{4,8},{8,4},{12,0},{1,13},{5,9},{9,5},{13,1},{2,14},{6,10},... | collective-permute-start | bytes 786440 | tf_op jit(solution)/shard_map/spans0_3/ppermute | solution.py:459
  13.5 1.6 %copy-done.1 = bf16[8,256,512]{2,1,0:T(8,128)(2,1)S(1)} copy-done((bf16[8,256,512]{2,1,0:T(8,128)(2,1)S(1)}, bf16[8,256,512]{2,1,0:T(8,128)(2,1)}, u32[]{:S(2)}) %copy-start.1) | copy-done | bytes 2097176
  15.1 4.3 %pack_spans.2 = (bf16[128,512]{1,0:T(8,128)(2,1)S(1)}, bf16[512,512]{1,0:T(8,128)(2,1)S(1)}, bf16[256,512]{1,0:T(8,128)(2,1)S(1)}, bf16[256,512]{1,0:T(8,128)(2,...) custom-call(s32[32]{0:T(128)S(1)} %copy-done.5, ...), custom_call_target="tpu_custom_call" | custom-call | tf_op jit(solution)/shard_map/pack_spans/pallas_call | solution.py:131
  19.5 14.7 %collective-permute-done.2 = bf16[128,512]{1,0:T(8,128)(2,1)S(1)} collective-permute-done((bf16[128,512]{1,0:T(8,128)(2,1)}, bf16[128,512]{1,0:T(8,128)(2,1)S(1)}, u32[]{:S(2)}, u32[]{:S(2)}) %collective-permute-start.2) | collective-permute-done | bytes 131104 | tf_op jit(solution)/shard_map/columns2/ppermute | solution.py:459
  34.3 1.6 %collective-permute-start.10 = (bf16[512,512]{1,0:T(8,128)(2,1)S(1)}, bf16[512,512]{1,0:T(8,128)(2,1)S(1)}, u32[]{:S(2)}, u32[]{:S(2)}) collective-permute-start(bf16[512,512]{1,0:T(8,128)(2,1)S(1)} %get-tuple-element.109), channel_id=1, source_target_pairs={{0,2},{1,3},{2,0},{3,1},{4,6},{5,7},{6,4},{7,5},{8,10},{9,11},{10,... | collective-permute-start | bytes 1572872 | tf_op jit(solution)/shard_map/hidden2/ppermute | solution.py:459
  35.9 5.3 %attend_spans.6 = (f32[4096,128]{1,0:T(8,128)S(1)}, f32[4096,128]{1,0:T(8,128)S(1)}, f32[4096,128]{1,0:T(8,128)S(1)}) custom-call(s32[16,10]{1,0:T(8,128)S(1)} %get-tuple-element.55.refs_0_, bf16[256,2048]{1,0:T(8,128)(2,1)S(1)} %bitcast.11, bf16[256,512]{1,0:T(8,128)(2,1)S(1)} %bitcast.17, bf16[8,256,512]{2,1,0:T(8,128)(2,1)S(1)} %copy-done.2), custom_call_target="tpu_custom_call" | custom-call | flops 25769803776 | tf_op jit(solution)/shard_map/attend_spans/pallas_call | solution.py:412
  41.1 3.4 %collective-permute-start.6 = (bf16[512,512]{1,0:T(8,128)(2,1)S(1)}, bf16[512,512]{1,0:T(8,128)(2,1)S(1)}, u32[]{:S(2)}, u32[]{:S(2)}) collective-permute-start(bf16[512,512]{1,0:T(8,128)(2,1)S(1)} %get-tuple-element.74), channel_id=1, source_target_pairs={{0,4},{4,0},{8,12},{12,8},{1,5},{5,1},{9,13},{13,9},{2,6},{6,2},{1... | collective-permute-start | bytes 1572872 | tf_op jit(solution)/shard_map/spans0_1/ppermute | solution.py:459
  44.7 4.5 %attend_spans.7 = (f32[4096,128]{1,0:T(8,128)S(1)}, f32[4096,128]{1,0:T(8,128)S(1)}, f32[4096,128]{1,0:T(8,128)S(1)}) custom-call(s32[16,10]{1,0:T(8,128)S(1)} %get-tuple-element.55.refs_0_, bf16[256,2048]{1,0:T(8,128)(2,1)S(1)} %bitcast.12, bf16[256,512]{1,0:T(8,128)(2,1)S(1)} %bitcast.18, bf16[8,256,512]{2,1,0:T(8,128)(2,1)S(1)} %copy-done.2, ...), custom_call_target="tpu_custom_call" | custom-call | flops 17179869184 | tf_op jit(solution)/shard_map/attend_spans/pallas_call | solution.py:412
  49.2 3.6 %collective-permute-start.8 = (bf16[256,512]{1,0:T(8,128)(2,1)S(1)}, bf16[256,512]{1,0:T(8,128)(2,1)S(1)}, u32[]{:S(2)}, u32[]{:S(2)}) collective-permute-start(bf16[256,512]{1,0:T(8,128)(2,1)S(1)} %get-tuple-element.82), channel_id=1, source_target_pairs={{0,12},{4,8},{8,4},{12,0},{1,13},{5,9},{9,5},{13,1},{2,14},{6,10},... | collective-permute-start | bytes 786440 | tf_op jit(solution)/shard_map/spans1_3/ppermute | solution.py:459
  52.9 2.0 %collective-permute-start.4 = (bf16[256,512]{1,0:T(8,128)(2,1)S(1)}, bf16[256,512]{1,0:T(8,128)(2,1)S(1)}, u32[]{:S(2)}, u32[]{:S(2)}) collective-permute-start(bf16[256,512]{1,0:T(8,128)(2,1)S(1)} %get-tuple-element.70), channel_id=1, source_target_pairs={{0,8},{4,12},{8,0},{12,4},{1,9},{5,13},{9,1},{13,5},{2,10},{6,14},... | collective-permute-start | bytes 786440 | tf_op jit(solution)/shard_map/spans1_2/ppermute | solution.py:459
  54.8 11.4 %collective-permute-done.6.refs_5_ = bf16[512,512]{1,0:T(8,128)(2,1)S(1)} collective-permute-done((bf16[512,512]{1,0:T(8,128)(2,1)S(1)}, bf16[512,512]{1,0:T(8,128)(2,1)S(1)}, u32[]{:S(2)}, u32[]{:S(2)}) %collective-permute-start.6) | collective-permute-done | bytes 524320 | tf_op jit(solution)/shard_map/spans0_1/ppermute | solution.py:459
  67.5 2.1 %collective-permute-start.12 = (bf16[2,128,512]{2,1,0:T(8,128)(2,1)S(1)}, bf16[2,128,512]{2,1,0:T(8,128)(2,1)S(1)}, u32[]{:S(2)}, u32[]{:S(2)}) collective-permute-start(bf16[2,128,512]{2,1,0:T(8,128)(2,1)S(1)} %get-tuple-element.88), channel_id=1, source_target_pairs={{0,4},{4,0},{8,12},{12,8},{1,5},{5,1},{9,13},{13,9},{2,6},{6,2},{1... | collective-permute-start | bytes 786440 | tf_op jit(solution)/shard_map/partial1/ppermute | solution.py:459
  69.6 8.2 %attend_spans.8 = (f32[4096,128]{1,0:T(8,128)S(1)}, f32[4096,128]{1,0:T(8,128)S(1)}, f32[4096,128]{1,0:T(8,128)S(1)}) custom-call(s32[16,10]{1,0:T(8,128)S(1)} %get-tuple-element.55.refs_0_, bf16[256,2048]{1,0:T(8,128)(2,1)S(1)} %bitcast.13, bf16[256,512]{1,0:T(8,128)(2,1)S(1)} %bitcast.19, bf16[256,512]{1,0:T(8,128)(2,1)S(1)} %collective-permute-done.5.refs_3_, ...), custom_call_target="tpu_custom_call" | custom-call | flops 38654705664 | tf_op jit(solution)/shard_map/attend_spans/pallas_call | solution.py:412
  79.2 1.5 %collective-permute-start.14 = (bf16[384,512]{1,0:T(8,128)(2,1)S(1)}, bf16[384,512]{1,0:T(8,128)(2,1)S(1)}, u32[]{:S(2)}, u32[]{:S(2)}) collective-permute-start(bf16[384,512]{1,0:T(8,128)(2,1)S(1)} %get-tuple-element.96), channel_id=1, source_target_pairs={{0,12},{4,8},{8,4},{12,0},{1,13},{5,9},{9,5},{13,1},{2,14},{6,10},... | collective-permute-start | bytes 1179656 | tf_op jit(solution)/shard_map/spans2_3/ppermute | solution.py:459
  80.8 11.0 %collective-permute-done.9.refs_5_ = bf16[512,512]{1,0:T(8,128)(2,1)S(1)} collective-permute-done((bf16[512,512]{1,0:T(8,128)(2,1)S(1)}, bf16[512,512]{1,0:T(8,128)(2,1)S(1)}, u32[]{:S(2)}, u32[]{:S(2)}) %collective-permute-start.9) | collective-permute-done | bytes 524320 | tf_op jit(solution)/shard_map/spans1_1/ppermute | solution.py:459
  91.7 13.3 %collective-permute-done.12 = bf16[2,128,512]{2,1,0:T(8,128)(2,1)S(1)} collective-permute-done((bf16[2,128,512]{2,1,0:T(8,128)(2,1)S(1)}, bf16[2,128,512]{2,1,0:T(8,128)(2,1)S(1)}, u32[]{:S(2)}, u32[]{:S(2)}) %collective-permute-start.12) | collective-permute-done | bytes 262176 | tf_op jit(solution)/shard_map/partial1/ppermute | solution.py:459
  106.4 7.4 %attend_spans.9 = (f32[4096,128]{1,0:T(8,128)S(1)}, f32[4096,128]{1,0:T(8,128)S(1)}, f32[4096,128]{1,0:T(8,128)S(1)}) custom-call(s32[16,10]{1,0:T(8,128)S(1)} %get-tuple-element.55.refs_0_, bf16[256,2048]{1,0:T(8,128)(2,1)S(1)} %bitcast.14, bf16[256,512]{1,0:T(8,128)(2,1)S(1)} %bitcast.20, bf16[256,512]{1,0:T(8,128)(2,1)S(1)} %collective-permute-done.8.refs_3_, ...), custom_call_target="tpu_custom_call" | custom-call | flops 34359738368 | tf_op jit(solution)/shard_map/attend_spans/pallas_call | solution.py:412
  113.8 1.8 %collective-permute-start.13 = (bf16[128,512]{1,0:T(8,128)(2,1)S(1)}, bf16[128,512]{1,0:T(8,128)(2,1)S(1)}, u32[]{:S(2)}, u32[]{:S(2)}) collective-permute-start(bf16[128,512]{1,0:T(8,128)(2,1)S(1)} %get-tuple-element.94), channel_id=1, source_target_pairs={{0,8},{4,12},{8,0},{12,4},{1,9},{5,13},{9,1},{13,5},{2,10},{6,14},... | collective-permute-start | bytes 393224 | tf_op jit(solution)/shard_map/spans3_2/ppermute | solution.py:459
  115.6 3.1 %collective-permute-start.16 = (bf16[128,512]{1,0:T(8,128)(2,1)S(1)}, bf16[128,512]{1,0:T(8,128)(2,1)S(1)}, u32[]{:S(2)}, u32[]{:S(2)}) collective-permute-start(bf16[128,512]{1,0:T(8,128)(2,1)S(1)} %get-tuple-element.103), channel_id=1, source_target_pairs={{0,12},{4,8},{8,4},{12,0},{1,13},{5,9},{9,5},{13,1},{2,14},{6,10},... | collective-permute-start | bytes 393224 | tf_op jit(solution)/shard_map/spans3_3/ppermute | solution.py:459
  118.7 5.9 %attend_spans.10 = (f32[4096,128]{1,0:T(8,128)S(1)}, f32[4096,128]{1,0:T(8,128)S(1)}, f32[4096,128]{1,0:T(8,128)S(1)}, bf16[128,512]{1,0:T(8,128)(2,1)}) custom-call(s32[16,10]{1,0:T(8,128)S(1)} %get-tuple-element.55.refs_0_, bf16[256,2048]{1,0:T(8,128)(2,1)S(1)} %bitcast.15, bf16[256,512]{1,0:T(8,128)(2,1)S(1)} %bitcast.21, ...), custom_call_target="tpu_custom_call" | custom-call | flops 25769803776 | tf_op jit(solution)/shard_map/attend_spans/pallas_call | solution.py:412
  126.1 3.5 %attend_spans.11 = bf16[256,2048]{1,0:T(8,128)(2,1)} custom-call(s32[16,10]{1,0:T(8,128)S(1)} %get-tuple-element.55.refs_0_, bf16[256,2048]{1,0:T(8,128)(2,1)S(1)} %bitcast.16, bf16[256,512]{1,0:T(8,128)(2,1)S(1)} %bitcast.22, bf16[128,512]{1,0:T(8,128)(2,1)S(1)} %collective-permute-done.13.refs_3_, bf16[128,512]{1,0:T(8,128)(2,1)S(1)} %collective-permute-done.16.refs_4_, ...), custom_call_target="tpu_custom_call" | custom-call | flops 8589934592 | tf_op jit(solution)/shard_map/attend_spans/pallas_call | solution.py:412
  (46 shorter events, 5.8 us)
Async XLA Ops:
  0.6 12.9 %copy-start = (bf16[1,16,8,8192]{3,2,1,0:T(8,128)(2,1)S(1)}, bf16[1,16,8,8192]{3,2,1,0:T(8,128)(2,1)}, u32[]{:S(2)}) copy-start(bf16[1,16,8,8192]{3,2,1,0:T(8,128)(2,1)} %param.14) | copy-start | bytes 6291460
  0.7 12.9 %copy-start.4 = (s32[4,16]{1,0:T(4,128)S(1)}, s32[4,16]{1,0:T(4,128)}, u32[]{:S(2)}) copy-start(s32[4,16]{1,0:T(4,128)} %refs_1_.3) | copy-start | bytes 772
  0.7 12.9 %copy-start.5 = (s32[32]{0:T(128)S(1)}, s32[32]{0:T(128)}, u32[]{:S(2)}) copy-start(s32[32]{0:T(128)} %refs_0_.3) | copy-start | bytes 388
  3.9 15.5 %collective-permute-start.1 = (bf16[128,512]{1,0:T(8,128)(2,1)}, bf16[128,512]{1,0:T(8,128)(2,1)S(1)}, u32[]{:S(2)}, u32[]{:S(2)}) collective-permute-start(bf16[128,512]{1,0:T(8,128)(2,1)} %get-tuple-element.62), channel_id=1, source_target_pairs={{0,4},{4,0},{8,12},{12,8},{1,5},{5,1},{9,13},{13,9},{2,6},{6,2},{1... | collective-permute-start | bytes 393224 | tf_op jit(solution)/shard_map/columns1/ppermute | solution.py:459
  7.0 27.2 %collective-permute-start.2 = (bf16[128,512]{1,0:T(8,128)(2,1)}, bf16[128,512]{1,0:T(8,128)(2,1)S(1)}, u32[]{:S(2)}, u32[]{:S(2)}) collective-permute-start(bf16[128,512]{1,0:T(8,128)(2,1)} %get-tuple-element.63), channel_id=1, source_target_pairs={{0,8},{4,12},{8,0},{12,4},{1,9},{5,13},{9,1},{13,5},{2,10},{6,14},... | collective-permute-start | bytes 393224 | tf_op jit(solution)/shard_map/columns2/ppermute | solution.py:459
  9.6 24.6 %collective-permute-start.3 = (bf16[128,512]{1,0:T(8,128)(2,1)}, bf16[128,512]{1,0:T(8,128)(2,1)S(1)}, u32[]{:S(2)}, u32[]{:S(2)}) collective-permute-start(bf16[128,512]{1,0:T(8,128)(2,1)} %get-tuple-element.64), channel_id=1, source_target_pairs={{0,12},{4,8},{8,4},{12,0},{1,13},{5,9},{9,5},{13,1},{2,14},{6,10},... | collective-permute-start | bytes 393224 | tf_op jit(solution)/shard_map/columns3/ppermute | solution.py:459
  9.6 39.6 %collective-permute-start.5 = (bf16[256,512]{1,0:T(8,128)(2,1)}, bf16[256,512]{1,0:T(8,128)(2,1)S(1)}, u32[]{:S(2)}, u32[]{:S(2)}) collective-permute-start(bf16[256,512]{1,0:T(8,128)(2,1)} %get-tuple-element.71), channel_id=1, source_target_pairs={{0,12},{4,8},{8,4},{12,0},{1,13},{5,9},{9,5},{13,1},{2,14},{6,10},... | collective-permute-start | bytes 786440 | tf_op jit(solution)/shard_map/spans0_3/ppermute | solution.py:459
  13.4 39.4 %collective-permute-start = (bf16[384,512]{1,0:T(8,128)(2,1)}, bf16[384,512]{1,0:T(8,128)(2,1)S(1)}, u32[]{:S(2)}, u32[]{:S(2)}) collective-permute-start(bf16[384,512]{1,0:T(8,128)(2,1)} %get-tuple-element.59), channel_id=1, source_target_pairs={{0,8},{4,12},{8,0},{12,4},{1,9},{5,13},{9,1},{13,5},{2,10},{6,14},... | collective-permute-start | bytes 1179656 | tf_op jit(solution)/shard_map/spans0_2/ppermute | solution.py:459
  15.1 20.7 %copy-start.2 = (bf16[8,256,512]{2,1,0:T(8,128)(2,1)S(1)}, bf16[8,256,512]{2,1,0:T(8,128)(2,1)}, u32[]{:S(2)}) copy-start(bf16[8,256,512]{2,1,0:T(8,128)(2,1)} %refs_3_.3) | copy-start | bytes 6291460
  15.1 20.7 %copy-start.6 = (bf16[1,256,2048]{2,1,0:T(8,128)(2,1)S(1)}, bf16[1,256,2048]{2,1,0:T(8,128)(2,1)}, u32[]{:S(2)}) copy-start(bf16[1,256,2048]{2,1,0:T(8,128)(2,1)} %param.8) | copy-start | bytes 3145732
  15.1 20.7 %copy-start.7 = (bf16[1,256,512]{2,1,0:T(8,128)(2,1)S(1)}, bf16[1,256,512]{2,1,0:T(8,128)(2,1)}, u32[]{:S(2)}) copy-start(bf16[1,256,512]{2,1,0:T(8,128)(2,1)} %param.9) | copy-start | bytes 786436
  34.3 10.2 %collective-permute-start.10 = (bf16[512,512]{1,0:T(8,128)(2,1)S(1)}, bf16[512,512]{1,0:T(8,128)(2,1)S(1)}, u32[]{:S(2)}, u32[]{:S(2)}) collective-permute-start(bf16[512,512]{1,0:T(8,128)(2,1)S(1)} %get-tuple-element.109), channel_id=1, source_target_pairs={{0,2},{1,3},{2,0},{3,1},{4,6},{5,7},{6,4},{7,5},{8,10},{9,11},{10,... | collective-permute-start | bytes 1572872 | tf_op jit(solution)/shard_map/hidden2/ppermute | solution.py:459
  41.1 25.1 %collective-permute-start.6 = (bf16[512,512]{1,0:T(8,128)(2,1)S(1)}, bf16[512,512]{1,0:T(8,128)(2,1)S(1)}, u32[]{:S(2)}, u32[]{:S(2)}) collective-permute-start(bf16[512,512]{1,0:T(8,128)(2,1)S(1)} %get-tuple-element.74), channel_id=1, source_target_pairs={{0,4},{4,0},{8,12},{12,8},{1,5},{5,1},{9,13},{13,9},{2,6},{6,2},{1... | collective-permute-start | bytes 1572872 | tf_op jit(solution)/shard_map/spans0_1/ppermute | solution.py:459
  44.6 21.7 %collective-permute-start.11 = (bf16[1024,512]{1,0:T(8,128)(2,1)S(1)}, bf16[1024,512]{1,0:T(8,128)(2,1)S(1)}, u32[]{:S(2)}, u32[]{:S(2)}) collective-permute-start(bf16[1024,512]{1,0:T(8,128)(2,1)S(1)} %constant_dynamic-update-slice_fusion.4.refs_0_), channel_id=1, source_target_pairs={{0,1},{1,0},{2,3},{3,2},{4,5},{5,4},{6,7},{7,6},{8,9},{9,8},{10,11... | collective-permute-start | bytes 3145736 | tf_op jit(solution)/shard_map/hidden1/ppermute | solution.py:459
  44.6 21.6 %copy-start.3 = (bf16[2048,512]{1,0:T(8,128)(2,1)S(1)}, bf16[2048,512]{1,0:T(8,128)(2,1)}, u32[]{:S(2)}) copy-start(bf16[2048,512]{1,0:T(8,128)(2,1)} %refs_2_.5) | copy-start | bytes 6291460
  49.2 30.0 %collective-permute-start.8 = (bf16[256,512]{1,0:T(8,128)(2,1)S(1)}, bf16[256,512]{1,0:T(8,128)(2,1)S(1)}, u32[]{:S(2)}, u32[]{:S(2)}) collective-permute-start(bf16[256,512]{1,0:T(8,128)(2,1)S(1)} %get-tuple-element.82), channel_id=1, source_target_pairs={{0,12},{4,8},{8,4},{12,0},{1,13},{5,9},{9,5},{13,1},{2,14},{6,10},... | collective-permute-start | bytes 786440 | tf_op jit(solution)/shard_map/spans1_3/ppermute | solution.py:459
  52.9 25.0 %collective-permute-start.4 = (bf16[256,512]{1,0:T(8,128)(2,1)S(1)}, bf16[256,512]{1,0:T(8,128)(2,1)S(1)}, u32[]{:S(2)}, u32[]{:S(2)}) collective-permute-start(bf16[256,512]{1,0:T(8,128)(2,1)S(1)} %get-tuple-element.70), channel_id=1, source_target_pairs={{0,8},{4,12},{8,0},{12,4},{1,9},{5,13},{9,1},{13,5},{2,10},{6,14},... | collective-permute-start | bytes 786440 | tf_op jit(solution)/shard_map/spans1_2/ppermute | solution.py:459
  66.2 25.5 %collective-permute-start.9 = (bf16[512,512]{1,0:T(8,128)(2,1)S(1)}, bf16[512,512]{1,0:T(8,128)(2,1)S(1)}, u32[]{:S(2)}, u32[]{:S(2)}) collective-permute-start(bf16[512,512]{1,0:T(8,128)(2,1)S(1)} %get-tuple-element.85), channel_id=1, source_target_pairs={{0,4},{4,0},{8,12},{12,8},{1,5},{5,1},{9,13},{13,9},{2,6},{6,2},{1... | collective-permute-start | bytes 1572872 | tf_op jit(solution)/shard_map/spans1_1/ppermute | solution.py:459
  67.5 37.5 %collective-permute-start.12 = (bf16[2,128,512]{2,1,0:T(8,128)(2,1)S(1)}, bf16[2,128,512]{2,1,0:T(8,128)(2,1)S(1)}, u32[]{:S(2)}, u32[]{:S(2)}) collective-permute-start(bf16[2,128,512]{2,1,0:T(8,128)(2,1)S(1)} %get-tuple-element.88), channel_id=1, source_target_pairs={{0,4},{4,0},{8,12},{12,8},{1,5},{5,1},{9,13},{13,9},{2,6},{6,2},{1... | collective-permute-start | bytes 786440 | tf_op jit(solution)/shard_map/partial1/ppermute | solution.py:459
  77.8 36.0 %collective-permute-start.7 = (bf16[256,512]{1,0:T(8,128)(2,1)S(1)}, bf16[256,512]{1,0:T(8,128)(2,1)S(1)}, u32[]{:S(2)}, u32[]{:S(2)}) collective-permute-start(bf16[256,512]{1,0:T(8,128)(2,1)S(1)} %get-tuple-element.80), channel_id=1, source_target_pairs={{0,8},{4,12},{8,0},{12,4},{1,9},{5,13},{9,1},{13,5},{2,10},{6,14},... | collective-permute-start | bytes 786440 | tf_op jit(solution)/shard_map/spans2_2/ppermute | solution.py:459
  79.2 34.6 %collective-permute-start.14 = (bf16[384,512]{1,0:T(8,128)(2,1)S(1)}, bf16[384,512]{1,0:T(8,128)(2,1)S(1)}, u32[]{:S(2)}, u32[]{:S(2)}) collective-permute-start(bf16[384,512]{1,0:T(8,128)(2,1)S(1)} %get-tuple-element.96), channel_id=1, source_target_pairs={{0,12},{4,8},{8,4},{12,0},{1,13},{5,9},{9,5},{13,1},{2,14},{6,10},... | collective-permute-start | bytes 1179656 | tf_op jit(solution)/shard_map/spans2_3/ppermute | solution.py:459
  105.1 13.6 %collective-permute-start.15 = (bf16[1,128,512]{2,1,0:T(8,128)(2,1)S(1)}, bf16[1,128,512]{2,1,0:T(8,128)(2,1)S(1)}, u32[]{:S(2)}, u32[]{:S(2)}) collective-permute-start(bf16[1,128,512]{2,1,0:T(8,128)(2,1)S(1)} %slice.19), channel_id=1, source_target_pairs={{0,8},{4,12},{8,0},{12,4},{1,9},{5,13},{9,1},{13,5},{2,10},{6,14},... | collective-permute-start | bytes 393224 | tf_op jit(solution)/shard_map/partial2/ppermute | solution.py:459
  113.8 12.3 %collective-permute-start.13 = (bf16[128,512]{1,0:T(8,128)(2,1)S(1)}, bf16[128,512]{1,0:T(8,128)(2,1)S(1)}, u32[]{:S(2)}, u32[]{:S(2)}) collective-permute-start(bf16[128,512]{1,0:T(8,128)(2,1)S(1)} %get-tuple-element.94), channel_id=1, source_target_pairs={{0,8},{4,12},{8,0},{12,4},{1,9},{5,13},{9,1},{13,5},{2,10},{6,14},... | collective-permute-start | bytes 393224 | tf_op jit(solution)/shard_map/spans3_2/ppermute | solution.py:459
  115.6 10.5 %collective-permute-start.16 = (bf16[128,512]{1,0:T(8,128)(2,1)S(1)}, bf16[128,512]{1,0:T(8,128)(2,1)S(1)}, u32[]{:S(2)}, u32[]{:S(2)}) collective-permute-start(bf16[128,512]{1,0:T(8,128)(2,1)S(1)} %get-tuple-element.103), channel_id=1, source_target_pairs={{0,12},{4,8},{8,4},{12,0},{1,13},{5,9},{9,5},{13,1},{2,14},{6,10},... | collective-permute-start | bytes 393224 | tf_op jit(solution)/shard_map/spans3_3/ppermute | solution.py:459
  (2 other events, 14.4 us)

commit v8 on v7

--- a/solution.py
+++ b/solution.py
@@ -12,6 +12,7 @@
 EXP_SCALE = math.log2(math.e) * HEAD_WIDTH ** (-0.5)
 EXP_LIMIT = 64.0
 PAIR = 2
+WINDOW = 3
 VMEM_LIMIT = 28 * 1024 * 1024
 FIRST_VMEM_LIMIT = 60 * 1024 * 1024
 
@@ -474,9 +475,7 @@
             return [span_len]
         if distance == 1:
             return [2 * span_len, (per_pair - 2) * span_len]
-        if distance % 2:
-            return [span_len] * (per_pair - 2) + [span_len + half, half]
-        return [span_len + half] + [span_len] * (per_pair - 2) + [half]
+        return [span_len] * (per_pair - 1) + [half] * 2
 
     def pieces_of(first, length):
         pieces = []
@@ -492,88 +491,87 @@
         first = 0
         for number, length in enumerate(cuts(d)):
             if length:
-                messages[d, number] = (d, False, pieces_of(first, length))
+                messages[d, number] = (d, not number, pieces_of(first, length))
             first += length
+    outbox, _ = packed([messages[d, 0] for d in away])
+    coming = [exchange(piece, d, "store", "spans0_") for piece, d in zip(outbox, away)]
     count = 1 + max(number for _, number in messages)
-    soon = [(d, 0) for d in away if d > 1]
-    later = [key for number in range(count) for d in away for key in [(d, number)] if key in messages]
-    later = [key for key in later if key not in soon]
-    outbox, _ = packed([(d, True, []) for d in away] + [messages[key] for key in soon])
-    hidden_in = {d: exchange(piece, d, "store", "columns") for d, piece in zip(away, outbox)}
-    coming = [exchange(piece, key[0], "store", "spans0_") for key, piece in zip(soon, outbox[len(away) :])]
+    later = [(d, number) for number in range(1, count) for d in away if (d, number) in messages]
     (hidden_own, *outbox), table = packed(
         [(0, True, [])] + [messages[key] for key in later], recompute_rows[0]
     )
     outbox = dict(zip(later, outbox))
-    coming.append(exchange(after(outbox[1, 0], hidden_in[1]), 1, "store", "spans0_"))
 
     def behind(pieces, state):
         return [after(piece, state[0]) for piece in pieces]
 
-    def block(keys, state, own=(), with_question=False, fresh=None, last=False):
-        parts = [(span, 0, span_len, 0, 0) for span in own]
+    def block(keys, state, fresh=None, last=False):
+        parts = []
         for source, (d, number) in enumerate(keys):
             offset = 0
             for span, start, rows in messages[d, number][2]:
                 parts.append((d * per_pair + span, start, rows, source, offset))
                 offset += rows
+        if not keys:
+            parts = [(span, 0, span_len, 0, 0) for span in range(per_pair)]
         return attend(
             table, query_rows, question, parts, [arrived[key] for key in keys],
-            key_value_store if own else None, fresh, state, with_question, last,
+            None if keys else key_value_store, fresh, state, not keys, last,
         )
 
     def recomputed():
-        blocks = [hidden_own] + [hidden_in[d] for d in away[::-1]]
+        blocks = [hidden_own]
+        for d in away[::-1]:
+            piece = arrived[d, 0]
+            blocks.append(piece[piece.shape[0] - hidden_own.shape[0] :])
         distances = [0]
         for step, bit in enumerate(reversed(range(n_tensor.bit_length() - 1))):
             distances += [distance ^ (1 << bit) for distance in distances]
             gathered = jnp.concatenate(blocks, axis=0)
-            if not step:
-                yield gathered
             blocks = [gathered, exchange(gathered, 1 << bit, "tensor", "hidden")]
         partial, sent = project(blocks, kv_weight, n_store, shard_rows, distances)
         bits = n_store.bit_length() - 1
         for bit in range(bits):
             if bit:
                 sent = partial[1::2].astype(jnp.bfloat16)
-            if bit == 1:
-                yield sent
+            yield sent
             other = exchange(sent, 1 << bit, "store", "partial")
             if bit + 1 < bits:
                 partial = partial[0::2] + other.astype(jnp.float32)
         yield partial[0], other[0]
 
     arrived = {}
+    state, _ = block([], None)
+    arrived.update(zip([(d, 0) for d in away], behind(coming, state)))
     steps = recomputed()
-    middle = (per_pair + 1) // 2
-    state, _ = block([], None, range(middle), True)
-    state = [after(state[0], next(steps)), *state[1:]]
-    if per_pair > 1:
-        state, _ = block([], state, range(middle, per_pair))
-    arrived.update(zip(soon + [(1, 0)], behind(coming, state)))
-    fresh = rows = None
+    turns = [(d, number) for number in range(count) for d in away if d > 1]
+
+    def leave(key):
+        piece, (d, number) = outbox[key], key
+        turn = turns.index(key if d > 1 else (away[0], number)) - WINDOW
+        if turn >= 0:
+            piece = after(piece, arrived[turns[turn]])
+        return exchange(piece, d, "store", "spans%d_" % number)
+
     for number in range(1, count):
         keys = [key for key in later if key[1] == number]
-        coming = [
-            exchange(after(outbox[key], arrived[key[0], number - 1]), key[0], "store", "spans%d_" % number)
-            for key in keys
-        ]
-        if number == 2:
+        coming = [leave(key) for key in keys]
+        here = [(d, number - 1) for d in away if (d, number - 1) in arrived]
+        if 2 <= number < n_store.bit_length() + 1:
             state = [after(state[0], next(steps)), *state[1:]]
-        if number == count - 1:
-            *_, fresh = steps
-        here = [(d, number - 1) for d in away if (d, number - 1) in arrived]
-        state, rows = block(here, state, fresh=fresh)
+        state, _ = block(here, state)
         arrived.update(zip(keys, behind(coming, state)))
+
     keys = [(d, count - 1) for d in away[::-1] if (d, count - 1) in arrived]
     size = 6
     batches = [keys[i : i + size] for i in range(0, len(keys), size)]
+    *_, fresh = steps
     for i, keys in enumerate(batches):
-        joins, last = rows is None, i == len(batches) - 1
-        if joins:
-            *_, fresh = steps
-        state, now = block(keys, state, fresh=fresh if joins else None, last=last)
-        rows = now if joins else rows
+        last = i == len(batches) - 1
+        if i:
+            arrived.update(zip(keys, behind([arrived[key] for key in keys], state)))
+            fresh = behind(fresh, state)
+        state, rows = block(keys, state, fresh if last else None, last)
     return (state[0][None], rows.reshape(1, span_count, recomp, kv_cols))
 
 

time: 130 us -> 124 us (0.954)
  starting transfers between devices: 31.3 us -> 22.8 us
  waiting for transfers between devices: 51.8 us -> 53.2 us
    ppermute x17 -> x16, starting transfers between devices: 31.3 us -> 22.8 us  [exchange(): return lax.ppermute(piece, axis, [(i, i ^ distance) for i in range(size)])]
    ppermute x17 -> x16, waiting for transfers between devices: 51.8 us -> 53.2 us  [exchange(): return lax.ppermute(piece, axis, [(i, i ^ distance) for i in range(size)])]
  transfers between devices with their start and end apart: 17 -> 16, of which waited for: 5 -> 7; matrix products, arithmetic and copies ran while one was open for 0% -> 1% of each run, Pallas kernels for 28% -> 29%
where the time goes in v8:
time: 124 us; the launch traced here: 123 us
  waiting for transfers between devices  53.2 us (43%)
  Pallas kernels  43.8 us (35%)
  starting transfers between devices  22.8 us (18%)
  local copies, waits for them, and re-layouts  2.51 us (2%)
    ppermute x16, waiting for transfers between devices, exchange(): return lax.ppermute(piece, axis, [(i, i ^ distance) for i in range(size)])  53.2 us
    pallas_call x6, Pallas kernels, attend(): pl.pallas_call(functools.partial(attend_kernel, tuple(parts), len(pieces)...  35.3 us
    ppermute x16, starting transfers between devices, exchange(): return lax.ppermute(piece, axis, [(i, i ^ distance) for i in range(size)])  22.8 us
    pallas_call x2, Pallas kernels, pack(): pl.pallas_call(functools.partial(pack_kernel, messages, shard, with_table...  7.27 us
  transfers between devices with their start and end apart: 16, of which 7 were waited for; matrix products, arithmetic and copies ran while one was open for 1% of the time, Pallas kernels for 29%

profile of v8, /device:TPU:0, one launch (start us, length us, event | category | flops | bytes accessed | tf_op | source)
XLA Modules:
  0.0 123.5 jit_solution(12402890973484007413)
XLA Ops:
  0.7 3.6 %pack_spans.3 = (bf16[384,512]{1,0:T(8,128)(2,1)}, bf16[384,512]{1,0:T(8,128)(2,1)}, bf16[640,512]{1,0:T(8,128)(2,1)}) custom-call(s32[32]{0:T(128)} %refs_0_.3, s32[4,16]{1,0:T(4,128)} %refs_1_.3, bf16[8,256,512]{2,1,0:T(8,128)(2,1)} %refs_3_.1, bf16[128,8192]{1,0:T(8,128)(2,1)} %bitcast.9), custom_call_target="tpu_custom_call" | custom-call | tf_op jit(solution)/shard_map/pack_spans/pallas_call | solution.py:132
  4.3 5.1 %collective-permute-start = (bf16[384,512]{1,0:T(8,128)(2,1)}, bf16[384,512]{1,0:T(8,128)(2,1)S(1)}, u32[]{:S(2)}, u32[]{:S(2)}) collective-permute-start(bf16[384,512]{1,0:T(8,128)(2,1)} %get-tuple-element.60), channel_id=1, source_target_pairs={{0,12},{4,8},{8,4},{12,0},{1,13},{5,9},{9,5},{13,1},{2,14},{6,10},... | collective-permute-start | bytes 1179656 | tf_op jit(solution)/shard_map/spans0_3/ppermute | solution.py:460
  10.8 1.6 %copy-done.1 = bf16[8,256,512]{2,1,0:T(8,128)(2,1)S(1)} copy-done((bf16[8,256,512]{2,1,0:T(8,128)(2,1)S(1)}, bf16[8,256,512]{2,1,0:T(8,128)(2,1)}, u32[]{:S(2)}) %copy-start.1) | copy-done | bytes 2097176
  12.4 3.7 %pack_spans.2 = (bf16[128,512]{1,0:T(8,128)(2,1)S(1)}, bf16[256,512]{1,0:T(8,128)(2,1)S(1)}, bf16[256,512]{1,0:T(8,128)(2,1)S(1)}, bf16[512,512]{1,0:T(8,128)(2,...) custom-call(s32[32]{0:T(128)S(1)} %copy-done.5, ...), custom_call_target="tpu_custom_call" | custom-call | tf_op jit(solution)/shard_map/pack_spans/pallas_call | solution.py:132
  16.1 8.7 %attend_spans.6 = (f32[4096,128]{1,0:T(8,128)S(1)}, f32[4096,128]{1,0:T(8,128)S(1)}, f32[4096,128]{1,0:T(8,128)S(1)}) custom-call(s32[16,10]{1,0:T(8,128)S(1)} %get-tuple-element.56.refs_0_, bf16[256,2048]{1,0:T(8,128)(2,1)S(1)} %bitcast.11, bf16[256,512]{1,0:T(8,128)(2,1)S(1)} %bitcast.17, bf16[8,256,512]{2,1,0:T(8,128)(2,1)S(1)} %copy-done.2), custom_call_target="tpu_custom_call" | custom-call | flops 42949672960 | tf_op jit(solution)/shard_map/attend_spans/pallas_call | solution.py:413
  24.8 18.3 %collective-permute-done.2.refs_4_ = bf16[384,512]{1,0:T(8,128)(2,1)S(1)} collective-permute-done((bf16[384,512]{1,0:T(8,128)(2,1)}, bf16[384,512]{1,0:T(8,128)(2,1)S(1)}, u32[]{:S(2)}, u32[]{:S(2)}) %collective-permute-start.2) | collective-permute-done | bytes 393248 | tf_op jit(solution)/shard_map/spans0_2/ppermute | solution.py:460
  43.3 1.6 %collective-permute-start.8 = (bf16[512,512]{1,0:T(8,128)(2,1)S(1)}, bf16[512,512]{1,0:T(8,128)(2,1)S(1)}, u32[]{:S(2)}, u32[]{:S(2)}) collective-permute-start(bf16[512,512]{1,0:T(8,128)(2,1)S(1)} %pad_maximum_fusion), channel_id=1, source_target_pairs={{0,2},{1,3},{2,0},{3,1},{4,6},{5,7},{6,4},{7,5},{8,10},{9,11},{10,... | collective-permute-start | bytes 1572872 | tf_op jit(solution)/shard_map/hidden2/ppermute | solution.py:460
  44.8 2.5 %collective-permute-start.6 = (bf16[256,512]{1,0:T(8,128)(2,1)S(1)}, bf16[256,512]{1,0:T(8,128)(2,1)S(1)}, u32[]{:S(2)}, u32[]{:S(2)}) collective-permute-start(bf16[256,512]{1,0:T(8,128)(2,1)S(1)} %get-tuple-element.75), channel_id=1, source_target_pairs={{0,12},{4,8},{8,4},{12,0},{1,13},{5,9},{9,5},{13,1},{2,14},{6,10},... | collective-permute-start | bytes 786440 | tf_op jit(solution)/shard_map/spans1_3/ppermute | solution.py:460
  47.3 1.9 %collective-permute-start.1 = (bf16[256,512]{1,0:T(8,128)(2,1)S(1)}, bf16[256,512]{1,0:T(8,128)(2,1)S(1)}, u32[]{:S(2)}, u32[]{:S(2)}) collective-permute-start(bf16[256,512]{1,0:T(8,128)(2,1)S(1)} %get-tuple-element.63), channel_id=1, source_target_pairs={{0,8},{4,12},{8,0},{12,4},{1,9},{5,13},{9,1},{13,5},{2,10},{6,14},... | collective-permute-start | bytes 786440 | tf_op jit(solution)/shard_map/spans1_2/ppermute | solution.py:460
  49.2 2.5 %collective-permute-start.5 = (bf16[256,512]{1,0:T(8,128)(2,1)S(1)}, bf16[256,512]{1,0:T(8,128)(2,1)S(1)}, u32[]{:S(2)}, u32[]{:S(2)}) collective-permute-start(bf16[256,512]{1,0:T(8,128)(2,1)S(1)} %get-tuple-element.74), channel_id=1, source_target_pairs={{0,12},{4,8},{8,4},{12,0},{1,13},{5,9},{9,5},{13,1},{2,14},{6,10},... | collective-permute-start | bytes 786440 | tf_op jit(solution)/shard_map/spans2_3/ppermute | solution.py:460
  51.7 4.6 %collective-permute-done.8 = bf16[512,512]{1,0:T(8,128)(2,1)S(1)} collective-permute-done((bf16[512,512]{1,0:T(8,128)(2,1)S(1)}, bf16[512,512]{1,0:T(8,128)(2,1)S(1)}, u32[]{:S(2)}, u32[]{:S(2)}) %collective-permute-start.8) | collective-permute-done | bytes 524320 | tf_op jit(solution)/shard_map/hidden2/ppermute | solution.py:460
  56.4 7.7 %attend_spans.7 = (f32[4096,128]{1,0:T(8,128)S(1)}, f32[4096,128]{1,0:T(8,128)S(1)}, f32[4096,128]{1,0:T(8,128)S(1)}) custom-call(s32[16,10]{1,0:T(8,128)S(1)} %get-tuple-element.56.refs_0_, bf16[256,2048]{1,0:T(8,128)(2,1)S(1)} %bitcast.12, bf16[256,512]{1,0:T(8,128)(2,1)S(1)} %bitcast.18, bf16[384,512]{1,0:T(8,128)(2,1)S(1)} %collective-permute-done.refs_3_, ...), custom_call_target="tpu_custom_call" | custom-call | flops 34359738368 | tf_op jit(solution)/shard_map/attend_spans/pallas_call | solution.py:413
  64.1 6.8 %collective-permute-done.1.refs_4_ = bf16[256,512]{1,0:T(8,128)(2,1)S(1)} collective-permute-done((bf16[256,512]{1,0:T(8,128)(2,1)S(1)}, bf16[256,512]{1,0:T(8,128)(2,1)S(1)}, u32[]{:S(2)}, u32[]{:S(2)}) %collective-permute-start.1) | collective-permute-done | bytes 262176 | tf_op jit(solution)/shard_map/spans1_2/ppermute | solution.py:460
  70.9 1.4 %collective-permute-start.4 = (bf16[128,512]{1,0:T(8,128)(2,1)S(1)}, bf16[128,512]{1,0:T(8,128)(2,1)S(1)}, u32[]{:S(2)}, u32[]{:S(2)}) collective-permute-start(bf16[128,512]{1,0:T(8,128)(2,1)S(1)} %get-tuple-element.72), channel_id=1, source_target_pairs={{0,12},{4,8},{8,4},{12,0},{1,13},{5,9},{9,5},{13,1},{2,14},{6,10},... | collective-permute-start | bytes 393224 | tf_op jit(solution)/shard_map/spans3_3/ppermute | solution.py:460
  72.7 2.2 %collective-permute-start.10 = (bf16[256,512]{1,0:T(8,128)(2,1)S(1)}, bf16[256,512]{1,0:T(8,128)(2,1)S(1)}, u32[]{:S(2)}, u32[]{:S(2)}) collective-permute-start(bf16[256,512]{1,0:T(8,128)(2,1)S(1)} %get-tuple-element.87), channel_id=1, source_target_pairs={{0,8},{4,12},{8,0},{12,4},{1,9},{5,13},{9,1},{13,5},{2,10},{6,14},... | collective-permute-start | bytes 786440 | tf_op jit(solution)/shard_map/spans2_2/ppermute | solution.py:460
  76.7 7.5 %attend_spans.8 = (f32[4096,128]{1,0:T(8,128)S(1)}, f32[4096,128]{1,0:T(8,128)S(1)}, f32[4096,128]{1,0:T(8,128)S(1)}) custom-call(s32[16,10]{1,0:T(8,128)S(1)} %get-tuple-element.56.refs_0_, bf16[256,2048]{1,0:T(8,128)(2,1)S(1)} %bitcast.13, bf16[256,512]{1,0:T(8,128)(2,1)S(1)} %bitcast.19, bf16[256,512]{1,0:T(8,128)(2,1)S(1)} %collective-permute-done.6.refs_3_, ...), custom_call_target="tpu_custom_call" | custom-call | flops 34359738368 | tf_op jit(solution)/shard_map/attend_spans/pallas_call | solution.py:413
  84.2 11.8 %collective-permute-done.10.refs_4_ = bf16[256,512]{1,0:T(8,128)(2,1)S(1)} collective-permute-done((bf16[256,512]{1,0:T(8,128)(2,1)S(1)}, bf16[256,512]{1,0:T(8,128)(2,1)S(1)}, u32[]{:S(2)}, u32[]{:S(2)}) %collective-permute-start.10) | collective-permute-done | bytes 262176 | tf_op jit(solution)/shard_map/spans2_2/ppermute | solution.py:460
  96.0 1.4 %collective-permute-start.14 = (bf16[128,512]{1,0:T(8,128)(2,1)S(1)}, bf16[128,512]{1,0:T(8,128)(2,1)S(1)}, u32[]{:S(2)}, u32[]{:S(2)}) collective-permute-start(bf16[128,512]{1,0:T(8,128)(2,1)S(1)} %get-tuple-element.104), channel_id=1, source_target_pairs={{0,12},{4,8},{8,4},{12,0},{1,13},{5,9},{9,5},{13,1},{2,14},{6,10},... | collective-permute-start | bytes 393224 | tf_op jit(solution)/shard_map/spans4_3/ppermute | solution.py:460
  97.5 2.1 %collective-permute-start.15 = (bf16[1,128,512]{2,1,0:T(8,128)(2,1)S(1)}, bf16[1,128,512]{2,1,0:T(8,128)(2,1)S(1)}, u32[]{:S(2)}, u32[]{:S(2)}) collective-permute-start(bf16[1,128,512]{2,1,0:T(8,128)(2,1)S(1)} %slice.34), channel_id=1, source_target_pairs={{0,8},{4,12},{8,0},{12,4},{1,9},{5,13},{9,1},{13,5},{2,10},{6,14},... | collective-permute-start | bytes 393224 | tf_op jit(solution)/shard_map/partial2/ppermute | solution.py:460
  99.6 4.4 %attend_spans.9 = (f32[4096,128]{1,0:T(8,128)S(1)}, f32[4096,128]{1,0:T(8,128)S(1)}, f32[4096,128]{1,0:T(8,128)S(1)}) custom-call(s32[16,10]{1,0:T(8,128)S(1)} %get-tuple-element.56.refs_0_, bf16[256,2048]{1,0:T(8,128)(2,1)S(1)} %bitcast.14, bf16[256,512]{1,0:T(8,128)(2,1)S(1)} %bitcast.20, bf16[256,512]{1,0:T(8,128)(2,1)S(1)} %collective-permute-done.5.refs_3_, ...), custom_call_target="tpu_custom_call" | custom-call | flops 17179869184 | tf_op jit(solution)/shard_map/attend_spans/pallas_call | solution.py:413
  105.0 5.9 %collective-permute-done.13.refs_4_ = bf16[128,512]{1,0:T(8,128)(2,1)S(1)} collective-permute-done((bf16[128,512]{1,0:T(8,128)(2,1)S(1)}, bf16[128,512]{1,0:T(8,128)(2,1)S(1)}, u32[]{:S(2)}, u32[]{:S(2)}) %collective-permute-start.13) | collective-permute-done | bytes 131104 | tf_op jit(solution)/shard_map/spans3_2/ppermute | solution.py:460
  110.9 2.7 %attend_spans.10 = (f32[4096,128]{1,0:T(8,128)S(1)}, f32[4096,128]{1,0:T(8,128)S(1)}, f32[4096,128]{1,0:T(8,128)S(1)}) custom-call(s32[16,10]{1,0:T(8,128)S(1)} %get-tuple-element.56.refs_0_, bf16[256,2048]{1,0:T(8,128)(2,1)S(1)} %bitcast.15, bf16[256,512]{1,0:T(8,128)(2,1)S(1)} %bitcast.21, bf16[128,512]{1,0:T(8,128)(2,1)S(1)} %collective-permute-done.4.refs_3_, ...), custom_call_target="tpu_custom_call" | custom-call | flops 8589934592 | tf_op jit(solution)/shard_map/attend_spans/pallas_call | solution.py:413
  113.6 5.3 %collective-permute-done.12.refs_3_ = bf16[128,512]{1,0:T(8,128)(2,1)S(1)} collective-permute-done((bf16[128,512]{1,0:T(8,128)(2,1)S(1)}, bf16[128,512]{1,0:T(8,128)(2,1)S(1)}, u32[]{:S(2)}, u32[]{:S(2)}) %collective-permute-start.12) | collective-permute-done | bytes 131104 | tf_op jit(solution)/shard_map/spans4_2/ppermute | solution.py:460
  118.9 4.4 %attend_spans.11 = (bf16[256,2048]{1,0:T(8,128)(2,1)}, bf16[128,512]{1,0:T(8,128)(2,1)}) custom-call(s32[16,10]{1,0:T(8,128)S(1)} %get-tuple-element.56.refs_0_, bf16[256,2048]{1,0:T(8,128)(2,1)S(1)} %bitcast.16, bf16[256,512]{1,0:T(8,128)(2,1)S(1)} %bitcast.22, bf16[128,512]{1,0:T(8,128)(2,1)S(1)} %collective-permute-done.12.refs_3_, ...), custom_call_target="tpu_custom_call" | custom-call | flops 12884901888 | tf_op jit(solution)/shard_map/attend_spans/pallas_call | solution.py:413
  (43 shorter events, 4.9 us)
Async XLA Ops:
  0.6 10.1 %copy-start = (bf16[1,16,8,8192]{3,2,1,0:T(8,128)(2,1)S(1)}, bf16[1,16,8,8192]{3,2,1,0:T(8,128)(2,1)}, u32[]{:S(2)}) copy-start(bf16[1,16,8,8192]{3,2,1,0:T(8,128)(2,1)} %param.14) | copy-start | bytes 6291460
  0.6 10.1 %copy-start.4 = (s32[4,16]{1,0:T(4,128)S(1)}, s32[4,16]{1,0:T(4,128)}, u32[]{:S(2)}) copy-start(s32[4,16]{1,0:T(4,128)} %refs_1_.3) | copy-start | bytes 772
  0.7 10.1 %copy-start.5 = (s32[32]{0:T(128)S(1)}, s32[32]{0:T(128)}, u32[]{:S(2)}) copy-start(s32[32]{0:T(128)} %refs_0_.3) | copy-start | bytes 388
  4.3 20.5 %collective-permute-start = (bf16[384,512]{1,0:T(8,128)(2,1)}, bf16[384,512]{1,0:T(8,128)(2,1)S(1)}, u32[]{:S(2)}, u32[]{:S(2)}) collective-permute-start(bf16[384,512]{1,0:T(8,128)(2,1)} %get-tuple-element.60), channel_id=1, source_target_pairs={{0,12},{4,8},{8,4},{12,0},{1,13},{5,9},{9,5},{13,1},{2,14},{6,10},... | collective-permute-start | bytes 1179656 | tf_op jit(solution)/shard_map/spans0_3/ppermute | solution.py:460
  9.4 33.8 %collective-permute-start.2 = (bf16[384,512]{1,0:T(8,128)(2,1)}, bf16[384,512]{1,0:T(8,128)(2,1)S(1)}, u32[]{:S(2)}, u32[]{:S(2)}) collective-permute-start(bf16[384,512]{1,0:T(8,128)(2,1)} %get-tuple-element.64), channel_id=1, source_target_pairs={{0,8},{4,12},{8,0},{12,4},{1,9},{5,13},{9,1},{13,5},{2,10},{6,14},... | collective-permute-start | bytes 1179656 | tf_op jit(solution)/shard_map/spans0_2/ppermute | solution.py:460
  9.4 33.8 %collective-permute-start.3 = (bf16[640,512]{1,0:T(8,128)(2,1)}, bf16[640,512]{1,0:T(8,128)(2,1)S(1)}, u32[]{:S(2)}, u32[]{:S(2)}) collective-permute-start(bf16[640,512]{1,0:T(8,128)(2,1)} %get-tuple-element.66), channel_id=1, source_target_pairs={{0,4},{4,0},{8,12},{12,8},{1,5},{5,1},{9,13},{13,9},{2,6},{6,2},{1... | collective-permute-start | bytes 1966088 | tf_op jit(solution)/shard_map/spans0_1/ppermute | solution.py:460
  10.8 1.6 %copy-start.1 = (bf16[8,256,512]{2,1,0:T(8,128)(2,1)S(1)}, bf16[8,256,512]{2,1,0:T(8,128)(2,1)}, u32[]{:S(2)}) copy-start(bf16[8,256,512]{2,1,0:T(8,128)(2,1)} %refs_3_.1) | copy-start | bytes 6291460
  12.4 3.7 %copy-start.2 = (bf16[8,256,512]{2,1,0:T(8,128)(2,1)S(1)}, bf16[8,256,512]{2,1,0:T(8,128)(2,1)}, u32[]{:S(2)}) copy-start(bf16[8,256,512]{2,1,0:T(8,128)(2,1)} %refs_3_.1) | copy-start | bytes 6291460
  12.4 3.7 %copy-start.6 = (bf16[1,256,2048]{2,1,0:T(8,128)(2,1)S(1)}, bf16[1,256,2048]{2,1,0:T(8,128)(2,1)}, u32[]{:S(2)}) copy-start(bf16[1,256,2048]{2,1,0:T(8,128)(2,1)} %param.8) | copy-start | bytes 3145732
  12.4 3.7 %copy-start.7 = (bf16[1,256,512]{2,1,0:T(8,128)(2,1)S(1)}, bf16[1,256,512]{2,1,0:T(8,128)(2,1)}, u32[]{:S(2)}) copy-start(bf16[1,256,512]{2,1,0:T(8,128)(2,1)} %param.9) | copy-start | bytes 786436
  43.3 13.0 %collective-permute-start.8 = (bf16[512,512]{1,0:T(8,128)(2,1)S(1)}, bf16[512,512]{1,0:T(8,128)(2,1)S(1)}, u32[]{:S(2)}, u32[]{:S(2)}) collective-permute-start(bf16[512,512]{1,0:T(8,128)(2,1)S(1)} %pad_maximum_fusion), channel_id=1, source_target_pairs={{0,2},{1,3},{2,0},{3,1},{4,6},{5,7},{6,4},{7,5},{8,10},{9,11},{10,... | collective-permute-start | bytes 1572872 | tf_op jit(solution)/shard_map/hidden2/ppermute | solution.py:460
  44.8 27.5 %collective-permute-start.6 = (bf16[256,512]{1,0:T(8,128)(2,1)S(1)}, bf16[256,512]{1,0:T(8,128)(2,1)S(1)}, u32[]{:S(2)}, u32[]{:S(2)}) collective-permute-start(bf16[256,512]{1,0:T(8,128)(2,1)S(1)} %get-tuple-element.75), channel_id=1, source_target_pairs={{0,12},{4,8},{8,4},{12,0},{1,13},{5,9},{9,5},{13,1},{2,14},{6,10},... | collective-permute-start | bytes 786440 | tf_op jit(solution)/shard_map/spans1_3/ppermute | solution.py:460
  47.3 25.4 %collective-permute-start.7 = (bf16[512,512]{1,0:T(8,128)(2,1)S(1)}, bf16[512,512]{1,0:T(8,128)(2,1)S(1)}, u32[]{:S(2)}, u32[]{:S(2)}) collective-permute-start(bf16[512,512]{1,0:T(8,128)(2,1)S(1)} %get-tuple-element.77), channel_id=1, source_target_pairs={{0,4},{4,0},{8,12},{12,8},{1,5},{5,1},{9,13},{13,9},{2,6},{6,2},{1... | collective-permute-start | bytes 1572872 | tf_op jit(solution)/shard_map/spans1_1/ppermute | solution.py:460
  47.3 23.7 %collective-permute-start.1 = (bf16[256,512]{1,0:T(8,128)(2,1)S(1)}, bf16[256,512]{1,0:T(8,128)(2,1)S(1)}, u32[]{:S(2)}, u32[]{:S(2)}) collective-permute-start(bf16[256,512]{1,0:T(8,128)(2,1)S(1)} %get-tuple-element.63), channel_id=1, source_target_pairs={{0,8},{4,12},{8,0},{12,4},{1,9},{5,13},{9,1},{13,5},{2,10},{6,14},... | collective-permute-start | bytes 786440 | tf_op jit(solution)/shard_map/spans1_2/ppermute | solution.py:460
  49.2 35.0 %collective-permute-start.5 = (bf16[256,512]{1,0:T(8,128)(2,1)S(1)}, bf16[256,512]{1,0:T(8,128)(2,1)S(1)}, u32[]{:S(2)}, u32[]{:S(2)}) collective-permute-start(bf16[256,512]{1,0:T(8,128)(2,1)S(1)} %get-tuple-element.74), channel_id=1, source_target_pairs={{0,12},{4,8},{8,4},{12,0},{1,13},{5,9},{9,5},{13,1},{2,14},{6,10},... | collective-permute-start | bytes 786440 | tf_op jit(solution)/shard_map/spans2_3/ppermute | solution.py:460
  56.3 18.5 %collective-permute-start.9 = (bf16[1024,512]{1,0:T(8,128)(2,1)S(1)}, bf16[1024,512]{1,0:T(8,128)(2,1)S(1)}, u32[]{:S(2)}, u32[]{:S(2)}) collective-permute-start(bf16[1024,512]{1,0:T(8,128)(2,1)S(1)} %constant_dynamic-update-slice_fusion.refs_0_), channel_id=1, source_target_pairs={{0,1},{1,0},{2,3},{3,2},{4,5},{5,4},{6,7},{7,6},{8,9},{9,8},{10,11... | collective-permute-start | bytes 3145736 | tf_op jit(solution)/shard_map/hidden1/ppermute | solution.py:460
  56.4 18.5 %copy-start.3 = (bf16[2048,512]{1,0:T(8,128)(2,1)S(1)}, bf16[2048,512]{1,0:T(8,128)(2,1)}, u32[]{:S(2)}) copy-start(bf16[2048,512]{1,0:T(8,128)(2,1)} %refs_2_.5) | copy-start | bytes 6291460
  70.9 33.1 %collective-permute-start.4 = (bf16[128,512]{1,0:T(8,128)(2,1)S(1)}, bf16[128,512]{1,0:T(8,128)(2,1)S(1)}, u32[]{:S(2)}, u32[]{:S(2)}) collective-permute-start(bf16[128,512]{1,0:T(8,128)(2,1)S(1)} %get-tuple-element.72), channel_id=1, source_target_pairs={{0,12},{4,8},{8,4},{12,0},{1,13},{5,9},{9,5},{13,1},{2,14},{6,10},... | collective-permute-start | bytes 393224 | tf_op jit(solution)/shard_map/spans3_3/ppermute | solution.py:460
  72.7 23.3 %collective-permute-start.10 = (bf16[256,512]{1,0:T(8,128)(2,1)S(1)}, bf16[256,512]{1,0:T(8,128)(2,1)S(1)}, u32[]{:S(2)}, u32[]{:S(2)}) collective-permute-start(bf16[256,512]{1,0:T(8,128)(2,1)S(1)} %get-tuple-element.87), channel_id=1, source_target_pairs={{0,8},{4,12},{8,0},{12,4},{1,9},{5,13},{9,1},{13,5},{2,10},{6,14},... | collective-permute-start | bytes 786440 | tf_op jit(solution)/shard_map/spans2_2/ppermute | solution.py:460
  76.1 21.3 %collective-permute-start.11 = (bf16[2,128,512]{2,1,0:T(8,128)(2,1)S(1)}, bf16[2,128,512]{2,1,0:T(8,128)(2,1)S(1)}, u32[]{:S(2)}, u32[]{:S(2)}) collective-permute-start(bf16[2,128,512]{2,1,0:T(8,128)(2,1)S(1)} %get-tuple-element.80), channel_id=1, source_target_pairs={{0,4},{4,0},{8,12},{12,8},{1,5},{5,1},{9,13},{13,9},{2,6},{6,2},{1... | collective-permute-start | bytes 786440 | tf_op jit(solution)/shard_map/partial1/ppermute | solution.py:460
  96.0 14.9 %collective-permute-start.13 = (bf16[128,512]{1,0:T(8,128)(2,1)S(1)}, bf16[128,512]{1,0:T(8,128)(2,1)S(1)}, u32[]{:S(2)}, u32[]{:S(2)}) collective-permute-start(bf16[128,512]{1,0:T(8,128)(2,1)S(1)} %get-tuple-element.97), channel_id=1, source_target_pairs={{0,8},{4,12},{8,0},{12,4},{1,9},{5,13},{9,1},{13,5},{2,10},{6,14},... | collective-permute-start | bytes 393224 | tf_op jit(solution)/shard_map/spans3_2/ppermute | solution.py:460
  96.0 17.6 %collective-permute-start.14 = (bf16[128,512]{1,0:T(8,128)(2,1)S(1)}, bf16[128,512]{1,0:T(8,128)(2,1)S(1)}, u32[]{:S(2)}, u32[]{:S(2)}) collective-permute-start(bf16[128,512]{1,0:T(8,128)(2,1)S(1)} %get-tuple-element.104), channel_id=1, source_target_pairs={{0,12},{4,8},{8,4},{12,0},{1,13},{5,9},{9,5},{13,1},{2,14},{6,10},... | collective-permute-start | bytes 393224 | tf_op jit(solution)/shard_map/spans4_3/ppermute | solution.py:460
  97.5 21.4 %collective-permute-start.15 = (bf16[1,128,512]{2,1,0:T(8,128)(2,1)S(1)}, bf16[1,128,512]{2,1,0:T(8,128)(2,1)S(1)}, u32[]{:S(2)}, u32[]{:S(2)}) collective-permute-start(bf16[1,128,512]{2,1,0:T(8,128)(2,1)S(1)} %slice.34), channel_id=1, source_target_pairs={{0,8},{4,12},{8,0},{12,4},{1,9},{5,13},{9,1},{13,5},{2,10},{6,14},... | collective-permute-start | bytes 393224 | tf_op jit(solution)/shard_map/partial2/ppermute | solution.py:460
  104.0 14.9 %collective-permute-start.12 = (bf16[128,512]{1,0:T(8,128)(2,1)S(1)}, bf16[128,512]{1,0:T(8,128)(2,1)S(1)}, u32[]{:S(2)}, u32[]{:S(2)}) collective-permute-start(bf16[128,512]{1,0:T(8,128)(2,1)S(1)} %get-tuple-element.95), channel_id=1, source_target_pairs={{0,8},{4,12},{8,0},{12,4},{1,9},{5,13},{9,1},{13,5},{2,10},{6,14},... | collective-permute-start | bytes 393224 | tf_op jit(solution)/shard_map/spans4_2/ppermute | solution.py:460

commit v9 on v8

--- a/solution.py
+++ b/solution.py
@@ -474,8 +474,8 @@
         if per_pair == 1:
             return [span_len]
         if distance == 1:
-            return [2 * span_len, (per_pair - 2) * span_len]
-        return [span_len] * (per_pair - 1) + [half] * 2
+            return [2 * span_len + half, 0, 0, (per_pair - 3) * span_len + half]
+        return [span_len] * (per_pair - 1) + [span_len - half // 2, half // 2]
 
     def pieces_of(first, length):
         pieces = []
@@ -540,7 +540,7 @@
                 partial = partial[0::2] + other.astype(jnp.float32)
         yield partial[0], other[0]
 
-    arrived = {}
+    arrived, fresh, rows = {}, None, None
     state, _ = block([], None)
     arrived.update(zip([(d, 0) for d in away], behind(coming, state)))
     steps = recomputed()
@@ -548,7 +548,9 @@
 
     def leave(key):
         piece, (d, number) = outbox[key], key
-        turn = turns.index(key if d > 1 else (away[0], number)) - WINDOW
+        turn = turns.index(key if d > 1 else (away[-2], number)) - WINDOW
+        if d == 1:
+            turn += 1
         if turn >= 0:
             piece = after(piece, arrived[turns[turn]])
         return exchange(piece, d, "store", "spans%d_" % number)
@@ -559,19 +561,20 @@
         here = [(d, number - 1) for d in away if (d, number - 1) in arrived]
         if 2 <= number < n_store.bit_length() + 1:
             state = [after(state[0], next(steps)), *state[1:]]
-        state, _ = block(here, state)
+        if number == count - 1:
+            *_, fresh = steps
+        state, rows = block(here, state, fresh)
         arrived.update(zip(keys, behind(coming, state)))
 
     keys = [(d, count - 1) for d in away[::-1] if (d, count - 1) in arrived]
     size = 6
     batches = [keys[i : i + size] for i in range(0, len(keys), size)]
-    *_, fresh = steps
     for i, keys in enumerate(batches):
-        last = i == len(batches) - 1
-        if i:
-            arrived.update(zip(keys, behind([arrived[key] for key in keys], state)))
-            fresh = behind(fresh, state)
-        state, rows = block(keys, state, fresh if last else None, last)
+        joins, last = rows is None, i == len(batches) - 1
+        if joins:
+            *_, fresh = steps
+        state, now = block(keys, state, fresh if joins else None, last)
+        rows = now if joins else rows
     return (state[0][None], rows.reshape(1, span_count, recomp, kv_cols))
 
 

time: 124 us -> 134 us (1.081)
  waiting for transfers between devices: 53.2 us -> 60.3 us
  Pallas kernels: 43.8 us -> 45.8 us
    ppermute x16, waiting for transfers between devices: 53.2 us -> 60.3 us  [exchange(): return lax.ppermute(piece, axis, [(i, i ^ distance) for i in range(size)])]
    pallas_call x6, Pallas kernels: 35.3 us -> 37 us  [attend(): pl.pallas_call(functools.partial(attend_kernel, tuple(parts), len(pieces)...]
  transfers between devices with their start and end apart: 16 -> 16, of which waited for: 7 -> 7; matrix products, arithmetic and copies ran while one was open for 1% -> 0% of each run, Pallas kernels for 29% -> 29%
where the time goes in v9:
time: 134 us
  waiting for transfers between devices  60.3 us (45%)
  Pallas kernels  45.8 us (34%)
  starting transfers between devices  23.8 us (18%)
  local copies, waits for them, and re-layouts  2.73 us (2%)
    ppermute x16, waiting for transfers between devices, exchange(): return lax.ppermute(piece, axis, [(i, i ^ distance) for i in range(size)])  60.3 us
    pallas_call x6, Pallas kernels, attend(): pl.pallas_call(functools.partial(attend_kernel, tuple(parts), len(pieces)...  37 us
    ppermute x16, starting transfers between devices, exchange(): return lax.ppermute(piece, axis, [(i, i ^ distance) for i in range(size)])  23.8 us
    pallas_call x2, Pallas kernels, pack(): pl.pallas_call(functools.partial(pack_kernel, messages, shard, with_table...  7.53 us
  transfers between devices with their start and end apart: 16, of which 7 were waited for; matrix products, arithmetic and copies ran while one was open for 0% of the time, Pallas kernels for 29%

profile of v9, /device:TPU:0, one launch (start us, length us, event | category | flops | bytes accessed | tf_op | source)
XLA Modules:
  0.0 133.8 jit_solution(1861373903854555099)
XLA Ops:
  0.7 3.7 %pack_spans.3 = (bf16[384,512]{1,0:T(8,128)(2,1)}, bf16[384,512]{1,0:T(8,128)(2,1)}, bf16[768,512]{1,0:T(8,128)(2,1)}) custom-call(s32[32]{0:T(128)} %refs_0_.3, s32[4,16]{1,0:T(4,128)} %refs_1_.3, bf16[8,256,512]{2,1,0:T(8,128)(2,1)} %refs_3_.1, bf16[128,8192]{1,0:T(8,128)(2,1)} %bitcast.9), custom_call_target="tpu_custom_call" | custom-call | tf_op jit(solution)/shard_map/pack_spans/pallas_call | solution.py:132
  4.4 5.1 %collective-permute-start = (bf16[384,512]{1,0:T(8,128)(2,1)}, bf16[384,512]{1,0:T(8,128)(2,1)S(1)}, u32[]{:S(2)}, u32[]{:S(2)}) collective-permute-start(bf16[384,512]{1,0:T(8,128)(2,1)} %get-tuple-element.60), channel_id=1, source_target_pairs={{0,12},{4,8},{8,4},{12,0},{1,13},{5,9},{9,5},{13,1},{2,14},{6,10},... | collective-permute-start | bytes 1179656 | tf_op jit(solution)/shard_map/spans0_3/ppermute | solution.py:460
  10.2 1.6 %copy-done.1 = bf16[8,256,512]{2,1,0:T(8,128)(2,1)S(1)} copy-done((bf16[8,256,512]{2,1,0:T(8,128)(2,1)S(1)}, bf16[8,256,512]{2,1,0:T(8,128)(2,1)}, u32[]{:S(2)}) %copy-start.1) | copy-done | bytes 2097176
  11.8 3.8 %pack_spans.2 = (bf16[128,512]{1,0:T(8,128)(2,1)S(1)}, bf16[256,512]{1,0:T(8,128)(2,1)S(1)}, bf16[256,512]{1,0:T(8,128)(2,1)S(1)}, bf16[256,512]{1,0:T(8,128)(2,...) custom-call(s32[32]{0:T(128)S(1)} %copy-done.5, ...), custom_call_target="tpu_custom_call" | custom-call | tf_op jit(solution)/shard_map/pack_spans/pallas_call | solution.py:132
  15.7 8.7 %attend_spans.6 = (f32[4096,128]{1,0:T(8,128)S(1)}, f32[4096,128]{1,0:T(8,128)S(1)}, f32[4096,128]{1,0:T(8,128)S(1)}) custom-call(s32[16,10]{1,0:T(8,128)S(1)} %get-tuple-element.56.refs_0_, bf16[256,2048]{1,0:T(8,128)(2,1)S(1)} %bitcast.11, bf16[256,512]{1,0:T(8,128)(2,1)S(1)} %bitcast.17, bf16[8,256,512]{2,1,0:T(8,128)(2,1)S(1)} %copy-done.2), custom_call_target="tpu_custom_call" | custom-call | flops 42949672960 | tf_op jit(solution)/shard_map/attend_spans/pallas_call | solution.py:413
  24.4 19.0 %collective-permute-done.2.refs_4_ = bf16[384,512]{1,0:T(8,128)(2,1)S(1)} collective-permute-done((bf16[384,512]{1,0:T(8,128)(2,1)}, bf16[384,512]{1,0:T(8,128)(2,1)S(1)}, u32[]{:S(2)}, u32[]{:S(2)}) %collective-permute-start.2) | collective-permute-done | bytes 393248 | tf_op jit(solution)/shard_map/spans0_2/ppermute | solution.py:460
  45.3 1.6 %collective-permute-start.7 = (bf16[512,512]{1,0:T(8,128)(2,1)S(1)}, bf16[512,512]{1,0:T(8,128)(2,1)S(1)}, u32[]{:S(2)}, u32[]{:S(2)}) collective-permute-start(bf16[512,512]{1,0:T(8,128)(2,1)S(1)} %pad_maximum_fusion), channel_id=1, source_target_pairs={{0,2},{1,3},{2,0},{3,1},{4,6},{5,7},{6,4},{7,5},{8,10},{9,11},{10,... | collective-permute-start | bytes 1572872 | tf_op jit(solution)/shard_map/hidden2/ppermute | solution.py:460
  46.9 3.5 %collective-permute-start.6 = (bf16[256,512]{1,0:T(8,128)(2,1)S(1)}, bf16[256,512]{1,0:T(8,128)(2,1)S(1)}, u32[]{:S(2)}, u32[]{:S(2)}) collective-permute-start(bf16[256,512]{1,0:T(8,128)(2,1)S(1)} %get-tuple-element.75), channel_id=1, source_target_pairs={{0,12},{4,8},{8,4},{12,0},{1,13},{5,9},{9,5},{13,1},{2,14},{6,10},... | collective-permute-start | bytes 786440 | tf_op jit(solution)/shard_map/spans1_3/ppermute | solution.py:460
  51.4 7.8 %collective-permute-done.7 = bf16[512,512]{1,0:T(8,128)(2,1)S(1)} collective-permute-done((bf16[512,512]{1,0:T(8,128)(2,1)S(1)}, bf16[512,512]{1,0:T(8,128)(2,1)S(1)}, u32[]{:S(2)}, u32[]{:S(2)}) %collective-permute-start.7) | collective-permute-done | bytes 524320 | tf_op jit(solution)/shard_map/hidden2/ppermute | solution.py:460
  59.4 9.2 %attend_spans.7 = (f32[4096,128]{1,0:T(8,128)S(1)}, f32[4096,128]{1,0:T(8,128)S(1)}, f32[4096,128]{1,0:T(8,128)S(1)}) custom-call(s32[16,10]{1,0:T(8,128)S(1)} %get-tuple-element.56.refs_0_, bf16[256,2048]{1,0:T(8,128)(2,1)S(1)} %bitcast.12, bf16[256,512]{1,0:T(8,128)(2,1)S(1)} %bitcast.18, bf16[384,512]{1,0:T(8,128)(2,1)S(1)} %collective-permute-done.refs_3_, ...), custom_call_target="tpu_custom_call" | custom-call | flops 38654705664 | tf_op jit(solution)/shard_map/attend_spans/pallas_call | solution.py:413
  68.6 10.7 %collective-permute-done.1.refs_4_ = bf16[256,512]{1,0:T(8,128)(2,1)S(1)} collective-permute-done((bf16[256,512]{1,0:T(8,128)(2,1)S(1)}, bf16[256,512]{1,0:T(8,128)(2,1)S(1)}, u32[]{:S(2)}, u32[]{:S(2)}) %collective-permute-start.1) | collective-permute-done | bytes 262176 | tf_op jit(solution)/shard_map/spans1_2/ppermute | solution.py:460
  79.3 1.8 %collective-permute-start.4 = (bf16[192,512]{1,0:T(8,128)(2,1)S(1)}, bf16[192,512]{1,0:T(8,128)(2,1)S(1)}, u32[]{:S(2)}, u32[]{:S(2)}) collective-permute-start(bf16[192,512]{1,0:T(8,128)(2,1)S(1)} %get-tuple-element.72), channel_id=1, source_target_pairs={{0,12},{4,8},{8,4},{12,0},{1,13},{5,9},{9,5},{13,1},{2,14},{6,10},... | collective-permute-start | bytes 589832 | tf_op jit(solution)/shard_map/spans3_3/ppermute | solution.py:460
  81.1 1.2 project_rows.1
  82.4 2.6 %collective-permute-start.10 = (bf16[2,128,512]{2,1,0:T(8,128)(2,1)S(1)}, bf16[2,128,512]{2,1,0:T(8,128)(2,1)S(1)}, u32[]{:S(2)}, u32[]{:S(2)}) collective-permute-start(bf16[2,128,512]{2,1,0:T(8,128)(2,1)S(1)} %get-tuple-element.78), channel_id=1, source_target_pairs={{0,4},{4,0},{8,12},{12,8},{1,5},{5,1},{9,13},{13,9},{2,6},{6,2},{1... | collective-permute-start | bytes 786440 | tf_op jit(solution)/shard_map/partial1/ppermute | solution.py:460
  85.0 4.4 %attend_spans.8 = (f32[4096,128]{1,0:T(8,128)S(1)}, f32[4096,128]{1,0:T(8,128)S(1)}, f32[4096,128]{1,0:T(8,128)S(1)}) custom-call(s32[16,10]{1,0:T(8,128)S(1)} %get-tuple-element.56.refs_0_, bf16[256,2048]{1,0:T(8,128)(2,1)S(1)} %bitcast.13, bf16[256,512]{1,0:T(8,128)(2,1)S(1)} %bitcast.19, bf16[256,512]{1,0:T(8,128)(2,1)S(1)} %collective-permute-done.6.refs_3_, ...), custom_call_target="tpu_custom_call" | custom-call | flops 17179869184 | tf_op jit(solution)/shard_map/attend_spans/pallas_call | solution.py:413
  89.4 13.4 %collective-permute-done.9.refs_4_ = bf16[256,512]{1,0:T(8,128)(2,1)S(1)} collective-permute-done((bf16[256,512]{1,0:T(8,128)(2,1)S(1)}, bf16[256,512]{1,0:T(8,128)(2,1)S(1)}, u32[]{:S(2)}, u32[]{:S(2)}) %collective-permute-start.9) | collective-permute-done | bytes 262176 | tf_op jit(solution)/shard_map/spans2_2/ppermute | solution.py:460
  102.7 2.9 %collective-permute-start.13 = (bf16[384,512]{1,0:T(8,128)(2,1)S(1)}, bf16[384,512]{1,0:T(8,128)(2,1)S(1)}, u32[]{:S(2)}, u32[]{:S(2)}) collective-permute-start(bf16[384,512]{1,0:T(8,128)(2,1)S(1)} %get-tuple-element.98), channel_id=1, source_target_pairs={{0,4},{4,0},{8,12},{12,8},{1,5},{5,1},{9,13},{13,9},{2,6},{6,2},{1... | collective-permute-start | bytes 1179656 | tf_op jit(solution)/shard_map/spans3_1/ppermute | solution.py:460
  105.7 1.5 %collective-permute-start.15 = (bf16[64,512]{1,0:T(8,128)(2,1)S(1)}, bf16[64,512]{1,0:T(8,128)(2,1)S(1)}, u32[]{:S(2)}, u32[]{:S(2)}) collective-permute-start(bf16[64,512]{1,0:T(8,128)(2,1)S(1)} %get-tuple-element.105), channel_id=1, source_target_pairs={{0,12},{4,8},{8,4},{12,0},{1,13},{5,9},{9,5},{13,1},{2,14},{6,10},... | collective-permute-start | bytes 196616 | tf_op jit(solution)/shard_map/spans4_3/ppermute | solution.py:460
  107.3 4.4 %attend_spans.9 = (f32[4096,128]{1,0:T(8,128)S(1)}, f32[4096,128]{1,0:T(8,128)S(1)}, f32[4096,128]{1,0:T(8,128)S(1)}) custom-call(s32[16,10]{1,0:T(8,128)S(1)} %get-tuple-element.56.refs_0_, bf16[256,2048]{1,0:T(8,128)(2,1)S(1)} %bitcast.14, bf16[256,512]{1,0:T(8,128)(2,1)S(1)} %bitcast.20, bf16[256,512]{1,0:T(8,128)(2,1)S(1)} %collective-permute-done.5.refs_3_, ...), custom_call_target="tpu_custom_call" | custom-call | flops 17179869184 | tf_op jit(solution)/shard_map/attend_spans/pallas_call | solution.py:413
  111.8 3.0 %collective-permute-start.11 = (bf16[64,512]{1,0:T(8,128)(2,1)S(1)}, bf16[64,512]{1,0:T(8,128)(2,1)S(1)}, u32[]{:S(2)}, u32[]{:S(2)}) collective-permute-start(bf16[64,512]{1,0:T(8,128)(2,1)S(1)} %get-tuple-element.93), channel_id=1, source_target_pairs={{0,8},{4,12},{8,0},{12,4},{1,9},{5,13},{9,1},{13,5},{2,10},{6,14},... | collective-permute-start | bytes 196616 | tf_op jit(solution)/shard_map/spans4_2/ppermute | solution.py:460
  114.8 7.0 %collective-permute-done.13.refs_5_ = bf16[384,512]{1,0:T(8,128)(2,1)S(1)} collective-permute-done((bf16[384,512]{1,0:T(8,128)(2,1)S(1)}, bf16[384,512]{1,0:T(8,128)(2,1)S(1)}, u32[]{:S(2)}, u32[]{:S(2)}) %collective-permute-start.13) | collective-permute-done | bytes 393248 | tf_op jit(solution)/shard_map/spans3_1/ppermute | solution.py:460
  121.8 1.5 %collective-permute-done.14 = bf16[1,128,512]{2,1,0:T(8,128)(2,1)S(1)} collective-permute-done((bf16[1,128,512]{2,1,0:T(8,128)(2,1)S(1)}, bf16[1,128,512]{2,1,0:T(8,128)(2,1)S(1)}, u32[]{:S(2)}, u32[]{:S(2)}) %collective-permute-start.14) | collective-permute-done | bytes 131104 | tf_op jit(solution)/shard_map/partial2/ppermute | solution.py:460
  123.3 7.2 %attend_spans.10 = (f32[4096,128]{1,0:T(8,128)S(1)}, f32[4096,128]{1,0:T(8,128)S(1)}, f32[4096,128]{1,0:T(8,128)S(1)}, bf16[128,512]{1,0:T(8,128)(2,1)}) custom-call(s32[16,10]{1,0:T(8,128)S(1)} %get-tuple-element.56.refs_0_, bf16[256,2048]{1,0:T(8,128)(2,1)S(1)} %bitcast.15, bf16[256,512]{1,0:T(8,128)(2,1)S(1)} %bitcast.21, ...), custom_call_target="tpu_custom_call" | custom-call | flops 30064771072 | tf_op jit(solution)/shard_map/attend_spans/pallas_call | solution.py:413
  130.5 3.1 %attend_spans.11 = bf16[256,2048]{1,0:T(8,128)(2,1)} custom-call(s32[16,10]{1,0:T(8,128)S(1)} %get-tuple-element.56.refs_0_, bf16[256,2048]{1,0:T(8,128)(2,1)S(1)} %bitcast.16, bf16[256,512]{1,0:T(8,128)(2,1)S(1)} %bitcast.22, bf16[64,512]{1,0:T(8,128)(2,1)S(1)} %collective-permute-done.11.refs_3_, bf16[64,512]{1,0:T(8,128)(2,1)S(1)} %collective-permute-done.15.refs_4_, ...), custom_call_target="tpu_custom_call" | custom-call | flops 4294967296 | tf_op jit(solution)/shard_map/attend_spans/pallas_call | solution.py:413
  (45 shorter events, 4.0 us)
Async XLA Ops:
  0.6 9.5 %copy-start.8 = (s32[1,16,8]{1,2,0:T(8,128)S(1)}, s32[1,16,8]{1,2,0:T(8,128)}, u32[]{:S(2)}) copy-start(s32[1,16,8]{1,2,0:T(8,128)} %param.13) | copy-start | bytes 1540
  0.6 9.6 %copy-start = (bf16[1,16,8,8192]{3,2,1,0:T(8,128)(2,1)S(1)}, bf16[1,16,8,8192]{3,2,1,0:T(8,128)(2,1)}, u32[]{:S(2)}) copy-start(bf16[1,16,8,8192]{3,2,1,0:T(8,128)(2,1)} %param.14) | copy-start | bytes 6291460
  0.7 9.6 %copy-start.4 = (s32[4,16]{1,0:T(4,128)S(1)}, s32[4,16]{1,0:T(4,128)}, u32[]{:S(2)}) copy-start(s32[4,16]{1,0:T(4,128)} %refs_1_.3) | copy-start | bytes 772
  0.7 9.5 %copy-start.5 = (s32[32]{0:T(128)S(1)}, s32[32]{0:T(128)}, u32[]{:S(2)}) copy-start(s32[32]{0:T(128)} %refs_0_.3) | copy-start | bytes 388
  4.4 20.0 %collective-permute-start = (bf16[384,512]{1,0:T(8,128)(2,1)}, bf16[384,512]{1,0:T(8,128)(2,1)S(1)}, u32[]{:S(2)}, u32[]{:S(2)}) collective-permute-start(bf16[384,512]{1,0:T(8,128)(2,1)} %get-tuple-element.60), channel_id=1, source_target_pairs={{0,12},{4,8},{8,4},{12,0},{1,13},{5,9},{9,5},{13,1},{2,14},{6,10},... | collective-permute-start | bytes 1179656 | tf_op jit(solution)/shard_map/spans0_3/ppermute | solution.py:460
  9.5 33.9 %collective-permute-start.2 = (bf16[384,512]{1,0:T(8,128)(2,1)}, bf16[384,512]{1,0:T(8,128)(2,1)S(1)}, u32[]{:S(2)}, u32[]{:S(2)}) collective-permute-start(bf16[384,512]{1,0:T(8,128)(2,1)} %get-tuple-element.64), channel_id=1, source_target_pairs={{0,8},{4,12},{8,0},{12,4},{1,9},{5,13},{9,1},{13,5},{2,10},{6,14},... | collective-permute-start | bytes 1179656 | tf_op jit(solution)/shard_map/spans0_2/ppermute | solution.py:460
  9.5 34.8 %collective-permute-start.3 = (bf16[768,512]{1,0:T(8,128)(2,1)}, bf16[768,512]{1,0:T(8,128)(2,1)}, u32[]{:S(2)}, u32[]{:S(2)}) collective-permute-start(bf16[768,512]{1,0:T(8,128)(2,1)} %get-tuple-element.66), channel_id=1, source_target_pairs={{0,4},{4,0},{8,12},{12,8},{1,5},{5,1},{9,13},{13,9},{2,6},{6,2},{1... | collective-permute-start | bytes 2359304 | tf_op jit(solution)/shard_map/spans0_1/ppermute | solution.py:460
  11.8 3.9 %copy-start.2 = (bf16[8,256,512]{2,1,0:T(8,128)(2,1)S(1)}, bf16[8,256,512]{2,1,0:T(8,128)(2,1)}, u32[]{:S(2)}) copy-start(bf16[8,256,512]{2,1,0:T(8,128)(2,1)} %refs_3_.1) | copy-start | bytes 6291460
  11.8 3.9 %copy-start.6 = (bf16[1,256,2048]{2,1,0:T(8,128)(2,1)S(1)}, bf16[1,256,2048]{2,1,0:T(8,128)(2,1)}, u32[]{:S(2)}) copy-start(bf16[1,256,2048]{2,1,0:T(8,128)(2,1)} %param.8) | copy-start | bytes 3145732
  11.8 3.9 %copy-start.7 = (bf16[1,256,512]{2,1,0:T(8,128)(2,1)S(1)}, bf16[1,256,512]{2,1,0:T(8,128)(2,1)}, u32[]{:S(2)}) copy-start(bf16[1,256,512]{2,1,0:T(8,128)(2,1)} %param.9) | copy-start | bytes 786436
  45.3 13.9 %collective-permute-start.7 = (bf16[512,512]{1,0:T(8,128)(2,1)S(1)}, bf16[512,512]{1,0:T(8,128)(2,1)S(1)}, u32[]{:S(2)}, u32[]{:S(2)}) collective-permute-start(bf16[512,512]{1,0:T(8,128)(2,1)S(1)} %pad_maximum_fusion), channel_id=1, source_target_pairs={{0,2},{1,3},{2,0},{3,1},{4,6},{5,7},{6,4},{7,5},{8,10},{9,11},{10,... | collective-permute-start | bytes 1572872 | tf_op jit(solution)/shard_map/hidden2/ppermute | solution.py:460
  46.9 34.2 %collective-permute-start.6 = (bf16[256,512]{1,0:T(8,128)(2,1)S(1)}, bf16[256,512]{1,0:T(8,128)(2,1)S(1)}, u32[]{:S(2)}, u32[]{:S(2)}) collective-permute-start(bf16[256,512]{1,0:T(8,128)(2,1)S(1)} %get-tuple-element.75), channel_id=1, source_target_pairs={{0,12},{4,8},{8,4},{12,0},{1,13},{5,9},{9,5},{13,1},{2,14},{6,10},... | collective-permute-start | bytes 786440 | tf_op jit(solution)/shard_map/spans1_3/ppermute | solution.py:460
  50.4 28.8 %collective-permute-start.1 = (bf16[256,512]{1,0:T(8,128)(2,1)S(1)}, bf16[256,512]{1,0:T(8,128)(2,1)S(1)}, u32[]{:S(2)}, u32[]{:S(2)}) collective-permute-start(bf16[256,512]{1,0:T(8,128)(2,1)S(1)} %get-tuple-element.63), channel_id=1, source_target_pairs={{0,8},{4,12},{8,0},{12,4},{1,9},{5,13},{9,1},{13,5},{2,10},{6,14},... | collective-permute-start | bytes 786440 | tf_op jit(solution)/shard_map/spans1_2/ppermute | solution.py:460
  50.4 38.9 %collective-permute-start.5 = (bf16[256,512]{1,0:T(8,128)(2,1)S(1)}, bf16[256,512]{1,0:T(8,128)(2,1)S(1)}, u32[]{:S(2)}, u32[]{:S(2)}) collective-permute-start(bf16[256,512]{1,0:T(8,128)(2,1)S(1)} %get-tuple-element.74), channel_id=1, source_target_pairs={{0,12},{4,8},{8,4},{12,0},{1,13},{5,9},{9,5},{13,1},{2,14},{6,10},... | collective-permute-start | bytes 786440 | tf_op jit(solution)/shard_map/spans2_3/ppermute | solution.py:460
  59.3 21.8 %collective-permute-start.8 = (bf16[1024,512]{1,0:T(8,128)(2,1)S(1)}, bf16[1024,512]{1,0:T(8,128)(2,1)S(1)}, u32[]{:S(2)}, u32[]{:S(2)}) collective-permute-start(bf16[1024,512]{1,0:T(8,128)(2,1)S(1)} %constant_dynamic-update-slice_fusion.refs_0_), channel_id=1, source_target_pairs={{0,1},{1,0},{2,3},{3,2},{4,5},{5,4},{6,7},{7,6},{8,9},{9,8},{10,11... | collective-permute-start | bytes 3145736 | tf_op jit(solution)/shard_map/hidden1/ppermute | solution.py:460
  59.3 21.7 %copy-start.3 = (bf16[2048,512]{1,0:T(8,128)(2,1)S(1)}, bf16[2048,512]{1,0:T(8,128)(2,1)}, u32[]{:S(2)}) copy-start(bf16[2048,512]{1,0:T(8,128)(2,1)} %refs_2_.5) | copy-start | bytes 6291460
  79.3 32.5 %collective-permute-start.4 = (bf16[192,512]{1,0:T(8,128)(2,1)S(1)}, bf16[192,512]{1,0:T(8,128)(2,1)S(1)}, u32[]{:S(2)}, u32[]{:S(2)}) collective-permute-start(bf16[192,512]{1,0:T(8,128)(2,1)S(1)} %get-tuple-element.72), channel_id=1, source_target_pairs={{0,12},{4,8},{8,4},{12,0},{1,13},{5,9},{9,5},{13,1},{2,14},{6,10},... | collective-permute-start | bytes 589832 | tf_op jit(solution)/shard_map/spans3_3/ppermute | solution.py:460
  81.1 21.6 %collective-permute-start.9 = (bf16[256,512]{1,0:T(8,128)(2,1)S(1)}, bf16[256,512]{1,0:T(8,128)(2,1)S(1)}, u32[]{:S(2)}, u32[]{:S(2)}) collective-permute-start(bf16[256,512]{1,0:T(8,128)(2,1)S(1)} %get-tuple-element.85), channel_id=1, source_target_pairs={{0,8},{4,12},{8,0},{12,4},{1,9},{5,13},{9,1},{13,5},{2,10},{6,14},... | collective-permute-start | bytes 786440 | tf_op jit(solution)/shard_map/spans2_2/ppermute | solution.py:460
  82.4 24.8 %collective-permute-start.10 = (bf16[2,128,512]{2,1,0:T(8,128)(2,1)S(1)}, bf16[2,128,512]{2,1,0:T(8,128)(2,1)S(1)}, u32[]{:S(2)}, u32[]{:S(2)}) collective-permute-start(bf16[2,128,512]{2,1,0:T(8,128)(2,1)S(1)} %get-tuple-element.78), channel_id=1, source_target_pairs={{0,4},{4,0},{8,12},{12,8},{1,5},{5,1},{9,13},{13,9},{2,6},{6,2},{1... | collective-permute-start | bytes 786440 | tf_op jit(solution)/shard_map/partial1/ppermute | solution.py:460
  102.7 12.0 %collective-permute-start.12 = (bf16[192,512]{1,0:T(8,128)(2,1)S(1)}, bf16[192,512]{1,0:T(8,128)(2,1)S(1)}, u32[]{:S(2)}, u32[]{:S(2)}) collective-permute-start(bf16[192,512]{1,0:T(8,128)(2,1)S(1)} %get-tuple-element.95), channel_id=1, source_target_pairs={{0,8},{4,12},{8,0},{12,4},{1,9},{5,13},{9,1},{13,5},{2,10},{6,14},... | collective-permute-start | bytes 589832 | tf_op jit(solution)/shard_map/spans3_2/ppermute | solution.py:460
  102.7 19.1 %collective-permute-start.13 = (bf16[384,512]{1,0:T(8,128)(2,1)S(1)}, bf16[384,512]{1,0:T(8,128)(2,1)S(1)}, u32[]{:S(2)}, u32[]{:S(2)}) collective-permute-start(bf16[384,512]{1,0:T(8,128)(2,1)S(1)} %get-tuple-element.98), channel_id=1, source_target_pairs={{0,4},{4,0},{8,12},{12,8},{1,5},{5,1},{9,13},{13,9},{2,6},{6,2},{1... | collective-permute-start | bytes 1179656 | tf_op jit(solution)/shard_map/spans3_1/ppermute | solution.py:460
  105.7 24.8 %collective-permute-start.15 = (bf16[64,512]{1,0:T(8,128)(2,1)S(1)}, bf16[64,512]{1,0:T(8,128)(2,1)S(1)}, u32[]{:S(2)}, u32[]{:S(2)}) collective-permute-start(bf16[64,512]{1,0:T(8,128)(2,1)S(1)} %get-tuple-element.105), channel_id=1, source_target_pairs={{0,12},{4,8},{8,4},{12,0},{1,13},{5,9},{9,5},{13,1},{2,14},{6,10},... | collective-permute-start | bytes 196616 | tf_op jit(solution)/shard_map/spans4_3/ppermute | solution.py:460
  107.2 16.1 %collective-permute-start.14 = (bf16[1,128,512]{2,1,0:T(8,128)(2,1)S(1)}, bf16[1,128,512]{2,1,0:T(8,128)(2,1)S(1)}, u32[]{:S(2)}, u32[]{:S(2)}) collective-permute-start(bf16[1,128,512]{2,1,0:T(8,128)(2,1)S(1)} %slice.34), channel_id=1, source_target_pairs={{0,8},{4,12},{8,0},{12,4},{1,9},{5,13},{9,1},{13,5},{2,10},{6,14},... | collective-permute-start | bytes 393224 | tf_op jit(solution)/shard_map/partial2/ppermute | solution.py:460
  111.8 18.7 %collective-permute-start.11 = (bf16[64,512]{1,0:T(8,128)(2,1)S(1)}, bf16[64,512]{1,0:T(8,128)(2,1)S(1)}, u32[]{:S(2)}, u32[]{:S(2)}) collective-permute-start(bf16[64,512]{1,0:T(8,128)(2,1)S(1)} %get-tuple-element.93), channel_id=1, source_target_pairs={{0,8},{4,12},{8,0},{12,4},{1,9},{5,13},{9,1},{13,5},{2,10},{6,14},... | collective-permute-start | bytes 196616 | tf_op jit(solution)/shard_map/spans4_2/ppermute | solution.py:460
  (1 other events, 1.6 us)

commit v10 on v9

--- a/solution.py
+++ b/solution.py
@@ -474,7 +474,7 @@
         if per_pair == 1:
             return [span_len]
         if distance == 1:
-            return [2 * span_len + half, 0, 0, (per_pair - 3) * span_len + half]
+            return [2 * span_len, (per_pair - 2) * span_len]
         return [span_len] * (per_pair - 1) + [span_len - half // 2, half // 2]
 
     def pieces_of(first, length):
@@ -548,17 +548,22 @@
 
     def leave(key):
         piece, (d, number) = outbox[key], key
-        turn = turns.index(key if d > 1 else (away[-2], number)) - WINDOW
         if d == 1:
-            turn += 1
-        if turn >= 0:
-            piece = after(piece, arrived[turns[turn]])
+            before = (away[0], number - 1)
+        else:
+            turn = turns.index(key) - WINDOW
+            before = turns[turn] if turn >= 0 else None
+        if before in arrived:
+            piece = after(piece, arrived[before])
         return exchange(piece, d, "store", "spans%d_" % number)
 
     for number in range(1, count):
         keys = [key for key in later if key[1] == number]
         coming = [leave(key) for key in keys]
         here = [(d, number - 1) for d in away if (d, number - 1) in arrived]
+        if number == 2:
+            state, _ = block([key for key in here if key[0] > 1], state)
+            here = [key for key in here if key[0] == 1]
         if 2 <= number < n_store.bit_length() + 1:
             state = [after(state[0], next(steps)), *state[1:]]
         if number == count - 1:

time: 134 us -> 125 us (0.933)
  waiting for transfers between devices: 60.3 us -> 44.8 us
  starting transfers between devices: 23.8 us -> 31 us
    ppermute x16, waiting for transfers between devices: 60.3 us -> 44.8 us  [exchange(): return lax.ppermute(piece, axis, [(i, i ^ distance) for i in range(size)])]
    ppermute x16, starting transfers between devices: 23.8 us -> 31 us  [exchange(): return lax.ppermute(piece, axis, [(i, i ^ distance) for i in range(size)])]
    pallas_call x6 -> x7, Pallas kernels: 37 us -> 36.8 us  [attend(): pl.pallas_call(functools.partial(attend_kernel, tuple(parts), len(pieces)...]
  transfers between devices with their start and end apart: 16 -> 16, of which waited for: 7 -> 6; matrix products, arithmetic and copies ran while one was open for 0% -> 1% of each run, Pallas kernels for 29% -> 31%
where the time goes in v10:
time: 125 us
  Pallas kernels  45.3 us (36%)
  waiting for transfers between devices  44.8 us (36%)
  starting transfers between devices  31 us (25%)
  local copies, waits for them, and re-layouts  2.51 us (2%)
    ppermute x16, waiting for transfers between devices, exchange(): return lax.ppermute(piece, axis, [(i, i ^ distance) for i in range(size)])  44.8 us
    pallas_call x7, Pallas kernels, attend(): pl.pallas_call(functools.partial(attend_kernel, tuple(parts), len(pieces)...  36.8 us
    ppermute x16, starting transfers between devices, exchange(): return lax.ppermute(piece, axis, [(i, i ^ distance) for i in range(size)])  31 us
    pallas_call x2, Pallas kernels, pack(): pl.pallas_call(functools.partial(pack_kernel, messages, shard, with_table...  7.25 us
  transfers between devices with their start and end apart: 16, of which 6 were waited for; matrix products, arithmetic and copies ran while one was open for 1% of the time, Pallas kernels for 31%

profile of v10, /device:TPU:0, one launch (start us, length us, event | category | flops | bytes accessed | tf_op | source)
XLA Modules:
  0.0 124.7 jit_solution(2590264209273446521)
XLA Ops:
  0.7 3.6 %pack_spans.3 = (bf16[384,512]{1,0:T(8,128)(2,1)}, bf16[384,512]{1,0:T(8,128)(2,1)}, bf16[640,512]{1,0:T(8,128)(2,1)}) custom-call(s32[32]{0:T(128)} %refs_0_.3, s32[4,16]{1,0:T(4,128)} %refs_1_.3, bf16[8,256,512]{2,1,0:T(8,128)(2,1)} %refs_3_.1, bf16[128,8192]{1,0:T(8,128)(2,1)} %bitcast.9), custom_call_target="tpu_custom_call" | custom-call | tf_op jit(solution)/shard_map/pack_spans/pallas_call | solution.py:132
  4.3 5.1 %collective-permute-start = (bf16[384,512]{1,0:T(8,128)(2,1)}, bf16[384,512]{1,0:T(8,128)(2,1)S(1)}, u32[]{:S(2)}, u32[]{:S(2)}) collective-permute-start(bf16[384,512]{1,0:T(8,128)(2,1)} %get-tuple-element.63), channel_id=1, source_target_pairs={{0,12},{4,8},{8,4},{12,0},{1,13},{5,9},{9,5},{13,1},{2,14},{6,10},... | collective-permute-start | bytes 1179656 | tf_op jit(solution)/shard_map/spans0_3/ppermute | solution.py:460
  10.8 1.6 %copy-done.1 = bf16[8,256,512]{2,1,0:T(8,128)(2,1)S(1)} copy-done((bf16[8,256,512]{2,1,0:T(8,128)(2,1)S(1)}, bf16[8,256,512]{2,1,0:T(8,128)(2,1)}, u32[]{:S(2)}) %copy-start.1) | copy-done | bytes 2097176
  12.4 3.7 %pack_spans.2 = (bf16[128,512]{1,0:T(8,128)(2,1)S(1)}, bf16[256,512]{1,0:T(8,128)(2,1)S(1)}, bf16[256,512]{1,0:T(8,128)(2,1)S(1)}, bf16[512,512]{1,0:T(8,128)(2,...) custom-call(s32[32]{0:T(128)S(1)} %copy-done.5, ...), custom_call_target="tpu_custom_call" | custom-call | tf_op jit(solution)/shard_map/pack_spans/pallas_call | solution.py:132
  16.1 3.8 %collective-permute-start.7 = (bf16[256,512]{1,0:T(8,128)(2,1)S(1)}, bf16[256,512]{1,0:T(8,128)(2,1)S(1)}, u32[]{:S(2)}, u32[]{:S(2)}) collective-permute-start(bf16[256,512]{1,0:T(8,128)(2,1)S(1)} %get-tuple-element.81), channel_id=1, source_target_pairs={{0,12},{4,8},{8,4},{12,0},{1,13},{5,9},{9,5},{13,1},{2,14},{6,10},... | collective-permute-start | bytes 786440 | tf_op jit(solution)/shard_map/spans1_3/ppermute | solution.py:460
  19.9 8.7 %attend_spans.7 = (f32[4096,128]{1,0:T(8,128)S(1)}, f32[4096,128]{1,0:T(8,128)S(1)}, f32[4096,128]{1,0:T(8,128)S(1)}) custom-call(s32[16,10]{1,0:T(8,128)S(1)} %get-tuple-element.59.refs_0_, bf16[256,2048]{1,0:T(8,128)(2,1)S(1)} %bitcast.11, bf16[256,512]{1,0:T(8,128)(2,1)S(1)} %bitcast.18, bf16[8,256,512]{2,1,0:T(8,128)(2,1)S(1)} %copy-done.2), custom_call_target="tpu_custom_call" | custom-call | flops 42949672960 | tf_op jit(solution)/shard_map/attend_spans/pallas_call | solution.py:413
  28.6 8.9 %collective-permute-start.1 = (bf16[256,512]{1,0:T(8,128)(2,1)S(1)}, bf16[256,512]{1,0:T(8,128)(2,1)S(1)}, u32[]{:S(2)}, u32[]{:S(2)}) collective-permute-start(bf16[256,512]{1,0:T(8,128)(2,1)S(1)} %get-tuple-element.66), channel_id=1, source_target_pairs={{0,8},{4,12},{8,0},{12,4},{1,9},{5,13},{9,1},{13,5},{2,10},{6,14},... | collective-permute-start | bytes 786440 | tf_op jit(solution)/shard_map/spans1_2/ppermute | solution.py:460
  37.4 17.9 %collective-permute-done.2.refs_4_ = bf16[384,512]{1,0:T(8,128)(2,1)S(1)} collective-permute-done((bf16[384,512]{1,0:T(8,128)(2,1)}, bf16[384,512]{1,0:T(8,128)(2,1)S(1)}, u32[]{:S(2)}, u32[]{:S(2)}) %collective-permute-start.2) | collective-permute-done | bytes 393248 | tf_op jit(solution)/shard_map/spans0_2/ppermute | solution.py:460
  55.3 2.7 %collective-permute-start.5 = (bf16[256,512]{1,0:T(8,128)(2,1)S(1)}, bf16[256,512]{1,0:T(8,128)(2,1)S(1)}, u32[]{:S(2)}, u32[]{:S(2)}) collective-permute-start(bf16[256,512]{1,0:T(8,128)(2,1)S(1)} %get-tuple-element.77), channel_id=1, source_target_pairs={{0,12},{4,8},{8,4},{12,0},{1,13},{5,9},{9,5},{13,1},{2,14},{6,10},... | collective-permute-start | bytes 786440 | tf_op jit(solution)/shard_map/spans2_3/ppermute | solution.py:460
  58.1 1.6 %collective-permute-start.8 = (bf16[512,512]{1,0:T(8,128)(2,1)S(1)}, bf16[512,512]{1,0:T(8,128)(2,1)S(1)}, u32[]{:S(2)}, u32[]{:S(2)}) collective-permute-start(bf16[512,512]{1,0:T(8,128)(2,1)S(1)} %pad_maximum_fusion), channel_id=1, source_target_pairs={{0,2},{1,3},{2,0},{3,1},{4,6},{5,7},{6,4},{7,5},{8,10},{9,11},{10,... | collective-permute-start | bytes 1572872 | tf_op jit(solution)/shard_map/hidden2/ppermute | solution.py:460
  59.7 7.5 %attend_spans.8 = (f32[4096,128]{1,0:T(8,128)S(1)}, f32[4096,128]{1,0:T(8,128)S(1)}, f32[4096,128]{1,0:T(8,128)S(1)}) custom-call(s32[16,10]{1,0:T(8,128)S(1)} %get-tuple-element.59.refs_0_, bf16[256,2048]{1,0:T(8,128)(2,1)S(1)} %bitcast.12, bf16[256,512]{1,0:T(8,128)(2,1)S(1)} %bitcast.19, bf16[384,512]{1,0:T(8,128)(2,1)S(1)} %collective-permute-done.refs_3_, ...), custom_call_target="tpu_custom_call" | custom-call | flops 34359738368 | tf_op jit(solution)/shard_map/attend_spans/pallas_call | solution.py:413
  67.2 5.0 %collective-permute-done.1.refs_4_ = bf16[256,512]{1,0:T(8,128)(2,1)S(1)} collective-permute-done((bf16[256,512]{1,0:T(8,128)(2,1)S(1)}, bf16[256,512]{1,0:T(8,128)(2,1)S(1)}, u32[]{:S(2)}, u32[]{:S(2)}) %collective-permute-start.1) | collective-permute-done | bytes 262176 | tf_op jit(solution)/shard_map/spans1_2/ppermute | solution.py:460
  72.2 2.7 %collective-permute-start.4 = (bf16[192,512]{1,0:T(8,128)(2,1)S(1)}, bf16[192,512]{1,0:T(8,128)(2,1)S(1)}, u32[]{:S(2)}, u32[]{:S(2)}) collective-permute-start(bf16[192,512]{1,0:T(8,128)(2,1)S(1)} %get-tuple-element.75), channel_id=1, source_target_pairs={{0,12},{4,8},{8,4},{12,0},{1,13},{5,9},{9,5},{13,1},{2,14},{6,10},... | collective-permute-start | bytes 589832 | tf_op jit(solution)/shard_map/spans3_3/ppermute | solution.py:460
  75.0 4.4 %attend_spans.9 = (f32[4096,128]{1,0:T(8,128)S(1)}, f32[4096,128]{1,0:T(8,128)S(1)}, f32[4096,128]{1,0:T(8,128)S(1)}) custom-call(s32[16,10]{1,0:T(8,128)S(1)} %get-tuple-element.59.refs_0_, bf16[256,2048]{1,0:T(8,128)(2,1)S(1)} %bitcast.13, bf16[256,512]{1,0:T(8,128)(2,1)S(1)} %bitcast.20, bf16[256,512]{1,0:T(8,128)(2,1)S(1)} %collective-permute-done.7.refs_3_, ...), custom_call_target="tpu_custom_call" | custom-call | flops 17179869184 | tf_op jit(solution)/shard_map/attend_spans/pallas_call | solution.py:413
  79.4 3.4 %collective-permute-done.6.refs_3_ = bf16[512,512]{1,0:T(8,128)(2,1)S(1)} collective-permute-done((bf16[512,512]{1,0:T(8,128)(2,1)S(1)}, bf16[512,512]{1,0:T(8,128)(2,1)S(1)}, u32[]{:S(2)}, u32[]{:S(2)}) %collective-permute-start.6) | collective-permute-done | bytes 524320 | tf_op jit(solution)/shard_map/spans1_1/ppermute | solution.py:460
  84.1 4.4 %attend_spans.10 = (f32[4096,128]{1,0:T(8,128)S(1)}, f32[4096,128]{1,0:T(8,128)S(1)}, f32[4096,128]{1,0:T(8,128)S(1)}) custom-call(s32[16,10]{1,0:T(8,128)S(1)} %get-tuple-element.59.refs_0_, bf16[256,2048]{1,0:T(8,128)(2,1)S(1)} %bitcast.14, bf16[256,512]{1,0:T(8,128)(2,1)S(1)} %bitcast.21, bf16[512,512]{1,0:T(8,128)(2,1)S(1)} %collective-permute-done.6.refs_3_, ...), custom_call_target="tpu_custom_call" | custom-call | flops 17179869184 | tf_op jit(solution)/shard_map/attend_spans/pallas_call | solution.py:413
  88.6 7.9 %collective-permute-done.10.refs_4_ = bf16[256,512]{1,0:T(8,128)(2,1)S(1)} collective-permute-done((bf16[256,512]{1,0:T(8,128)(2,1)S(1)}, bf16[256,512]{1,0:T(8,128)(2,1)S(1)}, u32[]{:S(2)}, u32[]{:S(2)}) %collective-permute-start.10) | collective-permute-done | bytes 262176 | tf_op jit(solution)/shard_map/spans2_2/ppermute | solution.py:460
  96.5 2.5 %collective-permute-start.15 = (bf16[64,512]{1,0:T(8,128)(2,1)S(1)}, bf16[64,512]{1,0:T(8,128)(2,1)S(1)}, u32[]{:S(2)}, u32[]{:S(2)}) collective-permute-start(bf16[64,512]{1,0:T(8,128)(2,1)S(1)} %get-tuple-element.111), channel_id=1, source_target_pairs={{0,12},{4,8},{8,4},{12,0},{1,13},{5,9},{9,5},{13,1},{2,14},{6,10},... | collective-permute-start | bytes 196616 | tf_op jit(solution)/shard_map/spans4_3/ppermute | solution.py:460
  99.1 2.1 %collective-permute-start.14 = (bf16[1,128,512]{2,1,0:T(8,128)(2,1)S(1)}, bf16[1,128,512]{2,1,0:T(8,128)(2,1)S(1)}, u32[]{:S(2)}, u32[]{:S(2)}) collective-permute-start(bf16[1,128,512]{2,1,0:T(8,128)(2,1)S(1)} %slice.34), channel_id=1, source_target_pairs={{0,8},{4,12},{8,0},{12,4},{1,9},{5,13},{9,1},{13,5},{2,10},{6,14},... | collective-permute-start | bytes 393224 | tf_op jit(solution)/shard_map/partial2/ppermute | solution.py:460
  101.2 4.4 %attend_spans.11 = (f32[4096,128]{1,0:T(8,128)S(1)}, f32[4096,128]{1,0:T(8,128)S(1)}, f32[4096,128]{1,0:T(8,128)S(1)}) custom-call(s32[16,10]{1,0:T(8,128)S(1)} %get-tuple-element.59.refs_0_, bf16[256,2048]{1,0:T(8,128)(2,1)S(1)} %bitcast.15, bf16[256,512]{1,0:T(8,128)(2,1)S(1)} %bitcast.22, bf16[256,512]{1,0:T(8,128)(2,1)S(1)} %collective-permute-done.5.refs_3_, ...), custom_call_target="tpu_custom_call" | custom-call | flops 17179869184 | tf_op jit(solution)/shard_map/attend_spans/pallas_call | solution.py:413
  106.6 6.4 %collective-permute-done.13.refs_4_ = bf16[192,512]{1,0:T(8,128)(2,1)S(1)} collective-permute-done((bf16[192,512]{1,0:T(8,128)(2,1)S(1)}, bf16[192,512]{1,0:T(8,128)(2,1)S(1)}, u32[]{:S(2)}, u32[]{:S(2)}) %collective-permute-start.13) | collective-permute-done | bytes 196640 | tf_op jit(solution)/shard_map/spans3_2/ppermute | solution.py:460
  112.9 4.2 %collective-permute-done.14 = bf16[1,128,512]{2,1,0:T(8,128)(2,1)S(1)} collective-permute-done((bf16[1,128,512]{2,1,0:T(8,128)(2,1)S(1)}, bf16[1,128,512]{2,1,0:T(8,128)(2,1)S(1)}, u32[]{:S(2)}, u32[]{:S(2)}) %collective-permute-start.14) | collective-permute-done | bytes 131104 | tf_op jit(solution)/shard_map/partial2/ppermute | solution.py:460
  117.1 4.3 %attend_spans.12 = (f32[4096,128]{1,0:T(8,128)S(1)}, f32[4096,128]{1,0:T(8,128)S(1)}, f32[4096,128]{1,0:T(8,128)S(1)}, bf16[128,512]{1,0:T(8,128)(2,1)}) custom-call(s32[16,10]{1,0:T(8,128)S(1)} %get-tuple-element.59.refs_0_, bf16[256,2048]{1,0:T(8,128)(2,1)S(1)} %bitcast.16, bf16[256,512]{1,0:T(8,128)(2,1)S(1)} %bitcast.23, ...), custom_call_target="tpu_custom_call" | custom-call | flops 17179869184 | tf_op jit(solution)/shard_map/attend_spans/pallas_call | solution.py:413
  121.5 3.1 %attend_spans.13 = bf16[256,2048]{1,0:T(8,128)(2,1)} custom-call(s32[16,10]{1,0:T(8,128)S(1)} %get-tuple-element.59.refs_0_, bf16[256,2048]{1,0:T(8,128)(2,1)S(1)} %bitcast.17, bf16[256,512]{1,0:T(8,128)(2,1)S(1)} %bitcast.24, bf16[64,512]{1,0:T(8,128)(2,1)S(1)} %collective-permute-done.12.refs_3_, bf16[64,512]{1,0:T(8,128)(2,1)S(1)} %collective-permute-done.15.refs_4_, ...), custom_call_target="tpu_custom_call" | custom-call | flops 4294967296 | tf_op jit(solution)/shard_map/attend_spans/pallas_call | solution.py:413
  (44 shorter events, 4.1 us)
Async XLA Ops:
  0.6 10.1 %copy-start = (bf16[1,16,8,8192]{3,2,1,0:T(8,128)(2,1)S(1)}, bf16[1,16,8,8192]{3,2,1,0:T(8,128)(2,1)}, u32[]{:S(2)}) copy-start(bf16[1,16,8,8192]{3,2,1,0:T(8,128)(2,1)} %param.14) | copy-start | bytes 6291460
  0.6 10.1 %copy-start.4 = (s32[4,16]{1,0:T(4,128)S(1)}, s32[4,16]{1,0:T(4,128)}, u32[]{:S(2)}) copy-start(s32[4,16]{1,0:T(4,128)} %refs_1_.3) | copy-start | bytes 772
  0.7 10.1 %copy-start.5 = (s32[32]{0:T(128)S(1)}, s32[32]{0:T(128)}, u32[]{:S(2)}) copy-start(s32[32]{0:T(128)} %refs_0_.3) | copy-start | bytes 388
  4.3 24.3 %collective-permute-start = (bf16[384,512]{1,0:T(8,128)(2,1)}, bf16[384,512]{1,0:T(8,128)(2,1)S(1)}, u32[]{:S(2)}, u32[]{:S(2)}) collective-permute-start(bf16[384,512]{1,0:T(8,128)(2,1)} %get-tuple-element.63), channel_id=1, source_target_pairs={{0,12},{4,8},{8,4},{12,0},{1,13},{5,9},{9,5},{13,1},{2,14},{6,10},... | collective-permute-start | bytes 1179656 | tf_op jit(solution)/shard_map/spans0_3/ppermute | solution.py:460
  9.4 46.0 %collective-permute-start.2 = (bf16[384,512]{1,0:T(8,128)(2,1)}, bf16[384,512]{1,0:T(8,128)(2,1)S(1)}, u32[]{:S(2)}, u32[]{:S(2)}) collective-permute-start(bf16[384,512]{1,0:T(8,128)(2,1)} %get-tuple-element.67), channel_id=1, source_target_pairs={{0,8},{4,12},{8,0},{12,4},{1,9},{5,13},{9,1},{13,5},{2,10},{6,14},... | collective-permute-start | bytes 1179656 | tf_op jit(solution)/shard_map/spans0_2/ppermute | solution.py:460
  9.4 48.6 %collective-permute-start.3 = (bf16[640,512]{1,0:T(8,128)(2,1)}, bf16[640,512]{1,0:T(8,128)(2,1)S(1)}, u32[]{:S(2)}, u32[]{:S(2)}) collective-permute-start(bf16[640,512]{1,0:T(8,128)(2,1)} %get-tuple-element.69), channel_id=1, source_target_pairs={{0,4},{4,0},{8,12},{12,8},{1,5},{5,1},{9,13},{13,9},{2,6},{6,2},{1... | collective-permute-start | bytes 1966088 | tf_op jit(solution)/shard_map/spans0_1/ppermute | solution.py:460
  10.8 1.6 %copy-start.1 = (bf16[8,256,512]{2,1,0:T(8,128)(2,1)S(1)}, bf16[8,256,512]{2,1,0:T(8,128)(2,1)}, u32[]{:S(2)}) copy-start(bf16[8,256,512]{2,1,0:T(8,128)(2,1)} %refs_3_.1) | copy-start | bytes 6291460
  12.4 7.5 %copy-start.2 = (bf16[8,256,512]{2,1,0:T(8,128)(2,1)S(1)}, bf16[8,256,512]{2,1,0:T(8,128)(2,1)}, u32[]{:S(2)}) copy-start(bf16[8,256,512]{2,1,0:T(8,128)(2,1)} %refs_3_.1) | copy-start | bytes 6291460
  12.4 7.5 %copy-start.6 = (bf16[1,256,2048]{2,1,0:T(8,128)(2,1)S(1)}, bf16[1,256,2048]{2,1,0:T(8,128)(2,1)}, u32[]{:S(2)}) copy-start(bf16[1,256,2048]{2,1,0:T(8,128)(2,1)} %param.8) | copy-start | bytes 3145732
  12.4 7.5 %copy-start.7 = (bf16[1,256,512]{2,1,0:T(8,128)(2,1)S(1)}, bf16[1,256,512]{2,1,0:T(8,128)(2,1)}, u32[]{:S(2)}) copy-start(bf16[1,256,512]{2,1,0:T(8,128)(2,1)} %param.9) | copy-start | bytes 786436
  16.1 58.8 %collective-permute-start.7 = (bf16[256,512]{1,0:T(8,128)(2,1)S(1)}, bf16[256,512]{1,0:T(8,128)(2,1)S(1)}, u32[]{:S(2)}, u32[]{:S(2)}) collective-permute-start(bf16[256,512]{1,0:T(8,128)(2,1)S(1)} %get-tuple-element.81), channel_id=1, source_target_pairs={{0,12},{4,8},{8,4},{12,0},{1,13},{5,9},{9,5},{13,1},{2,14},{6,10},... | collective-permute-start | bytes 786440 | tf_op jit(solution)/shard_map/spans1_3/ppermute | solution.py:460
  28.6 43.6 %collective-permute-start.1 = (bf16[256,512]{1,0:T(8,128)(2,1)S(1)}, bf16[256,512]{1,0:T(8,128)(2,1)S(1)}, u32[]{:S(2)}, u32[]{:S(2)}) collective-permute-start(bf16[256,512]{1,0:T(8,128)(2,1)S(1)} %get-tuple-element.66), channel_id=1, source_target_pairs={{0,8},{4,12},{8,0},{12,4},{1,9},{5,13},{9,1},{13,5},{2,10},{6,14},... | collective-permute-start | bytes 786440 | tf_op jit(solution)/shard_map/spans1_2/ppermute | solution.py:460
  55.3 33.3 %collective-permute-start.5 = (bf16[256,512]{1,0:T(8,128)(2,1)S(1)}, bf16[256,512]{1,0:T(8,128)(2,1)S(1)}, u32[]{:S(2)}, u32[]{:S(2)}) collective-permute-start(bf16[256,512]{1,0:T(8,128)(2,1)S(1)} %get-tuple-element.77), channel_id=1, source_target_pairs={{0,12},{4,8},{8,4},{12,0},{1,13},{5,9},{9,5},{13,1},{2,14},{6,10},... | collective-permute-start | bytes 786440 | tf_op jit(solution)/shard_map/spans2_3/ppermute | solution.py:460
  58.0 24.8 %collective-permute-start.6 = (bf16[512,512]{1,0:T(8,128)(2,1)S(1)}, bf16[512,512]{1,0:T(8,128)(2,1)S(1)}, u32[]{:S(2)}, u32[]{:S(2)}) collective-permute-start(bf16[512,512]{1,0:T(8,128)(2,1)S(1)} %get-tuple-element.79), channel_id=1, source_target_pairs={{0,4},{4,0},{8,12},{12,8},{1,5},{5,1},{9,13},{13,9},{2,6},{6,2},{1... | collective-permute-start | bytes 1572872 | tf_op jit(solution)/shard_map/spans1_1/ppermute | solution.py:460
  58.1 16.7 %collective-permute-start.8 = (bf16[512,512]{1,0:T(8,128)(2,1)S(1)}, bf16[512,512]{1,0:T(8,128)(2,1)S(1)}, u32[]{:S(2)}, u32[]{:S(2)}) collective-permute-start(bf16[512,512]{1,0:T(8,128)(2,1)S(1)} %pad_maximum_fusion), channel_id=1, source_target_pairs={{0,2},{1,3},{2,0},{3,1},{4,6},{5,7},{6,4},{7,5},{8,10},{9,11},{10,... | collective-permute-start | bytes 1572872 | tf_op jit(solution)/shard_map/hidden2/ppermute | solution.py:460
  72.2 33.4 %collective-permute-start.4 = (bf16[192,512]{1,0:T(8,128)(2,1)S(1)}, bf16[192,512]{1,0:T(8,128)(2,1)S(1)}, u32[]{:S(2)}, u32[]{:S(2)}) collective-permute-start(bf16[192,512]{1,0:T(8,128)(2,1)S(1)} %get-tuple-element.75), channel_id=1, source_target_pairs={{0,12},{4,8},{8,4},{12,0},{1,13},{5,9},{9,5},{13,1},{2,14},{6,10},... | collective-permute-start | bytes 589832 | tf_op jit(solution)/shard_map/spans3_3/ppermute | solution.py:460
  74.8 21.7 %collective-permute-start.10 = (bf16[256,512]{1,0:T(8,128)(2,1)S(1)}, bf16[256,512]{1,0:T(8,128)(2,1)S(1)}, u32[]{:S(2)}, u32[]{:S(2)}) collective-permute-start(bf16[256,512]{1,0:T(8,128)(2,1)S(1)} %get-tuple-element.94), channel_id=1, source_target_pairs={{0,8},{4,12},{8,0},{12,4},{1,9},{5,13},{9,1},{13,5},{2,10},{6,14},... | collective-permute-start | bytes 786440 | tf_op jit(solution)/shard_map/spans2_2/ppermute | solution.py:460
  74.9 7.9 %collective-permute-start.9 = (bf16[1024,512]{1,0:T(8,128)(2,1)S(1)}, bf16[1024,512]{1,0:T(8,128)(2,1)S(1)}, u32[]{:S(2)}, u32[]{:S(2)}) collective-permute-start(bf16[1024,512]{1,0:T(8,128)(2,1)S(1)} %constant_dynamic-update-slice_fusion.refs_0_), channel_id=1, source_target_pairs={{0,1},{1,0},{2,3},{3,2},{4,5},{5,4},{6,7},{7,6},{8,9},{9,8},{10,11... | collective-permute-start | bytes 3145736 | tf_op jit(solution)/shard_map/hidden1/ppermute | solution.py:460
  75.0 7.8 %copy-start.3 = (bf16[2048,512]{1,0:T(8,128)(2,1)S(1)}, bf16[2048,512]{1,0:T(8,128)(2,1)}, u32[]{:S(2)}) copy-start(bf16[2048,512]{1,0:T(8,128)(2,1)} %refs_2_.5) | copy-start | bytes 6291460
  84.1 14.9 %collective-permute-start.11 = (bf16[2,128,512]{2,1,0:T(8,128)(2,1)S(1)}, bf16[2,128,512]{2,1,0:T(8,128)(2,1)S(1)}, u32[]{:S(2)}, u32[]{:S(2)}) collective-permute-start(bf16[2,128,512]{2,1,0:T(8,128)(2,1)S(1)} %get-tuple-element.87), channel_id=1, source_target_pairs={{0,4},{4,0},{8,12},{12,8},{1,5},{5,1},{9,13},{13,9},{2,6},{6,2},{1... | collective-permute-start | bytes 786440 | tf_op jit(solution)/shard_map/partial1/ppermute | solution.py:460
  96.5 16.4 %collective-permute-start.13 = (bf16[192,512]{1,0:T(8,128)(2,1)S(1)}, bf16[192,512]{1,0:T(8,128)(2,1)S(1)}, u32[]{:S(2)}, u32[]{:S(2)}) collective-permute-start(bf16[192,512]{1,0:T(8,128)(2,1)S(1)} %get-tuple-element.104), channel_id=1, source_target_pairs={{0,8},{4,12},{8,0},{12,4},{1,9},{5,13},{9,1},{13,5},{2,10},{6,14},... | collective-permute-start | bytes 589832 | tf_op jit(solution)/shard_map/spans3_2/ppermute | solution.py:460
  96.5 25.0 %collective-permute-start.15 = (bf16[64,512]{1,0:T(8,128)(2,1)S(1)}, bf16[64,512]{1,0:T(8,128)(2,1)S(1)}, u32[]{:S(2)}, u32[]{:S(2)}) collective-permute-start(bf16[64,512]{1,0:T(8,128)(2,1)S(1)} %get-tuple-element.111), channel_id=1, source_target_pairs={{0,12},{4,8},{8,4},{12,0},{1,13},{5,9},{9,5},{13,1},{2,14},{6,10},... | collective-permute-start | bytes 196616 | tf_op jit(solution)/shard_map/spans4_3/ppermute | solution.py:460
  99.1 18.0 %collective-permute-start.14 = (bf16[1,128,512]{2,1,0:T(8,128)(2,1)S(1)}, bf16[1,128,512]{2,1,0:T(8,128)(2,1)S(1)}, u32[]{:S(2)}, u32[]{:S(2)}) collective-permute-start(bf16[1,128,512]{2,1,0:T(8,128)(2,1)S(1)} %slice.34), channel_id=1, source_target_pairs={{0,8},{4,12},{8,0},{12,4},{1,9},{5,13},{9,1},{13,5},{2,10},{6,14},... | collective-permute-start | bytes 393224 | tf_op jit(solution)/shard_map/partial2/ppermute | solution.py:460
  105.6 15.9 %collective-permute-start.12 = (bf16[64,512]{1,0:T(8,128)(2,1)S(1)}, bf16[64,512]{1,0:T(8,128)(2,1)S(1)}, u32[]{:S(2)}, u32[]{:S(2)}) collective-permute-start(bf16[64,512]{1,0:T(8,128)(2,1)S(1)} %get-tuple-element.102), channel_id=1, source_target_pairs={{0,8},{4,12},{8,0},{12,4},{1,9},{5,13},{9,1},{13,5},{2,10},{6,14},... | collective-permute-start | bytes 196616 | tf_op jit(solution)/shard_map/spans4_2/ppermute | solution.py:460

commit v11 on v10

--- a/solution.py
+++ b/solution.py
@@ -540,7 +540,7 @@
                 partial = partial[0::2] + other.astype(jnp.float32)
         yield partial[0], other[0]
 
-    arrived, fresh, rows = {}, None, None
+    arrived = {}
     state, _ = block([], None)
     arrived.update(zip([(d, 0) for d in away], behind(coming, state)))
     steps = recomputed()
@@ -566,20 +566,16 @@
             here = [key for key in here if key[0] == 1]
         if 2 <= number < n_store.bit_length() + 1:
             state = [after(state[0], next(steps)), *state[1:]]
-        if number == count - 1:
-            *_, fresh = steps
-        state, rows = block(here, state, fresh)
+        state, _ = block(here, state)
         arrived.update(zip(keys, behind(coming, state)))
 
     keys = [(d, count - 1) for d in away[::-1] if (d, count - 1) in arrived]
     size = 6
     batches = [keys[i : i + size] for i in range(0, len(keys), size)]
+    *_, fresh = steps
     for i, keys in enumerate(batches):
-        joins, last = rows is None, i == len(batches) - 1
-        if joins:
-            *_, fresh = steps
-        state, now = block(keys, state, fresh if joins else None, last)
-        rows = now if joins else rows
+        last = i == len(batches) - 1
+        state, rows = block(keys, state, fresh if last else None, last)
     return (state[0][None], rows.reshape(1, span_count, recomp, kv_cols))
 
 

time: 125 us -> 122 us (0.976)
  waiting for transfers between devices: 44.8 us -> 42.4 us
    ppermute x16, waiting for transfers between devices: 44.8 us -> 42.4 us  [exchange(): return lax.ppermute(piece, axis, [(i, i ^ distance) for i in range(size)])]
where the time goes in v11:
time: 122 us
  Pallas kernels  44.9 us (37%)
  waiting for transfers between devices  42.4 us (35%)
  starting transfers between devices  31 us (25%)
  local copies, waits for them, and re-layouts  2.52 us (2%)
    ppermute x16, waiting for transfers between devices, exchange(): return lax.ppermute(piece, axis, [(i, i ^ distance) for i in range(size)])  42.4 us
    pallas_call x7, Pallas kernels, attend(): pl.pallas_call(functools.partial(attend_kernel, tuple(parts), len(pieces)...  36.4 us
    ppermute x16, starting transfers between devices, exchange(): return lax.ppermute(piece, axis, [(i, i ^ distance) for i in range(size)])  31 us
    pallas_call x2, Pallas kernels, pack(): pl.pallas_call(functools.partial(pack_kernel, messages, shard, with_table...  7.25 us
  transfers between devices with their start and end apart: 16, of which 6 were waited for; matrix products, arithmetic and copies ran while one was open for 1% of the time, Pallas kernels for 31%

profile of v11, /device:TPU:0, one launch (start us, length us, event | category | flops | bytes accessed | tf_op | source)
XLA Modules:
  0.0 122.0 jit_solution(10004253806100829712)
XLA Ops:
  0.7 3.6 %pack_spans.3 = (bf16[384,512]{1,0:T(8,128)(2,1)}, bf16[384,512]{1,0:T(8,128)(2,1)}, bf16[640,512]{1,0:T(8,128)(2,1)}) custom-call(s32[32]{0:T(128)} %refs_0_.3, s32[4,16]{1,0:T(4,128)} %refs_1_.3, bf16[8,256,512]{2,1,0:T(8,128)(2,1)} %refs_3_.1, bf16[128,8192]{1,0:T(8,128)(2,1)} %bitcast.9), custom_call_target="tpu_custom_call" | custom-call | tf_op jit(solution)/shard_map/pack_spans/pallas_call | solution.py:132
  4.3 5.1 %collective-permute-start = (bf16[384,512]{1,0:T(8,128)(2,1)}, bf16[384,512]{1,0:T(8,128)(2,1)S(1)}, u32[]{:S(2)}, u32[]{:S(2)}) collective-permute-start(bf16[384,512]{1,0:T(8,128)(2,1)} %get-tuple-element.64), channel_id=1, source_target_pairs={{0,12},{4,8},{8,4},{12,0},{1,13},{5,9},{9,5},{13,1},{2,14},{6,10},... | collective-permute-start | bytes 1179656 | tf_op jit(solution)/shard_map/spans0_3/ppermute | solution.py:460
  10.8 1.6 %copy-done.1 = bf16[8,256,512]{2,1,0:T(8,128)(2,1)S(1)} copy-done((bf16[8,256,512]{2,1,0:T(8,128)(2,1)S(1)}, bf16[8,256,512]{2,1,0:T(8,128)(2,1)}, u32[]{:S(2)}) %copy-start.1) | copy-done | bytes 2097176
  12.4 3.7 %pack_spans.2 = (bf16[128,512]{1,0:T(8,128)(2,1)S(1)}, bf16[256,512]{1,0:T(8,128)(2,1)S(1)}, bf16[256,512]{1,0:T(8,128)(2,1)S(1)}, bf16[512,512]{1,0:T(8,128)(2,...) custom-call(s32[32]{0:T(128)S(1)} %copy-done.5, ...), custom_call_target="tpu_custom_call" | custom-call | tf_op jit(solution)/shard_map/pack_spans/pallas_call | solution.py:132
  16.1 3.8 %collective-permute-start.7 = (bf16[256,512]{1,0:T(8,128)(2,1)S(1)}, bf16[256,512]{1,0:T(8,128)(2,1)S(1)}, u32[]{:S(2)}, u32[]{:S(2)}) collective-permute-start(bf16[256,512]{1,0:T(8,128)(2,1)S(1)} %get-tuple-element.82), channel_id=1, source_target_pairs={{0,12},{4,8},{8,4},{12,0},{1,13},{5,9},{9,5},{13,1},{2,14},{6,10},... | collective-permute-start | bytes 786440 | tf_op jit(solution)/shard_map/spans1_3/ppermute | solution.py:460
  19.9 8.7 %attend_spans.7 = (f32[4096,128]{1,0:T(8,128)S(1)}, f32[4096,128]{1,0:T(8,128)S(1)}, f32[4096,128]{1,0:T(8,128)S(1)}) custom-call(s32[16,10]{1,0:T(8,128)S(1)} %get-tuple-element.60.refs_0_, bf16[256,2048]{1,0:T(8,128)(2,1)S(1)} %bitcast.11, bf16[256,512]{1,0:T(8,128)(2,1)S(1)} %bitcast.18, bf16[8,256,512]{2,1,0:T(8,128)(2,1)S(1)} %copy-done.2), custom_call_target="tpu_custom_call" | custom-call | flops 42949672960 | tf_op jit(solution)/shard_map/attend_spans/pallas_call | solution.py:413
  28.6 8.9 %collective-permute-start.1 = (bf16[256,512]{1,0:T(8,128)(2,1)S(1)}, bf16[256,512]{1,0:T(8,128)(2,1)S(1)}, u32[]{:S(2)}, u32[]{:S(2)}) collective-permute-start(bf16[256,512]{1,0:T(8,128)(2,1)S(1)} %get-tuple-element.67), channel_id=1, source_target_pairs={{0,8},{4,12},{8,0},{12,4},{1,9},{5,13},{9,1},{13,5},{2,10},{6,14},... | collective-permute-start | bytes 786440 | tf_op jit(solution)/shard_map/spans1_2/ppermute | solution.py:460
  37.4 17.9 %collective-permute-done.2.refs_4_ = bf16[384,512]{1,0:T(8,128)(2,1)S(1)} collective-permute-done((bf16[384,512]{1,0:T(8,128)(2,1)}, bf16[384,512]{1,0:T(8,128)(2,1)S(1)}, u32[]{:S(2)}, u32[]{:S(2)}) %collective-permute-start.2) | collective-permute-done | bytes 393248 | tf_op jit(solution)/shard_map/spans0_2/ppermute | solution.py:460
  55.3 2.7 %collective-permute-start.5 = (bf16[256,512]{1,0:T(8,128)(2,1)S(1)}, bf16[256,512]{1,0:T(8,128)(2,1)S(1)}, u32[]{:S(2)}, u32[]{:S(2)}) collective-permute-start(bf16[256,512]{1,0:T(8,128)(2,1)S(1)} %get-tuple-element.78), channel_id=1, source_target_pairs={{0,12},{4,8},{8,4},{12,0},{1,13},{5,9},{9,5},{13,1},{2,14},{6,10},... | collective-permute-start | bytes 786440 | tf_op jit(solution)/shard_map/spans2_3/ppermute | solution.py:460
  58.1 1.6 %collective-permute-start.8 = (bf16[512,512]{1,0:T(8,128)(2,1)S(1)}, bf16[512,512]{1,0:T(8,128)(2,1)S(1)}, u32[]{:S(2)}, u32[]{:S(2)}) collective-permute-start(bf16[512,512]{1,0:T(8,128)(2,1)S(1)} %pad_maximum_fusion), channel_id=1, source_target_pairs={{0,2},{1,3},{2,0},{3,1},{4,6},{5,7},{6,4},{7,5},{8,10},{9,11},{10,... | collective-permute-start | bytes 1572872 | tf_op jit(solution)/shard_map/hidden2/ppermute | solution.py:460
  59.7 7.5 %attend_spans.8 = (f32[4096,128]{1,0:T(8,128)S(1)}, f32[4096,128]{1,0:T(8,128)S(1)}, f32[4096,128]{1,0:T(8,128)S(1)}) custom-call(s32[16,10]{1,0:T(8,128)S(1)} %get-tuple-element.60.refs_0_, bf16[256,2048]{1,0:T(8,128)(2,1)S(1)} %bitcast.12, bf16[256,512]{1,0:T(8,128)(2,1)S(1)} %bitcast.19, bf16[384,512]{1,0:T(8,128)(2,1)S(1)} %collective-permute-done.refs_3_, ...), custom_call_target="tpu_custom_call" | custom-call | flops 34359738368 | tf_op jit(solution)/shard_map/attend_spans/pallas_call | solution.py:413
  67.2 5.0 %collective-permute-done.1.refs_4_ = bf16[256,512]{1,0:T(8,128)(2,1)S(1)} collective-permute-done((bf16[256,512]{1,0:T(8,128)(2,1)S(1)}, bf16[256,512]{1,0:T(8,128)(2,1)S(1)}, u32[]{:S(2)}, u32[]{:S(2)}) %collective-permute-start.1) | collective-permute-done | bytes 262176 | tf_op jit(solution)/shard_map/spans1_2/ppermute | solution.py:460
  72.2 2.7 %collective-permute-start.4 = (bf16[192,512]{1,0:T(8,128)(2,1)S(1)}, bf16[192,512]{1,0:T(8,128)(2,1)S(1)}, u32[]{:S(2)}, u32[]{:S(2)}) collective-permute-start(bf16[192,512]{1,0:T(8,128)(2,1)S(1)} %get-tuple-element.76), channel_id=1, source_target_pairs={{0,12},{4,8},{8,4},{12,0},{1,13},{5,9},{9,5},{13,1},{2,14},{6,10},... | collective-permute-start | bytes 589832 | tf_op jit(solution)/shard_map/spans3_3/ppermute | solution.py:460
  75.0 4.4 %attend_spans.9 = (f32[4096,128]{1,0:T(8,128)S(1)}, f32[4096,128]{1,0:T(8,128)S(1)}, f32[4096,128]{1,0:T(8,128)S(1)}) custom-call(s32[16,10]{1,0:T(8,128)S(1)} %get-tuple-element.60.refs_0_, bf16[256,2048]{1,0:T(8,128)(2,1)S(1)} %bitcast.13, bf16[256,512]{1,0:T(8,128)(2,1)S(1)} %bitcast.20, bf16[256,512]{1,0:T(8,128)(2,1)S(1)} %collective-permute-done.7.refs_3_, ...), custom_call_target="tpu_custom_call" | custom-call | flops 17179869184 | tf_op jit(solution)/shard_map/attend_spans/pallas_call | solution.py:413
  79.4 3.4 %collective-permute-done.6.refs_3_ = bf16[512,512]{1,0:T(8,128)(2,1)S(1)} collective-permute-done((bf16[512,512]{1,0:T(8,128)(2,1)S(1)}, bf16[512,512]{1,0:T(8,128)(2,1)S(1)}, u32[]{:S(2)}, u32[]{:S(2)}) %collective-permute-start.6) | collective-permute-done | bytes 524320 | tf_op jit(solution)/shard_map/spans1_1/ppermute | solution.py:460
  84.1 4.4 %attend_spans.10 = (f32[4096,128]{1,0:T(8,128)S(1)}, f32[4096,128]{1,0:T(8,128)S(1)}, f32[4096,128]{1,0:T(8,128)S(1)}) custom-call(s32[16,10]{1,0:T(8,128)S(1)} %get-tuple-element.60.refs_0_, bf16[256,2048]{1,0:T(8,128)(2,1)S(1)} %bitcast.14, bf16[256,512]{1,0:T(8,128)(2,1)S(1)} %bitcast.21, bf16[512,512]{1,0:T(8,128)(2,1)S(1)} %collective-permute-done.6.refs_3_, ...), custom_call_target="tpu_custom_call" | custom-call | flops 17179869184 | tf_op jit(solution)/shard_map/attend_spans/pallas_call | solution.py:413
  88.6 7.9 %collective-permute-done.10.refs_4_ = bf16[256,512]{1,0:T(8,128)(2,1)S(1)} collective-permute-done((bf16[256,512]{1,0:T(8,128)(2,1)S(1)}, bf16[256,512]{1,0:T(8,128)(2,1)S(1)}, u32[]{:S(2)}, u32[]{:S(2)}) %collective-permute-start.10) | collective-permute-done | bytes 262176 | tf_op jit(solution)/shard_map/spans2_2/ppermute | solution.py:460
  96.5 2.5 %collective-permute-start.14 = (bf16[64,512]{1,0:T(8,128)(2,1)S(1)}, bf16[64,512]{1,0:T(8,128)(2,1)S(1)}, u32[]{:S(2)}, u32[]{:S(2)}) collective-permute-start(bf16[64,512]{1,0:T(8,128)(2,1)S(1)} %get-tuple-element.112), channel_id=1, source_target_pairs={{0,12},{4,8},{8,4},{12,0},{1,13},{5,9},{9,5},{13,1},{2,14},{6,10},... | collective-permute-start | bytes 196616 | tf_op jit(solution)/shard_map/spans4_3/ppermute | solution.py:460
  99.1 2.1 %collective-permute-start.15 = (bf16[1,128,512]{2,1,0:T(8,128)(2,1)S(1)}, bf16[1,128,512]{2,1,0:T(8,128)(2,1)S(1)}, u32[]{:S(2)}, u32[]{:S(2)}) collective-permute-start(bf16[1,128,512]{2,1,0:T(8,128)(2,1)S(1)} %slice.34), channel_id=1, source_target_pairs={{0,8},{4,12},{8,0},{12,4},{1,9},{5,13},{9,1},{13,5},{2,10},{6,14},... | collective-permute-start | bytes 393224 | tf_op jit(solution)/shard_map/partial2/ppermute | solution.py:460
  101.2 4.4 %attend_spans.11 = (f32[4096,128]{1,0:T(8,128)S(1)}, f32[4096,128]{1,0:T(8,128)S(1)}, f32[4096,128]{1,0:T(8,128)S(1)}) custom-call(s32[16,10]{1,0:T(8,128)S(1)} %get-tuple-element.60.refs_0_, bf16[256,2048]{1,0:T(8,128)(2,1)S(1)} %bitcast.15, bf16[256,512]{1,0:T(8,128)(2,1)S(1)} %bitcast.22, bf16[256,512]{1,0:T(8,128)(2,1)S(1)} %collective-permute-done.5.refs_3_, ...), custom_call_target="tpu_custom_call" | custom-call | flops 17179869184 | tf_op jit(solution)/shard_map/attend_spans/pallas_call | solution.py:413
  106.6 6.4 %collective-permute-done.13.refs_4_ = bf16[192,512]{1,0:T(8,128)(2,1)S(1)} collective-permute-done((bf16[192,512]{1,0:T(8,128)(2,1)S(1)}, bf16[192,512]{1,0:T(8,128)(2,1)S(1)}, u32[]{:S(2)}, u32[]{:S(2)}) %collective-permute-start.13) | collective-permute-done | bytes 196640 | tf_op jit(solution)/shard_map/spans3_2/ppermute | solution.py:460
  112.9 3.6 %attend_spans.12 = (f32[4096,128]{1,0:T(8,128)S(1)}, f32[4096,128]{1,0:T(8,128)S(1)}, f32[4096,128]{1,0:T(8,128)S(1)}) custom-call(s32[16,10]{1,0:T(8,128)S(1)} %get-tuple-element.60.refs_0_, bf16[256,2048]{1,0:T(8,128)(2,1)S(1)} %bitcast.16, bf16[256,512]{1,0:T(8,128)(2,1)S(1)} %bitcast.23, bf16[192,512]{1,0:T(8,128)(2,1)S(1)} %collective-permute-done.4.refs_3_, ...), custom_call_target="tpu_custom_call" | custom-call | flops 12884901888 | tf_op jit(solution)/shard_map/attend_spans/pallas_call | solution.py:413
  116.6 1.8 %collective-permute-done.12.refs_3_ = bf16[64,512]{1,0:T(8,128)(2,1)S(1)} collective-permute-done((bf16[64,512]{1,0:T(8,128)(2,1)S(1)}, bf16[64,512]{1,0:T(8,128)(2,1)S(1)}, u32[]{:S(2)}, u32[]{:S(2)}) %collective-permute-start.12) | collective-permute-done | bytes 65568 | tf_op jit(solution)/shard_map/spans4_2/ppermute | solution.py:460
  118.5 3.4 %attend_spans.13 = (bf16[256,2048]{1,0:T(8,128)(2,1)}, bf16[128,512]{1,0:T(8,128)(2,1)}) custom-call(s32[16,10]{1,0:T(8,128)S(1)} %get-tuple-element.60.refs_0_, bf16[256,2048]{1,0:T(8,128)(2,1)S(1)} %bitcast.17, bf16[256,512]{1,0:T(8,128)(2,1)S(1)} %bitcast.24, bf16[64,512]{1,0:T(8,128)(2,1)S(1)} %collective-permute-done.12.refs_3_, ...), custom_call_target="tpu_custom_call" | custom-call | flops 8589934592 | tf_op jit(solution)/shard_map/attend_spans/pallas_call | solution.py:413
  (44 shorter events, 4.1 us)
Async XLA Ops:
  0.6 10.1 %copy-start = (bf16[1,16,8,8192]{3,2,1,0:T(8,128)(2,1)S(1)}, bf16[1,16,8,8192]{3,2,1,0:T(8,128)(2,1)}, u32[]{:S(2)}) copy-start(bf16[1,16,8,8192]{3,2,1,0:T(8,128)(2,1)} %param.14) | copy-start | bytes 6291460
  0.6 10.1 %copy-start.4 = (s32[4,16]{1,0:T(4,128)S(1)}, s32[4,16]{1,0:T(4,128)}, u32[]{:S(2)}) copy-start(s32[4,16]{1,0:T(4,128)} %refs_1_.3) | copy-start | bytes 772
  0.7 10.1 %copy-start.5 = (s32[32]{0:T(128)S(1)}, s32[32]{0:T(128)}, u32[]{:S(2)}) copy-start(s32[32]{0:T(128)} %refs_0_.3) | copy-start | bytes 388
  4.3 24.3 %collective-permute-start = (bf16[384,512]{1,0:T(8,128)(2,1)}, bf16[384,512]{1,0:T(8,128)(2,1)S(1)}, u32[]{:S(2)}, u32[]{:S(2)}) collective-permute-start(bf16[384,512]{1,0:T(8,128)(2,1)} %get-tuple-element.64), channel_id=1, source_target_pairs={{0,12},{4,8},{8,4},{12,0},{1,13},{5,9},{9,5},{13,1},{2,14},{6,10},... | collective-permute-start | bytes 1179656 | tf_op jit(solution)/shard_map/spans0_3/ppermute | solution.py:460
  9.4 46.0 %collective-permute-start.2 = (bf16[384,512]{1,0:T(8,128)(2,1)}, bf16[384,512]{1,0:T(8,128)(2,1)S(1)}, u32[]{:S(2)}, u32[]{:S(2)}) collective-permute-start(bf16[384,512]{1,0:T(8,128)(2,1)} %get-tuple-element.68), channel_id=1, source_target_pairs={{0,8},{4,12},{8,0},{12,4},{1,9},{5,13},{9,1},{13,5},{2,10},{6,14},... | collective-permute-start | bytes 1179656 | tf_op jit(solution)/shard_map/spans0_2/ppermute | solution.py:460
  9.4 48.6 %collective-permute-start.3 = (bf16[640,512]{1,0:T(8,128)(2,1)}, bf16[640,512]{1,0:T(8,128)(2,1)S(1)}, u32[]{:S(2)}, u32[]{:S(2)}) collective-permute-start(bf16[640,512]{1,0:T(8,128)(2,1)} %get-tuple-element.70), channel_id=1, source_target_pairs={{0,4},{4,0},{8,12},{12,8},{1,5},{5,1},{9,13},{13,9},{2,6},{6,2},{1... | collective-permute-start | bytes 1966088 | tf_op jit(solution)/shard_map/spans0_1/ppermute | solution.py:460
  10.8 1.6 %copy-start.1 = (bf16[8,256,512]{2,1,0:T(8,128)(2,1)S(1)}, bf16[8,256,512]{2,1,0:T(8,128)(2,1)}, u32[]{:S(2)}) copy-start(bf16[8,256,512]{2,1,0:T(8,128)(2,1)} %refs_3_.1) | copy-start | bytes 6291460
  12.4 7.5 %copy-start.2 = (bf16[8,256,512]{2,1,0:T(8,128)(2,1)S(1)}, bf16[8,256,512]{2,1,0:T(8,128)(2,1)}, u32[]{:S(2)}) copy-start(bf16[8,256,512]{2,1,0:T(8,128)(2,1)} %refs_3_.1) | copy-start | bytes 6291460
  12.4 7.5 %copy-start.6 = (bf16[1,256,2048]{2,1,0:T(8,128)(2,1)S(1)}, bf16[1,256,2048]{2,1,0:T(8,128)(2,1)}, u32[]{:S(2)}) copy-start(bf16[1,256,2048]{2,1,0:T(8,128)(2,1)} %param.8) | copy-start | bytes 3145732
  12.4 7.5 %copy-start.7 = (bf16[1,256,512]{2,1,0:T(8,128)(2,1)S(1)}, bf16[1,256,512]{2,1,0:T(8,128)(2,1)}, u32[]{:S(2)}) copy-start(bf16[1,256,512]{2,1,0:T(8,128)(2,1)} %param.9) | copy-start | bytes 786436
  16.1 58.8 %collective-permute-start.7 = (bf16[256,512]{1,0:T(8,128)(2,1)S(1)}, bf16[256,512]{1,0:T(8,128)(2,1)S(1)}, u32[]{:S(2)}, u32[]{:S(2)}) collective-permute-start(bf16[256,512]{1,0:T(8,128)(2,1)S(1)} %get-tuple-element.82), channel_id=1, source_target_pairs={{0,12},{4,8},{8,4},{12,0},{1,13},{5,9},{9,5},{13,1},{2,14},{6,10},... | collective-permute-start | bytes 786440 | tf_op jit(solution)/shard_map/spans1_3/ppermute | solution.py:460
  28.6 43.6 %collective-permute-start.1 = (bf16[256,512]{1,0:T(8,128)(2,1)S(1)}, bf16[256,512]{1,0:T(8,128)(2,1)S(1)}, u32[]{:S(2)}, u32[]{:S(2)}) collective-permute-start(bf16[256,512]{1,0:T(8,128)(2,1)S(1)} %get-tuple-element.67), channel_id=1, source_target_pairs={{0,8},{4,12},{8,0},{12,4},{1,9},{5,13},{9,1},{13,5},{2,10},{6,14},... | collective-permute-start | bytes 786440 | tf_op jit(solution)/shard_map/spans1_2/ppermute | solution.py:460
  55.3 33.3 %collective-permute-start.5 = (bf16[256,512]{1,0:T(8,128)(2,1)S(1)}, bf16[256,512]{1,0:T(8,128)(2,1)S(1)}, u32[]{:S(2)}, u32[]{:S(2)}) collective-permute-start(bf16[256,512]{1,0:T(8,128)(2,1)S(1)} %get-tuple-element.78), channel_id=1, source_target_pairs={{0,12},{4,8},{8,4},{12,0},{1,13},{5,9},{9,5},{13,1},{2,14},{6,10},... | collective-permute-start | bytes 786440 | tf_op jit(solution)/shard_map/spans2_3/ppermute | solution.py:460
  58.0 24.8 %collective-permute-start.6 = (bf16[512,512]{1,0:T(8,128)(2,1)S(1)}, bf16[512,512]{1,0:T(8,128)(2,1)S(1)}, u32[]{:S(2)}, u32[]{:S(2)}) collective-permute-start(bf16[512,512]{1,0:T(8,128)(2,1)S(1)} %get-tuple-element.80), channel_id=1, source_target_pairs={{0,4},{4,0},{8,12},{12,8},{1,5},{5,1},{9,13},{13,9},{2,6},{6,2},{1... | collective-permute-start | bytes 1572872 | tf_op jit(solution)/shard_map/spans1_1/ppermute | solution.py:460
  58.1 16.7 %collective-permute-start.8 = (bf16[512,512]{1,0:T(8,128)(2,1)S(1)}, bf16[512,512]{1,0:T(8,128)(2,1)S(1)}, u32[]{:S(2)}, u32[]{:S(2)}) collective-permute-start(bf16[512,512]{1,0:T(8,128)(2,1)S(1)} %pad_maximum_fusion), channel_id=1, source_target_pairs={{0,2},{1,3},{2,0},{3,1},{4,6},{5,7},{6,4},{7,5},{8,10},{9,11},{10,... | collective-permute-start | bytes 1572872 | tf_op jit(solution)/shard_map/hidden2/ppermute | solution.py:460
  72.2 33.4 %collective-permute-start.4 = (bf16[192,512]{1,0:T(8,128)(2,1)S(1)}, bf16[192,512]{1,0:T(8,128)(2,1)S(1)}, u32[]{:S(2)}, u32[]{:S(2)}) collective-permute-start(bf16[192,512]{1,0:T(8,128)(2,1)S(1)} %get-tuple-element.76), channel_id=1, source_target_pairs={{0,12},{4,8},{8,4},{12,0},{1,13},{5,9},{9,5},{13,1},{2,14},{6,10},... | collective-permute-start | bytes 589832 | tf_op jit(solution)/shard_map/spans3_3/ppermute | solution.py:460
  74.8 21.7 %collective-permute-start.10 = (bf16[256,512]{1,0:T(8,128)(2,1)S(1)}, bf16[256,512]{1,0:T(8,128)(2,1)S(1)}, u32[]{:S(2)}, u32[]{:S(2)}) collective-permute-start(bf16[256,512]{1,0:T(8,128)(2,1)S(1)} %get-tuple-element.95), channel_id=1, source_target_pairs={{0,8},{4,12},{8,0},{12,4},{1,9},{5,13},{9,1},{13,5},{2,10},{6,14},... | collective-permute-start | bytes 786440 | tf_op jit(solution)/shard_map/spans2_2/ppermute | solution.py:460
  74.9 7.9 %collective-permute-start.9 = (bf16[1024,512]{1,0:T(8,128)(2,1)S(1)}, bf16[1024,512]{1,0:T(8,128)(2,1)S(1)}, u32[]{:S(2)}, u32[]{:S(2)}) collective-permute-start(bf16[1024,512]{1,0:T(8,128)(2,1)S(1)} %constant_dynamic-update-slice_fusion.refs_0_), channel_id=1, source_target_pairs={{0,1},{1,0},{2,3},{3,2},{4,5},{5,4},{6,7},{7,6},{8,9},{9,8},{10,11... | collective-permute-start | bytes 3145736 | tf_op jit(solution)/shard_map/hidden1/ppermute | solution.py:460
  75.0 7.8 %copy-start.3 = (bf16[2048,512]{1,0:T(8,128)(2,1)S(1)}, bf16[2048,512]{1,0:T(8,128)(2,1)}, u32[]{:S(2)}) copy-start(bf16[2048,512]{1,0:T(8,128)(2,1)} %refs_2_.5) | copy-start | bytes 6291460
  84.1 14.9 %collective-permute-start.11 = (bf16[2,128,512]{2,1,0:T(8,128)(2,1)S(1)}, bf16[2,128,512]{2,1,0:T(8,128)(2,1)S(1)}, u32[]{:S(2)}, u32[]{:S(2)}) collective-permute-start(bf16[2,128,512]{2,1,0:T(8,128)(2,1)S(1)} %get-tuple-element.88), channel_id=1, source_target_pairs={{0,4},{4,0},{8,12},{12,8},{1,5},{5,1},{9,13},{13,9},{2,6},{6,2},{1... | collective-permute-start | bytes 786440 | tf_op jit(solution)/shard_map/partial1/ppermute | solution.py:460
  96.5 16.4 %collective-permute-start.13 = (bf16[192,512]{1,0:T(8,128)(2,1)S(1)}, bf16[192,512]{1,0:T(8,128)(2,1)S(1)}, u32[]{:S(2)}, u32[]{:S(2)}) collective-permute-start(bf16[192,512]{1,0:T(8,128)(2,1)S(1)} %get-tuple-element.105), channel_id=1, source_target_pairs={{0,8},{4,12},{8,0},{12,4},{1,9},{5,13},{9,1},{13,5},{2,10},{6,14},... | collective-permute-start | bytes 589832 | tf_op jit(solution)/shard_map/spans3_2/ppermute | solution.py:460
  96.5 20.1 %collective-permute-start.14 = (bf16[64,512]{1,0:T(8,128)(2,1)S(1)}, bf16[64,512]{1,0:T(8,128)(2,1)S(1)}, u32[]{:S(2)}, u32[]{:S(2)}) collective-permute-start(bf16[64,512]{1,0:T(8,128)(2,1)S(1)} %get-tuple-element.112), channel_id=1, source_target_pairs={{0,12},{4,8},{8,4},{12,0},{1,13},{5,9},{9,5},{13,1},{2,14},{6,10},... | collective-permute-start | bytes 196616 | tf_op jit(solution)/shard_map/spans4_3/ppermute | solution.py:460
  99.1 19.4 %collective-permute-start.15 = (bf16[1,128,512]{2,1,0:T(8,128)(2,1)S(1)}, bf16[1,128,512]{2,1,0:T(8,128)(2,1)S(1)}, u32[]{:S(2)}, u32[]{:S(2)}) collective-permute-start(bf16[1,128,512]{2,1,0:T(8,128)(2,1)S(1)} %slice.34), channel_id=1, source_target_pairs={{0,8},{4,12},{8,0},{12,4},{1,9},{5,13},{9,1},{13,5},{2,10},{6,14},... | collective-permute-start | bytes 393224 | tf_op jit(solution)/shard_map/partial2/ppermute | solution.py:460
  105.6 12.9 %collective-permute-start.12 = (bf16[64,512]{1,0:T(8,128)(2,1)S(1)}, bf16[64,512]{1,0:T(8,128)(2,1)S(1)}, u32[]{:S(2)}, u32[]{:S(2)}) collective-permute-start(bf16[64,512]{1,0:T(8,128)(2,1)S(1)} %get-tuple-element.103), channel_id=1, source_target_pairs={{0,8},{4,12},{8,0},{12,4},{1,9},{5,13},{9,1},{13,5},{2,10},{6,14},... | collective-permute-start | bytes 196616 | tf_op jit(solution)/shard_map/spans4_2/ppermute | solution.py:460
